TPU v7x, 32 devices: a whole 2x2x4 slice. The times are simulated.
32 devices in a mesh: slab: 2 (over y), docs: 4 (over x, core), blk: 4 (over z).
Axes of the slice: x: 2, y: 2, z: 4, core: 2. Of those that a mesh axis runs over, the one named last changes fastest.
Arguments:
- pooled: bfloat16 [16384, 768], P(('slab', 'docs', 'blk')), parts along dimension 0, may hold values from -6 to 6
- proj_weight: bfloat16 [768, 768], replicated, may hold values from -0.21875 to 0.21875
- cluster: int32 [16384], P(('slab', 'docs', 'blk')), parts along dimension 0, may hold values from 0 to 143, as said below
Outputs:
- best_sim: float32 [16384], P(('slab', 'docs', 'blk')), parts along dimension 0
There are 2 independent parts, one for each index of `slab`. A program takes and returns all parts, laid end to end along the dimension named above; an argument that names none is the same for every part. Nothing has to cross between parts.
Inputs may be any that keep to these rules, and one draw needn't show every extreme that they name: Clusters below 16 are large, the others small. The documents of one device hold exactly 128 of large clusters and 384 of small ones. Among one device's documents at most 64 of large clusters share the value of cluster modulo the size of docs, and at most 48 of small clusters share the value of (cluster - 16) modulo the number of devices of docs and blk; in every draw one value of each kind holds exactly that many on every device.
All inputs are finite; a program needn't handle non-finite values.
Results may differ from a plain program's by a relative error of at most 0.0012.
Values may be sent and summed in bfloat16 or wider, within the bound.
No kernel may reach another device: no remote copies, remote signals or barrier semaphores. Data moves between devices by JAX's collectives and lax.ppermute only.
A program may use at most 64 MiB of HBM per device.

v0:
```python
import jax
import jax.numpy as jnp
from jax import lax
from jax.sharding import PartitionSpec as P

BIG_OWN = 4


def passed_along(shard, axis, by):
    count = lax.axis_size(axis)
    return lax.ppermute(shard, axis, [(i, (i + by) % count) for i in range(count)])


def score_block(queries, others):
    return lax.dot_general(
        queries, others, (((1,), (1,)), ((), ())), preferred_element_type=jnp.float32
    )


def masked_max(queries, query_ids, others, other_ids, query_pos, other_pos):
    scores = score_block(queries, others)
    allowed = (
        (query_ids[:, None] == other_ids[None, :])
        & (query_ids[:, None] >= 0)
        & (query_pos[:, None] != other_pos[None, :])
    )
    return jnp.max(jnp.where(allowed, scores, -1.0), axis=1)


def body(pooled, proj_weight, cluster):
    shards = lax.axis_size("docs")
    blocks = lax.axis_size("blk")
    doc_rows = pooled.shape[0]
    feature = proj_weight.shape[1]
    big_count = doc_rows // 4
    small_count = doc_rows - big_count
    cap_big = 2 * big_count // shards
    cap_small = 2 * small_count // (shards * blocks)
    projected = jnp.dot(pooled, proj_weight, preferred_element_type=jnp.float32)
    embedded = (
        projected / jnp.sqrt(jnp.sum(projected * projected, axis=1, keepdims=True) + 1e-06)
    ).astype(jnp.bfloat16)
    large_limit = BIG_OWN * shards
    is_big = cluster < large_limit
    big_owner = cluster % shards
    small_target = (cluster - large_limit) % (shards * blocks)
    bucket = jnp.where(is_big, big_owner, shards + small_target)
    buckets = shards + shards * blocks
    onehot = (bucket[:, None] == jnp.arange(buckets, dtype=jnp.int32)[None, :]).astype(jnp.int32)
    before = jnp.cumsum(onehot, axis=0) - onehot
    slot_rank = jnp.sum(before * onehot, axis=1)
    big_slot = jnp.where(is_big, big_owner * cap_big + slot_rank, shards * cap_big)
    small_slot = jnp.where(
        is_big, shards * blocks * cap_small, small_target * cap_small + slot_rank
    )
    send_big = (
        jnp.zeros((shards * cap_big, feature), jnp.bfloat16)
        .at[big_slot]
        .set(embedded, mode="drop")
        .reshape(shards, cap_big, feature)
    )
    big_ids = (
        jnp.full((shards * cap_big,), -1, jnp.int32)
        .at[big_slot]
        .set(cluster, mode="drop")
        .reshape(shards, cap_big)
    )
    send_small = (
        jnp.zeros((shards * blocks * cap_small, feature), jnp.bfloat16)
        .at[small_slot]
        .set(embedded, mode="drop")
    )
    small_ids = (
        jnp.full((shards * blocks * cap_small,), -1, jnp.int32)
        .at[small_slot]
        .set(cluster, mode="drop")
    )
    got_big, got_big_ids = (
        lax.all_to_all(send_big, "docs", split_axis=0, concat_axis=0, tiled=True),
        lax.all_to_all(big_ids, "docs", split_axis=0, concat_axis=0, tiled=True),
    )
    group_mine = got_big.reshape(-1, feature)
    group_ids = got_big_ids.reshape(-1)
    group_count = group_mine.shape[0]
    got_small, got_small_ids = (
        lax.all_to_all(
            send_small.reshape(shards * blocks, cap_small, feature),
            ("docs", "blk"),
            split_axis=0,
            concat_axis=0,
            tiled=True,
        ),
        lax.all_to_all(
            small_ids.reshape(shards * blocks, cap_small),
            ("docs", "blk"),
            split_axis=0,
            concat_axis=0,
            tiled=True,
        ),
    )
    small_rows = got_small.reshape(-1, feature)
    small_row_ids = got_small_ids.reshape(-1)
    small_total = small_rows.shape[0]
    small_pos = jnp.arange(small_total, dtype=jnp.int32)
    block_size = min(512, small_total)
    small_parts = []
    for first_row in range(0, small_total, block_size):
        last_row = min(first_row + block_size, small_total)
        small_parts.append(
            masked_max(
                small_rows[first_row:last_row],
                small_row_ids[first_row:last_row],
                small_rows,
                small_row_ids,
                small_pos[first_row:last_row],
                small_pos,
            )
        )
    best_small = jnp.concatenate(small_parts)
    local_pos = jnp.arange(group_count, dtype=jnp.int32)
    best_big = masked_max(group_mine, group_ids, group_mine, group_ids, local_pos, local_pos)
    for distance in range(1, blocks // 2 + 1):
        others, other_ids = passed_along((group_mine, group_ids), "blk", distance)
        scores = score_block(group_mine, others)
        allowed = (group_ids[:, None] == other_ids[None, :]) & (group_ids[:, None] >= 0)
        masked = jnp.where(allowed, scores, -1.0)
        best_big = jnp.maximum(best_big, jnp.max(masked, axis=1))
        column_best = jnp.max(masked, axis=0)
        returned = passed_along(column_best, "blk", -distance)
        best_big = jnp.maximum(best_big, returned)
    big_return = lax.all_to_all(
        best_big.reshape(shards, cap_big), "docs", split_axis=0, concat_axis=0, tiled=True
    ).reshape(-1)
    small_return = lax.all_to_all(
        best_small.reshape(shards * blocks, cap_small),
        ("docs", "blk"),
        split_axis=0,
        concat_axis=0,
        tiled=True,
    ).reshape(-1)
    from_big = big_return[jnp.minimum(big_slot, shards * cap_big - 1)]
    from_small = small_return[jnp.minimum(small_slot, shards * blocks * cap_small - 1)]
    return jnp.where(is_big, from_big, from_small)


def solution(mesh):
    in_specs = (P(("slab", "docs", "blk"), None), P(), P(("slab", "docs", "blk")))
    out_specs = P(("slab", "docs", "blk"))
    return jax.shard_map(body, mesh=mesh, in_specs=in_specs, out_specs=out_specs, check_vma=False)
```

profile of v0, /device:TPU:1, one launch (start us, length us, event | category | flops | bytes accessed | tf_op | source)
XLA Modules:
  0.0 124.2 jit_solution(11843956203275217251)
XLA Ops:
  0.0 0.0 copy-start
  0.0 0.8 add_select_fusion.4
  0.8 1.2 reduce-window.6
  2.0 0.2 slice_reduce_fusion
  2.2 0.1 broadcast_add_fusion
  2.4 0.7 compare_select_fusion
  3.1 2.6 %scatter_custom_fusion = s32[256]{0:T(256)S(1)} fusion(s32[512]{0:T(512)S(1)} %get-tuple-element.14, s32[512]{0:T(512)} %param.5, s32[]{:T(128)} %constant.21.clone.1), kind=kCustom, calls=%fused_computation.65 | custom fusion | bytes 1536 | tf_op jit(solution)/shard_map/scatter | solution.py:65
  5.7 0.7 all_to_all.30
  6.4 4.3 %all-to-all-start = ((s32[4,1,64]{2,1,0:T(1,128)}), s32[4,1,64]{2,1,0:T(1,128)S(1)}, u32[]{:S(2)}, u32[]{:S(2)}) async-start(s32[4,1,64]{2,1,0:T(1,128)} %all_to_all.30), calls=%async_computation | async-start | bytes 4096 | tf_op jit(solution)/shard_map/all_to_all | solution.py:80
  10.6 0.0 copy-done
  10.6 2.0 %multiply_reduce_fusion = (f32[512]{0:T(512)S(1)}, f32[512,768]{1,0:T(8,128)S(1)}) fusion(bf16[512,768]{1,0:T(8,128)(2,1)} %param.3, bf16[768,768]{1,0:T(8,128)(2,1)S(1)} %copy-done), kind=kOutput, calls=%fused_computation.9 | convolution fusion | flops 604765696 | bytes 3540992 | tf_op jit(solution)/shard_map/dot_general | solution.py:39
  12.6 2.6 %scatter_custom_fusion.2 = s32[768]{0:T(1024)S(1)} fusion(s32[512]{0:T(512)S(1)} %get-tuple-element.16, s32[512]{0:T(512)} %param.5, s32[]{:T(128)} %constant.21.clone.1), kind=kCustom, calls=%fused_computation.55 | custom fusion | bytes 3584 | tf_op jit(solution)/shard_map/scatter | solution.py:76
  15.2 0.7 all_to_all.35
  15.9 0.0 all-to-all-done
  15.9 6.8 %all-to-all-start.3 = ((s32[16,1,48]{2,1,0:T(1,128)}), s32[16,1,48]{2,1,0:T(1,128)S(1)}, u32[]{:S(2)}, u32[]{:S(2)}) async-start(s32[16,1,48]{2,1,0:T(1,128)} %all_to_all.35), calls=%async_computation.3 | async-start | bytes 16384 | tf_op jit(solution)/shard_map/all_to_all | solution.py:93
  22.7 3.4 %scatter_custom_fusion.1 = bf16[256,768]{1,0:T(8,128)(2,1)} fusion(s32[512]{0:T(512)S(1)} %get-tuple-element.14, bf16[]{:T(256)} %constant.57.clone.1, f32[512,768]{1,0:T(8,128)S(1)} %get-tuple-element.18, f32[512]{0:T(512)S(1)} %add_sqrt_fusion), kind=kCustom, calls=%fused_computation.29 | custom fusion | flops 786432 | bytes 1968130 | tf_op jit(solution)/shard_map/scatter | solution.py:59
  26.1 2.4 %all-to-all-done.3 = s32[16,1,48]{2,1,0:T(1,128)S(1)} async-done(((s32[16,1,48]{2,1,0:T(1,128)}), s32[16,1,48]{2,1,0:T(1,128)S(1)}, u32[]{:S(2)}, u32[]{:S(2)}) %all-to-all-start.3) | async-done | bytes 3104 | tf_op jit(solution)/shard_map/all_to_all | solution.py:93
  28.5 4.1 %all-to-all-start.1 = ((bf16[4,64,768]{2,1,0:T(8,128)(2,1)}), bf16[4,64,768]{2,1,0:T(8,128)(2,1)S(1)}, u32[]{:S(2)}, u32[]{:S(2)}) async-start(bf16[4,64,768]{2,1,0:T(8,128)(2,1)} %bitcast.2), calls=%async_computation.1 | async-start | bytes 786432 | tf_op jit(solution)/shard_map/all_to_all | solution.py:79
  32.6 3.6 %scatter_custom_fusion.3 = bf16[768,768]{1,0:T(8,128)(2,1)} fusion(s32[512]{0:T(512)S(1)} %get-tuple-element.16, bf16[]{:T(256)} %constant.57.clone.1, f32[512,768]{1,0:T(8,128)S(1)} %get-tuple-element.18, f32[512]{0:T(512)S(1)} %add_sqrt_fusion), kind=kCustom, calls=%fused_computation.18 | custom fusion | flops 786432 | bytes 2754562 | tf_op jit(solution)/shard_map/scatter | solution.py:71
  36.2 2.9 %all-to-all-done.1 = bf16[4,64,768]{2,1,0:T(8,128)(2,1)S(1)} async-done(((bf16[4,64,768]{2,1,0:T(8,128)(2,1)}), bf16[4,64,768]{2,1,0:T(8,128)(2,1)S(1)}, u32[]{:S(2)}, u32[]{:S(2)}) %all-to-all-start.1) | async-done | bytes 393248 | tf_op jit(solution)/shard_map/all_to_all | solution.py:79
  39.2 4.4 %all-to-all-start.4 = ((bf16[16,48,768]{2,1,0:T(8,128)(2,1)}), bf16[16,48,768]{2,1,0:T(8,128)(2,1)S(1)}, u32[]{:S(2)}, u32[]{:S(2)}) async-start(bf16[16,48,768]{2,1,0:T(8,128)(2,1)} %bitcast.24), calls=%async_computation.4 | async-start | bytes 2359296 | tf_op jit(solution)/shard_map/all_to_all | solution.py:86
  43.6 0.0 copy-start.1
  43.6 0.5 broadcast.121
  44.1 0.7 reduce.14
  44.8 0.1 eq.96
  44.9 1.4 %collective-permute-start = (s32[256]{0:T(256)S(1)}, s32[256]{0:T(256)S(1)}, u32[]{:S(2)}, u32[]{:S(2)}) collective-permute-start(s32[256]{0:T(256)S(1)} %eq.96), channel_id=1, source_target_pairs={{0,1},{1,2},{2,3},{3,0},{4,5},{5,6},{6,7},{7,4},{8,9},{9,10},{10,1... | collective-permute-start | bytes 3080 | tf_op jit(solution)/shard_map/ppermute | solution.py:11
  46.2 2.1 %collective-permute-start.3 = (s32[256]{0:T(256)S(1)}, s32[256]{0:T(256)S(1)}, u32[]{:S(2)}, u32[]{:S(2)}) collective-permute-start(s32[256]{0:T(256)S(1)} %eq.96), channel_id=1, source_target_pairs={{0,2},{1,3},{2,0},{3,1},{4,6},{5,7},{6,4},{7,5},{8,10},{9,11},{10,... | collective-permute-start | bytes 3080 | tf_op jit(solution)/shard_map/ppermute | solution.py:11
  48.3 0.7 reduce.16
  49.0 0.1 reshape.92
  49.1 0.3 collective-permute-start.4
  49.4 1.2 collective-permute-start.1
  50.6 46.8 %collective-permute-done.4 = bf16[256,768]{1,0:T(8,128)(2,1)S(1)} collective-permute-done((bf16[256,768]{1,0:T(8,128)(2,1)S(1)}, bf16[256,768]{1,0:T(8,128)(2,1)S(1)}, u32[]{:S(2)}, u32[]{:S(2)}) %collective-permute-start.4) | collective-permute-done | bytes 393248 | tf_op jit(solution)/shard_map/ppermute | solution.py:11
  97.5 0.3 fusion.24
  97.8 0.0 collective-permute-done
  97.8 0.0 collective-permute-done.3
  97.8 0.0 collective-permute-done.1
  97.8 0.4 fusion.10
  98.3 0.0 copy-done.1
  98.3 0.2 collective-permute-start.5
  98.5 0.2 collective-permute-start.2
  98.7 0.3 fusion.2
  99.0 2.7 %collective-permute-done.5 = f32[256]{0:T(256)S(1)} collective-permute-done((f32[256]{0:T(256)S(1)}, f32[256]{0:T(256)S(1)}, u32[]{:S(2)}, u32[]{:S(2)}) %collective-permute-start.5) | collective-permute-done | bytes 1056 | tf_op jit(solution)/shard_map/ppermute | solution.py:11
  101.7 0.0 collective-permute-done.2
  101.7 0.7 all_to_all.33
  102.3 0.0 all-to-all-done.4
  102.3 5.2 %all-to-all-start.2 = ((f32[4,1,64]{2,1,0:T(1,128)}), f32[4,1,64]{2,1,0:T(1,128)S(1)}, u32[]{:S(2)}, u32[]{:S(2)}) async-start(f32[4,1,64]{2,1,0:T(1,128)} %all_to_all.33), calls=%async_computation.2 | async-start | bytes 4096 | tf_op jit(solution)/shard_map/all_to_all | solution.py:131
  107.5 0.0 slice-start
  107.5 0.6 fusion.1
  108.2 0.0 slice-done
  108.2 1.1 select_reduce_fusion
  109.3 0.7 all_to_all.38
  110.0 0.6 all-to-all-done.2
  110.5 4.2 %all-to-all-start.5 = ((f32[16,1,48]{2,1,0:T(1,128)}), f32[16,1,48]{2,1,0:T(1,128)S(1)}, u32[]{:S(2)}, u32[]{:S(2)}) async-start(f32[16,1,48]{2,1,0:T(1,128)} %all_to_all.38), calls=%async_computation.5 | async-start | bytes 16384 | tf_op jit(solution)/shard_map/all_to_all | solution.py:134
  114.8 0.5 broadcast.122
  115.3 0.7 reduce.15
  115.9 0.1 reshape.91
  116.0 3.5 %gather_fusion = f32[512]{0:T(512)S(1)} fusion(f32[256]{0:T(256)S(1)} %reshape.91, s32[1024]{0:T(1024)S(1)} %get-tuple-element.20), kind=kCustom, calls=%fused_computation | custom fusion | bytes 6144 | tf_op jit(solution)/shard_map/gather | solution.py:141
  119.5 1.0 all-to-all-done.5
  120.5 0.7 reduce.17
  121.2 0.1 reshape.95
  121.3 2.3 %gather_fusion.1 = f32[512]{0:T(512)S(1)} fusion(f32[768]{0:T(1024)S(1)} %reshape.95, s32[1024]{0:T(1024)S(1)} %get-tuple-element.19), kind=kCustom, calls=%fused_computation.1 | custom fusion | bytes 6144 | tf_op jit(solution)/shard_map/gather | solution.py:142
  123.6 0.6 select_n.73
  (19 shorter events, 0.2 us)
Async XLA Ops:
  0.0 10.6 %copy-start = (bf16[768,768]{1,0:T(8,128)(2,1)S(1)}, bf16[768,768]{1,0:T(8,128)(2,1)}, u32[]{:S(2)}) copy-start(bf16[768,768]{1,0:T(8,128)(2,1)} %param.4) | copy-start | bytes 3538948
  6.4 9.6 %all-to-all-start = ((s32[4,1,64]{2,1,0:T(1,128)}), s32[4,1,64]{2,1,0:T(1,128)S(1)}, u32[]{:S(2)}, u32[]{:S(2)}) async-start(s32[4,1,64]{2,1,0:T(1,128)} %all_to_all.30), calls=%async_computation | async-start | bytes 4096 | tf_op jit(solution)/shard_map/all_to_all | solution.py:80
  15.9 12.6 %all-to-all-start.3 = ((s32[16,1,48]{2,1,0:T(1,128)}), s32[16,1,48]{2,1,0:T(1,128)S(1)}, u32[]{:S(2)}, u32[]{:S(2)}) async-start(s32[16,1,48]{2,1,0:T(1,128)} %all_to_all.35), calls=%async_computation.3 | async-start | bytes 16384 | tf_op jit(solution)/shard_map/all_to_all | solution.py:93
  28.5 10.7 %all-to-all-start.1 = ((bf16[4,64,768]{2,1,0:T(8,128)(2,1)}), bf16[4,64,768]{2,1,0:T(8,128)(2,1)S(1)}, u32[]{:S(2)}, u32[]{:S(2)}) async-start(bf16[4,64,768]{2,1,0:T(8,128)(2,1)} %bitcast.2), calls=%async_computation.1 | async-start | bytes 786432 | tf_op jit(solution)/shard_map/all_to_all | solution.py:79
  39.2 63.2 %all-to-all-start.4 = ((bf16[16,48,768]{2,1,0:T(8,128)(2,1)}), bf16[16,48,768]{2,1,0:T(8,128)(2,1)S(1)}, u32[]{:S(2)}, u32[]{:S(2)}) async-start(bf16[16,48,768]{2,1,0:T(8,128)(2,1)} %bitcast.24), calls=%async_computation.4 | async-start | bytes 2359296 | tf_op jit(solution)/shard_map/all_to_all | solution.py:86
  43.6 54.7 %copy-start.1 = (s32[768]{0:T(1024)}, s32[768]{0:T(1024)S(1)}, u32[]{:S(2)}) copy-start(s32[768]{0:T(1024)S(1)} %iota.24) | copy-start | bytes 9220
  44.9 52.9 %collective-permute-start = (s32[256]{0:T(256)S(1)}, s32[256]{0:T(256)S(1)}, u32[]{:S(2)}, u32[]{:S(2)}) collective-permute-start(s32[256]{0:T(256)S(1)} %eq.96), channel_id=1, source_target_pairs={{0,1},{1,2},{2,3},{3,0},{4,5},{5,6},{6,7},{7,4},{8,9},{9,10},{10,1... | collective-permute-start | bytes 3080 | tf_op jit(solution)/shard_map/ppermute | solution.py:11
  46.2 51.6 %collective-permute-start.3 = (s32[256]{0:T(256)S(1)}, s32[256]{0:T(256)S(1)}, u32[]{:S(2)}, u32[]{:S(2)}) collective-permute-start(s32[256]{0:T(256)S(1)} %eq.96), channel_id=1, source_target_pairs={{0,2},{1,3},{2,0},{3,1},{4,6},{5,7},{6,4},{7,5},{8,10},{9,11},{10,... | collective-permute-start | bytes 3080 | tf_op jit(solution)/shard_map/ppermute | solution.py:11
  49.1 48.4 %collective-permute-start.4 = (bf16[256,768]{1,0:T(8,128)(2,1)S(1)}, bf16[256,768]{1,0:T(8,128)(2,1)S(1)}, u32[]{:S(2)}, u32[]{:S(2)}) collective-permute-start(bf16[256,768]{1,0:T(8,128)(2,1)S(1)} %bitcast.25), channel_id=1, source_target_pairs={{0,2},{1,3},{2,0},{3,1},{4,6},{5,7},{6,4},{7,5},{8,10},{9,11},{10,... | collective-permute-start | bytes 1179656 | tf_op jit(solution)/shard_map/ppermute | solution.py:11
  49.4 48.4 %collective-permute-start.1 = (bf16[256,768]{1,0:T(8,128)(2,1)S(1)}, bf16[256,768]{1,0:T(8,128)(2,1)S(1)}, u32[]{:S(2)}, u32[]{:S(2)}) collective-permute-start(bf16[256,768]{1,0:T(8,128)(2,1)S(1)} %bitcast.26), channel_id=1, source_target_pairs={{0,1},{1,2},{2,3},{3,0},{4,5},{5,6},{6,7},{7,4},{8,9},{9,10},{10,1... | collective-permute-start | bytes 1179656 | tf_op jit(solution)/shard_map/ppermute | solution.py:11
  98.3 3.4 %collective-permute-start.5 = (f32[256]{0:T(256)S(1)}, f32[256]{0:T(256)S(1)}, u32[]{:S(2)}, u32[]{:S(2)}) collective-permute-start(f32[256]{0:T(256)S(1)} %get-tuple-element.9), channel_id=1, source_target_pairs={{0,2},{1,3},{2,0},{3,1},{4,6},{5,7},{6,4},{7,5},{8,10},{9,11},{10,... | collective-permute-start | bytes 3080 | tf_op jit(solution)/shard_map/ppermute | solution.py:11
  98.5 3.2 %collective-permute-start.2 = (f32[256]{0:T(256)S(1)}, f32[256]{0:T(256)S(1)}, u32[]{:S(2)}, u32[]{:S(2)}) collective-permute-start(f32[256]{0:T(256)S(1)} %get-tuple-element.6), channel_id=1, source_target_pairs={{0,3},{1,0},{2,1},{3,2},{4,7},{5,4},{6,5},{7,6},{8,11},{9,8},{10,9... | collective-permute-start | bytes 3080 | tf_op jit(solution)/shard_map/ppermute | solution.py:11
  102.3 8.2 %all-to-all-start.2 = ((f32[4,1,64]{2,1,0:T(1,128)}), f32[4,1,64]{2,1,0:T(1,128)S(1)}, u32[]{:S(2)}, u32[]{:S(2)}) async-start(f32[4,1,64]{2,1,0:T(1,128)} %all_to_all.33), calls=%async_computation.2 | async-start | bytes 4096 | tf_op jit(solution)/shard_map/all_to_all | solution.py:131
  107.5 0.7 slice-start
  110.5 10.0 %all-to-all-start.5 = ((f32[16,1,48]{2,1,0:T(1,128)}), f32[16,1,48]{2,1,0:T(1,128)S(1)}, u32[]{:S(2)}, u32[]{:S(2)}) async-start(f32[16,1,48]{2,1,0:T(1,128)} %all_to_all.38), calls=%async_computation.5 | async-start | bytes 16384 | tf_op jit(solution)/shard_map/all_to_all | solution.py:134
where the time goes:
time: 125 us; the launch traced here: 124 us
  waiting for transfers between devices  56.4 us (45%)
  starting transfers between devices  34.3 us (27%)
  local copies, waits for them, and re-layouts  15.3 us (12%)
  other arithmetic  13.2 us (11%)
  matrix products  4.74 us (4%)
    ppermute x6, waiting for transfers between devices, passed_along(): lax.ppermute(shard, axis, [(i, (i + by) % count) for i in range(count)])  49.5 us
    all_to_all x1, starting transfers between devices, body(): lax.all_to_all(small_ids.reshape(shards * blocks, cap_small), ('docs', 'b...  6.79 us
    ppermute x6, starting transfers between devices, passed_along(): lax.ppermute(shard, axis, [(i, (i + by) % count) for i in range(count)])  5.39 us
    all_to_all x1, starting transfers between devices, body(): lax.all_to_all(best_big.reshape(shards, cap_big), 'docs', split_axis=0, c...  5.21 us
    all_to_all x1, starting transfers between devices, body(): lax.all_to_all(send_small.reshape(shards * blocks, cap_small, feature), (...  4.38 us
    all_to_all x1, starting transfers between devices, body(): lax.all_to_all(big_ids, 'docs', split_axis=0, concat_axis=0, tiled=True)  4.26 us
    all_to_all x1, starting transfers between devices, body(): lax.all_to_all(best_small.reshape(shards * blocks, cap_small), ('docs', '...  4.21 us
    all_to_all x1, starting transfers between devices, body(): lax.all_to_all(send_big, 'docs', split_axis=0, concat_axis=0, tiled=True)  4.1 us
  transfers between devices with their start and end apart: 12, of which 6 were waited for; matrix products, arithmetic and copies ran while one was open for 17% of the time, Pallas kernels for 0%

commit v1 on v0

v1 whole, which is shorter than its diff:
```python
import functools

import jax
import jax.numpy as jnp
from jax import lax
from jax.experimental import pallas as pl
from jax.experimental.pallas import tpu as pltpu
from jax.sharding import PartitionSpec as P

BIG_OWN = 4
LANES = 128
VMEM = pl.BlockSpec(memory_space=pltpu.VMEM)
SMEM = pl.BlockSpec(memory_space=pltpu.SMEM)


def modulo(x, n):
    return x & (n - 1) if n & (n - 1) == 0 else lax.rem(x, jnp.int32(n))


def quotient(x, n):
    if n & (n - 1) == 0:
        return lax.shift_right_logical(x, jnp.int32(n.bit_length() - 1))
    return lax.div(x, jnp.int32(n))


def iota(shape, axis):
    return lax.broadcasted_iota(jnp.int32, shape, axis)


def dot_nt(a, b):
    return lax.dot_general(a, b, (((1,), (1,)), ((), ())), preferred_element_type=jnp.float32)


def tile_of(rows, most=256):
    tile = most
    while rows % tile:
        tile //= 2
    return tile


def home_of(docs, blocks):
    return max(blocks // 2 - 1, 0) + (docs % 2) * (1 if blocks > 1 else 0)


def arrive_kernel(shards, blocks, cap_big, cap_small, pooled_ref, weight_ref, cluster_ref,
                  small_ref, big_ref, ids_ref, where_ref, rows_ref):
    docs = pooled_ref.shape[0]
    devices = shards * blocks
    limit = BIG_OWN * shards
    small_slots = devices * cap_small
    slots = small_slots + shards * cap_big
    buckets = devices + shards

    projected = jnp.dot(pooled_ref[...], weight_ref[...], preferred_element_type=jnp.float32)
    squares = jnp.sum(projected * projected, axis=1, keepdims=True)
    rows_ref[...] = (projected / jnp.sqrt(squares + 1e-06)).astype(jnp.bfloat16)

    cluster = cluster_ref[...]
    is_big = cluster < limit
    owner = modulo(cluster, shards)
    past = jnp.maximum(cluster - limit, 0)
    target = modulo(past, devices)
    bucket = jnp.where(is_big, devices + owner, target)
    quota = jnp.where(is_big, quotient(cluster, shards), quotient(past, devices)) + 1

    padded = -(-buckets // 16) * 16
    hot = (iota((padded, docs), 0) == bucket).astype(jnp.float32)
    earlier = (iota((docs, docs), 0) < iota((docs, docs), 1)).astype(jnp.bfloat16)
    before = jnp.dot(hot.astype(jnp.bfloat16), earlier, preferred_element_type=jnp.float32)
    rank = jnp.sum(before * hot, axis=0, keepdims=True).astype(jnp.int32)
    slot = jnp.where(is_big, small_slots + owner * cap_big + rank, target * cap_small + rank)

    home = max(blocks // 2 - 1, 0) + (modulo(owner, 2) if blocks > 1 else 0)
    where_ref[0:1, :] = jnp.where(is_big, owner * blocks + home, target)
    where_ref[1:2, :] = jnp.where(is_big, cap_small + rank, rank)

    quotas = jnp.broadcast_to(quota.astype(jnp.float32), (8, docs)).astype(jnp.bfloat16)
    for ref, first in ((small_ref, 0), (big_ref, small_slots)):
        tile = tile_of(ref.shape[0])
        for at in range(0, ref.shape[0], tile):
            pick = (iota((tile, docs), 0) + (first + at) == slot).astype(jnp.float32).astype(jnp.bfloat16)
            ref[at:at + tile, :] = jnp.dot(
                pick, rows_ref[...], preferred_element_type=jnp.float32).astype(jnp.bfloat16)
            ids = dot_nt(quotas, pick)
            for lane in range(0, tile, LANES):
                ids_ref[0, (first + at + lane) // LANES:(first + at + lane) // LANES + 1, :] = ids[0:1, lane:lane + LANES]


def ids_kernel(shards, blocks, cap_big, cap_small, me_ref, all_ref, big_from_ref,
               small_row_ref, small_col_ref, big_row_ref, big_col_ref):
    devices = shards * blocks
    small_slots = devices * cap_small
    groups = all_ref.shape[1]
    me = me_ref[0] * blocks + me_ref[1]

    small = small_row_ref.shape[1]
    big = big_row_ref.shape[1]
    small_at = iota((1, small), 1)
    small_from = small_at // cap_small
    small_want = me * cap_small + lax.rem(small_at, jnp.int32(cap_small))
    big_want = small_slots + me_ref[0] * cap_big + lax.rem(iota((1, big), 1), jnp.int32(cap_big))
    small_sum = jnp.zeros((devices, small), jnp.float32)
    big_sum = jnp.zeros((devices, big), jnp.float32)
    for group in range(groups):
        values = all_ref[:, group, :].astype(jnp.bfloat16)
        low, high = group * LANES, (group + 1) * LANES
        if low < small_slots:
            pick = (iota((LANES, small), 0) + low == small_want).astype(jnp.float32).astype(jnp.bfloat16)
            small_sum += jnp.dot(values, pick, preferred_element_type=jnp.float32)
        if high > small_slots:
            pick = (iota((LANES, big), 0) + low == big_want).astype(jnp.float32).astype(jnp.bfloat16)
            big_sum += jnp.dot(values, pick, preferred_element_type=jnp.float32)
    small_row = jnp.sum(
        jnp.where(iota((devices, small), 0) == small_from, small_sum, 0.0), axis=0, keepdims=True)
    big_row = jnp.sum(
        jnp.where(iota((devices, big), 0) == big_from_ref[...], big_sum, 0.0), axis=0, keepdims=True)
    small_row_ref[...] = small_row
    big_row_ref[...] = big_row
    small_col_ref[...] = jnp.broadcast_to(small_row, (LANES, small)).T
    big_col_ref[...] = jnp.broadcast_to(big_row, (LANES, big)).T


def block_best(queries, col_ids, first_row, others, row_ids, first_col):
    scores = dot_nt(queries, others)
    allowed = (col_ids == row_ids) & (row_ids > 0.0)
    if first_row is not None:
        allowed &= (iota(scores.shape, 0) + first_row) != (iota(scores.shape, 1) + first_col)
    return jnp.max(jnp.where(allowed, scores, -1.0), axis=0, keepdims=True)


def small_kernel(rows_ref, row_ref, col_ref, best_ref):
    total = rows_ref.shape[0]
    tile = tile_of(total)
    best = jnp.full((1, total), -1.0, jnp.float32)
    for at in range(0, total, tile):
        best = jnp.maximum(best, block_best(
            rows_ref[at:at + tile, :], col_ref[at:at + tile, 0:1], at, rows_ref[...], row_ref[...], 0))
    best_ref[...] = best


def big_kernel(cap_big, cap_small, parts, *refs):
    blocks = refs[:parts]
    row_ref, col_ref, from_ref, small_ref, back_ref = refs[parts:]
    size = blocks[0].shape[0]
    devices = back_ref.shape[0]
    bests = []
    for col in range(parts):
        best = jnp.full((1, size), -1.0, jnp.float32)
        for row in range(parts):
            same = 0 if row == col else None
            best = jnp.maximum(best, block_best(
                blocks[row][...], col_ref[row * size:(row + 1) * size, 0:1], same,
                blocks[col][...], row_ref[:, col * size:(col + 1) * size], same))
        bests.append(best)
    best_big = jnp.concatenate(bests, axis=1)
    best_small = small_ref[...]

    def spread(best, sources, lane):
        total = best.shape[1]
        mine = jnp.where(iota((devices, total), 0) == sources, best, 0.0)
        place = (iota((total, LANES), 1) == lane).astype(jnp.float32)
        return jnp.dot(mine, place, precision=lax.Precision.HIGHEST, preferred_element_type=jnp.float32)

    small_total = best_small.shape[1]
    big_total = best_big.shape[1]
    back = spread(best_small, iota((1, small_total), 1) // cap_small,
                  lax.rem(iota((small_total, 1), 0), jnp.int32(cap_small)))
    back += spread(best_big, from_ref[...],
                   cap_small + lax.rem(iota((big_total, 1), 0), jnp.int32(cap_big)))
    for device in range(devices):
        back_ref[device, 0:1, :] = back[device:device + 1, :]


def finish_kernel(back_ref, where_ref, out_ref):
    devices = back_ref.shape[0]
    docs = where_ref.shape[1]
    values = jnp.concatenate([back_ref[device, 0:1, :] for device in range(devices)], axis=0)
    pick = (iota((devices, docs), 0) == where_ref[0:1, :]).astype(jnp.float32)
    found = lax.dot_general(values, pick, (((0,), (0,)), ((), ())),
                            precision=lax.Precision.HIGHEST, preferred_element_type=jnp.float32)
    out_ref[...] = jnp.sum(
        jnp.where(iota((LANES, docs), 0) == where_ref[1:2, :], found, 0.0), axis=0, keepdims=True)


def call(kernel, out_shape, in_specs, flops, moved, limit=16, scratch=()):
    multiple = isinstance(out_shape, (tuple, list))
    return pl.pallas_call(
        kernel,
        out_shape=out_shape,
        in_specs=in_specs,
        out_specs=tuple(VMEM for _ in out_shape) if multiple else VMEM,
        scratch_shapes=scratch,
        cost_estimate=pl.CostEstimate(flops=flops, bytes_accessed=moved, transcendentals=0),
        compiler_params=pltpu.CompilerParams(vmem_limit_bytes=limit << 20),
    )


def body(pooled, proj_weight, cluster):
    shards = lax.axis_size("docs")
    blocks = lax.axis_size("blk")
    devices = shards * blocks
    docs = pooled.shape[0]
    feature = proj_weight.shape[1]
    big_count = docs // 4
    small_count = docs - big_count
    cap_big = 2 * big_count // shards
    cap_small = 2 * small_count // devices
    small_slots = devices * cap_small
    slots = small_slots + shards * cap_big
    sizes = (shards, blocks, cap_big, cap_small)
    f32, bf16, i32 = jnp.float32, jnp.bfloat16, jnp.int32
    shape = jax.ShapeDtypeStruct

    send_small, send_big, slot_ids, where = call(
        functools.partial(arrive_kernel, *sizes),
        (shape((small_slots, feature), bf16), shape((shards * cap_big, feature), bf16),
         shape((1, slots // LANES, LANES), f32), shape((8, docs), i32)),
        (VMEM, VMEM, VMEM),
        2 * docs * feature * (pooled.shape[1] + slots), 4 << 20, 32,
        (pltpu.VMEM((docs, feature), bf16),),
    )(pooled, proj_weight, cluster.reshape(1, docs))

    got_small = lax.all_to_all(
        send_small.reshape(devices, cap_small, feature), ("docs", "blk"),
        split_axis=0, concat_axis=0, tiled=True).reshape(small_slots, feature)
    all_ids = lax.all_gather(slot_ids, ("docs", "blk"), axis=0, tiled=True)
    got_big = lax.all_to_all(
        send_big.reshape(shards, cap_big, feature), "docs",
        split_axis=0, concat_axis=0, tiled=True).reshape(shards * cap_big, feature)

    my_docs, my_blk = lax.axis_index("docs"), lax.axis_index("blk")
    others = [[blk for blk in range(blocks) if blk != home_of(d, blocks)] for d in range(shards)]
    parts = [got_big]
    for step in range(blocks - 1):
        pairs = [(d * blocks + others[d][step], d * blocks + home_of(d, blocks)) for d in range(shards)]
        parts.append(lax.ppermute(got_big, ("docs", "blk"), pairs))

    big_total = blocks * shards * cap_big
    order = jnp.asarray([[home_of(d, blocks)] + others[d] for d in range(2)], i32)[my_docs % 2]
    from_blk = jnp.repeat(order, shards * cap_big)
    from_docs = (jnp.arange(big_total, dtype=i32) // cap_big) % shards
    big_from = (from_docs * blocks + from_blk).reshape(1, big_total)

    small_row, small_col, big_row, big_col = call(
        functools.partial(ids_kernel, *sizes),
        (shape((1, small_slots), f32), shape((small_slots, LANES), f32),
         shape((1, big_total), f32), shape((big_total, LANES), f32)),
        (SMEM, VMEM, VMEM),
        2 * devices * slots * slots, 1 << 20,
    )(jnp.stack([my_docs, my_blk]).astype(i32), all_ids, big_from)

    best_small = call(
        small_kernel, shape((1, small_slots), f32), (VMEM, VMEM, VMEM),
        2 * small_slots * small_slots * feature, 2 << 20,
    )(got_small, small_row, small_col)

    back = call(
        functools.partial(big_kernel, cap_big, cap_small, blocks),
        shape((devices, 1, LANES), f32), (VMEM,) * (blocks + 4),
        2 * big_total * big_total * feature, 2 << 20,
    )(*parts, big_row, big_col, big_from, best_small)

    returned = lax.all_to_all(back, ("docs", "blk"), split_axis=0, concat_axis=0, tiled=True)
    out = call(
        finish_kernel, shape((1, docs), f32), (VMEM, VMEM),
        2 * docs * LANES * devices, 1 << 16,
    )(returned, where)
    return out.reshape(docs)


def solution(mesh):
    in_specs = (P(("slab", "docs", "blk"), None), P(), P(("slab", "docs", "blk")))
    out_specs = P(("slab", "docs", "blk"))
    return jax.shard_map(body, mesh=mesh, in_specs=in_specs, out_specs=out_specs, check_vma=False)
```

time: 125 us -> 102 us (0.82)
  blocking collectives: 0 us -> 77.9 us
  waiting for transfers between devices: 56.4 us -> 0.01 us
  starting transfers between devices: 34.3 us -> 9.01 us
  other arithmetic: 13.2 us -> 0.09 us
  local copies, waits for them, and re-layouts: 15.3 us -> 4.93 us
  Pallas kernels: 0 us -> 9 us
  matrix products: 4.74 us -> 0 us
    ppermute x6 -> x3, waiting for transfers between devices: 49.5 us -> 0.01 us  [body(): parts.append(lax.ppermute(got_big, ('docs', 'blk'), pairs))]
    all_gather x0 -> x1, blocking collectives: none -> 49.5 us  [body(): all_ids = lax.all_gather(slot_ids, ('docs', 'blk'), axis=0, tiled=True)]
    all_to_all x0 -> x2, blocking collectives: none -> 28.4 us  [the longest x1 18 us: body(): lax.all_to_all(back, ('docs', 'blk'), split_axis=0, concat_axis=0, tiled=...]
    all_to_all x6 -> x1, starting transfers between devices: 29 us -> 6.07 us  [body(): lax.all_to_all(send_small.reshape(devices, cap_small, feature), ('docs',...]
    pallas_call x0 -> x5, Pallas kernels: none -> 9 us  [the longest x1 3.26 us: body(): call(functools.partial(arrive_kernel, *sizes), (shape((small_slots, featu...]
    scatter x2 -> x0, other arithmetic: 7.07 us -> none  [the longest x1 3.64 us: body(): send_small = jnp.zeros((shards * blocks * cap_small, feature), jnp.bfloat...]
    all_to_all x6 -> x1, waiting for transfers between devices: 6.87 us -> 0.01 us  [body(): lax.all_to_all(send_small.reshape(devices, cap_small, feature), ('docs',...]
    gather x2 -> x0, local copies, waits for them, and re-layouts: 5.78 us -> none  [the longest x1 3.5 us: body(): from_big = big_return[jnp.minimum(big_slot, shards * cap_big - 1)]]
  transfers between devices with their start and end apart: 12 -> 4, of which waited for: 6 -> 0; matrix products, arithmetic and copies ran while one was open for 17% -> 0% of each run, Pallas kernels for 0% -> 2%
where the time goes in v1:
time: 102 us; the launch traced here: 101 us
  blocking collectives  77.9 us (76%)
  starting transfers between devices  9.01 us (9%)
  Pallas kernels  9 us (9%)
  local copies, waits for them, and re-layouts  4.93 us (5%)
    all_gather x1, blocking collectives, body(): all_ids = lax.all_gather(slot_ids, ('docs', 'blk'), axis=0, tiled=True)  49.5 us
    all_to_all x1, blocking collectives, body(): lax.all_to_all(back, ('docs', 'blk'), split_axis=0, concat_axis=0, tiled=...  18 us
    all_to_all x1, blocking collectives, body(): lax.all_to_all(send_big.reshape(shards, cap_big, feature), 'docs', split_...  10.4 us
    all_to_all x1, starting transfers between devices, body(): lax.all_to_all(send_small.reshape(devices, cap_small, feature), ('docs',...  6.07 us
    unnamed x14, local copies, waits for them, and re-layouts  4.92 us
    pallas_call x1, Pallas kernels, body(): call(functools.partial(arrive_kernel, *sizes), (shape((small_slots, featu...  3.26 us
    ppermute x3, starting transfers between devices, body(): parts.append(lax.ppermute(got_big, ('docs', 'blk'), pairs))  2.94 us
    pallas_call x1, Pallas kernels, body(): call(functools.partial(big_kernel, cap_big, cap_small, blocks), shape((de...  2.4 us
  transfers between devices with their start and end apart: 4, of which 0 were waited for; matrix products, arithmetic and copies ran while one was open for 0% of the time, Pallas kernels for 2%

profile of v1, /device:TPU:1, one launch (start us, length us, event | category | flops | bytes accessed | tf_op | source)
XLA Modules:
  0.0 101.0 jit_solution(5635344237340759522)
XLA Ops:
  0.0 0.0 copy-start
  0.0 1.3 %copy-done = bf16[768,768]{1,0:T(8,128)(2,1)S(1)} copy-done((bf16[768,768]{1,0:T(8,128)(2,1)S(1)}, bf16[768,768]{1,0:T(8,128)(2,1)}, u32[]{:S(2)}) %copy-start) | copy-done | bytes 1179672
  1.3 0.0 copy-start.1
  1.3 1.1 %copy-done.1 = bf16[512,768]{1,0:T(8,128)(2,1)S(1)} copy-done((bf16[512,768]{1,0:T(8,128)(2,1)S(1)}, bf16[512,768]{1,0:T(8,128)(2,1)}, u32[]{:S(2)}) %copy-start.1) | copy-done | bytes 786456
  2.4 0.0 copy-start.2
  2.4 0.7 copy-done.2
  3.1 3.3 %shard_map.46 = (bf16[768,768]{1,0:T(8,128)(2,1)}, bf16[256,768]{1,0:T(8,128)(2,1)S(1)}, f32[1,8,128]{2,1,0:T(8,128)S(1)}, s32[8,512]{1,0:T(8,128)S(1)}) custom-call(bf16[512,768]{1,0:T(8,128)(2,1)S(1)} %copy-done.1, bf16[768,768]{1,0:T(8,128)(2,1)S(1)} %copy-done, s32[1,512]{1,0:T(1,128)S(1)} %bitcast.20), custom_call_target="tpu_custom_call" | custom-call | flops 1409286144 | bytes 4194304 | tf_op jit(solution)/shard_map/pallas_call | solution.py:214
  6.3 10.4 %all_to_all.15 = bf16[4,64,768]{2,1,0:T(8,128)(2,1)S(1)} all-to-all(bf16[4,64,768]{2,1,0:T(8,128)(2,1)S(1)} %bitcast.19), channel_id=1, replica_groups=mesh['slab'=2,'docs'=4,'blk'=4] {'docs'}, dimensions={0} | all-to-all | bytes 786432 | tf_op jit(solution)/shard_map/all_to_all | solution.py:227
  16.8 0.0 copy-start.5
  16.8 6.1 %all-to-all-start.1 = ((bf16[16,48,768]{2,1,0:T(8,128)(2,1)}), bf16[16,48,768]{2,1,0:T(8,128)(2,1)S(1)}, u32[]{:S(2)}, u32[]{:S(2)}) async-start(bf16[16,48,768]{2,1,0:T(8,128)(2,1)} %bitcast.6), calls=%async_computation.1 | async-start | bytes 2359296 | tf_op jit(solution)/shard_map/all_to_all | solution.py:223
  22.9 0.0 copy-done.5
  22.9 0.1 broadcast_bitcast_fusion
  23.0 49.5 %all_gather.3.all_ref = f32[16,8,128]{2,1,0:T(8,128)S(1)} all-gather(f32[1,8,128]{2,1,0:T(8,128)S(1)} %get-tuple-element.14), channel_id=1, replica_groups=mesh['slab'=2,'docs'=4,'blk'=4] {'docs','blk'}, dimensions={0}, use_global_device_ids=true | all-gather | bytes 69632 | tf_op jit(solution)/shard_map/all_gather | solution.py:226
  72.4 1.6 %collective-permute-start = (bf16[256,768]{1,0:T(8,128)(2,1)S(1)}, bf16[256,768]{1,0:T(8,128)(2,1)S(1)}, u32[]{:S(2)}, u32[]{:S(2)}) collective-permute-start(bf16[256,768]{1,0:T(8,128)(2,1)S(1)} %bitcast.15), channel_id=1, source_target_pairs={{0,1},{4,6},{8,9},{12,14},{16,17},{20,22},{24,25},{28,30}} | collective-permute-start | bytes 1179656 | tf_op jit(solution)/shard_map/ppermute | solution.py:236
  74.0 0.7 collective-permute-start.1
  74.7 0.7 collective-permute-start.2
  75.4 0.1 pad_add_fusion.me_ref
  75.5 1.2 %shard_map.47 = (f32[1,768]{1,0:T(1,128)S(1)}, f32[768,128]{1,0:T(8,128)S(1)}, f32[1,1024]{1,0:T(1,128)S(1)}, f32[1024,128]{1,0:T(8,128)S(1)}) custom-call(s32[2]{0:T(128)S(1)} %pad_add_fusion.me_ref, f32[16,8,128]{2,1,0:T(8,128)S(1)} %all_gather.3.all_ref, s32[1,1024]{1,0:T(1,128)S(1)} %fusion.1.big_from_ref.refs_6_), custom_call_target="tpu_custom_call" | custom-call | flops 33554432 | bytes 1048576 | tf_op jit(solution)/shard_map/pallas_call | solution.py:244
  76.7 0.0 copy-start.3
  76.7 0.8 copy-done.3
  77.4 0.0 all-to-all-done.1
  77.4 0.0 copy-start.4
  77.4 1.0 copy-done.4
  78.4 1.2 %shard_map.48.refs_7_ = f32[1,768]{1,0:T(1,128)S(1)} custom-call(bf16[768,768]{1,0:T(8,128)(2,1)S(1)} %bitcast.14, f32[1,768]{1,0:T(1,128)S(1)} %get-tuple-element.18.row_ref, f32[768,128]{1,0:T(8,128)S(1)} %copy-done.4), custom_call_target="tpu_custom_call" | custom-call | flops 905969664 | bytes 2097152 | tf_op jit(solution)/shard_map/pallas_call | solution.py:252
  79.6 0.0 collective-permute-done.refs_1_
  79.6 0.0 collective-permute-done.1.refs_2_
  79.6 0.0 collective-permute-done.2.refs_3_
  79.6 2.4 %shard_map.49 = f32[16,1,128]{2,1,0:T(1,128)S(1)} custom-call(bf16[256,768]{1,0:T(8,128)(2,1)S(1)} %bitcast.18, bf16[256,768]{1,0:T(8,128)(2,1)S(1)} %collective-permute-done.refs_1_, bf16[256,768]{1,0:T(8,128)(2,1)S(1)} %collective-permute-done.1.refs_2_, bf16[256,768]{1,0:T(8,128)(2,1)S(1)} %collective-permute-done.2.refs_3_, ...), custom_call_target="tpu_custom_call" | custom-call | flops 1610612736 | bytes 2097152 | tf_op jit(solution)/shard_map/pallas_call | solution.py:257
  82.1 18.0 %all_to_all.16.back_ref = f32[16,1,128]{2,1,0:T(1,128)S(1)} all-to-all(f32[16,1,128]{2,1,0:T(1,128)S(1)} %shard_map.49), channel_id=1, replica_groups=mesh['slab'=2,'docs'=4,'blk'=4] {'docs','blk'}, dimensions={0} | all-to-all | bytes 16384 | tf_op jit(solution)/shard_map/all_to_all | solution.py:263
  100.0 1.0 shard_map.50
  (3 shorter events, 0.0 us)
Async XLA Ops:
  0.0 1.3 %copy-start = (bf16[768,768]{1,0:T(8,128)(2,1)S(1)}, bf16[768,768]{1,0:T(8,128)(2,1)}, u32[]{:S(2)}) copy-start(bf16[768,768]{1,0:T(8,128)(2,1)} %weight_ref.1) | copy-start | bytes 3538948
  1.3 1.1 %copy-start.1 = (bf16[512,768]{1,0:T(8,128)(2,1)S(1)}, bf16[512,768]{1,0:T(8,128)(2,1)}, u32[]{:S(2)}) copy-start(bf16[512,768]{1,0:T(8,128)(2,1)} %pooled_ref.1) | copy-start | bytes 2359300
  2.4 0.7 copy-start.2
  16.8 6.1 %copy-start.5 = (s32[2,4]{1,0:T(2,128)S(1)}, s32[2,4]{1,0:T(2,128)}, u32[]{:S(2)}) copy-start(s32[2,4]{1,0:T(2,128)} %constant.54.clone) | copy-start | bytes 100
  16.8 60.7 %all-to-all-start.1 = ((bf16[16,48,768]{2,1,0:T(8,128)(2,1)}), bf16[16,48,768]{2,1,0:T(8,128)(2,1)S(1)}, u32[]{:S(2)}, u32[]{:S(2)}) async-start(bf16[16,48,768]{2,1,0:T(8,128)(2,1)} %bitcast.6), calls=%async_computation.1 | async-start | bytes 2359296 | tf_op jit(solution)/shard_map/all_to_all | solution.py:223
  72.4 7.2 %collective-permute-start = (bf16[256,768]{1,0:T(8,128)(2,1)S(1)}, bf16[256,768]{1,0:T(8,128)(2,1)S(1)}, u32[]{:S(2)}, u32[]{:S(2)}) collective-permute-start(bf16[256,768]{1,0:T(8,128)(2,1)S(1)} %bitcast.15), channel_id=1, source_target_pairs={{0,1},{4,6},{8,9},{12,14},{16,17},{20,22},{24,25},{28,30}} | collective-permute-start | bytes 1179656 | tf_op jit(solution)/shard_map/ppermute | solution.py:236
  74.0 5.6 %collective-permute-start.1 = (bf16[256,768]{1,0:T(8,128)(2,1)S(1)}, bf16[256,768]{1,0:T(8,128)(2,1)S(1)}, u32[]{:S(2)}, u32[]{:S(2)}) collective-permute-start(bf16[256,768]{1,0:T(8,128)(2,1)S(1)} %bitcast.16), channel_id=1, source_target_pairs={{2,1},{5,6},{10,9},{13,14},{18,17},{21,22},{26,25},{29,30}} | collective-permute-start | bytes 1179656 | tf_op jit(solution)/shard_map/ppermute | solution.py:236
  74.7 4.9 %collective-permute-start.2 = (bf16[256,768]{1,0:T(8,128)(2,1)S(1)}, bf16[256,768]{1,0:T(8,128)(2,1)S(1)}, u32[]{:S(2)}, u32[]{:S(2)}) collective-permute-start(bf16[256,768]{1,0:T(8,128)(2,1)S(1)} %bitcast.17), channel_id=1, source_target_pairs={{3,1},{7,6},{11,9},{15,14},{19,17},{23,22},{27,25},{31,30}} | collective-permute-start | bytes 1179656 | tf_op jit(solution)/shard_map/ppermute | solution.py:236
  76.7 0.8 copy-start.3
  77.4 1.0 copy-start.4

commit v2 on v1

v2 whole, which is shorter than its diff:
```python
import functools

import jax
import jax.numpy as jnp
from jax import lax
from jax.experimental import pallas as pl
from jax.experimental.pallas import tpu as pltpu
from jax.sharding import PartitionSpec as P

BIG_OWN = 4
LANES = 128


def modulo(x, n):
    return x & (n - 1) if n & (n - 1) == 0 else lax.rem(x, jnp.int32(n))


def quotient(x, n):
    if n & (n - 1) == 0:
        return lax.shift_right_logical(x, jnp.int32(n.bit_length() - 1))
    return lax.div(x, jnp.int32(n))


def iota(shape, axis):
    return lax.broadcasted_iota(jnp.int32, shape, axis)


def dot_nt(a, b):
    return lax.dot_general(a, b, (((1,), (1,)), ((), ())), preferred_element_type=jnp.float32)


def tile_of(rows, most=256):
    tile = most
    while rows % tile:
        tile //= 2
    return tile


def home_of(docs, blocks):
    return max(blocks // 2 - 1, 0) + (docs & min(blocks - 1, 1))


def sort_kernel(shards, blocks, cap_big, cap_small, pooled_hbm, weight_hbm, cluster_hbm,
                small_hbm, rows_ref, info_ref, pooled_ref, weight_ref, cluster_ref, stage_ref, sems, out_sems):
    docs = pooled_ref.shape[0]
    devices = shards * blocks
    limit = BIG_OWN * shards
    small_slots = devices * cap_small
    buckets = devices + shards

    fetches = [pltpu.make_async_copy(source, target, sems.at[n]) for n, (source, target) in enumerate(
        ((cluster_hbm, cluster_ref), (weight_hbm, weight_ref), (pooled_hbm, pooled_ref)))]
    for fetch in fetches:
        fetch.start()
    fetches[0].wait()

    cluster = cluster_ref[...]
    is_big = cluster < limit
    owner = modulo(cluster, shards)
    past = jnp.maximum(cluster - limit, 0)
    target = modulo(past, devices)
    bucket = jnp.where(is_big, devices + owner, target)
    quota = jnp.where(is_big, quotient(cluster, shards), quotient(past, devices)) + 1

    padded = -(-buckets // 16) * 16
    hot = (iota((padded, docs), 0) == bucket).astype(jnp.float32)
    earlier = (iota((docs, docs), 0) < iota((docs, docs), 1)).astype(jnp.float32).astype(jnp.bfloat16)
    before = jnp.dot(hot.astype(jnp.bfloat16), earlier, preferred_element_type=jnp.float32)
    rank = jnp.sum(before * hot, axis=0, keepdims=True).astype(jnp.int32)
    slot = jnp.where(is_big, small_slots + owner * cap_big + rank, target * cap_small + rank)

    home = home_of(owner, blocks)
    info_ref[0:1, :] = jnp.where(is_big, owner * blocks + home, target)
    info_ref[1:2, :] = jnp.where(is_big, cap_small + rank, rank)
    info_ref[2:3, :] = slot
    info_ref[3:4, :] = quota
    info_ref[4:5, :] = bucket

    for fetch in fetches[1:]:
        fetch.wait()
    projected = jnp.dot(pooled_ref[...], weight_ref[...], preferred_element_type=jnp.float32)
    squares = jnp.sum(projected * projected, axis=1, keepdims=True)
    rows_ref[...] = (projected / jnp.sqrt(squares + 1e-06)).astype(jnp.bfloat16)
    place_rows(rows_ref, slot, 0, stage_ref, small_hbm, out_sems)


def place_rows(rows_ref, slot, first, stage_ref, out_hbm, sems):
    total, docs = stage_ref.shape[0], rows_ref.shape[0]
    tile = total // sems.shape[0]
    sends = []
    for part in range(sems.shape[0]):
        at = part * tile
        pick = (iota((tile, docs), 0) + (first + at) == slot).astype(jnp.float32).astype(jnp.bfloat16)
        stage_ref[at:at + tile, :] = jnp.dot(
            pick, rows_ref[...], preferred_element_type=jnp.float32).astype(jnp.bfloat16)
        send = pltpu.make_async_copy(
            stage_ref.at[pl.ds(at, tile)], out_hbm.at[pl.ds(at, tile)], sems.at[part])
        send.start()
        sends.append(send)
    for send in sends:
        send.wait()


def sort_big_kernel(shards, blocks, cap_big, cap_small, rows_ref, info_ref, big_hbm, ids_hbm,
                    stage_ref, lanes_ref, out_sems, ids_sem):
    docs = rows_ref.shape[0]
    devices = shards * blocks
    lane, slot = info_ref[1:2, :], info_ref[2:3, :]
    quota, bucket = info_ref[3:4, :], info_ref[4:5, :]
    to = iota((devices, docs), 0)
    mine = (to == bucket) | (quotient(to, blocks) + devices == bucket)
    values = jnp.where(mine, quota.astype(jnp.float32), 0.0).astype(jnp.bfloat16)
    place = (iota((LANES, docs), 0) == lane).astype(jnp.float32).astype(jnp.bfloat16)
    store_rows(dot_nt(values, place), lanes_ref)
    send = pltpu.make_async_copy(lanes_ref, ids_hbm, ids_sem)
    send.start()
    place_rows(rows_ref, slot, devices * cap_small, stage_ref, big_hbm, out_sems)
    send.wait()


def store_rows(values, ref):
    for device in range(ref.shape[0]):
        ref[device, 0:1, :] = values[device:device + 1, :]


def load_rows(ref):
    return jnp.concatenate([ref[device, 0:1, :] for device in range(ref.shape[0])], axis=0)


def small_sources(total, cap_small):
    at = iota((1, total), 1)
    return at // cap_small, lax.rem(at, jnp.int32(cap_small))


def big_sources(total, my_docs, shards, blocks, cap_big, cap_small):
    at = iota((1, total), 1)
    part = at // (shards * cap_big)
    home = home_of(my_docs, blocks)
    blk = jnp.where(part == 0, home, jnp.where(part - 1 >= home, part, part - 1))
    docs = modulo(at // cap_big, shards)
    return docs * blocks + blk, cap_small + lax.rem(at, jnp.int32(cap_big))


def ids_kernel(shards, blocks, cap_big, cap_small, me_ref, ids_ref, small_ref, big_ref):
    devices = shards * blocks
    values = load_rows(ids_ref).astype(jnp.bfloat16)
    for ref, (source, lane) in (
        (small_ref, small_sources(small_ref.shape[1], cap_small)),
        (big_ref, big_sources(big_ref.shape[1], me_ref[0], shards, blocks, cap_big, cap_small)),
    ):
        total = ref.shape[1]
        pick = (iota((LANES, total), 0) == lane).astype(jnp.float32).astype(jnp.bfloat16)
        found = jnp.dot(values, pick, preferred_element_type=jnp.float32)
        ref[...] = jnp.sum(
            jnp.where(iota((devices, total), 0) == source, found, 0.0), axis=0, keepdims=True)


def as_column(row):
    return jnp.broadcast_to(row, (LANES, row.shape[1])).T[:, 0:1]


def block_best(queries, col_ids, first_row, others, row_ids, first_col):
    scores = dot_nt(queries, others)
    allowed = (col_ids == row_ids) & (row_ids > 0.0)
    if first_row is not None:
        allowed &= (iota(scores.shape, 0) + first_row) != (iota(scores.shape, 1) + first_col)
    return jnp.max(jnp.where(allowed, scores, -1.0), axis=0, keepdims=True)


def small_kernel(rows_ref, row_ref, best_ref):
    total = rows_ref.shape[0]
    tile = tile_of(total)
    best = jnp.full((1, total), -1.0, jnp.float32)
    for at in range(0, total, tile):
        best = jnp.maximum(best, block_best(
            rows_ref[at:at + tile, :], as_column(row_ref[:, at:at + tile]), at, rows_ref[...], row_ref[...], 0))
    best_ref[...] = best


def big_kernel(shards, blocks, cap_big, cap_small, me_ref, *refs):
    held = refs[:blocks]
    row_ref, small_ref, back_hbm, lanes_ref, sem = refs[blocks:]
    size = held[0].shape[0]
    devices = shards * blocks
    bests = [jnp.full((1, size), -1.0, jnp.float32) for _ in range(blocks)]
    for row in range(blocks):
        col_ids = as_column(row_ref[:, row * size:(row + 1) * size])
        for col in range(blocks):
            same = 0 if row == col else None
            bests[col] = jnp.maximum(bests[col], block_best(
                held[row][...], col_ids, same, held[col][...], row_ref[:, col * size:(col + 1) * size], same))
    best_big = jnp.concatenate(bests, axis=1)
    best_small = small_ref[...]

    def spread(best, source, lane):
        total = best.shape[1]
        mine = jnp.where(iota((devices, total), 0) == source, best, 0.0)
        place = (iota((LANES, total), 0) == lane).astype(jnp.float32)
        return lax.dot_general(mine, place, (((1,), (1,)), ((), ())),
                               precision=lax.Precision.HIGHEST, preferred_element_type=jnp.float32)

    back = spread(best_small, *small_sources(best_small.shape[1], cap_small))
    back += spread(best_big, *big_sources(best_big.shape[1], me_ref[0], shards, blocks, cap_big, cap_small))
    store_rows(back, lanes_ref)
    send = pltpu.make_async_copy(lanes_ref, back_hbm, sem)
    send.start()
    send.wait()


def finish_kernel(back_ref, where_ref, out_ref):
    devices = back_ref.shape[0]
    docs = where_ref.shape[1]
    values = load_rows(back_ref)
    pick = (iota((devices, docs), 0) == where_ref[0:1, :]).astype(jnp.float32)
    found = lax.dot_general(values, pick, (((0,), (0,)), ((), ())),
                            precision=lax.Precision.HIGHEST, preferred_element_type=jnp.float32)
    out_ref[...] = jnp.sum(
        jnp.where(iota((LANES, docs), 0) == where_ref[1:2, :], found, 0.0), axis=0, keepdims=True)


def call(kernel, outs, ins, flops, moved, limit=16, scratch=()):
    specs = [pl.BlockSpec(memory_space=space) for _, _, space in outs]
    return pl.pallas_call(
        kernel,
        out_shape=[space(shape, dtype) if space is pltpu.HBM else jax.ShapeDtypeStruct(shape, dtype)
                   for shape, dtype, space in outs],
        in_specs=[pl.BlockSpec(memory_space=space) for space in ins],
        out_specs=specs,
        scratch_shapes=scratch,
        cost_estimate=pl.CostEstimate(flops=flops, bytes_accessed=moved, transcendentals=0),
        compiler_params=pltpu.CompilerParams(vmem_limit_bytes=limit << 20),
    )


def body(pooled, proj_weight, cluster):
    shards = lax.axis_size("docs")
    blocks = lax.axis_size("blk")
    devices = shards * blocks
    docs = pooled.shape[0]
    feature = proj_weight.shape[1]
    big_count = docs // 4
    small_count = docs - big_count
    cap_big = 2 * big_count // shards
    cap_small = 2 * small_count // devices
    small_slots = devices * cap_small
    big_slots = shards * cap_big
    big_total = blocks * big_slots
    sizes = (shards, blocks, cap_big, cap_small)
    f32, bf16, i32 = jnp.float32, jnp.bfloat16, jnp.int32
    vmem, hbm, smem, dma = pltpu.VMEM, pltpu.HBM, pltpu.SMEM, pltpu.SemaphoreType.DMA

    send_small, rows, info = call(
        functools.partial(sort_kernel, *sizes),
        [((small_slots, feature), bf16, hbm), ((docs, feature), bf16, vmem), ((8, docs), i32, vmem)],
        [hbm, hbm, hbm],
        2 * docs * feature * (pooled.shape[1] + small_slots), 4 << 20, 32,
        [vmem(pooled.shape, bf16), vmem(proj_weight.shape, bf16), vmem((1, docs), i32),
         vmem((small_slots, feature), bf16), dma((3,)), dma((3,))],
    )(pooled, proj_weight, cluster.reshape(1, docs))

    got_small = lax.all_to_all(
        send_small.reshape(devices, cap_small, feature), ("docs", "blk"),
        split_axis=0, concat_axis=0, tiled=True).reshape(small_slots, feature)

    send_big, send_ids = call(
        functools.partial(sort_big_kernel, *sizes),
        [((big_slots, feature), bf16, hbm), ((devices, 1, LANES), f32, hbm)],
        [vmem, vmem],
        2 * docs * feature * big_slots, 2 << 20, 16,
        [vmem((big_slots, feature), bf16), vmem((devices, 1, LANES), f32), dma((1,)), dma],
    )(rows, info)
    got_big = lax.all_to_all(
        send_big.reshape(shards, cap_big, feature), "docs",
        split_axis=0, concat_axis=0, tiled=True).reshape(big_slots, feature)
    got_ids = lax.all_to_all(send_ids, ("docs", "blk"), split_axis=0, concat_axis=0, tiled=True)

    me = lax.axis_index("docs").astype(i32).reshape(1)
    held = [got_big]
    for step in range(blocks - 1):
        homes = [home_of(d, blocks) for d in range(shards)]
        pairs = [(d * blocks + (step if step < homes[d] else step + 1), d * blocks + homes[d])
                 for d in range(shards)]
        held.append(lax.ppermute(got_big, ("docs", "blk"), pairs))

    small_ids, big_ids = call(
        functools.partial(ids_kernel, *sizes),
        [((1, small_slots), f32, vmem), ((1, big_total), f32, vmem)],
        [smem, vmem],
        2 * devices * LANES * (small_slots + big_total), 1 << 16,
    )(me, got_ids)

    best_small, = call(
        small_kernel, [((1, small_slots), f32, vmem)], [vmem, vmem],
        2 * small_slots * small_slots * feature, 2 << 20,
    )(got_small, small_ids)

    back, = call(
        functools.partial(big_kernel, *sizes),
        [((devices, 1, LANES), f32, hbm)],
        [smem] + [vmem] * (blocks + 2),
        2 * big_total * big_total * feature, 2 << 20, 16,
        [vmem((devices, 1, LANES), f32), dma],
    )(me, *held, big_ids, best_small)

    returned = lax.all_to_all(back, ("docs", "blk"), split_axis=0, concat_axis=0, tiled=True)
    out, = call(
        finish_kernel, [((1, docs), f32, vmem)], [vmem, vmem],
        2 * docs * LANES * devices, 1 << 16,
    )(returned, info)
    return out.reshape(docs)


def solution(mesh):
    in_specs = (P(("slab", "docs", "blk"), None), P(), P(("slab", "docs", "blk")))
    out_specs = P(("slab", "docs", "blk"))
    return jax.shard_map(body, mesh=mesh, in_specs=in_specs, out_specs=out_specs, check_vma=False)
```

time: 102 us -> 88.6 us (0.87)
  blocking collectives: 77.9 us -> 35.6 us
  waiting for transfers between devices: 0.01 us -> 27.5 us
  Pallas kernels: 9 us -> 11.2 us
  local copies, waits for them, and re-layouts: 4.93 us -> 3.08 us
  starting transfers between devices: 9.01 us -> 10.1 us
    all_gather x1 -> x0, blocking collectives: 49.5 us -> none  [body(): all_ids = lax.all_gather(slot_ids, ('docs', 'blk'), axis=0, tiled=True)]
    all_to_all x1, waiting for transfers between devices: 0.01 us -> 27.5 us  [body(): lax.all_to_all(send_small.reshape(devices, cap_small, feature), ('docs',...]
    all_to_all x0 -> x1, blocking collectives: none -> 13.1 us  [body(): lax.all_to_all(send_ids, ('docs', 'blk'), split_axis=0, concat_axis=0, ti...]
    all_to_all x1, blocking collectives: 18 us -> 11.9 us  [body(): lax.all_to_all(back, ('docs', 'blk'), split_axis=0, concat_axis=0, tiled=...]
    ppermute x3, starting transfers between devices: 2.94 us -> 5.57 us  [body(): held.append(lax.ppermute(got_big, ('docs', 'blk'), pairs))]
    pallas_call x5 -> x6, Pallas kernels: 9 us -> 11.2 us  [the longest x1 4.18 us: body(): call(functools.partial(big_kernel, *sizes), [((devices, 1, LANES), f32, h...]
    unnamed x14 -> x6, local copies, waits for them, and re-layouts: 4.92 us -> 3.08 us
    all_to_all x1, starting transfers between devices: 6.07 us -> 4.55 us  [body(): lax.all_to_all(send_small.reshape(devices, cap_small, feature), ('docs',...]
  transfers between devices with their start and end apart: 4 -> 4, of which waited for: 0 -> 1; matrix products, arithmetic and copies ran while one was open for 0% -> 0% of each run, Pallas kernels for 2% -> 2%
where the time goes in v2:
time: 88.6 us; the launch traced here: 87.5 us
  blocking collectives  35.6 us (40%)
  waiting for transfers between devices  27.5 us (31%)
  Pallas kernels  11.2 us (13%)
  starting transfers between devices  10.1 us (11%)
  local copies, waits for them, and re-layouts  3.08 us (3%)
    all_to_all x1, waiting for transfers between devices, body(): lax.all_to_all(send_small.reshape(devices, cap_small, feature), ('docs',...  27.5 us
    all_to_all x1, blocking collectives, body(): lax.all_to_all(send_ids, ('docs', 'blk'), split_axis=0, concat_axis=0, ti...  13.1 us
    all_to_all x1, blocking collectives, body(): lax.all_to_all(back, ('docs', 'blk'), split_axis=0, concat_axis=0, tiled=...  11.9 us
    all_to_all x1, blocking collectives, body(): lax.all_to_all(send_big.reshape(shards, cap_big, feature), 'docs', split_...  10.5 us
    ppermute x3, starting transfers between devices, body(): held.append(lax.ppermute(got_big, ('docs', 'blk'), pairs))  5.57 us
    all_to_all x1, starting transfers between devices, body(): lax.all_to_all(send_small.reshape(devices, cap_small, feature), ('docs',...  4.55 us
    pallas_call x1, Pallas kernels, body(): call(functools.partial(big_kernel, *sizes), [((devices, 1, LANES), f32, h...  4.18 us
    pallas_call x1, Pallas kernels, body(): call(functools.partial(sort_kernel, *sizes), [((small_slots, feature), bf...  3.36 us
  transfers between devices with their start and end apart: 4, of which 1 were waited for; matrix products, arithmetic and copies ran while one was open for 0% of the time, Pallas kernels for 2%

profile of v2, /device:TPU:1, one launch (start us, length us, event | category | flops | bytes accessed | tf_op | source)
XLA Modules:
  0.0 87.5 jit_solution(18087097631708206044)
XLA Ops:
  0.0 0.0 copy-start
  0.0 1.3 %copy-done = bf16[768,768]{1,0:T(8,128)(2,1)S(1)} copy-done((bf16[768,768]{1,0:T(8,128)(2,1)S(1)}, bf16[768,768]{1,0:T(8,128)(2,1)}, u32[]{:S(2)}) %copy-start) | copy-done | bytes 1179672
  1.3 0.0 copy-start.1
  1.3 1.1 %copy-done.1 = bf16[512,768]{1,0:T(8,128)(2,1)S(1)} copy-done((bf16[512,768]{1,0:T(8,128)(2,1)S(1)}, bf16[512,768]{1,0:T(8,128)(2,1)}, u32[]{:S(2)}) %copy-start.1) | copy-done | bytes 786456
  2.4 0.0 copy-start.2
  2.4 0.7 copy-done.2
  3.1 3.4 %shard_map.37 = (bf16[768,768]{1,0:T(8,128)(2,1)}, bf16[512,768]{1,0:T(8,128)(2,1)S(1)}, s32[8,512]{1,0:T(8,128)S(1)}) custom-call(bf16[512,768]{1,0:T(8,128)(2,1)S(1)} %copy-done.1, bf16[768,768]{1,0:T(8,128)(2,1)S(1)} %copy-done, s32[1,512]{1,0:T(1,128)S(1)} %bitcast.12), custom_call_target="tpu_custom_call" | custom-call | flops 1207959552 | bytes 4194304 | tf_op jit(solution)/shard_map/pallas_call | solution.py:252
  6.5 1.2 %shard_map.38 = (bf16[256,768]{1,0:T(8,128)(2,1)}, f32[16,1,128]{2,1,0:T(1,128)}) custom-call(bf16[512,768]{1,0:T(8,128)(2,1)S(1)} %get-tuple-element.12.rows_ref, s32[8,512]{1,0:T(8,128)S(1)} %get-tuple-element.13.info_ref.where_ref), custom_call_target="tpu_custom_call" | custom-call | flops 201326592 | bytes 2097152 | tf_op jit(solution)/shard_map/pallas_call | solution.py:265
  7.7 13.1 %all_to_all.20.ids_ref = f32[16,1,128]{2,1,0:T(1,128)S(1)} all-to-all(f32[16,1,128]{2,1,0:T(1,128)} %get-tuple-element.15), channel_id=1, replica_groups=mesh['slab'=2,'docs'=4,'blk'=4] {'docs','blk'}, dimensions={0} | all-to-all | bytes 16384 | tf_op jit(solution)/shard_map/all_to_all | solution.py:275
  20.8 10.5 %all_to_all.21 = bf16[4,64,768]{2,1,0:T(8,128)(2,1)S(1)} all-to-all(bf16[4,64,768]{2,1,0:T(8,128)(2,1)} %bitcast.13), channel_id=1, replica_groups=mesh['slab'=2,'docs'=4,'blk'=4] {'docs'}, dimensions={0} | all-to-all | bytes 786432 | tf_op jit(solution)/shard_map/all_to_all | solution.py:272
  31.3 4.5 %all-to-all-start.2 = ((bf16[16,48,768]{2,1,0:T(8,128)(2,1)}), bf16[16,48,768]{2,1,0:T(8,128)(2,1)S(1)}, u32[]{:S(2)}, u32[]{:S(2)}) async-start(bf16[16,48,768]{2,1,0:T(8,128)(2,1)} %bitcast.4), calls=%async_computation.2 | async-start | bytes 2359296 | tf_op jit(solution)/shard_map/all_to_all | solution.py:261
  35.8 4.2 %collective-permute-start = (bf16[256,768]{1,0:T(8,128)(2,1)S(1)}, bf16[256,768]{1,0:T(8,128)(2,1)S(1)}, u32[]{:S(2)}, u32[]{:S(2)}) collective-permute-start(bf16[256,768]{1,0:T(8,128)(2,1)S(1)} %bitcast.8), channel_id=1, source_target_pairs={{0,1},{4,6},{8,9},{12,14},{16,17},{20,22},{24,25},{28,30}} | collective-permute-start | bytes 1179656 | tf_op jit(solution)/shard_map/ppermute | solution.py:283
  40.0 0.7 collective-permute-start.1
  40.7 0.7 collective-permute-start.2
  41.4 0.2 shard_map.39
  41.6 27.5 %all-to-all-done.2 = bf16[16,48,768]{2,1,0:T(8,128)(2,1)S(1)} async-done(((bf16[16,48,768]{2,1,0:T(8,128)(2,1)}), bf16[16,48,768]{2,1,0:T(8,128)(2,1)S(1)}, u32[]{:S(2)}, u32[]{:S(2)}) %all-to-all-start.2) | async-done | bytes 1179680 | tf_op jit(solution)/shard_map/all_to_all | solution.py:261
  69.1 1.2 %shard_map.40.refs_5_ = f32[1,768]{1,0:T(1,128)S(1)} custom-call(bf16[768,768]{1,0:T(8,128)(2,1)S(1)} %bitcast.7, f32[1,768]{1,0:T(1,128)S(1)} %get-tuple-element.18.row_ref), custom_call_target="tpu_custom_call" | custom-call | flops 905969664 | bytes 2097152 | tf_op jit(solution)/shard_map/pallas_call | solution.py:292
  70.3 0.0 collective-permute-done.refs_1_
  70.3 0.0 collective-permute-done.1.refs_2_
  70.4 0.0 collective-permute-done.2.refs_3_
  70.4 4.2 %shard_map.41 = f32[16,1,128]{2,1,0:T(1,128)} custom-call(s32[1]{0:T(128)} %bitcast.me_ref, bf16[256,768]{1,0:T(8,128)(2,1)S(1)} %bitcast.11, bf16[256,768]{1,0:T(8,128)(2,1)S(1)} %collective-permute-done.refs_1_, bf16[256,768]{1,0:T(8,128)(2,1)S(1)} %collective-permute-done.1.refs_2_, bf16[256,768]{1,0:T(8,128)(2,1)S(1)} %collective-permute-done.2.refs_3_, ...), custom_call_target="tpu_custom_call" | custom-call | flops 1610612736 | bytes 2097152 | tf_op jit(solution)/shard_map/pallas_call | solution.py:297
  74.6 11.9 %all_to_all.22.back_ref = f32[16,1,128]{2,1,0:T(1,128)S(1)} all-to-all(f32[16,1,128]{2,1,0:T(1,128)} %shard_map.41), channel_id=1, replica_groups=mesh['slab'=2,'docs'=4,'blk'=4] {'docs','blk'}, dimensions={0} | all-to-all | bytes 16384 | tf_op jit(solution)/shard_map/all_to_all | solution.py:305
  86.5 1.0 %shard_map.42 = f32[1,512]{1,0:T(1,128)} custom-call(f32[16,1,128]{2,1,0:T(1,128)S(1)} %all_to_all.22.back_ref, s32[8,512]{1,0:T(8,128)S(1)} %get-tuple-element.13.info_ref.where_ref), custom_call_target="tpu_custom_call" | custom-call | flops 2097152 | bytes 65536 | tf_op jit(solution)/shard_map/pallas_call | solution.py:306
Async XLA Ops:
  0.0 1.3 %copy-start = (bf16[768,768]{1,0:T(8,128)(2,1)S(1)}, bf16[768,768]{1,0:T(8,128)(2,1)}, u32[]{:S(2)}) copy-start(bf16[768,768]{1,0:T(8,128)(2,1)} %weight_hbm.1) | copy-start | bytes 3538948
  1.3 1.1 %copy-start.1 = (bf16[512,768]{1,0:T(8,128)(2,1)S(1)}, bf16[512,768]{1,0:T(8,128)(2,1)}, u32[]{:S(2)}) copy-start(bf16[512,768]{1,0:T(8,128)(2,1)} %pooled_hbm.1) | copy-start | bytes 2359300
  2.4 0.7 copy-start.2
  31.3 37.8 %all-to-all-start.2 = ((bf16[16,48,768]{2,1,0:T(8,128)(2,1)}), bf16[16,48,768]{2,1,0:T(8,128)(2,1)S(1)}, u32[]{:S(2)}, u32[]{:S(2)}) async-start(bf16[16,48,768]{2,1,0:T(8,128)(2,1)} %bitcast.4), calls=%async_computation.2 | async-start | bytes 2359296 | tf_op jit(solution)/shard_map/all_to_all | solution.py:261
  35.8 34.5 %collective-permute-start = (bf16[256,768]{1,0:T(8,128)(2,1)S(1)}, bf16[256,768]{1,0:T(8,128)(2,1)S(1)}, u32[]{:S(2)}, u32[]{:S(2)}) collective-permute-start(bf16[256,768]{1,0:T(8,128)(2,1)S(1)} %bitcast.8), channel_id=1, source_target_pairs={{0,1},{4,6},{8,9},{12,14},{16,17},{20,22},{24,25},{28,30}} | collective-permute-start | bytes 1179656 | tf_op jit(solution)/shard_map/ppermute | solution.py:283
  40.0 30.3 %collective-permute-start.1 = (bf16[256,768]{1,0:T(8,128)(2,1)S(1)}, bf16[256,768]{1,0:T(8,128)(2,1)S(1)}, u32[]{:S(2)}, u32[]{:S(2)}) collective-permute-start(bf16[256,768]{1,0:T(8,128)(2,1)S(1)} %bitcast.9), channel_id=1, source_target_pairs={{2,1},{5,6},{10,9},{13,14},{18,17},{21,22},{26,25},{29,30}} | collective-permute-start | bytes 1179656 | tf_op jit(solution)/shard_map/ppermute | solution.py:283
  40.7 29.6 %collective-permute-start.2 = (bf16[256,768]{1,0:T(8,128)(2,1)S(1)}, bf16[256,768]{1,0:T(8,128)(2,1)S(1)}, u32[]{:S(2)}, u32[]{:S(2)}) collective-permute-start(bf16[256,768]{1,0:T(8,128)(2,1)S(1)} %bitcast.10), channel_id=1, source_target_pairs={{3,1},{7,6},{11,9},{15,14},{19,17},{23,22},{27,25},{31,30}} | collective-permute-start | bytes 1179656 | tf_op jit(solution)/shard_map/ppermute | solution.py:283

commit v3 on v2

v3 whole, which is shorter than its diff:
```python
import functools

import jax
import jax.numpy as jnp
from jax import lax
from jax.experimental import pallas as pl
from jax.experimental.pallas import tpu as pltpu
from jax.sharding import PartitionSpec as P

BIG_OWN = 4
LANES = 128


def modulo(x, n):
    return x & (n - 1) if n & (n - 1) == 0 else lax.rem(x, jnp.int32(n))


def quotient(x, n):
    if n & (n - 1) == 0:
        return lax.shift_right_logical(x, jnp.int32(n.bit_length() - 1))
    return lax.div(x, jnp.int32(n))


def iota(shape, axis):
    return lax.broadcasted_iota(jnp.int32, shape, axis)


def dot_nt(a, b):
    return lax.dot_general(a, b, (((1,), (1,)), ((), ())), preferred_element_type=jnp.float32)


def tile_of(rows, most=256):
    tile = most
    while rows % tile:
        tile //= 2
    return tile


def home_of(docs, blocks):
    return max(blocks // 2 - 1, 0) + (docs & min(blocks - 1, 1))


def sort_kernel(shards, blocks, cap_big, cap_small, pooled_hbm, weight_hbm, cluster_hbm,
                small_hbm, rows_hbm, info_hbm, pooled_ref, weight_ref, cluster_ref, stage_ref, rows_ref, info_ref,
                sems, out_sems):
    docs = pooled_ref.shape[0]
    devices = shards * blocks
    limit = BIG_OWN * shards
    small_slots = devices * cap_small
    buckets = devices + shards

    fetches = [pltpu.make_async_copy(source, target, sems.at[n]) for n, (source, target) in enumerate(
        ((cluster_hbm, cluster_ref), (weight_hbm, weight_ref), (pooled_hbm, pooled_ref)))]
    for fetch in fetches:
        fetch.start()
    fetches[0].wait()

    cluster = cluster_ref[...]
    is_big = cluster < limit
    owner = modulo(cluster, shards)
    past = jnp.maximum(cluster - limit, 0)
    target = modulo(past, devices)
    bucket = jnp.where(is_big, devices + owner, target)
    quota = jnp.where(is_big, quotient(cluster, shards), quotient(past, devices)) + 1

    padded = -(-buckets // 16) * 16
    hot = (iota((padded, docs), 0) == bucket).astype(jnp.float32)
    earlier = (iota((docs, docs), 0) < iota((docs, docs), 1)).astype(jnp.float32).astype(jnp.bfloat16)
    before = jnp.dot(hot.astype(jnp.bfloat16), earlier, preferred_element_type=jnp.float32)
    rank = jnp.sum(before * hot, axis=0, keepdims=True).astype(jnp.int32)
    slot = jnp.where(is_big, small_slots + owner * cap_big + rank, target * cap_small + rank)

    home = home_of(owner, blocks)
    info_ref[0:1, :] = jnp.where(is_big, owner * blocks + home, target)
    info_ref[1:2, :] = jnp.where(is_big, cap_small + rank, rank)
    info_ref[2:3, :] = slot
    info_ref[3:4, :] = quota
    info_ref[4:5, :] = bucket
    info_ref[5:8, :] = jnp.zeros((3, docs), jnp.int32)
    keeps = [pltpu.make_async_copy(info_ref, info_hbm, sems.at[3]),
             pltpu.make_async_copy(rows_ref, rows_hbm, sems.at[4])]
    keeps[0].start()

    for fetch in fetches[1:]:
        fetch.wait()
    projected = jnp.dot(pooled_ref[...], weight_ref[...], preferred_element_type=jnp.float32)
    squares = jnp.sum(projected * projected, axis=1, keepdims=True)
    rows_ref[...] = (projected / jnp.sqrt(squares + 1e-06)).astype(jnp.bfloat16)
    keeps[1].start()

    tile = small_slots // out_sems.shape[0]
    for part in range(out_sems.shape[0]):
        at = part * tile
        stage_ref[at:at + tile, :] = picked_rows(rows_ref, slot, at, tile)
        keeps.append(pltpu.make_async_copy(
            stage_ref.at[pl.ds(at, tile)], small_hbm.at[pl.ds(at, tile)], out_sems.at[part]))
        keeps[-1].start()
    for keep in keeps:
        keep.wait()


def picked_rows(rows_ref, slot, first, count):
    docs = rows_ref.shape[0]
    pick = (iota((count, docs), 0) + first == slot).astype(jnp.float32).astype(jnp.bfloat16)
    return jnp.dot(pick, rows_ref[...], preferred_element_type=jnp.float32).astype(jnp.bfloat16)


def sort_big_kernel(shards, blocks, cap_big, cap_small, me_ref, rows_ref, info_ref, *out_refs):
    docs = rows_ref.shape[0]
    devices = shards * blocks
    lane, slot = info_ref[1:2, :], info_ref[2:3, :]
    quota, bucket = info_ref[3:4, :].astype(jnp.float32), info_ref[4:5, :]
    place = (iota((LANES, docs), 0) == lane).astype(jnp.float32).astype(jnp.bfloat16)
    for shift, ref in enumerate(out_refs):
        to = modulo(me_ref[0] + shift, shards)
        ref[0:cap_big, :] = picked_rows(rows_ref, slot, devices * cap_small + to * cap_big, cap_big)
        table = ref.shape[0] - cap_big
        blk = iota((table, docs), 0)
        mine = (blk < blocks) & ((blk + to * blocks == bucket) | (bucket == devices + to))
        values = jnp.where(mine, quota, 0.0).astype(jnp.bfloat16)
        ref[cap_big:, 0:LANES] = dot_nt(values, place).astype(jnp.bfloat16)
        ref[cap_big:, LANES:] = jnp.zeros((table, ref.shape[1] - LANES), jnp.bfloat16)


def group_kernel(shards, blocks, cap_big, me_ref, *refs):
    held, group_ref, ids_refs = refs[:shards], refs[shards], refs[shards + 1:]
    tables = []
    for shift, ref in enumerate(held):
        group_ref[shift * cap_big:(shift + 1) * cap_big, :] = ref[0:cap_big, :]
        tables.append(ref[cap_big:, 0:LANES].astype(jnp.float32))
    for step, ref in enumerate(ids_refs):
        to = modulo(me_ref[1] + step, blocks)
        ref[...] = jnp.zeros(ref.shape, jnp.float32)
        for shift, table in enumerate(tables):
            ref[shift:shift + 1, :] = jnp.sum(
                jnp.where(iota(table.shape, 0) == to, table, 0.0), axis=0, keepdims=True)


def store_rows(values, ref):
    for device in range(ref.shape[0]):
        ref[device, 0:1, :] = values[device:device + 1, :]


def load_rows(ref):
    return jnp.concatenate([ref[device, 0:1, :] for device in range(ref.shape[0])], axis=0)


def small_sources(total, blocks, cap_small):
    at = iota((1, total), 1)
    source = at // cap_small
    return source // blocks, modulo(source, blocks), lax.rem(at, jnp.int32(cap_small))


def big_sources(total, my_docs, shards, blocks, cap_big, cap_small):
    at = iota((1, total), 1)
    part = at // (shards * cap_big)
    home = home_of(my_docs, blocks)
    blk = jnp.where(part == 0, home, jnp.where(part - 1 >= home, part, part - 1))
    docs = modulo(my_docs + shards - modulo(at // cap_big, shards), shards)
    return docs, blk, cap_small + lax.rem(at, jnp.int32(cap_big))


def ids_kernel(shards, blocks, cap_big, cap_small, me_ref, *refs):
    tables, small_ref, big_ref = refs[:blocks], refs[blocks], refs[blocks + 1]
    high = tables[0].shape[0]
    values = jnp.concatenate([table[...] for table in tables], axis=0)
    values = jnp.concatenate([values, jnp.zeros_like(values)], axis=0).astype(jnp.bfloat16)
    for ref, (docs, blk, lane) in (
        (small_ref, small_sources(small_ref.shape[1], blocks, cap_small)),
        (big_ref, big_sources(big_ref.shape[1], me_ref[0], shards, blocks, cap_big, cap_small)),
    ):
        total = ref.shape[1]
        pick = (iota((LANES, total), 0) == lane).astype(jnp.float32).astype(jnp.bfloat16)
        found = jnp.dot(values, pick, preferred_element_type=jnp.float32)
        row = modulo(me_ref[1] + blocks - blk, blocks) * high + modulo(me_ref[0] + shards - docs, shards)
        ref[...] = jnp.sum(jnp.where(iota(found.shape, 0) == row, found, 0.0), axis=0, keepdims=True)


def as_column(row):
    return jnp.broadcast_to(row, (8, row.shape[1])).T[:, 0:1]


def block_best(queries, col_ids, first_row, others, row_ids, first_col):
    scores = dot_nt(queries, others)
    allowed = (col_ids == row_ids) & (row_ids > 0.0)
    if first_row is not None:
        allowed &= (iota(scores.shape, 0) + first_row) != (iota(scores.shape, 1) + first_col)
    return jnp.max(jnp.where(allowed, scores, -1.0), axis=0, keepdims=True)


def big_kernel(*refs):
    held, row_ref, best_ref = refs[:-2], refs[-2], refs[-1]
    size = held[0].shape[0]
    col_ids = as_column(row_ref[...])
    bests = [jnp.full((1, size), -1.0, jnp.float32) for _ in held]
    for row, queries in enumerate(held):
        for col, others in enumerate(held):
            same = 0 if row == col else None
            bests[col] = jnp.maximum(bests[col], block_best(
                queries[...], col_ids[row * size:(row + 1) * size], same,
                others[...], row_ref[:, col * size:(col + 1) * size], same))
    for col, best in enumerate(bests):
        best_ref[:, col * size:(col + 1) * size] = best


def small_kernel(shards, blocks, cap_big, cap_small, me_ref, rows_ref, row_ref, big_ref,
                 back_hbm, lanes_ref, sem):
    devices = shards * blocks
    total = rows_ref.shape[0]

    def spread(best, docs, blk, lane):
        mine = jnp.where(iota((devices, best.shape[1]), 0) == docs * blocks + blk, best, 0.0)
        place = (iota((LANES, best.shape[1]), 0) == lane).astype(jnp.float32)
        return lax.dot_general(mine, place, (((1,), (1,)), ((), ())),
                               precision=lax.Precision.HIGHEST, preferred_element_type=jnp.float32)

    back = spread(big_ref[...], *big_sources(big_ref.shape[1], me_ref[0], shards, blocks, cap_big, cap_small))
    col_ids = as_column(row_ref[...])
    tile = tile_of(total)
    best = jnp.full((1, total), -1.0, jnp.float32)
    for at in range(0, total, tile):
        best = jnp.maximum(best, block_best(
            rows_ref[at:at + tile, :], col_ids[at:at + tile], at, rows_ref[...], row_ref[...], 0))
    back += spread(best, *small_sources(total, blocks, cap_small))
    store_rows(back, lanes_ref)
    send = pltpu.make_async_copy(lanes_ref, back_hbm, sem)
    send.start()
    send.wait()


def masks_kernel(info_ref, device_ref, lane_ref):
    device_ref[...] = (iota(device_ref.shape, 0) == info_ref[0:1, :]).astype(jnp.float32)
    lane_ref[...] = (iota(lane_ref.shape, 0) == info_ref[1:2, :]).astype(jnp.float32)


def finish_kernel(back_ref, device_ref, lane_ref, out_ref):
    found = lax.dot_general(load_rows(back_ref), device_ref[...], (((0,), (0,)), ((), ())),
                            precision=lax.Precision.HIGHEST, preferred_element_type=jnp.float32)
    out_ref[...] = jnp.sum(jnp.where(lane_ref[...] > 0.0, found, 0.0), axis=0, keepdims=True)


def call(kernel, outs, ins, flops, moved, limit=16, scratch=()):
    specs = [pl.BlockSpec(memory_space=space) for _, _, space in outs]
    return pl.pallas_call(
        kernel,
        out_shape=[space(shape, dtype) if space is pltpu.HBM else jax.ShapeDtypeStruct(shape, dtype)
                   for shape, dtype, space in outs],
        in_specs=[pl.BlockSpec(memory_space=space) for space in ins],
        out_specs=specs,
        scratch_shapes=scratch,
        cost_estimate=pl.CostEstimate(flops=flops, bytes_accessed=moved, transcendentals=0),
        compiler_params=pltpu.CompilerParams(vmem_limit_bytes=limit << 20),
    )


def body(pooled, proj_weight, cluster):
    shards = lax.axis_size("docs")
    blocks = lax.axis_size("blk")
    devices = shards * blocks
    docs = pooled.shape[0]
    feature = proj_weight.shape[1]
    big_count = docs // 4
    small_count = docs - big_count
    cap_big = 2 * big_count // shards
    cap_small = 2 * small_count // devices
    small_slots = devices * cap_small
    big_slots = shards * cap_big
    big_total = blocks * big_slots
    sizes = (shards, blocks, cap_big, cap_small)
    f32, bf16, i32 = jnp.float32, jnp.bfloat16, jnp.int32
    vmem, hbm, smem, dma = pltpu.VMEM, pltpu.HBM, pltpu.SMEM, pltpu.SemaphoreType.DMA

    send_small, rows, info = call(
        functools.partial(sort_kernel, *sizes),
        [((small_slots, feature), bf16, hbm), ((docs, feature), bf16, hbm), ((8, docs), i32, hbm)],
        [hbm, hbm, hbm],
        2 * docs * feature * (pooled.shape[1] + small_slots), 4 << 20, 60,
        [vmem(pooled.shape, bf16), vmem(proj_weight.shape, bf16), vmem((1, docs), i32),
         vmem((small_slots, feature), bf16), vmem((docs, feature), bf16), vmem((8, docs), i32),
         dma((5,)), dma((3,))],
    )(pooled, proj_weight, cluster.reshape(1, docs))

    got_small = lax.all_to_all(
        send_small.reshape(devices, cap_small, feature), ("docs", "blk"),
        split_axis=0, concat_axis=0, tiled=True).reshape(small_slots, feature)

    def along(x, axis, count, by):
        return lax.ppermute(x, axis, [(i, (i + by) % count) for i in range(count)])

    me = jnp.stack([lax.axis_index("docs"), lax.axis_index("blk")]).astype(i32)
    table = -(-blocks // 16) * 16
    sent = call(
        functools.partial(sort_big_kernel, *sizes),
        [((cap_big + table, feature), bf16, vmem)] * shards,
        [smem, vmem, vmem],
        2 * docs * feature * big_slots, 2 << 20,
    )(me, rows, info)
    held = [sent[0]] + [along(sent[by], "docs", shards, by) for by in range(1, shards)]

    high = -(-shards // 8) * 8
    group, *tables = call(
        functools.partial(group_kernel, shards, blocks, cap_big),
        [((big_slots, feature), bf16, vmem)] + [((high, LANES), f32, vmem)] * blocks,
        [smem] + [vmem] * shards,
        big_slots * feature, 1 << 20,
    )(me, *held)

    parts = [group]
    for step in range(blocks - 1):
        homes = [home_of(d, blocks) for d in range(shards)]
        pairs = [(d * blocks + (step if step < homes[d] else step + 1), d * blocks + homes[d])
                 for d in range(shards)]
        parts.append(lax.ppermute(group, ("docs", "blk"), pairs))
    tables = [tables[0]] + [along(tables[by], "blk", blocks, by) for by in range(1, blocks)]

    small_ids, big_ids = call(
        functools.partial(ids_kernel, *sizes),
        [((1, small_slots), f32, vmem), ((1, big_total), f32, vmem)],
        [smem] + [vmem] * blocks,
        2 * high * blocks * LANES * (small_slots + big_total), 1 << 16,
    )(me, *tables)

    best_big, = call(
        big_kernel, [((1, big_total), f32, vmem)], [vmem] * (blocks + 1),
        2 * big_total * big_total * feature, 2 << 20,
    )(*parts, big_ids)

    back, = call(
        functools.partial(small_kernel, *sizes),
        [((devices, 1, LANES), f32, hbm)], [smem, vmem, vmem, vmem],
        2 * small_slots * small_slots * feature, 2 << 20, 16,
        [vmem((devices, 1, LANES), f32), dma],
    )(me, got_small, small_ids, best_big)

    returned = lax.all_to_all(back, ("docs", "blk"), split_axis=0, concat_axis=0, tiled=True)
    masks = call(
        masks_kernel, [((devices, docs), f32, vmem), ((LANES, docs), f32, vmem)], [vmem],
        docs * LANES, 1 << 18,
    )(info)
    out, = call(
        finish_kernel, [((1, docs), f32, vmem)], [vmem, vmem, vmem],
        2 * docs * LANES * devices, 1 << 18,
    )(returned, *masks)
    return out.reshape(docs)


def solution(mesh):
    in_specs = (P(("slab", "docs", "blk"), None), P(), P(("slab", "docs", "blk")))
    out_specs = P(("slab", "docs", "blk"))
    return jax.shard_map(body, mesh=mesh, in_specs=in_specs, out_specs=out_specs, check_vma=False)
```

time: 88.6 us -> 69.4 us (0.78)
  blocking collectives: 35.6 us -> 0 us
  starting transfers between devices: 10.1 us -> 21.2 us
  waiting for transfers between devices: 27.5 us -> 32.8 us
  local copies, waits for them, and re-layouts: 3.08 us -> 0.01 us
  Pallas kernels: 11.2 us -> 14.2 us
    all_to_all x3 -> x0, blocking collectives: 35.6 us -> none  [the longest x1 13.1 us: body(): lax.all_to_all(send_ids, ('docs', 'blk'), split_axis=0, concat_axis=0, ti...]
    all_to_all x1, waiting for transfers between devices: 27.5 us -> 0.01 us  [body(): lax.all_to_all(send_small.reshape(devices, cap_small, feature), ('docs',...]
    ppermute x3 -> x9, waiting for transfers between devices: 0.01 us -> 27.1 us  [the longest x6 27.1 us: along(): return lax.ppermute(x, axis, [(i, (i + by) % count) for i in range(count)])]
    all_to_all x0 -> x1, waiting for transfers between devices: none -> 5.77 us  [body(): lax.all_to_all(back, ('docs', 'blk'), split_axis=0, concat_axis=0, tiled=...]
    all_to_all x0 -> x1, starting transfers between devices: none -> 5.13 us  [body(): lax.all_to_all(back, ('docs', 'blk'), split_axis=0, concat_axis=0, tiled=...]
    unnamed x6 -> x4, local copies, waits for them, and re-layouts: 3.08 us -> 0.01 us
    ppermute x3 -> x9, starting transfers between devices: 5.57 us -> 8.64 us  [the longest x6 5.95 us: along(): return lax.ppermute(x, axis, [(i, (i + by) % count) for i in range(count)])]
    all_to_all x1, starting transfers between devices: 4.55 us -> 7.47 us  [body(): lax.all_to_all(send_small.reshape(devices, cap_small, feature), ('docs',...]
  transfers between devices with their start and end apart: 4 -> 11, of which waited for: 1 -> 6; matrix products, arithmetic and copies ran while one was open for 0% -> 0% of each run, Pallas kernels for 2% -> 7%
where the time goes in v3:
time: 69.4 us; the launch traced here: 68.5 us
  waiting for transfers between devices  32.8 us (47%)
  starting transfers between devices  21.2 us (31%)
  Pallas kernels  14.2 us (20%)
    ppermute x6, waiting for transfers between devices, along(): return lax.ppermute(x, axis, [(i, (i + by) % count) for i in range(count)])  27.1 us
    all_to_all x1, starting transfers between devices, body(): lax.all_to_all(send_small.reshape(devices, cap_small, feature), ('docs',...  7.47 us
    ppermute x6, starting transfers between devices, along(): return lax.ppermute(x, axis, [(i, (i + by) % count) for i in range(count)])  5.95 us
    all_to_all x1, waiting for transfers between devices, body(): lax.all_to_all(back, ('docs', 'blk'), split_axis=0, concat_axis=0, tiled=...  5.77 us
    all_to_all x1, starting transfers between devices, body(): lax.all_to_all(back, ('docs', 'blk'), split_axis=0, concat_axis=0, tiled=...  5.13 us
    pallas_call x1, Pallas kernels, body(): call(functools.partial(sort_kernel, *sizes), [((small_slots, feature), bf...  4.38 us
    pallas_call x1, Pallas kernels, body(): call(functools.partial(small_kernel, *sizes), [((devices, 1, LANES), f32,...  4.14 us
    ppermute x3, starting transfers between devices, body(): parts.append(lax.ppermute(group, ('docs', 'blk'), pairs))  2.69 us
  transfers between devices with their start and end apart: 11, of which 6 were waited for; matrix products, arithmetic and copies ran while one was open for 0% of the time, Pallas kernels for 7%

profile of v3, /device:TPU:1, one launch (start us, length us, event | category | flops | bytes accessed | tf_op | source)
XLA Modules:
  0.0 68.5 jit_solution(314859003980107585)
XLA Ops:
  0.0 4.4 %shard_map.37 = (bf16[768,768]{1,0:T(8,128)(2,1)}, bf16[512,768]{1,0:T(8,128)(2,1)}, s32[8,512]{1,0:T(8,128)}) custom-call(bf16[512,768]{1,0:T(8,128)(2,1)} %pooled_hbm.1, bf16[768,768]{1,0:T(8,128)(2,1)} %weight_hbm.1, s32[1,512]{1,0:T(1,128)} %bitcast.8), custom_call_target="tpu_custom_call" | custom-call | flops 1207959552 | bytes 4194304 | tf_op jit(solution)/shard_map/pallas_call | solution.py:273
  4.4 0.0 copy-start
  4.4 0.0 copy-start.1
  4.4 7.5 %all-to-all-start = ((bf16[16,48,768]{2,1,0:T(8,128)(2,1)}), bf16[16,48,768]{2,1,0:T(8,128)(2,1)S(1)}, u32[]{:S(2)}, u32[]{:S(2)}) async-start(bf16[16,48,768]{2,1,0:T(8,128)(2,1)} %bitcast.7), calls=%async_computation | async-start | bytes 2359296 | tf_op jit(solution)/shard_map/all_to_all | solution.py:283
  11.9 0.1 pad_add_fusion.me_ref
  11.9 0.0 copy-done
  12.0 0.0 copy-done.1
  12.0 1.3 %shard_map.38 = (bf16[80,768]{1,0:T(8,128)(2,1)S(1)}, bf16[80,768]{1,0:T(8,128)(2,1)S(1)}, bf16[80,768]{1,0:T(8,128)(2,1)S(1)}, bf16[80,768]{1,0:T(8,128)(2,1)S(1)}) custom-call(s32[2]{0:T(128)S(1)} %pad_add_fusion.me_ref, bf16[512,768]{1,0:T(8,128)(2,1)S(1)} %copy-done, s32[8,512]{1,0:T(8,128)S(1)} %copy-done.1), custom_call_target="tpu_custom_call" | custom-call | flops 201326592 | bytes 2097152 | tf_op jit(solution)/shard_map/pallas_call | solution.py:292
  13.3 1.7 %collective-permute-start = (bf16[80,768]{1,0:T(8,128)(2,1)S(1)}, bf16[80,768]{1,0:T(8,128)(2,1)S(1)}, u32[]{:S(2)}, u32[]{:S(2)}) collective-permute-start(bf16[80,768]{1,0:T(8,128)(2,1)S(1)} %get-tuple-element.25), channel_id=1, source_target_pairs={{0,4},{4,8},{8,12},{12,0},{1,5},{5,9},{9,13},{13,1},{2,6},{6,10},{... | collective-permute-start | bytes 368648 | tf_op jit(solution)/shard_map/ppermute | solution.py:288
  15.0 0.0 collective-permute-start.1
  15.0 0.5 collective-permute-start.2
  15.5 9.1 %collective-permute-done.refs_1_ = bf16[80,768]{1,0:T(8,128)(2,1)S(1)} collective-permute-done((bf16[80,768]{1,0:T(8,128)(2,1)S(1)}, bf16[80,768]{1,0:T(8,128)(2,1)S(1)}, u32[]{:S(2)}, u32[]{:S(2)}) %collective-permute-start) | collective-permute-done | bytes 122912 | tf_op jit(solution)/shard_map/ppermute | solution.py:288
  24.7 6.7 %collective-permute-done.1.refs_2_ = bf16[80,768]{1,0:T(8,128)(2,1)S(1)} collective-permute-done((bf16[80,768]{1,0:T(8,128)(2,1)S(1)}, bf16[80,768]{1,0:T(8,128)(2,1)S(1)}, u32[]{:S(2)}, u32[]{:S(2)}) %collective-permute-start.1) | collective-permute-done | bytes 122912 | tf_op jit(solution)/shard_map/ppermute | solution.py:288
  31.3 0.5 collective-permute-done.2.refs_3_
  31.8 0.6 shard_map.39
  32.4 1.3 %collective-permute-start.6 = (bf16[256,768]{1,0:T(8,128)(2,1)S(1)}, bf16[256,768]{1,0:T(8,128)(2,1)S(1)}, u32[]{:S(2)}, u32[]{:S(2)}) collective-permute-start(bf16[256,768]{1,0:T(8,128)(2,1)S(1)} %get-tuple-element.33.refs_0_), channel_id=1, source_target_pairs={{0,1},{4,6},{8,9},{12,14},{16,17},{20,22},{24,25},{28,30}} | collective-permute-start | bytes 1179656 | tf_op jit(solution)/shard_map/ppermute | solution.py:313
  33.7 0.7 %collective-permute-start.7 = (bf16[256,768]{1,0:T(8,128)(2,1)S(1)}, bf16[256,768]{1,0:T(8,128)(2,1)S(1)}, u32[]{:S(2)}, u32[]{:S(2)}) collective-permute-start(bf16[256,768]{1,0:T(8,128)(2,1)S(1)} %get-tuple-element.33.refs_0_), channel_id=1, source_target_pairs={{2,1},{5,6},{10,9},{13,14},{18,17},{21,22},{26,25},{29,30}} | collective-permute-start | bytes 1179656 | tf_op jit(solution)/shard_map/ppermute | solution.py:313
  34.4 0.7 %collective-permute-start.8 = (bf16[256,768]{1,0:T(8,128)(2,1)S(1)}, bf16[256,768]{1,0:T(8,128)(2,1)S(1)}, u32[]{:S(2)}, u32[]{:S(2)}) collective-permute-start(bf16[256,768]{1,0:T(8,128)(2,1)S(1)} %get-tuple-element.33.refs_0_), channel_id=1, source_target_pairs={{3,1},{7,6},{11,9},{15,14},{19,17},{23,22},{27,25},{31,30}} | collective-permute-start | bytes 1179656 | tf_op jit(solution)/shard_map/ppermute | solution.py:313
  35.1 0.5 collective-permute-start.3
  35.6 3.2 %collective-permute-start.4 = (f32[8,128]{1,0:T(8,128)S(1)}, f32[8,128]{1,0:T(8,128)S(1)}, u32[]{:S(2)}, u32[]{:S(2)}) collective-permute-start(f32[8,128]{1,0:T(8,128)S(1)} %get-tuple-element.30), channel_id=1, source_target_pairs={{0,2},{1,3},{2,0},{3,1},{4,6},{5,7},{6,4},{7,5},{8,10},{9,11},{10,... | collective-permute-start | bytes 12296 | tf_op jit(solution)/shard_map/ppermute | solution.py:288
  38.9 8.3 %collective-permute-done.3.refs_1_ = f32[8,128]{1,0:T(8,128)S(1)} collective-permute-done((f32[8,128]{1,0:T(8,128)S(1)}, f32[8,128]{1,0:T(8,128)S(1)}, u32[]{:S(2)}, u32[]{:S(2)}) %collective-permute-start.3) | collective-permute-done | bytes 4128 | tf_op jit(solution)/shard_map/ppermute | solution.py:288
  47.1 0.0 collective-permute-start.5
  47.1 0.0 collective-permute-done.4.refs_2_
  47.1 2.5 %collective-permute-done.5.refs_3_ = f32[8,128]{1,0:T(8,128)S(1)} collective-permute-done((f32[8,128]{1,0:T(8,128)S(1)}, f32[8,128]{1,0:T(8,128)S(1)}, u32[]{:S(2)}, u32[]{:S(2)}) %collective-permute-start.5) | collective-permute-done | bytes 4128 | tf_op jit(solution)/shard_map/ppermute | solution.py:288
  49.6 0.8 %shard_map.40 = (f32[1,768]{1,0:T(1,128)S(1)}, f32[1,1024]{1,0:T(1,128)S(1)}) custom-call(s32[2]{0:T(128)S(1)} %pad_add_fusion.me_ref, f32[8,128]{1,0:T(8,128)S(1)} %get-tuple-element.28.refs_0_, f32[8,128]{1,0:T(8,128)S(1)} %collective-permute-done.3.refs_1_, f32[8,128]{1,0:T(8,128)S(1)} %collective-permute-done.4.refs_2_, ...), custom_call_target="tpu_custom_call" | custom-call | flops 14680064 | bytes 65536 | tf_op jit(solution)/shard_map/pallas_call | solution.py:316
  50.4 0.0 collective-permute-done.6.refs_1_
  50.4 0.0 collective-permute-done.7.refs_2_
  50.4 0.0 collective-permute-done.8.refs_3_
  50.4 1.9 %shard_map.41.big_ref = f32[1,1024]{1,0:T(1,128)S(1)} custom-call(bf16[256,768]{1,0:T(8,128)(2,1)S(1)} %get-tuple-element.33.refs_0_, bf16[256,768]{1,0:T(8,128)(2,1)S(1)} %collective-permute-done.6.refs_1_, bf16[256,768]{1,0:T(8,128)(2,1)S(1)} %collective-permute-done.7.refs_2_, bf16[256,768]{1,0:T(8,128)(2,1)S(1)} %collective-permute-done.8.refs_3_, ...), custom_call_target="tpu_custom_call" | custom-call | flops 1610612736 | bytes 2097152 | tf_op jit(solution)/shard_map/pallas_call | solution.py:323
  52.4 0.0 all-to-all-done
  52.4 4.1 %shard_map.42 = f32[16,1,128]{2,1,0:T(1,128)} custom-call(s32[2]{0:T(128)S(1)} %pad_add_fusion.me_ref, bf16[768,768]{1,0:T(8,128)(2,1)S(1)} %bitcast.6, f32[1,768]{1,0:T(1,128)S(1)} %get-tuple-element.32.row_ref, f32[1,1024]{1,0:T(1,128)S(1)} %shard_map.41.big_ref), custom_call_target="tpu_custom_call" | custom-call | flops 905969664 | bytes 2097152 | tf_op jit(solution)/shard_map/pallas_call | solution.py:328
  56.5 5.1 %all-to-all-start.1 = ((f32[16,1,128]{2,1,0:T(1,128)}), f32[16,1,128]{2,1,0:T(1,128)S(1)}, u32[]{:S(2)}, u32[]{:S(2)}) async-start(f32[16,1,128]{2,1,0:T(1,128)} %shard_map.42), calls=%async_computation.1 | async-start | bytes 16384 | tf_op jit(solution)/shard_map/all_to_all | solution.py:335
  61.7 5.8 %all-to-all-done.1.back_ref = f32[16,1,128]{2,1,0:T(1,128)S(1)} async-done(((f32[16,1,128]{2,1,0:T(1,128)}), f32[16,1,128]{2,1,0:T(1,128)S(1)}, u32[]{:S(2)}, u32[]{:S(2)}) %all-to-all-start.1) | async-done | bytes 8224 | tf_op jit(solution)/shard_map/all_to_all | solution.py:335
  67.5 1.0 %shard_map.44 = f32[1,512]{1,0:T(1,128)} custom-call(f32[16,1,128]{2,1,0:T(1,128)S(1)} %all-to-all-done.1.back_ref, f32[16,512]{1,0:T(8,128)S(1)} %get-tuple-element.35.device_ref, f32[128,512]{1,0:T(8,128)S(1)} %get-tuple-element.36.lane_ref), custom_call_target="tpu_custom_call" | custom-call | flops 2097152 | bytes 262144 | tf_op jit(solution)/shard_map/pallas_call | solution.py:340
  (1 shorter events, 0.0 us)
Async XLA Ops:
  4.4 7.6 %copy-start = (bf16[512,768]{1,0:T(8,128)(2,1)S(1)}, bf16[512,768]{1,0:T(8,128)(2,1)}, u32[]{:S(2)}) copy-start(bf16[512,768]{1,0:T(8,128)(2,1)} %get-tuple-element.22.rows_ref) | copy-start | bytes 2359300
  4.4 7.6 %copy-start.1 = (s32[8,512]{1,0:T(8,128)S(1)}, s32[8,512]{1,0:T(8,128)}, u32[]{:S(2)}) copy-start(s32[8,512]{1,0:T(8,128)} %get-tuple-element.23.info_ref) | copy-start | bytes 49156
  4.4 48.0 %all-to-all-start = ((bf16[16,48,768]{2,1,0:T(8,128)(2,1)}), bf16[16,48,768]{2,1,0:T(8,128)(2,1)S(1)}, u32[]{:S(2)}, u32[]{:S(2)}) async-start(bf16[16,48,768]{2,1,0:T(8,128)(2,1)} %bitcast.7), calls=%async_computation | async-start | bytes 2359296 | tf_op jit(solution)/shard_map/all_to_all | solution.py:283
  13.3 11.4 %collective-permute-start = (bf16[80,768]{1,0:T(8,128)(2,1)S(1)}, bf16[80,768]{1,0:T(8,128)(2,1)S(1)}, u32[]{:S(2)}, u32[]{:S(2)}) collective-permute-start(bf16[80,768]{1,0:T(8,128)(2,1)S(1)} %get-tuple-element.25), channel_id=1, source_target_pairs={{0,4},{4,8},{8,12},{12,0},{1,5},{5,9},{9,13},{13,1},{2,6},{6,10},{... | collective-permute-start | bytes 368648 | tf_op jit(solution)/shard_map/ppermute | solution.py:288
  15.0 16.4 %collective-permute-start.1 = (bf16[80,768]{1,0:T(8,128)(2,1)S(1)}, bf16[80,768]{1,0:T(8,128)(2,1)S(1)}, u32[]{:S(2)}, u32[]{:S(2)}) collective-permute-start(bf16[80,768]{1,0:T(8,128)(2,1)S(1)} %get-tuple-element.26), channel_id=1, source_target_pairs={{0,8},{4,12},{8,0},{12,4},{1,9},{5,13},{9,1},{13,5},{2,10},{6,14},... | collective-permute-start | bytes 368648 | tf_op jit(solution)/shard_map/ppermute | solution.py:288
  15.0 16.8 %collective-permute-start.2 = (bf16[80,768]{1,0:T(8,128)(2,1)S(1)}, bf16[80,768]{1,0:T(8,128)(2,1)S(1)}, u32[]{:S(2)}, u32[]{:S(2)}) collective-permute-start(bf16[80,768]{1,0:T(8,128)(2,1)S(1)} %get-tuple-element.27), channel_id=1, source_target_pairs={{0,12},{4,0},{8,4},{12,8},{1,13},{5,1},{9,5},{13,9},{2,14},{6,2},{... | collective-permute-start | bytes 368648 | tf_op jit(solution)/shard_map/ppermute | solution.py:288
  32.4 18.0 %collective-permute-start.6 = (bf16[256,768]{1,0:T(8,128)(2,1)S(1)}, bf16[256,768]{1,0:T(8,128)(2,1)S(1)}, u32[]{:S(2)}, u32[]{:S(2)}) collective-permute-start(bf16[256,768]{1,0:T(8,128)(2,1)S(1)} %get-tuple-element.33.refs_0_), channel_id=1, source_target_pairs={{0,1},{4,6},{8,9},{12,14},{16,17},{20,22},{24,25},{28,30}} | collective-permute-start | bytes 1179656 | tf_op jit(solution)/shard_map/ppermute | solution.py:313
  33.7 16.7 %collective-permute-start.7 = (bf16[256,768]{1,0:T(8,128)(2,1)S(1)}, bf16[256,768]{1,0:T(8,128)(2,1)S(1)}, u32[]{:S(2)}, u32[]{:S(2)}) collective-permute-start(bf16[256,768]{1,0:T(8,128)(2,1)S(1)} %get-tuple-element.33.refs_0_), channel_id=1, source_target_pairs={{2,1},{5,6},{10,9},{13,14},{18,17},{21,22},{26,25},{29,30}} | collective-permute-start | bytes 1179656 | tf_op jit(solution)/shard_map/ppermute | solution.py:313
  34.4 16.0 %collective-permute-start.8 = (bf16[256,768]{1,0:T(8,128)(2,1)S(1)}, bf16[256,768]{1,0:T(8,128)(2,1)S(1)}, u32[]{:S(2)}, u32[]{:S(2)}) collective-permute-start(bf16[256,768]{1,0:T(8,128)(2,1)S(1)} %get-tuple-element.33.refs_0_), channel_id=1, source_target_pairs={{3,1},{7,6},{11,9},{15,14},{19,17},{23,22},{27,25},{31,30}} | collective-permute-start | bytes 1179656 | tf_op jit(solution)/shard_map/ppermute | solution.py:313
  35.1 12.0 %collective-permute-start.3 = (f32[8,128]{1,0:T(8,128)S(1)}, f32[8,128]{1,0:T(8,128)S(1)}, u32[]{:S(2)}, u32[]{:S(2)}) collective-permute-start(f32[8,128]{1,0:T(8,128)S(1)} %get-tuple-element.29), channel_id=1, source_target_pairs={{0,1},{1,2},{2,3},{3,0},{4,5},{5,6},{6,7},{7,4},{8,9},{9,10},{10,1... | collective-permute-start | bytes 12296 | tf_op jit(solution)/shard_map/ppermute | solution.py:288
  35.6 11.5 %collective-permute-start.4 = (f32[8,128]{1,0:T(8,128)S(1)}, f32[8,128]{1,0:T(8,128)S(1)}, u32[]{:S(2)}, u32[]{:S(2)}) collective-permute-start(f32[8,128]{1,0:T(8,128)S(1)} %get-tuple-element.30), channel_id=1, source_target_pairs={{0,2},{1,3},{2,0},{3,1},{4,6},{5,7},{6,4},{7,5},{8,10},{9,11},{10,... | collective-permute-start | bytes 12296 | tf_op jit(solution)/shard_map/ppermute | solution.py:288
  47.1 2.5 %collective-permute-start.5 = (f32[8,128]{1,0:T(8,128)S(1)}, f32[8,128]{1,0:T(8,128)S(1)}, u32[]{:S(2)}, u32[]{:S(2)}) collective-permute-start(f32[8,128]{1,0:T(8,128)S(1)} %get-tuple-element.31), channel_id=1, source_target_pairs={{0,3},{1,0},{2,1},{3,2},{4,7},{5,4},{6,5},{7,6},{8,11},{9,8},{10,9... | collective-permute-start | bytes 12296 | tf_op jit(solution)/shard_map/ppermute | solution.py:288
  56.5 10.9 %all-to-all-start.1 = ((f32[16,1,128]{2,1,0:T(1,128)}), f32[16,1,128]{2,1,0:T(1,128)S(1)}, u32[]{:S(2)}, u32[]{:S(2)}) async-start(f32[16,1,128]{2,1,0:T(1,128)} %shard_map.42), calls=%async_computation.1 | async-start | bytes 16384 | tf_op jit(solution)/shard_map/all_to_all | solution.py:335

commit v4 on v3

v4 whole, which is shorter than its diff:
```python
import functools

import jax
import jax.numpy as jnp
from jax import lax
from jax.experimental import pallas as pl
from jax.experimental.pallas import tpu as pltpu
from jax.sharding import PartitionSpec as P

BIG_OWN = 4
LANES = 128


def modulo(x, n):
    return x & (n - 1) if n & (n - 1) == 0 else lax.rem(x, jnp.int32(n))


def quotient(x, n):
    if n & (n - 1) == 0:
        return lax.shift_right_logical(x, jnp.int32(n.bit_length() - 1))
    return lax.div(x, jnp.int32(n))


def iota(shape, axis):
    return lax.broadcasted_iota(jnp.int32, shape, axis)


def dot_nt(a, b):
    return lax.dot_general(a, b, (((1,), (1,)), ((), ())), preferred_element_type=jnp.float32)


def tile_of(rows, most=256):
    tile = most
    while rows % tile:
        tile //= 2
    return tile


def home_of(docs, blocks):
    return max(blocks // 2 - 1, 0) + (docs & min(blocks - 1, 1))


def sort_kernel(shards, blocks, cap_big, cap_small, relative, me_ref, pooled_hbm, weight_hbm, cluster_hbm, *refs):
    devices = shards * blocks
    (pooled_ref, weight_ref, cluster_ref, rows_ref, info_ref, small_ref, big_ref, sems, small_sems, big_sems) = refs[-10:]
    info_hbm, outs = refs[0], refs[1:-10]
    small_hbm, big_hbm = outs[:-shards], outs[-shards:]
    docs, feature = rows_ref.shape
    limit = BIG_OWN * shards
    small_slots = devices * cap_small
    buckets = devices + shards
    my_docs, my_blk = me_ref[0], me_ref[1]

    fetches = [pltpu.make_async_copy(source, target, sems.at[n]) for n, (source, target) in enumerate(
        ((cluster_hbm, cluster_ref), (weight_hbm, weight_ref), (pooled_hbm, pooled_ref)))]
    for fetch in fetches:
        fetch.start()
    fetches[0].wait()

    cluster = cluster_ref[...]
    is_big = cluster < limit
    owner = modulo(cluster, shards)
    past = jnp.maximum(cluster - limit, 0)
    target = modulo(past, devices)
    bucket = jnp.where(is_big, devices + owner, target)
    quota = (jnp.where(is_big, quotient(cluster, shards), quotient(past, devices)) + 1).astype(jnp.float32)

    padded = -(-buckets // 16) * 16
    hot = (iota((padded, docs), 0) == bucket).astype(jnp.float32)
    earlier = (iota((docs, docs), 0) < iota((docs, docs), 1)).astype(jnp.float32).astype(jnp.bfloat16)
    before = jnp.dot(hot.astype(jnp.bfloat16), earlier, preferred_element_type=jnp.float32)
    rank = jnp.sum(before * hot, axis=0, keepdims=True).astype(jnp.int32)
    lane = jnp.where(is_big, cap_small + rank, rank)

    info_ref[0:1, :] = jnp.where(is_big, owner * blocks + home_of(owner, blocks), target)
    info_ref[1:2, :] = lane
    info_ref[2:8, :] = jnp.zeros((6, docs), jnp.int32)
    sends = [pltpu.make_async_copy(info_ref, info_hbm, sems.at[3])]
    sends[0].start()

    place = (iota((LANES, docs), 0) == lane).astype(jnp.float32).astype(jnp.bfloat16)
    high = big_ref.shape[0] // shards
    table = high - cap_big
    for shift in range(shards):
        to = modulo(my_docs + shift, shards)
        blk = iota((table, docs), 0)
        mine = (blk < blocks) & ((blk + to * blocks == bucket) | (bucket == devices + to))
        values = jnp.where(mine, quota, 0.0).astype(jnp.bfloat16)
        at = shift * high + cap_big
        big_ref[at:at + table, 0:LANES] = dot_nt(values, place).astype(jnp.bfloat16)
        big_ref[at:at + table, LANES:] = jnp.zeros((table, feature - LANES), jnp.bfloat16)

    big_at = modulo(owner + shards - my_docs, shards)
    small_at = target
    if relative:
        small_at = (modulo(quotient(target, blocks) + shards - my_docs, shards) * blocks
                    + modulo(modulo(target, blocks) + blocks - my_blk, blocks))
    big_slot = jnp.where(is_big, big_at * cap_big + rank, -1)
    small_slot = jnp.where(is_big, -1, small_at * cap_small + rank)

    for fetch in fetches[1:]:
        fetch.wait()
    projected = jnp.dot(pooled_ref[...], weight_ref[...], preferred_element_type=jnp.float32)
    squares = jnp.sum(projected * projected, axis=1, keepdims=True)
    rows_ref[...] = (projected / jnp.sqrt(squares + 1e-06)).astype(jnp.bfloat16)

    def picked_rows(slot, first, count):
        pick = (iota((count, docs), 0) + first == slot).astype(jnp.float32).astype(jnp.bfloat16)
        return jnp.dot(pick, rows_ref[...], preferred_element_type=jnp.float32).astype(jnp.bfloat16)

    picked = picked_rows(big_slot, 0, shards * cap_big)
    for shift, out in enumerate(big_hbm):
        big_ref[shift * high:shift * high + cap_big, :] = picked[shift * cap_big:(shift + 1) * cap_big, :]
        sends.append(pltpu.make_async_copy(big_ref.at[pl.ds(shift * high, high)], out, big_sems.at[shift]))
        sends[-1].start()

    rows = small_slots // len(small_hbm)
    tile = rows * (-(-len(small_hbm) // 4)) if relative else rows
    for at in range(0, small_slots, tile):
        small_ref[at:at + tile, :] = picked_rows(small_slot, at, tile)
        for part in range(at // rows, (at + tile) // rows):
            sends.append(pltpu.make_async_copy(
                small_ref.at[pl.ds(part * rows, rows)], small_hbm[part], small_sems.at[part]))
            sends[-1].start()
    for send in sends:
        send.wait()


def group_kernel(shards, blocks, cap_big, me_ref, *refs):
    held, group_ref, ids_refs = refs[:shards], refs[shards], refs[shards + 1:]
    tables = []
    for shift, ref in enumerate(held):
        group_ref[shift * cap_big:(shift + 1) * cap_big, :] = ref[0:cap_big, :]
        tables.append(ref[cap_big:, 0:LANES].astype(jnp.float32))
    for step, ref in enumerate(ids_refs):
        to = modulo(me_ref[1] + step, blocks)
        ref[...] = jnp.zeros(ref.shape, jnp.float32)
        for shift, table in enumerate(tables):
            ref[shift:shift + 1, :] = jnp.sum(
                jnp.where(iota(table.shape, 0) == to, table, 0.0), axis=0, keepdims=True)


def store_rows(values, ref):
    for device in range(ref.shape[0]):
        ref[device, 0:1, :] = values[device:device + 1, :]


def load_rows(ref):
    return jnp.concatenate([ref[device, 0:1, :] for device in range(ref.shape[0])], axis=0)


def small_sources(total, me_ref, shards, blocks, cap_small, relative):
    at = iota((1, total), 1)
    source = at // cap_small
    docs, blk = source // blocks, modulo(source, blocks)
    if relative:
        docs, blk = modulo(me_ref[0] + shards - docs, shards), modulo(me_ref[1] + blocks - blk, blocks)
    return docs, blk, lax.rem(at, jnp.int32(cap_small))


def big_sources(total, my_docs, shards, blocks, cap_big, cap_small):
    at = iota((1, total), 1)
    part = at // (shards * cap_big)
    home = home_of(my_docs, blocks)
    blk = jnp.where(part == 0, home, jnp.where(part - 1 >= home, part, part - 1))
    docs = modulo(my_docs + shards - modulo(at // cap_big, shards), shards)
    return docs, blk, cap_small + lax.rem(at, jnp.int32(cap_big))


def ids_kernel(shards, blocks, cap_big, cap_small, relative, me_ref, *refs):
    tables, small_ref, big_ref = refs[:blocks], refs[blocks], refs[blocks + 1]
    high = tables[0].shape[0]
    values = jnp.concatenate([table[...] for table in tables], axis=0)
    values = jnp.concatenate([values, jnp.zeros_like(values)], axis=0).astype(jnp.bfloat16)
    for ref, (docs, blk, lane) in (
        (small_ref, small_sources(small_ref.shape[1], me_ref, shards, blocks, cap_small, relative)),
        (big_ref, big_sources(big_ref.shape[1], me_ref[0], shards, blocks, cap_big, cap_small)),
    ):
        total = ref.shape[1]
        pick = (iota((LANES, total), 0) == lane).astype(jnp.float32).astype(jnp.bfloat16)
        found = jnp.dot(values, pick, preferred_element_type=jnp.float32)
        row = modulo(me_ref[1] + blocks - blk, blocks) * high + modulo(me_ref[0] + shards - docs, shards)
        ref[...] = jnp.sum(jnp.where(iota(found.shape, 0) == row, found, 0.0), axis=0, keepdims=True)


def as_column(row):
    return jnp.broadcast_to(row, (8, row.shape[1])).T[:, 0:1]


def block_best(queries, col_ids, first_row, others, row_ids, first_col):
    scores = dot_nt(queries, others)
    allowed = (col_ids == row_ids) & (row_ids > 0.0)
    if first_row is not None:
        allowed &= (iota(scores.shape, 0) + first_row) != (iota(scores.shape, 1) + first_col)
    return jnp.max(jnp.where(allowed, scores, -1.0), axis=0, keepdims=True)


def spread(best, docs, blk, lane, shards, blocks):
    total, devices = best.shape[1], shards * blocks
    mine = jnp.where(iota((devices, total), 0) == docs * blocks + blk, best, 0.0)
    place = (iota((LANES, total), 0) == lane).astype(jnp.float32).astype(jnp.bfloat16)
    found = dot_nt(thirds(mine), place)
    return found[:devices] + found[devices:2 * devices] + found[2 * devices:]


def thirds(values):
    high = values.astype(jnp.bfloat16)
    rest = values - high.astype(jnp.float32)
    middle = rest.astype(jnp.bfloat16)
    low = (rest - middle.astype(jnp.float32)).astype(jnp.bfloat16)
    return jnp.concatenate([high, middle, low], axis=0)


def big_kernel(shards, blocks, cap_big, cap_small, me_ref, *refs):
    held, row_ref, back_ref = refs[:-2], refs[-2], refs[-1]
    size = held[0].shape[0]
    col_ids = as_column(row_ref[...])
    bests = [jnp.full((1, size), -1.0, jnp.float32) for _ in held]
    for row, queries in enumerate(held):
        for col, others in enumerate(held):
            same = 0 if row == col else None
            bests[col] = jnp.maximum(bests[col], block_best(
                queries[...], col_ids[row * size:(row + 1) * size], same,
                others[...], row_ref[:, col * size:(col + 1) * size], same))
    best = jnp.concatenate(bests, axis=1)
    back_ref[...] = spread(
        best, *big_sources(best.shape[1], me_ref[0], shards, blocks, cap_big, cap_small), shards, blocks)


def small_kernel(shards, blocks, cap_small, relative, me_ref, *refs):
    parts, (row_ref, big_ref, back_hbm, rows_ref, lanes_ref, sem) = refs[:-6], refs[-6:]
    total = rows_ref.shape[0]
    size = parts[0].shape[0]
    for at, part in enumerate(parts):
        rows_ref[at * size:(at + 1) * size, :] = part[...]
    col_ids = as_column(row_ref[...])
    tile = tile_of(total)
    best = jnp.full((1, total), -1.0, jnp.float32)
    for at in range(0, total, tile):
        best = jnp.maximum(best, block_best(
            rows_ref[at:at + tile, :], col_ids[at:at + tile], at, rows_ref[...], row_ref[...], 0))
    back = spread(best, *small_sources(total, me_ref, shards, blocks, cap_small, relative), shards, blocks)
    store_rows(big_ref[...] + back, lanes_ref)
    send = pltpu.make_async_copy(lanes_ref, back_hbm, sem)
    send.start()
    send.wait()


def masks_kernel(info_ref, device_ref, lane_ref):
    device = (iota((device_ref.shape[0] // 3, device_ref.shape[1]), 0) == info_ref[0:1, :]).astype(jnp.float32)
    device_ref[...] = jnp.concatenate([device] * 3, axis=0).astype(jnp.bfloat16)
    lane_ref[...] = (iota(lane_ref.shape, 0) == info_ref[1:2, :]).astype(jnp.float32)


def finish_kernel(back_ref, device_ref, lane_ref, out_ref):
    found = lax.dot_general(thirds(load_rows(back_ref)), device_ref[...], (((0,), (0,)), ((), ())),
                            preferred_element_type=jnp.float32)
    out_ref[...] = jnp.sum(jnp.where(lane_ref[...] > 0.0, found, 0.0), axis=0, keepdims=True)


def call(kernel, outs, ins, flops, moved, limit=16, scratch=()):
    specs = [pl.BlockSpec(memory_space=space) for _, _, space in outs]
    return pl.pallas_call(
        kernel,
        out_shape=[space(shape, dtype) if space is pltpu.HBM else jax.ShapeDtypeStruct(shape, dtype)
                   for shape, dtype, space in outs],
        in_specs=[pl.BlockSpec(memory_space=space) for space in ins],
        out_specs=specs,
        scratch_shapes=scratch,
        cost_estimate=pl.CostEstimate(flops=flops, bytes_accessed=moved, transcendentals=0),
        compiler_params=pltpu.CompilerParams(vmem_limit_bytes=limit << 20),
    )


def body(pooled, proj_weight, cluster):
    shards = lax.axis_size("docs")
    blocks = lax.axis_size("blk")
    devices = shards * blocks
    docs = pooled.shape[0]
    feature = proj_weight.shape[1]
    big_count = docs // 4
    small_count = docs - big_count
    cap_big = 2 * big_count // shards
    cap_small = 2 * small_count // devices
    small_slots = devices * cap_small
    big_slots = shards * cap_big
    big_total = blocks * big_slots
    sizes = (shards, blocks, cap_big, cap_small)
    f32, bf16, i32 = jnp.float32, jnp.bfloat16, jnp.int32
    vmem, hbm, smem, dma = pltpu.VMEM, pltpu.HBM, pltpu.SMEM, pltpu.SemaphoreType.DMA

    me = jnp.stack([lax.axis_index("docs"), lax.axis_index("blk")]).astype(i32)
    table = -(-blocks // 16) * 16
    relative = devices <= 16
    pieces = devices if relative else 1
    info, *sent = call(
        functools.partial(sort_kernel, *sizes, relative),
        [((8, docs), i32, hbm)] + [((small_slots // pieces, feature), bf16, hbm)] * pieces
        + [((cap_big + table, feature), bf16, hbm)] * shards,
        [smem, hbm, hbm, hbm],
        2 * docs * feature * (pooled.shape[1] + small_slots + big_slots), 5 << 20, 60,
        [vmem(pooled.shape, bf16), vmem(proj_weight.shape, bf16), vmem((1, docs), i32),
         vmem((docs, feature), bf16), vmem((8, docs), i32), vmem((small_slots, feature), bf16),
         vmem((shards * (cap_big + table), feature), bf16), dma((4,)), dma((pieces,)), dma((shards,))],
    )(me, pooled, proj_weight, cluster.reshape(1, docs))
    small_sent, big_sent = sent[:pieces], sent[pieces:]

    def along(x, axis, count, by):
        return lax.ppermute(x, axis, [(i, (i + by) % count) for i in range(count)])

    held = [big_sent[0]] + [along(big_sent[by], "docs", shards, by) for by in range(1, shards)]

    if relative:
        small_got = [None] * devices
        small_got[0] = small_sent[0]
        far_first = sorted(range(blocks), key=lambda by: -min(by, blocks - by))
        for by_blk in far_first:
            for by_docs in range(shards):
                pairs = [(d * blocks + b, (d + by_docs) % shards * blocks + (b + by_blk) % blocks)
                         for d in range(shards) for b in range(blocks)]
                piece = by_docs * blocks + by_blk
                if piece:
                    small_got[piece] = lax.ppermute(small_sent[piece], ("docs", "blk"), pairs)
    else:
        small_got = [lax.all_to_all(
            small_sent[0].reshape(devices, cap_small, feature), ("docs", "blk"),
            split_axis=0, concat_axis=0, tiled=True).reshape(small_slots, feature)]

    high = -(-shards // 8) * 8
    group, *tables = call(
        functools.partial(group_kernel, shards, blocks, cap_big),
        [((big_slots, feature), bf16, vmem)] + [((high, LANES), f32, vmem)] * blocks,
        [smem] + [vmem] * shards,
        big_slots * feature, 1 << 20,
    )(me, *held)

    parts = [group]
    for step in range(blocks - 1):
        homes = [home_of(d, blocks) for d in range(shards)]
        pairs = [(d * blocks + (step if step < homes[d] else step + 1), d * blocks + homes[d])
                 for d in range(shards)]
        parts.append(lax.ppermute(group, ("docs", "blk"), pairs))
    tables = [tables[0]] + [along(tables[by], "blk", blocks, by) for by in range(1, blocks)]

    small_ids, big_ids = call(
        functools.partial(ids_kernel, *sizes, relative),
        [((1, small_slots), f32, vmem), ((1, big_total), f32, vmem)],
        [smem] + [vmem] * blocks,
        2 * high * blocks * LANES * (small_slots + big_total), 1 << 16,
    )(me, *tables)

    back_big, = call(
        functools.partial(big_kernel, *sizes),
        [((devices, LANES), f32, vmem)], [smem] + [vmem] * (blocks + 1),
        2 * big_total * big_total * feature, 2 << 20,
    )(me, *parts, big_ids)

    back, = call(
        functools.partial(small_kernel, shards, blocks, cap_small, relative),
        [((devices, 1, LANES), f32, hbm)], [smem] + [vmem] * (pieces + 2),
        2 * small_slots * small_slots * feature, 2 << 20, 16,
        [vmem((small_slots, feature), bf16), vmem((devices, 1, LANES), f32), dma],
    )(me, *small_got, small_ids, back_big)

    returned = lax.all_to_all(back, ("docs", "blk"), split_axis=0, concat_axis=0, tiled=True)
    masks = call(
        masks_kernel, [((3 * devices, docs), bf16, vmem), ((LANES, docs), f32, vmem)], [vmem],
        docs * LANES, 1 << 18,
    )(info)
    out, = call(
        finish_kernel, [((1, docs), f32, vmem)], [vmem, vmem, vmem],
        2 * docs * LANES * devices, 1 << 18,
    )(returned, *masks)
    return out.reshape(docs)


def solution(mesh):
    in_specs = (P(("slab", "docs", "blk"), None), P(), P(("slab", "docs", "blk")))
    out_specs = P(("slab", "docs", "blk"))
    return jax.shard_map(body, mesh=mesh, in_specs=in_specs, out_specs=out_specs, check_vma=False)
```

time: 69.4 us -> 93.8 us (1.35)
  starting transfers between devices: 21.2 us -> 37.8 us
  waiting for transfers between devices: 32.8 us -> 40.6 us
  Pallas kernels: 14.2 us -> 13 us
    ppermute x0 -> x15, waiting for transfers between devices: none -> 28.5 us  [body(): small_got[piece] = lax.ppermute(small_sent[piece], ('docs', 'blk'), pairs)]
    ppermute x6, waiting for transfers between devices: 27.1 us -> 6.39 us  [along(): return lax.ppermute(x, axis, [(i, (i + by) % count) for i in range(count)])]
    ppermute x0 -> x15, starting transfers between devices: none -> 20.3 us  [body(): small_got[piece] = lax.ppermute(small_sent[piece], ('docs', 'blk'), pairs)]
    all_to_all x1 -> x0, starting transfers between devices: 7.47 us -> none  [body(): lax.all_to_all(send_small.reshape(devices, cap_small, feature), ('docs',...]
    ppermute x3, starting transfers between devices: 2.69 us -> 6.42 us  [body(): parts.append(lax.ppermute(group, ('docs', 'blk'), pairs))]
    pallas_call x6 -> x5, Pallas kernels: 12.6 us -> 11.6 us  [the longest x1 5.5 us: body(): call(functools.partial(sort_kernel, *sizes, relative), [((8, docs), i32,...]
  transfers between devices with their start and end apart: 11 -> 25, of which waited for: 6 -> 16; matrix products, arithmetic and copies ran while one was open for 0% -> 0% of each run, Pallas kernels for 7% -> 4%
where the time goes in v4:
time: 93.8 us; the launch traced here: 93 us
  waiting for transfers between devices  40.6 us (43%)
  starting transfers between devices  37.8 us (40%)
  Pallas kernels  13 us (14%)
    ppermute x15, waiting for transfers between devices, body(): small_got[piece] = lax.ppermute(small_sent[piece], ('docs', 'blk'), pairs)  28.5 us
    ppermute x15, starting transfers between devices, body(): small_got[piece] = lax.ppermute(small_sent[piece], ('docs', 'blk'), pairs)  20.3 us
    ppermute x6, starting transfers between devices, along(): return lax.ppermute(x, axis, [(i, (i + by) % count) for i in range(count)])  6.5 us
    ppermute x3, starting transfers between devices, body(): parts.append(lax.ppermute(group, ('docs', 'blk'), pairs))  6.42 us
    ppermute x6, waiting for transfers between devices, along(): return lax.ppermute(x, axis, [(i, (i + by) % count) for i in range(count)])  6.39 us
    all_to_all x1, waiting for transfers between devices, body(): lax.all_to_all(back, ('docs', 'blk'), split_axis=0, concat_axis=0, tiled=...  5.75 us
    pallas_call x1, Pallas kernels, body(): call(functools.partial(sort_kernel, *sizes, relative), [((8, docs), i32,...  5.5 us
    all_to_all x1, starting transfers between devices, body(): lax.all_to_all(back, ('docs', 'blk'), split_axis=0, concat_axis=0, tiled=...  4.55 us
  transfers between devices with their start and end apart: 25, of which 16 were waited for; matrix products, arithmetic and copies ran while one was open for 0% of the time, Pallas kernels for 4%

profile of v4, /device:TPU:1, one launch (start us, length us, event | category | flops | bytes accessed | tf_op | source)
XLA Modules:
  0.0 93.0 jit_solution(15261838686077069552)
XLA Ops:
  0.0 0.6 pad_add_fusion.me_ref
  0.6 0.0 copy-start.2
  0.6 5.5 %shard_map.37 = (s32[8,512]{1,0:T(8,128)}, bf16[48,768]{1,0:T(8,128)(2,1)}, bf16[48,768]{1,0:T(8,128)(2,1)}, bf16[48,768]{1,0:T(8,128)(2,1)}, bf16[48,768]{1,0:T...) custom-call(s32[2]{0:T(128)} %pad_add_fusion.me_ref, ...), custom_call_target="tpu_custom_call" | custom-call | flops 1409286144 | bytes 5242880 | tf_op jit(solution)/shard_map/pallas_call | solution.py:296
  6.1 2.7 %collective-permute-start.15 = (bf16[80,768]{1,0:T(8,128)(2,1)}, bf16[80,768]{1,0:T(8,128)(2,1)S(1)}, u32[]{:S(2)}, u32[]{:S(2)}) collective-permute-start(bf16[80,768]{1,0:T(8,128)(2,1)} %get-tuple-element.52), channel_id=1, source_target_pairs={{0,4},{4,8},{8,12},{12,0},{1,5},{5,9},{9,13},{13,1},{2,6},{6,10},{... | collective-permute-start | bytes 368648 | tf_op jit(solution)/shard_map/ppermute | solution.py:309
  8.7 0.0 collective-permute-start.16
  8.7 0.5 collective-permute-start.17
  9.2 2.4 %collective-permute-done.15.refs_1_ = bf16[80,768]{1,0:T(8,128)(2,1)S(1)} collective-permute-done((bf16[80,768]{1,0:T(8,128)(2,1)}, bf16[80,768]{1,0:T(8,128)(2,1)S(1)}, u32[]{:S(2)}, u32[]{:S(2)}) %collective-permute-start.15) | collective-permute-done | bytes 122912 | tf_op jit(solution)/shard_map/ppermute | solution.py:309
  11.6 2.6 %collective-permute-done.16.refs_2_ = bf16[80,768]{1,0:T(8,128)(2,1)S(1)} collective-permute-done((bf16[80,768]{1,0:T(8,128)(2,1)}, bf16[80,768]{1,0:T(8,128)(2,1)S(1)}, u32[]{:S(2)}, u32[]{:S(2)}) %collective-permute-start.16) | collective-permute-done | bytes 122912 | tf_op jit(solution)/shard_map/ppermute | solution.py:309
  14.2 0.4 collective-permute-done.17.refs_3_
  14.6 0.0 copy-done.2
  14.6 0.0 copy-start
  14.6 0.9 copy-done
  15.5 0.6 shard_map.38
  16.1 5.0 %collective-permute-start.21 = (bf16[256,768]{1,0:T(8,128)(2,1)S(1)}, bf16[256,768]{1,0:T(8,128)(2,1)S(1)}, u32[]{:S(2)}, u32[]{:S(2)}) collective-permute-start(bf16[256,768]{1,0:T(8,128)(2,1)S(1)} %get-tuple-element.60.refs_0_), channel_id=1, source_target_pairs={{0,1},{4,6},{8,9},{12,14},{16,17},{20,22},{24,25},{28,30}} | collective-permute-start | bytes 1179656 | tf_op jit(solution)/shard_map/ppermute | solution.py:342
  21.2 0.7 collective-permute-start.22
  21.9 0.7 collective-permute-start.23
  22.6 0.9 %collective-permute-start = (bf16[48,768]{1,0:T(8,128)(2,1)}, bf16[48,768]{1,0:T(8,128)(2,1)S(1)}, u32[]{:S(2)}, u32[]{:S(2)}) collective-permute-start(bf16[48,768]{1,0:T(8,128)(2,1)} %get-tuple-element.36), channel_id=1, source_target_pairs={{0,1},{1,2},{2,3},{3,0},{4,5},{5,6},{6,7},{7,4},{8,9},{9,10},{10,1... | collective-permute-start | bytes 221192 | tf_op jit(solution)/shard_map/ppermute | solution.py:323
  23.5 1.8 %collective-permute-start.1 = (bf16[48,768]{1,0:T(8,128)(2,1)}, bf16[48,768]{1,0:T(8,128)(2,1)S(1)}, u32[]{:S(2)}, u32[]{:S(2)}) collective-permute-start(bf16[48,768]{1,0:T(8,128)(2,1)} %get-tuple-element.37), channel_id=1, source_target_pairs={{0,2},{1,3},{2,0},{3,1},{4,6},{5,7},{6,4},{7,5},{8,10},{9,11},{10,... | collective-permute-start | bytes 221192 | tf_op jit(solution)/shard_map/ppermute | solution.py:323
  25.3 10.7 %collective-permute-done.refs_1_ = bf16[48,768]{1,0:T(8,128)(2,1)S(1)} collective-permute-done((bf16[48,768]{1,0:T(8,128)(2,1)}, bf16[48,768]{1,0:T(8,128)(2,1)S(1)}, u32[]{:S(2)}, u32[]{:S(2)}) %collective-permute-start) | collective-permute-done | bytes 73760 | tf_op jit(solution)/shard_map/ppermute | solution.py:323
  36.0 0.0 collective-permute-start.2
  36.0 0.0 collective-permute-done.1.refs_2_
  36.0 0.1 collective-permute-start.3
  36.1 3.6 %collective-permute-done.2.refs_3_ = bf16[48,768]{1,0:T(8,128)(2,1)S(1)} collective-permute-done((bf16[48,768]{1,0:T(8,128)(2,1)}, bf16[48,768]{1,0:T(8,128)(2,1)S(1)}, u32[]{:S(2)}, u32[]{:S(2)}) %collective-permute-start.2) | collective-permute-done | bytes 73760 | tf_op jit(solution)/shard_map/ppermute | solution.py:323
  39.7 0.4 collective-permute-start.4
  40.1 0.0 collective-permute-done.3.refs_4_
  40.1 2.5 %collective-permute-start.5 = (bf16[48,768]{1,0:T(8,128)(2,1)}, bf16[48,768]{1,0:T(8,128)(2,1)S(1)}, u32[]{:S(2)}, u32[]{:S(2)}) collective-permute-start(bf16[48,768]{1,0:T(8,128)(2,1)} %get-tuple-element.41), channel_id=1, source_target_pairs={{0,6},{1,7},{2,4},{3,5},{4,10},{5,11},{6,8},{7,9},{8,14},{9,15},{1... | collective-permute-start | bytes 221192 | tf_op jit(solution)/shard_map/ppermute | solution.py:323
  42.7 3.6 %collective-permute-done.4.refs_5_ = bf16[48,768]{1,0:T(8,128)(2,1)S(1)} collective-permute-done((bf16[48,768]{1,0:T(8,128)(2,1)}, bf16[48,768]{1,0:T(8,128)(2,1)S(1)}, u32[]{:S(2)}, u32[]{:S(2)}) %collective-permute-start.4) | collective-permute-done | bytes 73760 | tf_op jit(solution)/shard_map/ppermute | solution.py:323
  46.3 1.2 %collective-permute-start.6 = (bf16[48,768]{1,0:T(8,128)(2,1)}, bf16[48,768]{1,0:T(8,128)(2,1)S(1)}, u32[]{:S(2)}, u32[]{:S(2)}) collective-permute-start(bf16[48,768]{1,0:T(8,128)(2,1)} %get-tuple-element.42), channel_id=1, source_target_pairs={{0,7},{1,4},{2,5},{3,6},{4,11},{5,8},{6,9},{7,10},{8,15},{9,12},{1... | collective-permute-start | bytes 221192 | tf_op jit(solution)/shard_map/ppermute | solution.py:323
  47.5 1.5 %collective-permute-done.5.refs_6_ = bf16[48,768]{1,0:T(8,128)(2,1)S(1)} collective-permute-done((bf16[48,768]{1,0:T(8,128)(2,1)}, bf16[48,768]{1,0:T(8,128)(2,1)S(1)}, u32[]{:S(2)}, u32[]{:S(2)}) %collective-permute-start.5) | collective-permute-done | bytes 73760 | tf_op jit(solution)/shard_map/ppermute | solution.py:323
  48.9 1.8 %collective-permute-start.7 = (bf16[48,768]{1,0:T(8,128)(2,1)}, bf16[48,768]{1,0:T(8,128)(2,1)S(1)}, u32[]{:S(2)}, u32[]{:S(2)}) collective-permute-start(bf16[48,768]{1,0:T(8,128)(2,1)} %get-tuple-element.43), channel_id=1, source_target_pairs={{0,8},{1,9},{2,10},{3,11},{4,12},{5,13},{6,14},{7,15},{8,0},{9,1},... | collective-permute-start | bytes 221192 | tf_op jit(solution)/shard_map/ppermute | solution.py:323
  50.7 0.0 collective-permute-done.6.refs_7_
  50.7 0.7 collective-permute-start.18
  51.4 2.0 %collective-permute-done.7.refs_8_ = bf16[48,768]{1,0:T(8,128)(2,1)S(1)} collective-permute-done((bf16[48,768]{1,0:T(8,128)(2,1)}, bf16[48,768]{1,0:T(8,128)(2,1)S(1)}, u32[]{:S(2)}, u32[]{:S(2)}) %collective-permute-start.7) | collective-permute-done | bytes 73760 | tf_op jit(solution)/shard_map/ppermute | solution.py:323
  53.5 1.2 %collective-permute-start.19 = (f32[8,128]{1,0:T(8,128)S(1)}, f32[8,128]{1,0:T(8,128)S(1)}, u32[]{:S(2)}, u32[]{:S(2)}) collective-permute-start(f32[8,128]{1,0:T(8,128)S(1)} %get-tuple-element.57), channel_id=1, source_target_pairs={{0,2},{1,3},{2,0},{3,1},{4,6},{5,7},{6,4},{7,5},{8,10},{9,11},{10,... | collective-permute-start | bytes 12296 | tf_op jit(solution)/shard_map/ppermute | solution.py:309
  54.7 0.7 collective-permute-done.18.refs_1_
  55.4 1.5 %collective-permute-start.20 = (f32[8,128]{1,0:T(8,128)S(1)}, f32[8,128]{1,0:T(8,128)S(1)}, u32[]{:S(2)}, u32[]{:S(2)}) collective-permute-start(f32[8,128]{1,0:T(8,128)S(1)} %get-tuple-element.58), channel_id=1, source_target_pairs={{0,3},{1,0},{2,1},{3,2},{4,7},{5,4},{6,5},{7,6},{8,11},{9,8},{10,9... | collective-permute-start | bytes 12296 | tf_op jit(solution)/shard_map/ppermute | solution.py:309
  56.9 0.0 collective-permute-done.19.refs_2_
  56.9 1.0 %collective-permute-start.8 = (bf16[48,768]{1,0:T(8,128)(2,1)}, bf16[48,768]{1,0:T(8,128)(2,1)S(1)}, u32[]{:S(2)}, u32[]{:S(2)}) collective-permute-start(bf16[48,768]{1,0:T(8,128)(2,1)} %get-tuple-element.44), channel_id=1, source_target_pairs={{0,9},{1,10},{2,11},{3,8},{4,13},{5,14},{6,15},{7,12},{8,1},{9,2},... | collective-permute-start | bytes 221192 | tf_op jit(solution)/shard_map/ppermute | solution.py:323
  57.9 0.3 collective-permute-done.20.refs_3_
  58.2 1.6 %collective-permute-start.9 = (bf16[48,768]{1,0:T(8,128)(2,1)}, bf16[48,768]{1,0:T(8,128)(2,1)S(1)}, u32[]{:S(2)}, u32[]{:S(2)}) collective-permute-start(bf16[48,768]{1,0:T(8,128)(2,1)} %get-tuple-element.45), channel_id=1, source_target_pairs={{0,10},{1,11},{2,8},{3,9},{4,14},{5,15},{6,12},{7,13},{8,2},{9,3},... | collective-permute-start | bytes 221192 | tf_op jit(solution)/shard_map/ppermute | solution.py:323
  59.8 0.8 shard_map.39
  60.6 2.5 %collective-permute-done.8.refs_9_ = bf16[48,768]{1,0:T(8,128)(2,1)S(1)} collective-permute-done((bf16[48,768]{1,0:T(8,128)(2,1)}, bf16[48,768]{1,0:T(8,128)(2,1)S(1)}, u32[]{:S(2)}, u32[]{:S(2)}) %collective-permute-start.8) | collective-permute-done | bytes 73760 | tf_op jit(solution)/shard_map/ppermute | solution.py:323
  63.0 0.0 collective-permute-start.10
  63.0 1.5 %collective-permute-done.9.refs_10_ = bf16[48,768]{1,0:T(8,128)(2,1)S(1)} collective-permute-done((bf16[48,768]{1,0:T(8,128)(2,1)}, bf16[48,768]{1,0:T(8,128)(2,1)S(1)}, u32[]{:S(2)}, u32[]{:S(2)}) %collective-permute-start.9) | collective-permute-done | bytes 73760 | tf_op jit(solution)/shard_map/ppermute | solution.py:323
  64.6 4.9 %collective-permute-start.11 = (bf16[48,768]{1,0:T(8,128)(2,1)}, bf16[48,768]{1,0:T(8,128)(2,1)S(1)}, u32[]{:S(2)}, u32[]{:S(2)}) collective-permute-start(bf16[48,768]{1,0:T(8,128)(2,1)} %get-tuple-element.47), channel_id=1, source_target_pairs={{0,12},{1,13},{2,14},{3,15},{4,0},{5,1},{6,2},{7,3},{8,4},{9,5},{1... | collective-permute-start | bytes 221192 | tf_op jit(solution)/shard_map/ppermute | solution.py:323
  69.5 0.0 collective-permute-done.21.refs_1_
  69.5 0.2 collective-permute-start.12
  69.7 0.0 collective-permute-done.22.refs_2_
  69.7 2.2 %collective-permute-start.13 = (bf16[48,768]{1,0:T(8,128)(2,1)}, bf16[48,768]{1,0:T(8,128)(2,1)S(1)}, u32[]{:S(2)}, u32[]{:S(2)}) collective-permute-start(bf16[48,768]{1,0:T(8,128)(2,1)} %get-tuple-element.49), channel_id=1, source_target_pairs={{0,14},{1,15},{2,12},{3,13},{4,2},{5,3},{6,0},{7,1},{8,6},{9,7},{1... | collective-permute-start | bytes 221192 | tf_op jit(solution)/shard_map/ppermute | solution.py:323
  72.0 0.0 collective-permute-done.23.refs_3_
  72.0 1.6 %collective-permute-start.14 = (bf16[48,768]{1,0:T(8,128)(2,1)}, bf16[48,768]{1,0:T(8,128)(2,1)S(1)}, u32[]{:S(2)}, u32[]{:S(2)}) collective-permute-start(bf16[48,768]{1,0:T(8,128)(2,1)} %get-tuple-element.50), channel_id=1, source_target_pairs={{0,15},{1,12},{2,13},{3,14},{4,3},{5,0},{6,1},{7,2},{8,7},{9,4},{1... | collective-permute-start | bytes 221192 | tf_op jit(solution)/shard_map/ppermute | solution.py:323
  73.6 0.0 copy-start.3
  73.6 2.7 %shard_map.40.refs_17_ = f32[16,128]{1,0:T(8,128)S(1)} custom-call(s32[2]{0:T(128)S(1)} %copy-done.2, bf16[256,768]{1,0:T(8,128)(2,1)S(1)} %get-tuple-element.60.refs_0_, bf16[256,768]{1,0:T(8,128)(2,1)S(1)} %collective-permute-done.21.refs_1_, bf16[256,768]{1,0:T(8,128)(2,1)S(1)} %collective-permute-done.22.refs_2_, ...), custom_call_target="tpu_custom_call" | custom-call | flops 1610612736 | bytes 2097152 | tf_op jit(solution)/shard_map/pallas_call | solution.py:352
  76.3 0.0 collective-permute-done.10.refs_11_
  76.3 0.0 collective-permute-done.11.refs_12_
  76.3 0.8 collective-permute-done.12.refs_13_
  77.1 1.9 %collective-permute-done.13.refs_14_ = bf16[48,768]{1,0:T(8,128)(2,1)S(1)} collective-permute-done((bf16[48,768]{1,0:T(8,128)(2,1)}, bf16[48,768]{1,0:T(8,128)(2,1)S(1)}, u32[]{:S(2)}, u32[]{:S(2)}) %collective-permute-start.13) | collective-permute-done | bytes 73760 | tf_op jit(solution)/shard_map/ppermute | solution.py:323
  79.0 0.2 collective-permute-done.14.refs_15_
  79.3 0.0 copy-done.3
  79.3 2.5 %shard_map.41 = f32[16,1,128]{2,1,0:T(1,128)} custom-call(s32[2]{0:T(128)S(1)} %copy-done.2, bf16[48,768]{1,0:T(8,128)(2,1)S(1)} %copy-done.3, bf16[48,768]{1,0:T(8,128)(2,1)S(1)} %collective-permute-done.refs_1_, bf16[48,768]{1,0:T(8,128)(2,1)S(1)} %collective-permute-done.1.refs_2_, bf16[48,768]{1,0:T(8,128)(2,1)S(1)} %collective-permute-done.2.refs_3_, ...), custom_call_target="tpu_custom_call" | custom-call | flops 905969664 | bytes 2097152 | tf_op jit(solution)/shard_map/pallas_call | solution.py:358
  81.8 4.6 %all-to-all-start = ((f32[16,1,128]{2,1,0:T(1,128)}), f32[16,1,128]{2,1,0:T(1,128)S(1)}, u32[]{:S(2)}, u32[]{:S(2)}) async-start(f32[16,1,128]{2,1,0:T(1,128)} %shard_map.41), calls=%async_computation | async-start | bytes 16384 | tf_op jit(solution)/shard_map/all_to_all | solution.py:365
  86.4 0.0 copy-done.1
  86.4 5.7 %all-to-all-done.back_ref = f32[16,1,128]{2,1,0:T(1,128)S(1)} async-done(((f32[16,1,128]{2,1,0:T(1,128)}), f32[16,1,128]{2,1,0:T(1,128)S(1)}, u32[]{:S(2)}, u32[]{:S(2)}) %all-to-all-start) | async-done | bytes 8224 | tf_op jit(solution)/shard_map/all_to_all | solution.py:365
  92.1 0.8 shard_map.43
  (2 shorter events, 0.0 us)
Async XLA Ops:
  0.6 14.0 %copy-start.2 = (s32[2]{0:T(128)S(1)}, s32[2]{0:T(128)}, u32[]{:S(2)}) copy-start(s32[2]{0:T(128)} %pad_add_fusion.me_ref) | copy-start | bytes 28
  6.1 5.5 %collective-permute-start.15 = (bf16[80,768]{1,0:T(8,128)(2,1)}, bf16[80,768]{1,0:T(8,128)(2,1)S(1)}, u32[]{:S(2)}, u32[]{:S(2)}) collective-permute-start(bf16[80,768]{1,0:T(8,128)(2,1)} %get-tuple-element.52), channel_id=1, source_target_pairs={{0,4},{4,8},{8,12},{12,0},{1,5},{5,9},{9,13},{13,1},{2,6},{6,10},{... | collective-permute-start | bytes 368648 | tf_op jit(solution)/shard_map/ppermute | solution.py:309
  8.7 5.5 %collective-permute-start.16 = (bf16[80,768]{1,0:T(8,128)(2,1)}, bf16[80,768]{1,0:T(8,128)(2,1)S(1)}, u32[]{:S(2)}, u32[]{:S(2)}) collective-permute-start(bf16[80,768]{1,0:T(8,128)(2,1)} %get-tuple-element.53), channel_id=1, source_target_pairs={{0,8},{4,12},{8,0},{12,4},{1,9},{5,13},{9,1},{13,5},{2,10},{6,14},... | collective-permute-start | bytes 368648 | tf_op jit(solution)/shard_map/ppermute | solution.py:309
  8.7 5.9 %collective-permute-start.17 = (bf16[80,768]{1,0:T(8,128)(2,1)}, bf16[80,768]{1,0:T(8,128)(2,1)S(1)}, u32[]{:S(2)}, u32[]{:S(2)}) collective-permute-start(bf16[80,768]{1,0:T(8,128)(2,1)} %get-tuple-element.54), channel_id=1, source_target_pairs={{0,12},{4,0},{8,4},{12,8},{1,13},{5,1},{9,5},{13,9},{2,14},{6,2},{... | collective-permute-start | bytes 368648 | tf_op jit(solution)/shard_map/ppermute | solution.py:309
  14.6 0.9 copy-start
  16.1 53.4 %collective-permute-start.21 = (bf16[256,768]{1,0:T(8,128)(2,1)S(1)}, bf16[256,768]{1,0:T(8,128)(2,1)S(1)}, u32[]{:S(2)}, u32[]{:S(2)}) collective-permute-start(bf16[256,768]{1,0:T(8,128)(2,1)S(1)} %get-tuple-element.60.refs_0_), channel_id=1, source_target_pairs={{0,1},{4,6},{8,9},{12,14},{16,17},{20,22},{24,25},{28,30}} | collective-permute-start | bytes 1179656 | tf_op jit(solution)/shard_map/ppermute | solution.py:342
  21.2 48.6 %collective-permute-start.22 = (bf16[256,768]{1,0:T(8,128)(2,1)S(1)}, bf16[256,768]{1,0:T(8,128)(2,1)S(1)}, u32[]{:S(2)}, u32[]{:S(2)}) collective-permute-start(bf16[256,768]{1,0:T(8,128)(2,1)S(1)} %get-tuple-element.60.refs_0_), channel_id=1, source_target_pairs={{2,1},{5,6},{10,9},{13,14},{18,17},{21,22},{26,25},{29,30}} | collective-permute-start | bytes 1179656 | tf_op jit(solution)/shard_map/ppermute | solution.py:342
  21.9 50.1 %collective-permute-start.23 = (bf16[256,768]{1,0:T(8,128)(2,1)S(1)}, bf16[256,768]{1,0:T(8,128)(2,1)S(1)}, u32[]{:S(2)}, u32[]{:S(2)}) collective-permute-start(bf16[256,768]{1,0:T(8,128)(2,1)S(1)} %get-tuple-element.60.refs_0_), channel_id=1, source_target_pairs={{3,1},{7,6},{11,9},{15,14},{19,17},{23,22},{27,25},{31,30}} | collective-permute-start | bytes 1179656 | tf_op jit(solution)/shard_map/ppermute | solution.py:342
  22.6 13.4 %collective-permute-start = (bf16[48,768]{1,0:T(8,128)(2,1)}, bf16[48,768]{1,0:T(8,128)(2,1)S(1)}, u32[]{:S(2)}, u32[]{:S(2)}) collective-permute-start(bf16[48,768]{1,0:T(8,128)(2,1)} %get-tuple-element.36), channel_id=1, source_target_pairs={{0,1},{1,2},{2,3},{3,0},{4,5},{5,6},{6,7},{7,4},{8,9},{9,10},{10,1... | collective-permute-start | bytes 221192 | tf_op jit(solution)/shard_map/ppermute | solution.py:323
  23.5 12.5 %collective-permute-start.1 = (bf16[48,768]{1,0:T(8,128)(2,1)}, bf16[48,768]{1,0:T(8,128)(2,1)S(1)}, u32[]{:S(2)}, u32[]{:S(2)}) collective-permute-start(bf16[48,768]{1,0:T(8,128)(2,1)} %get-tuple-element.37), channel_id=1, source_target_pairs={{0,2},{1,3},{2,0},{3,1},{4,6},{5,7},{6,4},{7,5},{8,10},{9,11},{10,... | collective-permute-start | bytes 221192 | tf_op jit(solution)/shard_map/ppermute | solution.py:323
  36.0 3.7 %collective-permute-start.2 = (bf16[48,768]{1,0:T(8,128)(2,1)}, bf16[48,768]{1,0:T(8,128)(2,1)S(1)}, u32[]{:S(2)}, u32[]{:S(2)}) collective-permute-start(bf16[48,768]{1,0:T(8,128)(2,1)} %get-tuple-element.38), channel_id=1, source_target_pairs={{0,3},{1,0},{2,1},{3,2},{4,7},{5,4},{6,5},{7,6},{8,11},{9,8},{10,9... | collective-permute-start | bytes 221192 | tf_op jit(solution)/shard_map/ppermute | solution.py:323
  36.0 4.1 %collective-permute-start.3 = (bf16[48,768]{1,0:T(8,128)(2,1)}, bf16[48,768]{1,0:T(8,128)(2,1)S(1)}, u32[]{:S(2)}, u32[]{:S(2)}) collective-permute-start(bf16[48,768]{1,0:T(8,128)(2,1)} %get-tuple-element.39), channel_id=1, source_target_pairs={{0,4},{1,5},{2,6},{3,7},{4,8},{5,9},{6,10},{7,11},{8,12},{9,13},{1... | collective-permute-start | bytes 221192 | tf_op jit(solution)/shard_map/ppermute | solution.py:323
  39.7 6.5 %collective-permute-start.4 = (bf16[48,768]{1,0:T(8,128)(2,1)}, bf16[48,768]{1,0:T(8,128)(2,1)S(1)}, u32[]{:S(2)}, u32[]{:S(2)}) collective-permute-start(bf16[48,768]{1,0:T(8,128)(2,1)} %get-tuple-element.40), channel_id=1, source_target_pairs={{0,5},{1,6},{2,7},{3,4},{4,9},{5,10},{6,11},{7,8},{8,13},{9,14},{1... | collective-permute-start | bytes 221192 | tf_op jit(solution)/shard_map/ppermute | solution.py:323
  40.1 8.8 %collective-permute-start.5 = (bf16[48,768]{1,0:T(8,128)(2,1)}, bf16[48,768]{1,0:T(8,128)(2,1)S(1)}, u32[]{:S(2)}, u32[]{:S(2)}) collective-permute-start(bf16[48,768]{1,0:T(8,128)(2,1)} %get-tuple-element.41), channel_id=1, source_target_pairs={{0,6},{1,7},{2,4},{3,5},{4,10},{5,11},{6,8},{7,9},{8,14},{9,15},{1... | collective-permute-start | bytes 221192 | tf_op jit(solution)/shard_map/ppermute | solution.py:323
  46.3 4.5 %collective-permute-start.6 = (bf16[48,768]{1,0:T(8,128)(2,1)}, bf16[48,768]{1,0:T(8,128)(2,1)S(1)}, u32[]{:S(2)}, u32[]{:S(2)}) collective-permute-start(bf16[48,768]{1,0:T(8,128)(2,1)} %get-tuple-element.42), channel_id=1, source_target_pairs={{0,7},{1,4},{2,5},{3,6},{4,11},{5,8},{6,9},{7,10},{8,15},{9,12},{1... | collective-permute-start | bytes 221192 | tf_op jit(solution)/shard_map/ppermute | solution.py:323
  48.9 4.5 %collective-permute-start.7 = (bf16[48,768]{1,0:T(8,128)(2,1)}, bf16[48,768]{1,0:T(8,128)(2,1)S(1)}, u32[]{:S(2)}, u32[]{:S(2)}) collective-permute-start(bf16[48,768]{1,0:T(8,128)(2,1)} %get-tuple-element.43), channel_id=1, source_target_pairs={{0,8},{1,9},{2,10},{3,11},{4,12},{5,13},{6,14},{7,15},{8,0},{9,1},... | collective-permute-start | bytes 221192 | tf_op jit(solution)/shard_map/ppermute | solution.py:323
  50.7 4.7 %collective-permute-start.18 = (f32[8,128]{1,0:T(8,128)S(1)}, f32[8,128]{1,0:T(8,128)S(1)}, u32[]{:S(2)}, u32[]{:S(2)}) collective-permute-start(f32[8,128]{1,0:T(8,128)S(1)} %get-tuple-element.56), channel_id=1, source_target_pairs={{0,1},{1,2},{2,3},{3,0},{4,5},{5,6},{6,7},{7,4},{8,9},{9,10},{10,1... | collective-permute-start | bytes 12296 | tf_op jit(solution)/shard_map/ppermute | solution.py:309
  53.5 3.4 %collective-permute-start.19 = (f32[8,128]{1,0:T(8,128)S(1)}, f32[8,128]{1,0:T(8,128)S(1)}, u32[]{:S(2)}, u32[]{:S(2)}) collective-permute-start(f32[8,128]{1,0:T(8,128)S(1)} %get-tuple-element.57), channel_id=1, source_target_pairs={{0,2},{1,3},{2,0},{3,1},{4,6},{5,7},{6,4},{7,5},{8,10},{9,11},{10,... | collective-permute-start | bytes 12296 | tf_op jit(solution)/shard_map/ppermute | solution.py:309
  55.4 2.8 %collective-permute-start.20 = (f32[8,128]{1,0:T(8,128)S(1)}, f32[8,128]{1,0:T(8,128)S(1)}, u32[]{:S(2)}, u32[]{:S(2)}) collective-permute-start(f32[8,128]{1,0:T(8,128)S(1)} %get-tuple-element.58), channel_id=1, source_target_pairs={{0,3},{1,0},{2,1},{3,2},{4,7},{5,4},{6,5},{7,6},{8,11},{9,8},{10,9... | collective-permute-start | bytes 12296 | tf_op jit(solution)/shard_map/ppermute | solution.py:309
  56.9 6.2 %collective-permute-start.8 = (bf16[48,768]{1,0:T(8,128)(2,1)}, bf16[48,768]{1,0:T(8,128)(2,1)S(1)}, u32[]{:S(2)}, u32[]{:S(2)}) collective-permute-start(bf16[48,768]{1,0:T(8,128)(2,1)} %get-tuple-element.44), channel_id=1, source_target_pairs={{0,9},{1,10},{2,11},{3,8},{4,13},{5,14},{6,15},{7,12},{8,1},{9,2},... | collective-permute-start | bytes 221192 | tf_op jit(solution)/shard_map/ppermute | solution.py:323
  58.2 6.4 %collective-permute-start.9 = (bf16[48,768]{1,0:T(8,128)(2,1)}, bf16[48,768]{1,0:T(8,128)(2,1)S(1)}, u32[]{:S(2)}, u32[]{:S(2)}) collective-permute-start(bf16[48,768]{1,0:T(8,128)(2,1)} %get-tuple-element.45), channel_id=1, source_target_pairs={{0,10},{1,11},{2,8},{3,9},{4,14},{5,15},{6,12},{7,13},{8,2},{9,3},... | collective-permute-start | bytes 221192 | tf_op jit(solution)/shard_map/ppermute | solution.py:323
  63.0 13.3 %collective-permute-start.10 = (bf16[48,768]{1,0:T(8,128)(2,1)}, bf16[48,768]{1,0:T(8,128)(2,1)S(1)}, u32[]{:S(2)}, u32[]{:S(2)}) collective-permute-start(bf16[48,768]{1,0:T(8,128)(2,1)} %get-tuple-element.46), channel_id=1, source_target_pairs={{0,11},{1,8},{2,9},{3,10},{4,15},{5,12},{6,13},{7,14},{8,3},{9,0},... | collective-permute-start | bytes 221192 | tf_op jit(solution)/shard_map/ppermute | solution.py:323
  64.6 11.7 %collective-permute-start.11 = (bf16[48,768]{1,0:T(8,128)(2,1)}, bf16[48,768]{1,0:T(8,128)(2,1)S(1)}, u32[]{:S(2)}, u32[]{:S(2)}) collective-permute-start(bf16[48,768]{1,0:T(8,128)(2,1)} %get-tuple-element.47), channel_id=1, source_target_pairs={{0,12},{1,13},{2,14},{3,15},{4,0},{5,1},{6,2},{7,3},{8,4},{9,5},{1... | collective-permute-start | bytes 221192 | tf_op jit(solution)/shard_map/ppermute | solution.py:323
  69.5 7.6 %collective-permute-start.12 = (bf16[48,768]{1,0:T(8,128)(2,1)}, bf16[48,768]{1,0:T(8,128)(2,1)S(1)}, u32[]{:S(2)}, u32[]{:S(2)}) collective-permute-start(bf16[48,768]{1,0:T(8,128)(2,1)} %get-tuple-element.48), channel_id=1, source_target_pairs={{0,13},{1,14},{2,15},{3,12},{4,1},{5,2},{6,3},{7,0},{8,5},{9,6},{1... | collective-permute-start | bytes 221192 | tf_op jit(solution)/shard_map/ppermute | solution.py:323
  69.7 9.3 %collective-permute-start.13 = (bf16[48,768]{1,0:T(8,128)(2,1)}, bf16[48,768]{1,0:T(8,128)(2,1)S(1)}, u32[]{:S(2)}, u32[]{:S(2)}) collective-permute-start(bf16[48,768]{1,0:T(8,128)(2,1)} %get-tuple-element.49), channel_id=1, source_target_pairs={{0,14},{1,15},{2,12},{3,13},{4,2},{5,3},{6,0},{7,1},{8,6},{9,7},{1... | collective-permute-start | bytes 221192 | tf_op jit(solution)/shard_map/ppermute | solution.py:323
  72.0 7.3 %collective-permute-start.14 = (bf16[48,768]{1,0:T(8,128)(2,1)}, bf16[48,768]{1,0:T(8,128)(2,1)S(1)}, u32[]{:S(2)}, u32[]{:S(2)}) collective-permute-start(bf16[48,768]{1,0:T(8,128)(2,1)} %get-tuple-element.50), channel_id=1, source_target_pairs={{0,15},{1,12},{2,13},{3,14},{4,3},{5,0},{6,1},{7,2},{8,7},{9,4},{1... | collective-permute-start | bytes 221192 | tf_op jit(solution)/shard_map/ppermute | solution.py:323
  73.6 5.7 %copy-start.3 = (bf16[48,768]{1,0:T(8,128)(2,1)S(1)}, bf16[48,768]{1,0:T(8,128)(2,1)}, u32[]{:S(2)}) copy-start(bf16[48,768]{1,0:T(8,128)(2,1)} %get-tuple-element.35.refs_0_) | copy-start | bytes 221188
  79.3 7.1 %copy-start.1 = (s32[8,512]{1,0:T(8,128)S(1)}, s32[8,512]{1,0:T(8,128)}, u32[]{:S(2)}) copy-start(s32[8,512]{1,0:T(8,128)} %get-tuple-element.62.info_ref) | copy-start | bytes 49156
  81.8 10.3 %all-to-all-start = ((f32[16,1,128]{2,1,0:T(1,128)}), f32[16,1,128]{2,1,0:T(1,128)S(1)}, u32[]{:S(2)}, u32[]{:S(2)}) async-start(f32[16,1,128]{2,1,0:T(1,128)} %shard_map.41), calls=%async_computation | async-start | bytes 16384 | tf_op jit(solution)/shard_map/all_to_all | solution.py:365

commit v5 on v4

v5 whole, which is shorter than its diff:
```python
import functools

import jax
import jax.numpy as jnp
from jax import lax
from jax.experimental import pallas as pl
from jax.experimental.pallas import tpu as pltpu
from jax.sharding import PartitionSpec as P

BIG_OWN = 4
LANES = 128


def modulo(x, n):
    return x & (n - 1) if n & (n - 1) == 0 else lax.rem(x, jnp.int32(n))


def quotient(x, n):
    if n & (n - 1) == 0:
        return lax.shift_right_logical(x, jnp.int32(n.bit_length() - 1))
    return lax.div(x, jnp.int32(n))


def iota(shape, axis):
    return lax.broadcasted_iota(jnp.int32, shape, axis)


def dot_nt(a, b):
    return lax.dot_general(a, b, (((1,), (1,)), ((), ())), preferred_element_type=jnp.float32)


def tile_of(rows, most=256):
    tile = most
    while rows % tile:
        tile //= 2
    return tile


def home_of(docs, blocks):
    return max(blocks // 2 - 1, 0) + (docs & min(blocks - 1, 1))


def picked_rows(rows_ref, slot, first, count):
    pick = (iota((count, rows_ref.shape[0]), 0) + first == slot).astype(jnp.float32).astype(jnp.bfloat16)
    return jnp.dot(pick, rows_ref[...], preferred_element_type=jnp.float32).astype(jnp.bfloat16)


def sort_kernel(shards, blocks, cap_big, cap_small, me_ref, pooled_hbm, weight_hbm, cluster_hbm, *refs):
    pooled_ref, weight_ref, cluster_ref, rows_ref, info_ref, big_ref, sems, big_sems = refs[-8:]
    rows_hbm, info_hbm, big_hbm = refs[0], refs[1], refs[2:-8]
    docs = rows_ref.shape[0]
    devices = shards * blocks
    limit = BIG_OWN * shards
    buckets = devices + shards

    fetches = [pltpu.make_async_copy(source, target, sems.at[n]) for n, (source, target) in enumerate(
        ((cluster_hbm, cluster_ref), (weight_hbm, weight_ref), (pooled_hbm, pooled_ref)))]
    for fetch in fetches:
        fetch.start()
    fetches[0].wait()

    cluster = cluster_ref[...]
    is_big = cluster < limit
    owner = modulo(cluster, shards)
    past = jnp.maximum(cluster - limit, 0)
    target = modulo(past, devices)
    bucket = jnp.where(is_big, devices + owner, target)

    padded = -(-buckets // 16) * 16
    hot = (iota((padded, docs), 0) == bucket).astype(jnp.float32)
    earlier = (iota((docs, docs), 0) < iota((docs, docs), 1)).astype(jnp.float32).astype(jnp.bfloat16)
    before = jnp.dot(hot.astype(jnp.bfloat16), earlier, preferred_element_type=jnp.float32)
    rank = jnp.sum(before * hot, axis=0, keepdims=True).astype(jnp.int32)

    info_ref[0:1, :] = jnp.where(is_big, owner * blocks + home_of(owner, blocks), target)
    info_ref[1:2, :] = jnp.where(is_big, cap_small + rank, rank)
    info_ref[2:3, :] = jnp.where(is_big, -1, target * cap_small + rank)
    info_ref[3:4, :] = jnp.where(is_big, quotient(cluster, shards), quotient(past, devices)) + 1
    info_ref[4:5, :] = bucket
    info_ref[5:8, :] = jnp.zeros((3, docs), jnp.int32)
    sends = [pltpu.make_async_copy(info_ref, info_hbm, sems.at[3])]
    sends[0].start()

    for fetch in fetches[1:]:
        fetch.wait()
    projected = jnp.dot(pooled_ref[...], weight_ref[...], preferred_element_type=jnp.float32)
    squares = jnp.sum(projected * projected, axis=1, keepdims=True)
    rows_ref[...] = (projected / jnp.sqrt(squares + 1e-06)).astype(jnp.bfloat16)
    sends.append(pltpu.make_async_copy(rows_ref, rows_hbm, sems.at[4]))
    sends[-1].start()

    kinds = 2 if blocks > 1 and shards > 1 else 1
    half = shards // kinds * cap_big
    place = modulo(owner, kinds) * half + owner // kinds * cap_big + rank
    big_ref[...] = picked_rows(rows_ref, jnp.where(is_big, place, -1), 0, shards * cap_big)
    for step, out in enumerate(big_hbm):
        kind = kind_of(me_ref[1] - step + blocks, blocks, kinds)
        sends.append(pltpu.make_async_copy(
            big_ref.at[pl.ds(pl.multiple_of(kind * half, half), half)], out, big_sems.at[step]))
        sends[-1].start()
    for send in sends:
        send.wait()


def kind_of(blk, blocks, kinds):
    return jnp.where(modulo(blk, blocks) == home_of(1, blocks), kinds - 1, 0)


def sort_small_kernel(shards, blocks, cap_small, me_ref, rows_ref, info_ref, small_hbm, *refs):
    ids_refs, (small_ref, sems) = refs[:-2], refs[-2:]
    docs = rows_ref.shape[0]
    devices = shards * blocks
    slot = info_ref[2:3, :]
    tile = small_ref.shape[0] // sems.shape[0]
    sends = []
    for part in range(sems.shape[0]):
        small_ref[part * tile:(part + 1) * tile, :] = picked_rows(rows_ref, slot, part * tile, tile)
        sends.append(pltpu.make_async_copy(
            small_ref.at[pl.ds(part * tile, tile)], small_hbm.at[pl.ds(part * tile, tile)], sems.at[part]))
        sends[-1].start()
    quota, bucket = info_ref[3:4, :].astype(jnp.float32), info_ref[4:5, :]
    place = (iota((LANES, docs), 0) == info_ref[1:2, :]).astype(jnp.float32).astype(jnp.bfloat16)
    for shift, ref in enumerate(ids_refs):
        to = modulo(me_ref[0] + shift, shards)
        blk = iota((2 * ref.shape[0], docs), 0)
        mine = (blk < blocks) & ((blk + to * blocks == bucket) | (bucket == devices + to))
        values = jnp.where(mine, quota, 0.0).astype(jnp.bfloat16)
        ref[...] = dot_nt(values, place)[0:ref.shape[0], :]
    for send in sends:
        send.wait()


def group_kernel(shards, blocks, cap_big, me_ref, *refs):
    held, outs = refs[:blocks], refs[blocks:]
    kinds = 2 if blocks > 1 and shards > 1 else 1
    for shift, out in enumerate(outs):
        at = pl.multiple_of(modulo(me_ref[0] + shards - shift, shards) // kinds * cap_big, cap_big)
        for step, block in enumerate(held):
            out[step * cap_big:(step + 1) * cap_big, :] = block[pl.ds(at, cap_big), :]


def turn_kernel(blocks, me_ref, *refs):
    held, outs = refs[:-blocks], refs[-blocks:]
    for step, out in enumerate(outs):
        to = modulo(me_ref[1] + step, blocks)
        out[...] = jnp.zeros(out.shape, jnp.float32)
        for shift, table in enumerate(held):
            out[shift:shift + 1, :] = jnp.sum(
                jnp.where(iota(table.shape, 0) == to, table[...], 0.0), axis=0, keepdims=True)


def store_rows(values, ref):
    for device in range(ref.shape[0]):
        ref[device, 0:1, :] = values[device:device + 1, :]


def load_rows(ref):
    return jnp.concatenate([ref[device, 0:1, :] for device in range(ref.shape[0])], axis=0)


def small_sources(total, blocks, cap_small):
    at = iota((1, total), 1)
    source = at // cap_small
    return source // blocks, modulo(source, blocks), lax.rem(at, jnp.int32(cap_small))


def big_sources(total, me_ref, shards, blocks, cap_big, cap_small):
    at = iota((1, total), 1)
    part, step = at // (blocks * cap_big), modulo(at // cap_big, blocks)
    return (modulo(me_ref[0] + part, shards), modulo(me_ref[1] + step, blocks),
            cap_small + lax.rem(at, jnp.int32(cap_big)))


def ids_kernel(shards, blocks, cap_big, cap_small, me_ref, *refs):
    tables, small_ref, big_ref = refs[:blocks], refs[blocks], refs[blocks + 1]
    high = tables[0].shape[0]
    values = jnp.concatenate([table[...] for table in tables], axis=0)
    values = jnp.concatenate([values, jnp.zeros_like(values)], axis=0).astype(jnp.bfloat16)
    for ref, (docs, blk, lane) in (
        (small_ref, small_sources(small_ref.shape[1], blocks, cap_small)),
        (big_ref, big_sources(big_ref.shape[1], me_ref, shards, blocks, cap_big, cap_small)),
    ):
        total = ref.shape[1]
        pick = (iota((LANES, total), 0) == lane).astype(jnp.float32).astype(jnp.bfloat16)
        found = jnp.dot(values, pick, preferred_element_type=jnp.float32)
        row = modulo(me_ref[1] + blocks - blk, blocks) * high + modulo(me_ref[0] + shards - docs, shards)
        ref[...] = jnp.sum(jnp.where(iota(found.shape, 0) == row, found, 0.0), axis=0, keepdims=True)


def as_column(row):
    return jnp.broadcast_to(row, (8, row.shape[1])).T[:, 0:1]


def block_best(queries, col_ids, first_row, others, row_ids, first_col):
    scores = dot_nt(queries, others)
    allowed = (col_ids == row_ids) & (row_ids > 0.0)
    if first_row is not None:
        allowed &= (iota(scores.shape, 0) + first_row) != (iota(scores.shape, 1) + first_col)
    return jnp.max(jnp.where(allowed, scores, -1.0), axis=0, keepdims=True)


def spread(best, docs, blk, lane, shards, blocks):
    total, devices = best.shape[1], shards * blocks
    mine = jnp.where(iota((devices, total), 0) == docs * blocks + blk, best, 0.0)
    place = (iota((LANES, total), 0) == lane).astype(jnp.float32).astype(jnp.bfloat16)
    found = dot_nt(thirds(mine), place)
    return found[:devices] + found[devices:2 * devices] + found[2 * devices:]


def thirds(values):
    high = values.astype(jnp.bfloat16)
    rest = values - high.astype(jnp.float32)
    middle = rest.astype(jnp.bfloat16)
    low = (rest - middle.astype(jnp.float32)).astype(jnp.bfloat16)
    return jnp.concatenate([high, middle, low], axis=0)


def big_kernel(shards, blocks, cap_big, cap_small, me_ref, *refs):
    held, row_ref, back_ref = refs[:-2], refs[-2], refs[-1]
    size = held[0].shape[0]
    col_ids = as_column(row_ref[...])
    bests = [jnp.full((1, size), -1.0, jnp.float32) for _ in held]
    for row, queries in enumerate(held):
        for col, others in enumerate(held):
            same = 0 if row == col else None
            bests[col] = jnp.maximum(bests[col], block_best(
                queries[...], col_ids[row * size:(row + 1) * size], same,
                others[...], row_ref[:, col * size:(col + 1) * size], same))
    best = jnp.concatenate(bests, axis=1)
    back_ref[...] = spread(
        best, *big_sources(best.shape[1], me_ref, shards, blocks, cap_big, cap_small), shards, blocks)


def small_kernel(shards, blocks, cap_small, rows_ref, row_ref, big_ref, back_hbm, lanes_ref, sem):
    total = rows_ref.shape[0]
    col_ids = as_column(row_ref[...])
    tile = tile_of(total)
    best = jnp.full((1, total), -1.0, jnp.float32)
    for at in range(0, total, tile):
        best = jnp.maximum(best, block_best(
            rows_ref[at:at + tile, :], col_ids[at:at + tile], at, rows_ref[...], row_ref[...], 0))
    back = spread(best, *small_sources(total, blocks, cap_small), shards, blocks)
    store_rows(big_ref[...] + back, lanes_ref)
    send = pltpu.make_async_copy(lanes_ref, back_hbm, sem)
    send.start()
    send.wait()


def masks_kernel(info_ref, device_ref, lane_ref):
    device = (iota((device_ref.shape[0] // 3, device_ref.shape[1]), 0) == info_ref[0:1, :]).astype(jnp.float32)
    device_ref[...] = jnp.concatenate([device] * 3, axis=0).astype(jnp.bfloat16)
    lane_ref[...] = (iota(lane_ref.shape, 0) == info_ref[1:2, :]).astype(jnp.float32)


def finish_kernel(back_ref, device_ref, lane_ref, out_ref):
    found = lax.dot_general(thirds(load_rows(back_ref)), device_ref[...], (((0,), (0,)), ((), ())),
                            preferred_element_type=jnp.float32)
    out_ref[...] = jnp.sum(jnp.where(lane_ref[...] > 0.0, found, 0.0), axis=0, keepdims=True)


def call(kernel, outs, ins, flops, moved, limit=16, scratch=()):
    specs = [pl.BlockSpec(memory_space=space) for _, _, space in outs]
    return pl.pallas_call(
        kernel,
        out_shape=[space(shape, dtype) if space is pltpu.HBM else jax.ShapeDtypeStruct(shape, dtype)
                   for shape, dtype, space in outs],
        in_specs=[pl.BlockSpec(memory_space=space) for space in ins],
        out_specs=specs,
        scratch_shapes=scratch,
        cost_estimate=pl.CostEstimate(flops=flops, bytes_accessed=moved, transcendentals=0),
        compiler_params=pltpu.CompilerParams(vmem_limit_bytes=limit << 20),
    )


def body(pooled, proj_weight, cluster):
    shards = lax.axis_size("docs")
    blocks = lax.axis_size("blk")
    devices = shards * blocks
    docs = pooled.shape[0]
    feature = proj_weight.shape[1]
    big_count = docs // 4
    small_count = docs - big_count
    cap_big = 2 * big_count // shards
    cap_small = 2 * small_count // devices
    small_slots = devices * cap_small
    big_slots = shards * cap_big
    big_total = blocks * big_slots
    sizes = (shards, blocks, cap_big, cap_small)
    f32, bf16, i32 = jnp.float32, jnp.bfloat16, jnp.int32
    vmem, hbm, smem, dma = pltpu.VMEM, pltpu.HBM, pltpu.SMEM, pltpu.SemaphoreType.DMA

    me = jnp.stack([lax.axis_index("docs"), lax.axis_index("blk")]).astype(i32)
    kinds = 2 if blocks > 1 and shards > 1 else 1
    half = big_slots // kinds
    rows, info, *big_sent = call(
        functools.partial(sort_kernel, *sizes),
        [((docs, feature), bf16, hbm), ((8, docs), i32, hbm)] + [((half, feature), bf16, hbm)] * blocks,
        [smem, hbm, hbm, hbm],
        2 * docs * feature * (pooled.shape[1] + big_slots), 4 << 20, 60,
        [vmem(pooled.shape, bf16), vmem(proj_weight.shape, bf16), vmem((1, docs), i32),
         vmem((docs, feature), bf16), vmem((8, docs), i32), vmem((big_slots, feature), bf16),
         dma((5,)), dma((blocks,))],
    )(me, pooled, proj_weight, cluster.reshape(1, docs))

    homes = [home_of(d, blocks) for d in range(kinds)]
    big_held = [big_sent[0]]
    for step in range(1, blocks):
        pairs = [(d * blocks + (home + step) % blocks, d * blocks + home) for d in range(shards) for home in homes]
        big_held.append(lax.ppermute(big_sent[step], ("docs", "blk"), pairs))

    table = -(-blocks // 8) * 8
    small_sent, *tables = call(
        functools.partial(sort_small_kernel, shards, blocks, cap_small),
        [((small_slots, feature), bf16, hbm)] + [((table, LANES), f32, vmem)] * shards,
        [smem, vmem, vmem],
        2 * docs * feature * small_slots, 2 << 20, 16,
        [vmem((small_slots, feature), bf16), dma((3,))],
    )(me, rows, info)

    got_small = lax.all_to_all(
        small_sent.reshape(devices, cap_small, feature), ("docs", "blk"),
        split_axis=0, concat_axis=0, tiled=True).reshape(small_slots, feature)

    def along(x, axis, count, by):
        return lax.ppermute(x, axis, [(i, (i + by) % count) for i in range(count)])

    tables = [tables[0]] + [along(tables[by], "docs", shards, by) for by in range(1, shards)]

    grouped = call(
        functools.partial(group_kernel, shards, blocks, cap_big),
        [((blocks * cap_big, feature), bf16, vmem)] * shards,
        [smem] + [vmem] * blocks,
        shards * blocks * cap_big * feature, 4 << 20,
    )(me, *big_held)
    parts = [grouped[0]]
    for shift in range(1, shards):
        pairs = [((d + shift) % shards * blocks + home_of(d, blocks), d * blocks + home_of(d, blocks))
                 for d in range(shards)]
        parts.append(lax.ppermute(grouped[shift], ("docs", "blk"), pairs))

    high = -(-shards // 8) * 8
    tables = call(
        functools.partial(turn_kernel, blocks),
        [((high, LANES), f32, vmem)] * blocks, [smem] + [vmem] * shards,
        shards * blocks * LANES, 1 << 16,
    )(me, *tables)
    tables = [tables[0]] + [along(tables[by], "blk", blocks, by) for by in range(1, blocks)]

    small_ids, big_ids = call(
        functools.partial(ids_kernel, *sizes),
        [((1, small_slots), f32, vmem), ((1, big_total), f32, vmem)],
        [smem] + [vmem] * blocks,
        2 * high * blocks * LANES * (small_slots + big_total), 1 << 16,
    )(me, *tables)

    back_big, = call(
        functools.partial(big_kernel, *sizes),
        [((devices, LANES), f32, vmem)], [smem] + [vmem] * (shards + 1),
        2 * big_total * big_total * feature, 2 << 20,
    )(me, *parts, big_ids)

    back, = call(
        functools.partial(small_kernel, shards, blocks, cap_small),
        [((devices, 1, LANES), f32, hbm)], [vmem, vmem, vmem],
        2 * small_slots * small_slots * feature, 2 << 20, 16,
        [vmem((devices, 1, LANES), f32), dma],
    )(got_small, small_ids, back_big)

    returned = lax.all_to_all(back, ("docs", "blk"), split_axis=0, concat_axis=0, tiled=True)
    masks = call(
        masks_kernel, [((3 * devices, docs), bf16, vmem), ((LANES, docs), f32, vmem)], [vmem],
        docs * LANES, 1 << 18,
    )(info)
    out, = call(
        finish_kernel, [((1, docs), f32, vmem)], [vmem, vmem, vmem],
        2 * docs * LANES * devices, 1 << 18,
    )(returned, *masks)
    return out.reshape(docs)


def solution(mesh):
    in_specs = (P(("slab", "docs", "blk"), None), P(), P(("slab", "docs", "blk")))
    out_specs = P(("slab", "docs", "blk"))
    return jax.shard_map(body, mesh=mesh, in_specs=in_specs, out_specs=out_specs, check_vma=False)
```

time: 93.8 us -> 96.6 us (1.030)
  waiting for transfers between devices: 40.6 us -> 31.7 us
  starting transfers between devices: 37.8 us -> 46.6 us
  Pallas kernels: 13 us -> 14.6 us
    ppermute x6, starting transfers between devices: 6.5 us -> 24.1 us  [along(): return lax.ppermute(x, axis, [(i, (i + by) % count) for i in range(count)])]
    ppermute x18 -> x6, starting transfers between devices: 26.8 us -> 9.75 us  [the longest x3 7.69 us: body(): big_held.append(lax.ppermute(big_sent[step], ('docs', 'blk'), pairs))]
    ppermute x18 -> x6, waiting for transfers between devices: 28.5 us -> 20.4 us  [the longest x3 20.4 us: body(): big_held.append(lax.ppermute(big_sent[step], ('docs', 'blk'), pairs))]
    all_to_all x0 -> x1, starting transfers between devices: none -> 7.47 us  [body(): lax.all_to_all(small_sent.reshape(devices, cap_small, feature), ('docs',...]
    pallas_call x4 -> x6, Pallas kernels: 9.4 us -> 11 us  [the longest x1 4.88 us: body(): call(functools.partial(sort_kernel, *sizes), [((docs, feature), bf16, hbm...]
  transfers between devices with their start and end apart: 25 -> 14, of which waited for: 16 -> 9; matrix products, arithmetic and copies ran while one was open for 0% -> 0% of each run, Pallas kernels for 4% -> 5%
where the time goes in v5:
time: 96.6 us; the launch traced here: 95.5 us
  starting transfers between devices  46.6 us (48%)
  waiting for transfers between devices  31.7 us (33%)
  Pallas kernels  14.6 us (15%)
  local copies, waits for them, and re-layouts  1.87 us (2%)
    ppermute x6, starting transfers between devices, along(): return lax.ppermute(x, axis, [(i, (i + by) % count) for i in range(count)])  24.1 us
    ppermute x3, waiting for transfers between devices, body(): big_held.append(lax.ppermute(big_sent[step], ('docs', 'blk'), pairs))  20.4 us
    ppermute x3, starting transfers between devices, body(): big_held.append(lax.ppermute(big_sent[step], ('docs', 'blk'), pairs))  7.69 us
    all_to_all x1, starting transfers between devices, body(): lax.all_to_all(small_sent.reshape(devices, cap_small, feature), ('docs',...  7.47 us
    all_to_all x1, waiting for transfers between devices, body(): lax.all_to_all(back, ('docs', 'blk'), split_axis=0, concat_axis=0, tiled=...  5.75 us
    ppermute x6, waiting for transfers between devices, along(): return lax.ppermute(x, axis, [(i, (i + by) % count) for i in range(count)])  5.56 us
    all_to_all x1, starting transfers between devices, body(): lax.all_to_all(back, ('docs', 'blk'), split_axis=0, concat_axis=0, tiled=...  5.22 us
    pallas_call x1, Pallas kernels, body(): call(functools.partial(sort_kernel, *sizes), [((docs, feature), bf16, hbm...  4.88 us
  transfers between devices with their start and end apart: 14, of which 9 were waited for; matrix products, arithmetic and copies ran while one was open for 0% of the time, Pallas kernels for 5%

profile of v5, /device:TPU:1, one launch (start us, length us, event | category | flops | bytes accessed | tf_op | source)
XLA Modules:
  0.0 95.5 jit_solution(13627625425551278948)
XLA Ops:
  0.0 0.6 pad_add_fusion.me_ref
  0.6 0.0 copy-start.3
  0.6 4.9 %shard_map.37 = (bf16[512,768]{1,0:T(8,128)(2,1)}, s32[8,512]{1,0:T(8,128)}, bf16[128,768]{1,0:T(8,128)(2,1)}, bf16[128,768]{1,0:T(8,128)(2,1)}, bf16[128,768]{1,0:T(8,128)(2,1)}, /*index=5*/bf16[128,768]{1,0:T(8,128)(2,1)}) custom-call(s32[2]{0:T(128)} %pad_add_fusion.me_ref, bf16[512,768]{1,0:T(8,128)(2,1)} %pooled_hbm.1, bf16[768,768]{1,0:T(8,128)(2,1)} %weight_hbm.1, ...), custom_call_target="tpu_custom_call" | custom-call | flops 805306368 | bytes 4194304 | tf_op jit(solution)/shard_map/pallas_call | solution.py:295
  5.5 0.0 copy-done.3
  5.5 0.0 copy-start.1
  5.5 0.7 copy-done.1
  6.2 0.0 copy-start.4
  6.2 1.1 %copy-done.4 = bf16[512,768]{1,0:T(8,128)(2,1)S(1)} copy-done((bf16[512,768]{1,0:T(8,128)(2,1)S(1)}, bf16[512,768]{1,0:T(8,128)(2,1)}, u32[]{:S(2)}) %copy-start.4) | copy-done | bytes 786456
  7.3 2.2 %shard_map.38 = (bf16[768,768]{1,0:T(8,128)(2,1)}, f32[8,128]{1,0:T(8,128)S(1)}, f32[8,128]{1,0:T(8,128)S(1)}, f32[8,128]{1,0:T(8,128)S(1)}, f32[8,128]{1,0:T(8,128)S(1)}) custom-call(s32[2]{0:T(128)S(1)} %copy-done.3, bf16[512,768]{1,0:T(8,128)(2,1)S(1)} %copy-done.4, s32[8,512]{1,0:T(8,128)S(1)} %copy-done.1), custom_call_target="tpu_custom_call" | custom-call | flops 603979776 | bytes 2097152 | tf_op jit(solution)/shard_map/pallas_call | solution.py:312
  9.5 0.0 copy-start.7
  9.5 0.0 copy-start.6
  9.5 0.0 copy-start.5
  9.5 0.0 copy-start
  9.6 7.5 %all-to-all-start = ((bf16[16,48,768]{2,1,0:T(8,128)(2,1)}), bf16[16,48,768]{2,1,0:T(8,128)(2,1)S(1)}, u32[]{:S(2)}, u32[]{:S(2)}) async-start(bf16[16,48,768]{2,1,0:T(8,128)(2,1)} %bitcast.7), calls=%async_computation | async-start | bytes 2359296 | tf_op jit(solution)/shard_map/all_to_all | solution.py:320
  17.0 0.0 copy-done.7
  17.0 0.7 collective-permute-start.6
  17.7 0.0 copy-done.6
  17.7 5.7 %collective-permute-start.7 = (bf16[128,768]{1,0:T(8,128)(2,1)S(1)}, bf16[128,768]{1,0:T(8,128)(2,1)S(1)}, u32[]{:S(2)}, u32[]{:S(2)}) collective-permute-start(bf16[128,768]{1,0:T(8,128)(2,1)S(1)} %copy-done.6), channel_id=1, source_target_pairs={{3,1},{0,2},{7,5},{4,6},{11,9},{8,10},{15,13},{12,14},{19,17},{16,... | collective-permute-start | bytes 589832 | tf_op jit(solution)/shard_map/ppermute | solution.py:309
  23.4 0.0 copy-done.5
  23.5 1.3 %collective-permute-start.8 = (bf16[128,768]{1,0:T(8,128)(2,1)S(1)}, bf16[128,768]{1,0:T(8,128)(2,1)S(1)}, u32[]{:S(2)}, u32[]{:S(2)}) collective-permute-start(bf16[128,768]{1,0:T(8,128)(2,1)S(1)} %copy-done.5), channel_id=1, source_target_pairs={{0,1},{1,2},{4,5},{5,6},{8,9},{9,10},{12,13},{13,14},{16,17},{17,1... | collective-permute-start | bytes 589832 | tf_op jit(solution)/shard_map/ppermute | solution.py:309
  24.8 0.0 collective-permute-done.6.refs_1_
  24.8 16.2 %collective-permute-done.7.refs_2_ = bf16[128,768]{1,0:T(8,128)(2,1)S(1)} collective-permute-done((bf16[128,768]{1,0:T(8,128)(2,1)S(1)}, bf16[128,768]{1,0:T(8,128)(2,1)S(1)}, u32[]{:S(2)}, u32[]{:S(2)}) %collective-permute-start.7) | collective-permute-done | bytes 196640 | tf_op jit(solution)/shard_map/ppermute | solution.py:309
  41.0 4.2 %collective-permute-done.8.refs_3_ = bf16[128,768]{1,0:T(8,128)(2,1)S(1)} collective-permute-done((bf16[128,768]{1,0:T(8,128)(2,1)S(1)}, bf16[128,768]{1,0:T(8,128)(2,1)S(1)}, u32[]{:S(2)}, u32[]{:S(2)}) %collective-permute-start.8) | collective-permute-done | bytes 196640 | tf_op jit(solution)/shard_map/ppermute | solution.py:309
  45.2 0.0 copy-done
  45.2 0.7 shard_map.41
  45.9 0.7 collective-permute-start.9
  46.5 0.7 collective-permute-start.10
  47.2 0.7 collective-permute-start.11
  47.9 1.7 %collective-permute-start = (f32[8,128]{1,0:T(8,128)S(1)}, f32[8,128]{1,0:T(8,128)S(1)}, u32[]{:S(2)}, u32[]{:S(2)}) collective-permute-start(f32[8,128]{1,0:T(8,128)S(1)} %get-tuple-element.32), channel_id=1, source_target_pairs={{0,4},{4,8},{8,12},{12,0},{1,5},{5,9},{9,13},{13,1},{2,6},{6,10},{... | collective-permute-start | bytes 12296 | tf_op jit(solution)/shard_map/ppermute | solution.py:325
  49.7 0.3 collective-permute-start.1
  49.9 0.5 collective-permute-done.refs_1_
  50.4 1.2 %collective-permute-start.2 = (f32[8,128]{1,0:T(8,128)S(1)}, f32[8,128]{1,0:T(8,128)S(1)}, u32[]{:S(2)}, u32[]{:S(2)}) collective-permute-start(f32[8,128]{1,0:T(8,128)S(1)} %get-tuple-element.34), channel_id=1, source_target_pairs={{0,12},{4,0},{8,4},{12,8},{1,13},{5,1},{9,5},{13,9},{2,14},{6,2},{... | collective-permute-start | bytes 12296 | tf_op jit(solution)/shard_map/ppermute | solution.py:325
  51.6 0.5 collective-permute-done.1.refs_2_
  52.1 1.9 %collective-permute-done.2.refs_3_ = f32[8,128]{1,0:T(8,128)S(1)} collective-permute-done((f32[8,128]{1,0:T(8,128)S(1)}, f32[8,128]{1,0:T(8,128)S(1)}, u32[]{:S(2)}, u32[]{:S(2)}) %collective-permute-start.2) | collective-permute-done | bytes 4128 | tf_op jit(solution)/shard_map/ppermute | solution.py:325
  54.0 0.6 shard_map.39
  54.6 19.6 %collective-permute-start.3 = (f32[8,128]{1,0:T(8,128)S(1)}, f32[8,128]{1,0:T(8,128)S(1)}, u32[]{:S(2)}, u32[]{:S(2)}) collective-permute-start(f32[8,128]{1,0:T(8,128)S(1)} %get-tuple-element.36), channel_id=1, source_target_pairs={{0,1},{1,2},{2,3},{3,0},{4,5},{5,6},{6,7},{7,4},{8,9},{9,10},{10,1... | collective-permute-start | bytes 12296 | tf_op jit(solution)/shard_map/ppermute | solution.py:325
  74.1 0.0 collective-permute-start.4
  74.1 0.8 collective-permute-done.3.refs_1_
  74.9 1.4 %collective-permute-start.5 = (f32[8,128]{1,0:T(8,128)S(1)}, f32[8,128]{1,0:T(8,128)S(1)}, u32[]{:S(2)}, u32[]{:S(2)}) collective-permute-start(f32[8,128]{1,0:T(8,128)S(1)} %get-tuple-element.38), channel_id=1, source_target_pairs={{0,3},{1,0},{2,1},{3,2},{4,7},{5,4},{6,5},{7,6},{8,11},{9,8},{10,9... | collective-permute-start | bytes 12296 | tf_op jit(solution)/shard_map/ppermute | solution.py:325
  76.3 1.2 %collective-permute-done.4.refs_2_ = f32[8,128]{1,0:T(8,128)S(1)} collective-permute-done((f32[8,128]{1,0:T(8,128)S(1)}, f32[8,128]{1,0:T(8,128)S(1)}, u32[]{:S(2)}, u32[]{:S(2)}) %collective-permute-start.4) | collective-permute-done | bytes 4128 | tf_op jit(solution)/shard_map/ppermute | solution.py:325
  77.5 0.7 collective-permute-done.5.refs_3_
  78.2 0.8 shard_map.40
  79.0 0.0 collective-permute-done.9.refs_1_
  79.0 0.0 collective-permute-done.10.refs_2_
  79.0 0.0 collective-permute-done.11.refs_3_
  79.0 2.7 %shard_map.42.big_ref = f32[16,128]{1,0:T(8,128)S(1)} custom-call(s32[2]{0:T(128)S(1)} %copy-done.3, bf16[256,768]{1,0:T(8,128)(2,1)S(1)} %get-tuple-element.44.refs_0_, bf16[256,768]{1,0:T(8,128)(2,1)S(1)} %collective-permute-done.9.refs_1_, bf16[256,768]{1,0:T(8,128)(2,1)S(1)} %collective-permute-done.10.refs_2_, ...), custom_call_target="tpu_custom_call" | custom-call | flops 1610612736 | bytes 2097152 | tf_op jit(solution)/shard_map/pallas_call | solution.py:356
  81.7 0.0 all-to-all-done
  81.7 0.0 copy-start.2
  81.7 2.0 %shard_map.43 = f32[16,1,128]{2,1,0:T(1,128)} custom-call(bf16[768,768]{1,0:T(8,128)(2,1)S(1)} %bitcast.6, f32[1,768]{1,0:T(1,128)S(1)} %get-tuple-element.39.row_ref, f32[16,128]{1,0:T(8,128)S(1)} %shard_map.42.big_ref), custom_call_target="tpu_custom_call" | custom-call | flops 905969664 | bytes 2097152 | tf_op jit(solution)/shard_map/pallas_call | solution.py:362
  83.7 5.2 %all-to-all-start.1 = ((f32[16,1,128]{2,1,0:T(1,128)}), f32[16,1,128]{2,1,0:T(1,128)S(1)}, u32[]{:S(2)}, u32[]{:S(2)}) async-start(f32[16,1,128]{2,1,0:T(1,128)} %shard_map.43), calls=%async_computation.1 | async-start | bytes 16384 | tf_op jit(solution)/shard_map/all_to_all | solution.py:369
  88.9 0.0 copy-done.2
  89.0 5.7 %all-to-all-done.1.back_ref = f32[16,1,128]{2,1,0:T(1,128)S(1)} async-done(((f32[16,1,128]{2,1,0:T(1,128)}), f32[16,1,128]{2,1,0:T(1,128)S(1)}, u32[]{:S(2)}, u32[]{:S(2)}) %all-to-all-start.1) | async-done | bytes 8224 | tf_op jit(solution)/shard_map/all_to_all | solution.py:369
  94.7 0.8 shard_map.45
  (1 shorter events, 0.0 us)
Async XLA Ops:
  0.6 4.9 %copy-start.3 = (s32[2]{0:T(128)S(1)}, s32[2]{0:T(128)}, u32[]{:S(2)}) copy-start(s32[2]{0:T(128)} %pad_add_fusion.me_ref) | copy-start | bytes 28
  5.5 0.7 copy-start.1
  6.2 1.1 %copy-start.4 = (bf16[512,768]{1,0:T(8,128)(2,1)S(1)}, bf16[512,768]{1,0:T(8,128)(2,1)}, u32[]{:S(2)}) copy-start(bf16[512,768]{1,0:T(8,128)(2,1)} %get-tuple-element.28.rows_ref) | copy-start | bytes 2359300
  9.5 7.5 %copy-start.7 = (bf16[128,768]{1,0:T(8,128)(2,1)S(1)}, bf16[128,768]{1,0:T(8,128)(2,1)}, u32[]{:S(2)}) copy-start(bf16[128,768]{1,0:T(8,128)(2,1)} %get-tuple-element.41) | copy-start | bytes 589828
  9.5 8.2 %copy-start.6 = (bf16[128,768]{1,0:T(8,128)(2,1)S(1)}, bf16[128,768]{1,0:T(8,128)(2,1)}, u32[]{:S(2)}) copy-start(bf16[128,768]{1,0:T(8,128)(2,1)} %get-tuple-element.42) | copy-start | bytes 589828
  9.5 13.9 %copy-start.5 = (bf16[128,768]{1,0:T(8,128)(2,1)S(1)}, bf16[128,768]{1,0:T(8,128)(2,1)}, u32[]{:S(2)}) copy-start(bf16[128,768]{1,0:T(8,128)(2,1)} %get-tuple-element.43) | copy-start | bytes 589828
  9.5 35.6 %copy-start = (bf16[128,768]{1,0:T(8,128)(2,1)S(1)}, bf16[128,768]{1,0:T(8,128)(2,1)}, u32[]{:S(2)}) copy-start(bf16[128,768]{1,0:T(8,128)(2,1)} %get-tuple-element.40.refs_0_) | copy-start | bytes 589828
  9.6 72.2 %all-to-all-start = ((bf16[16,48,768]{2,1,0:T(8,128)(2,1)}), bf16[16,48,768]{2,1,0:T(8,128)(2,1)S(1)}, u32[]{:S(2)}, u32[]{:S(2)}) async-start(bf16[16,48,768]{2,1,0:T(8,128)(2,1)} %bitcast.7), calls=%async_computation | async-start | bytes 2359296 | tf_op jit(solution)/shard_map/all_to_all | solution.py:320
  17.0 7.7 %collective-permute-start.6 = (bf16[128,768]{1,0:T(8,128)(2,1)S(1)}, bf16[128,768]{1,0:T(8,128)(2,1)S(1)}, u32[]{:S(2)}, u32[]{:S(2)}) collective-permute-start(bf16[128,768]{1,0:T(8,128)(2,1)S(1)} %copy-done.7), channel_id=1, source_target_pairs={{2,1},{3,2},{6,5},{7,6},{10,9},{11,10},{14,13},{15,14},{18,17},{19... | collective-permute-start | bytes 589832 | tf_op jit(solution)/shard_map/ppermute | solution.py:309
  17.7 23.3 %collective-permute-start.7 = (bf16[128,768]{1,0:T(8,128)(2,1)S(1)}, bf16[128,768]{1,0:T(8,128)(2,1)S(1)}, u32[]{:S(2)}, u32[]{:S(2)}) collective-permute-start(bf16[128,768]{1,0:T(8,128)(2,1)S(1)} %copy-done.6), channel_id=1, source_target_pairs={{3,1},{0,2},{7,5},{4,6},{11,9},{8,10},{15,13},{12,14},{19,17},{16,... | collective-permute-start | bytes 589832 | tf_op jit(solution)/shard_map/ppermute | solution.py:309
  23.5 21.7 %collective-permute-start.8 = (bf16[128,768]{1,0:T(8,128)(2,1)S(1)}, bf16[128,768]{1,0:T(8,128)(2,1)S(1)}, u32[]{:S(2)}, u32[]{:S(2)}) collective-permute-start(bf16[128,768]{1,0:T(8,128)(2,1)S(1)} %copy-done.5), channel_id=1, source_target_pairs={{0,1},{1,2},{4,5},{5,6},{8,9},{9,10},{12,13},{13,14},{16,17},{17,1... | collective-permute-start | bytes 589832 | tf_op jit(solution)/shard_map/ppermute | solution.py:309
  45.9 33.1 %collective-permute-start.9 = (bf16[256,768]{1,0:T(8,128)(2,1)S(1)}, bf16[256,768]{1,0:T(8,128)(2,1)S(1)}, u32[]{:S(2)}, u32[]{:S(2)}) collective-permute-start(bf16[256,768]{1,0:T(8,128)(2,1)S(1)} %get-tuple-element.45), channel_id=1, source_target_pairs={{5,1},{10,6},{13,9},{2,14},{21,17},{26,22},{29,25},{18,30}} | collective-permute-start | bytes 1179656 | tf_op jit(solution)/shard_map/ppermute | solution.py:339
  46.5 32.4 %collective-permute-start.10 = (bf16[256,768]{1,0:T(8,128)(2,1)S(1)}, bf16[256,768]{1,0:T(8,128)(2,1)S(1)}, u32[]{:S(2)}, u32[]{:S(2)}) collective-permute-start(bf16[256,768]{1,0:T(8,128)(2,1)S(1)} %get-tuple-element.46), channel_id=1, source_target_pairs={{9,1},{14,6},{1,9},{6,14},{25,17},{30,22},{17,25},{22,30}} | collective-permute-start | bytes 1179656 | tf_op jit(solution)/shard_map/ppermute | solution.py:339
  47.2 31.8 %collective-permute-start.11 = (bf16[256,768]{1,0:T(8,128)(2,1)S(1)}, bf16[256,768]{1,0:T(8,128)(2,1)S(1)}, u32[]{:S(2)}, u32[]{:S(2)}) collective-permute-start(bf16[256,768]{1,0:T(8,128)(2,1)S(1)} %get-tuple-element.47), channel_id=1, source_target_pairs={{13,1},{2,6},{5,9},{10,14},{29,17},{18,22},{21,25},{26,30}} | collective-permute-start | bytes 1179656 | tf_op jit(solution)/shard_map/ppermute | solution.py:339
  47.9 2.5 %collective-permute-start = (f32[8,128]{1,0:T(8,128)S(1)}, f32[8,128]{1,0:T(8,128)S(1)}, u32[]{:S(2)}, u32[]{:S(2)}) collective-permute-start(f32[8,128]{1,0:T(8,128)S(1)} %get-tuple-element.32), channel_id=1, source_target_pairs={{0,4},{4,8},{8,12},{12,0},{1,5},{5,9},{9,13},{13,1},{2,6},{6,10},{... | collective-permute-start | bytes 12296 | tf_op jit(solution)/shard_map/ppermute | solution.py:325
  49.7 2.5 %collective-permute-start.1 = (f32[8,128]{1,0:T(8,128)S(1)}, f32[8,128]{1,0:T(8,128)S(1)}, u32[]{:S(2)}, u32[]{:S(2)}) collective-permute-start(f32[8,128]{1,0:T(8,128)S(1)} %get-tuple-element.33), channel_id=1, source_target_pairs={{0,8},{4,12},{8,0},{12,4},{1,9},{5,13},{9,1},{13,5},{2,10},{6,14},... | collective-permute-start | bytes 12296 | tf_op jit(solution)/shard_map/ppermute | solution.py:325
  50.4 3.6 %collective-permute-start.2 = (f32[8,128]{1,0:T(8,128)S(1)}, f32[8,128]{1,0:T(8,128)S(1)}, u32[]{:S(2)}, u32[]{:S(2)}) collective-permute-start(f32[8,128]{1,0:T(8,128)S(1)} %get-tuple-element.34), channel_id=1, source_target_pairs={{0,12},{4,0},{8,4},{12,8},{1,13},{5,1},{9,5},{13,9},{2,14},{6,2},{... | collective-permute-start | bytes 12296 | tf_op jit(solution)/shard_map/ppermute | solution.py:325
  54.6 20.3 %collective-permute-start.3 = (f32[8,128]{1,0:T(8,128)S(1)}, f32[8,128]{1,0:T(8,128)S(1)}, u32[]{:S(2)}, u32[]{:S(2)}) collective-permute-start(f32[8,128]{1,0:T(8,128)S(1)} %get-tuple-element.36), channel_id=1, source_target_pairs={{0,1},{1,2},{2,3},{3,0},{4,5},{5,6},{6,7},{7,4},{8,9},{9,10},{10,1... | collective-permute-start | bytes 12296 | tf_op jit(solution)/shard_map/ppermute | solution.py:325
  74.1 3.4 %collective-permute-start.4 = (f32[8,128]{1,0:T(8,128)S(1)}, f32[8,128]{1,0:T(8,128)S(1)}, u32[]{:S(2)}, u32[]{:S(2)}) collective-permute-start(f32[8,128]{1,0:T(8,128)S(1)} %get-tuple-element.37), channel_id=1, source_target_pairs={{0,2},{1,3},{2,0},{3,1},{4,6},{5,7},{6,4},{7,5},{8,10},{9,11},{10,... | collective-permute-start | bytes 12296 | tf_op jit(solution)/shard_map/ppermute | solution.py:325
  74.9 3.3 %collective-permute-start.5 = (f32[8,128]{1,0:T(8,128)S(1)}, f32[8,128]{1,0:T(8,128)S(1)}, u32[]{:S(2)}, u32[]{:S(2)}) collective-permute-start(f32[8,128]{1,0:T(8,128)S(1)} %get-tuple-element.38), channel_id=1, source_target_pairs={{0,3},{1,0},{2,1},{3,2},{4,7},{5,4},{6,5},{7,6},{8,11},{9,8},{10,9... | collective-permute-start | bytes 12296 | tf_op jit(solution)/shard_map/ppermute | solution.py:325
  81.7 7.2 %copy-start.2 = (s32[8,512]{1,0:T(8,128)S(1)}, s32[8,512]{1,0:T(8,128)}, u32[]{:S(2)}) copy-start(s32[8,512]{1,0:T(8,128)} %get-tuple-element.29.info_ref) | copy-start | bytes 49156
  83.7 11.0 %all-to-all-start.1 = ((f32[16,1,128]{2,1,0:T(1,128)}), f32[16,1,128]{2,1,0:T(1,128)S(1)}, u32[]{:S(2)}, u32[]{:S(2)}) async-start(f32[16,1,128]{2,1,0:T(1,128)} %shard_map.43), calls=%async_computation.1 | async-start | bytes 16384 | tf_op jit(solution)/shard_map/all_to_all | solution.py:369

commit v6 on v5

--- a/solution.py
+++ b/solution.py
@@ -45,9 +45,9 @@
     return jnp.dot(pick, rows_ref[...], preferred_element_type=jnp.float32).astype(jnp.bfloat16)
 
 
-def sort_kernel(shards, blocks, cap_big, cap_small, me_ref, pooled_hbm, weight_hbm, cluster_hbm, *refs):
-    pooled_ref, weight_ref, cluster_ref, rows_ref, info_ref, big_ref, sems, big_sems = refs[-8:]
-    rows_hbm, info_hbm, big_hbm = refs[0], refs[1], refs[2:-8]
+def sort_kernel(shards, blocks, cap_big, cap_small, docs_at, blk_at, pooled_hbm, weight_hbm, cluster_hbm, *refs):
+    pooled_ref, weight_ref, cluster_ref, rows_ref, info_ref, big_ref, ids_ref, sems, big_sems, ids_sems = refs[-10:]
+    rows_hbm, info_hbm, big_hbm, ids_hbm = refs[0], refs[1], refs[2:2 + blocks], refs[2 + blocks:-10]
     docs = rows_ref.shape[0]
     devices = shards * blocks
     limit = BIG_OWN * shards
@@ -72,14 +72,25 @@
     before = jnp.dot(hot.astype(jnp.bfloat16), earlier, preferred_element_type=jnp.float32)
     rank = jnp.sum(before * hot, axis=0, keepdims=True).astype(jnp.int32)
 
+    lane = jnp.where(is_big, cap_small + rank, rank)
+    quota = jnp.where(is_big, quotient(cluster, shards), quotient(past, devices)) + 1
     info_ref[0:1, :] = jnp.where(is_big, owner * blocks + home_of(owner, blocks), target)
-    info_ref[1:2, :] = jnp.where(is_big, cap_small + rank, rank)
+    info_ref[1:2, :] = lane
     info_ref[2:3, :] = jnp.where(is_big, -1, target * cap_small + rank)
-    info_ref[3:4, :] = jnp.where(is_big, quotient(cluster, shards), quotient(past, devices)) + 1
-    info_ref[4:5, :] = bucket
-    info_ref[5:8, :] = jnp.zeros((3, docs), jnp.int32)
+    info_ref[3:8, :] = jnp.zeros((5, docs), jnp.int32)
     sends = [pltpu.make_async_copy(info_ref, info_hbm, sems.at[3])]
     sends[0].start()
+
+    lanes = (iota((LANES, docs), 0) == lane).astype(jnp.float32).astype(jnp.bfloat16)
+    high = ids_ref.shape[1]
+    for shift, out in enumerate(ids_hbm):
+        to = modulo(docs_at[0] + shift, shards)
+        blk = iota((2 * high, docs), 0)
+        mine = (blk < blocks) & ((blk + to * blocks == bucket) | (bucket == devices + to))
+        values = jnp.where(mine, quota.astype(jnp.float32), 0.0).astype(jnp.bfloat16)
+        ids_ref[shift] = dot_nt(values, lanes)[0:high, :]
+        sends.append(pltpu.make_async_copy(ids_ref.at[shift], out, ids_sems.at[shift]))
+        sends[-1].start()
 
     for fetch in fetches[1:]:
         fetch.wait()
@@ -94,7 +105,7 @@
     place = modulo(owner, kinds) * half + owner // kinds * cap_big + rank
     big_ref[...] = picked_rows(rows_ref, jnp.where(is_big, place, -1), 0, shards * cap_big)
     for step, out in enumerate(big_hbm):
-        kind = kind_of(me_ref[1] - step + blocks, blocks, kinds)
+        kind = kind_of(blk_at[0] - step + blocks, blocks, kinds)
         sends.append(pltpu.make_async_copy(
             big_ref.at[pl.ds(pl.multiple_of(kind * half, half), half)], out, big_sems.at[step]))
         sends[-1].start()
@@ -106,45 +117,30 @@
     return jnp.where(modulo(blk, blocks) == home_of(1, blocks), kinds - 1, 0)
 
 
-def sort_small_kernel(shards, blocks, cap_small, me_ref, rows_ref, info_ref, small_hbm, *refs):
-    ids_refs, (small_ref, sems) = refs[:-2], refs[-2:]
-    docs = rows_ref.shape[0]
-    devices = shards * blocks
-    slot = info_ref[2:3, :]
+def sort_small_kernel(rows_ref, info_ref, small_hbm, small_ref, sems):
     tile = small_ref.shape[0] // sems.shape[0]
     sends = []
     for part in range(sems.shape[0]):
-        small_ref[part * tile:(part + 1) * tile, :] = picked_rows(rows_ref, slot, part * tile, tile)
+        small_ref[part * tile:(part + 1) * tile, :] = picked_rows(rows_ref, info_ref[2:3, :], part * tile, tile)
         sends.append(pltpu.make_async_copy(
             small_ref.at[pl.ds(part * tile, tile)], small_hbm.at[pl.ds(part * tile, tile)], sems.at[part]))
         sends[-1].start()
-    quota, bucket = info_ref[3:4, :].astype(jnp.float32), info_ref[4:5, :]
-    place = (iota((LANES, docs), 0) == info_ref[1:2, :]).astype(jnp.float32).astype(jnp.bfloat16)
-    for shift, ref in enumerate(ids_refs):
-        to = modulo(me_ref[0] + shift, shards)
-        blk = iota((2 * ref.shape[0], docs), 0)
-        mine = (blk < blocks) & ((blk + to * blocks == bucket) | (bucket == devices + to))
-        values = jnp.where(mine, quota, 0.0).astype(jnp.bfloat16)
-        ref[...] = dot_nt(values, place)[0:ref.shape[0], :]
     for send in sends:
         send.wait()
 
 
-def group_kernel(shards, blocks, cap_big, me_ref, *refs):
-    held, outs = refs[:blocks], refs[blocks:]
+def group_kernel(shards, blocks, cap_big, docs_at, blk_at, small_in, *refs):
+    held, tables = refs[:blocks], refs[blocks:blocks + shards]
+    rows_refs, ids_refs = refs[blocks + shards + 1:-blocks], refs[-blocks:]
     kinds = 2 if blocks > 1 and shards > 1 else 1
-    for shift, out in enumerate(outs):
-        at = pl.multiple_of(modulo(me_ref[0] + shards - shift, shards) // kinds * cap_big, cap_big)
+    for shift, out in enumerate(rows_refs):
+        at = pl.multiple_of(modulo(docs_at[0] + shards - shift, shards) // kinds * cap_big, cap_big)
         for step, block in enumerate(held):
             out[step * cap_big:(step + 1) * cap_big, :] = block[pl.ds(at, cap_big), :]
-
-
-def turn_kernel(blocks, me_ref, *refs):
-    held, outs = refs[:-blocks], refs[-blocks:]
-    for step, out in enumerate(outs):
-        to = modulo(me_ref[1] + step, blocks)
+    for step, out in enumerate(ids_refs):
+        to = modulo(blk_at[0] + step, blocks)
         out[...] = jnp.zeros(out.shape, jnp.float32)
-        for shift, table in enumerate(held):
+        for shift, table in enumerate(tables):
             out[shift:shift + 1, :] = jnp.sum(
                 jnp.where(iota(table.shape, 0) == to, table[...], 0.0), axis=0, keepdims=True)
 
@@ -164,26 +160,26 @@
     return source // blocks, modulo(source, blocks), lax.rem(at, jnp.int32(cap_small))
 
 
-def big_sources(total, me_ref, shards, blocks, cap_big, cap_small):
+def big_sources(total, docs_at, blk_at, shards, blocks, cap_big, cap_small):
     at = iota((1, total), 1)
     part, step = at // (blocks * cap_big), modulo(at // cap_big, blocks)
-    return (modulo(me_ref[0] + part, shards), modulo(me_ref[1] + step, blocks),
+    return (modulo(docs_at[0] + part, shards), modulo(blk_at[0] + step, blocks),
             cap_small + lax.rem(at, jnp.int32(cap_big)))
 
 
-def ids_kernel(shards, blocks, cap_big, cap_small, me_ref, *refs):
+def ids_kernel(shards, blocks, cap_big, cap_small, docs_at, blk_at, *refs):
     tables, small_ref, big_ref = refs[:blocks], refs[blocks], refs[blocks + 1]
     high = tables[0].shape[0]
     values = jnp.concatenate([table[...] for table in tables], axis=0)
     values = jnp.concatenate([values, jnp.zeros_like(values)], axis=0).astype(jnp.bfloat16)
     for ref, (docs, blk, lane) in (
         (small_ref, small_sources(small_ref.shape[1], blocks, cap_small)),
-        (big_ref, big_sources(big_ref.shape[1], me_ref, shards, blocks, cap_big, cap_small)),
+        (big_ref, big_sources(big_ref.shape[1], docs_at, blk_at, shards, blocks, cap_big, cap_small)),
     ):
         total = ref.shape[1]
         pick = (iota((LANES, total), 0) == lane).astype(jnp.float32).astype(jnp.bfloat16)
         found = jnp.dot(values, pick, preferred_element_type=jnp.float32)
-        row = modulo(me_ref[1] + blocks - blk, blocks) * high + modulo(me_ref[0] + shards - docs, shards)
+        row = modulo(blk_at[0] + blocks - blk, blocks) * high + modulo(docs_at[0] + shards - docs, shards)
         ref[...] = jnp.sum(jnp.where(iota(found.shape, 0) == row, found, 0.0), axis=0, keepdims=True)
 
 
@@ -215,7 +211,7 @@
     return jnp.concatenate([high, middle, low], axis=0)
 
 
-def big_kernel(shards, blocks, cap_big, cap_small, me_ref, *refs):
+def big_kernel(shards, blocks, cap_big, cap_small, docs_at, blk_at, *refs):
     held, row_ref, back_ref = refs[:-2], refs[-2], refs[-1]
     size = held[0].shape[0]
     col_ids = as_column(row_ref[...])
@@ -228,7 +224,7 @@
                 others[...], row_ref[:, col * size:(col + 1) * size], same))
     best = jnp.concatenate(bests, axis=1)
     back_ref[...] = spread(
-        best, *big_sources(best.shape[1], me_ref, shards, blocks, cap_big, cap_small), shards, blocks)
+        best, *big_sources(best.shape[1], docs_at, blk_at, shards, blocks, cap_big, cap_small), shards, blocks)
 
 
 def small_kernel(shards, blocks, cap_small, rows_ref, row_ref, big_ref, back_hbm, lanes_ref, sem):
@@ -258,7 +254,7 @@
     out_ref[...] = jnp.sum(jnp.where(lane_ref[...] > 0.0, found, 0.0), axis=0, keepdims=True)
 
 
-def call(kernel, outs, ins, flops, moved, limit=16, scratch=()):
+def call(kernel, outs, ins, flops, moved, limit=16, scratch=(), aliases=None):
     specs = [pl.BlockSpec(memory_space=space) for _, _, space in outs]
     return pl.pallas_call(
         kernel,
@@ -267,6 +263,7 @@
         in_specs=[pl.BlockSpec(memory_space=space) for space in ins],
         out_specs=specs,
         scratch_shapes=scratch,
+        input_output_aliases=aliases or {},
         cost_estimate=pl.CostEstimate(flops=flops, bytes_accessed=moved, transcendentals=0),
         compiler_params=pltpu.CompilerParams(vmem_limit_bytes=limit << 20),
     )
@@ -289,75 +286,73 @@
     f32, bf16, i32 = jnp.float32, jnp.bfloat16, jnp.int32
     vmem, hbm, smem, dma = pltpu.VMEM, pltpu.HBM, pltpu.SMEM, pltpu.SemaphoreType.DMA
 
-    me = jnp.stack([lax.axis_index("docs"), lax.axis_index("blk")]).astype(i32)
+    me = tuple(lax.axis_index(axis).astype(i32).reshape(1) for axis in ("docs", "blk"))
     kinds = 2 if blocks > 1 and shards > 1 else 1
     half = big_slots // kinds
-    rows, info, *big_sent = call(
+    table = -(-blocks // 8) * 8
+    rows, info, *sent = call(
         functools.partial(sort_kernel, *sizes),
-        [((docs, feature), bf16, hbm), ((8, docs), i32, hbm)] + [((half, feature), bf16, hbm)] * blocks,
-        [smem, hbm, hbm, hbm],
+        [((docs, feature), bf16, hbm), ((8, docs), i32, hbm)] + [((half, feature), bf16, hbm)] * blocks
+        + [((table, LANES), f32, hbm)] * shards,
+        [smem, smem, hbm, hbm, hbm],
         2 * docs * feature * (pooled.shape[1] + big_slots), 4 << 20, 60,
         [vmem(pooled.shape, bf16), vmem(proj_weight.shape, bf16), vmem((1, docs), i32),
          vmem((docs, feature), bf16), vmem((8, docs), i32), vmem((big_slots, feature), bf16),
-         dma((5,)), dma((blocks,))],
-    )(me, pooled, proj_weight, cluster.reshape(1, docs))
+         vmem((shards, table, LANES), f32), dma((5,)), dma((blocks,)), dma((shards,))],
+    )(*me, pooled, proj_weight, cluster.reshape(1, docs))
+    big_sent, tables = sent[:blocks], sent[blocks:]
+
+    def along(x, axis, count, by):
+        return lax.ppermute(x, axis, [(i, (i + by) % count) for i in range(count)])
 
     homes = [home_of(d, blocks) for d in range(kinds)]
     big_held = [big_sent[0]]
     for step in range(1, blocks):
         pairs = [(d * blocks + (home + step) % blocks, d * blocks + home) for d in range(shards) for home in homes]
         big_held.append(lax.ppermute(big_sent[step], ("docs", "blk"), pairs))
-
-    table = -(-blocks // 8) * 8
-    small_sent, *tables = call(
-        functools.partial(sort_small_kernel, shards, blocks, cap_small),
-        [((small_slots, feature), bf16, hbm)] + [((table, LANES), f32, vmem)] * shards,
-        [smem, vmem, vmem],
+    tables = [tables[0]] + [along(tables[by], "docs", shards, by) for by in range(1, shards)]
+
+    small_sent, = call(
+        sort_small_kernel,
+        [((small_slots, feature), bf16, hbm)],
+        [vmem, vmem],
         2 * docs * feature * small_slots, 2 << 20, 16,
         [vmem((small_slots, feature), bf16), dma((3,))],
-    )(me, rows, info)
+    )(rows, info)
+
+    high = -(-shards // 8) * 8
+    small_sent, *sent = call(
+        functools.partial(group_kernel, shards, blocks, cap_big),
+        [((small_slots, feature), bf16, hbm)] + [((blocks * cap_big, feature), bf16, vmem)] * shards
+        + [((high, LANES), f32, vmem)] * blocks,
+        [smem, smem, hbm] + [vmem] * (blocks + shards),
+        shards * blocks * cap_big * feature, 4 << 20, aliases={2: 0},
+    )(*me, small_sent, *big_held, *tables)
+    grouped, tables = sent[:shards], sent[shards:]
 
     got_small = lax.all_to_all(
         small_sent.reshape(devices, cap_small, feature), ("docs", "blk"),
         split_axis=0, concat_axis=0, tiled=True).reshape(small_slots, feature)
 
-    def along(x, axis, count, by):
-        return lax.ppermute(x, axis, [(i, (i + by) % count) for i in range(count)])
-
-    tables = [tables[0]] + [along(tables[by], "docs", shards, by) for by in range(1, shards)]
-
-    grouped = call(
-        functools.partial(group_kernel, shards, blocks, cap_big),
-        [((blocks * cap_big, feature), bf16, vmem)] * shards,
-        [smem] + [vmem] * blocks,
-        shards * blocks * cap_big * feature, 4 << 20,
-    )(me, *big_held)
+    tables = [tables[0]] + [along(tables[by], "blk", blocks, by) for by in range(1, blocks)]
     parts = [grouped[0]]
     for shift in range(1, shards):
         pairs = [((d + shift) % shards * blocks + home_of(d, blocks), d * blocks + home_of(d, blocks))
                  for d in range(shards)]
         parts.append(lax.ppermute(grouped[shift], ("docs", "blk"), pairs))
 
-    high = -(-shards // 8) * 8
-    tables = call(
-        functools.partial(turn_kernel, blocks),
-        [((high, LANES), f32, vmem)] * blocks, [smem] + [vmem] * shards,
-        shards * blocks * LANES, 1 << 16,
-    )(me, *tables)
-    tables = [tables[0]] + [along(tables[by], "blk", blocks, by) for by in range(1, blocks)]
-
     small_ids, big_ids = call(
         functools.partial(ids_kernel, *sizes),
         [((1, small_slots), f32, vmem), ((1, big_total), f32, vmem)],
-        [smem] + [vmem] * blocks,
+        [smem, smem] + [vmem] * blocks,
         2 * high * blocks * LANES * (small_slots + big_total), 1 << 16,
-    )(me, *tables)
+    )(*me, *tables)
 
     back_big, = call(
         functools.partial(big_kernel, *sizes),
-        [((devices, LANES), f32, vmem)], [smem] + [vmem] * (shards + 1),
+        [((devices, LANES), f32, vmem)], [smem, smem] + [vmem] * (shards + 1),
         2 * big_total * big_total * feature, 2 << 20,
-    )(me, *parts, big_ids)
+    )(*me, *parts, big_ids)
 
     back, = call(
         functools.partial(small_kernel, shards, blocks, cap_small),

time: 96.6 us -> 74.8 us (0.77)
  starting transfers between devices: 46.6 us -> 33.7 us
  waiting for transfers between devices: 31.7 us -> 27 us
  Pallas kernels: 14.6 us -> 11 us
    ppermute x3, waiting for transfers between devices: 20.4 us -> 0.01 us  [body(): big_held.append(lax.ppermute(big_sent[step], ('docs', 'blk'), pairs))]
    ppermute x6, waiting for transfers between devices: 5.56 us -> 21.3 us  [along(): return lax.ppermute(x, axis, [(i, (i + by) % count) for i in range(count)])]
    ppermute x6, starting transfers between devices: 24.1 us -> 10.3 us  [along(): return lax.ppermute(x, axis, [(i, (i + by) % count) for i in range(count)])]
    all_to_all x1, starting transfers between devices: 5.22 us -> 6.99 us  [body(): lax.all_to_all(back, ('docs', 'blk'), split_axis=0, concat_axis=0, tiled=...]
    all_to_all x1, starting transfers between devices: 7.47 us -> 5.76 us  [body(): lax.all_to_all(small_sent.reshape(devices, cap_small, feature), ('docs',...]
    pallas_call x3 -> x2, Pallas kernels: 3.4 us -> 1.71 us  [the longest x1 1.58 us: body(): call(sort_small_kernel, [((small_slots, feature), bf16, hbm)], [vmem, vme...]
  transfers between devices with their start and end apart: 14 -> 14, of which waited for: 9 -> 5; matrix products, arithmetic and copies ran while one was open for 0% -> 0% of each run, Pallas kernels for 5% -> 5%
where the time goes in v6:
time: 74.8 us; the launch traced here: 73.8 us
  starting transfers between devices  33.7 us (45%)
  waiting for transfers between devices  27 us (36%)
  Pallas kernels  11 us (15%)
  local copies, waits for them, and re-layouts  1.86 us (2%)
    ppermute x6, waiting for transfers between devices, along(): return lax.ppermute(x, axis, [(i, (i + by) % count) for i in range(count)])  21.3 us
    ppermute x6, starting transfers between devices, along(): return lax.ppermute(x, axis, [(i, (i + by) % count) for i in range(count)])  10.3 us
    ppermute x3, starting transfers between devices, body(): big_held.append(lax.ppermute(big_sent[step], ('docs', 'blk'), pairs))  8.57 us
    all_to_all x1, starting transfers between devices, body(): lax.all_to_all(back, ('docs', 'blk'), split_axis=0, concat_axis=0, tiled=...  6.99 us
    all_to_all x1, starting transfers between devices, body(): lax.all_to_all(small_sent.reshape(devices, cap_small, feature), ('docs',...  5.76 us
    all_to_all x1, waiting for transfers between devices, body(): lax.all_to_all(back, ('docs', 'blk'), split_axis=0, concat_axis=0, tiled=...  5.75 us
    pallas_call x1, Pallas kernels, body(): call(functools.partial(sort_kernel, *sizes), [((docs, feature), bf16, hbm...  4.13 us
    pallas_call x1, Pallas kernels, body(): call(functools.partial(big_kernel, *sizes), [((devices, LANES), f32, vmem...  2.12 us
  transfers between devices with their start and end apart: 14, of which 5 were waited for; matrix products, arithmetic and copies ran while one was open for 0% of the time, Pallas kernels for 5%

profile of v6, /device:TPU:1, one launch (start us, length us, event | category | flops | bytes accessed | tf_op | source)
XLA Modules:
  0.0 73.8 jit_solution(8795337505249118817)
XLA Ops:
  0.0 4.1 %shard_map.37 = (bf16[512,768]{1,0:T(8,128)(2,1)}, s32[8,512]{1,0:T(8,128)}, bf16[128,768]{1,0:T(8,128)(2,1)}, bf16[128,768]{1,0:T(8,128)(2,1)}, bf16[128,768]{1...) custom-call(s32[1]{0:T(128)} %bitcast.docs_at, ...), custom_call_target="tpu_custom_call" | custom-call | flops 805306368 | bytes 4194304 | tf_op jit(solution)/shard_map/pallas_call | solution.py:293
  4.1 0.0 copy-start
  4.1 0.8 %collective-permute-start = (bf16[128,768]{1,0:T(8,128)(2,1)}, bf16[128,768]{1,0:T(8,128)(2,1)S(1)}, u32[]{:S(2)}, u32[]{:S(2)}) collective-permute-start(bf16[128,768]{1,0:T(8,128)(2,1)} %get-tuple-element.31), channel_id=1, source_target_pairs={{2,1},{3,2},{6,5},{7,6},{10,9},{11,10},{14,13},{15,14},{18,17},{19... | collective-permute-start | bytes 589832 | tf_op jit(solution)/shard_map/ppermute | solution.py:312
  5.0 6.5 %collective-permute-start.1 = (bf16[128,768]{1,0:T(8,128)(2,1)}, bf16[128,768]{1,0:T(8,128)(2,1)S(1)}, u32[]{:S(2)}, u32[]{:S(2)}) collective-permute-start(bf16[128,768]{1,0:T(8,128)(2,1)} %get-tuple-element.32), channel_id=1, source_target_pairs={{3,1},{0,2},{7,5},{4,6},{11,9},{8,10},{15,13},{12,14},{19,17},{16,... | collective-permute-start | bytes 589832 | tf_op jit(solution)/shard_map/ppermute | solution.py:312
  11.4 1.3 %collective-permute-start.2 = (bf16[128,768]{1,0:T(8,128)(2,1)}, bf16[128,768]{1,0:T(8,128)(2,1)S(1)}, u32[]{:S(2)}, u32[]{:S(2)}) collective-permute-start(bf16[128,768]{1,0:T(8,128)(2,1)} %get-tuple-element.33), channel_id=1, source_target_pairs={{0,1},{1,2},{4,5},{5,6},{8,9},{9,10},{12,13},{13,14},{16,17},{17,1... | collective-permute-start | bytes 589832 | tf_op jit(solution)/shard_map/ppermute | solution.py:312
  12.7 2.4 %collective-permute-start.3 = (f32[8,128]{1,0:T(8,128)}, f32[8,128]{1,0:T(8,128)S(1)}, u32[]{:S(2)}, u32[]{:S(2)}) collective-permute-start(f32[8,128]{1,0:T(8,128)} %get-tuple-element.35), channel_id=1, source_target_pairs={{0,4},{4,8},{8,12},{12,0},{1,5},{5,9},{9,13},{13,1},{2,6},{6,10},{... | collective-permute-start | bytes 12296 | tf_op jit(solution)/shard_map/ppermute | solution.py:306
  15.1 0.3 collective-permute-start.4
  15.4 0.7 collective-permute-done.3.refs_5_
  16.1 1.2 %collective-permute-start.5 = (f32[8,128]{1,0:T(8,128)}, f32[8,128]{1,0:T(8,128)S(1)}, u32[]{:S(2)}, u32[]{:S(2)}) collective-permute-start(f32[8,128]{1,0:T(8,128)} %get-tuple-element.37), channel_id=1, source_target_pairs={{0,12},{4,0},{8,4},{12,8},{1,13},{5,1},{9,5},{13,9},{2,14},{6,2},{... | collective-permute-start | bytes 12296 | tf_op jit(solution)/shard_map/ppermute | solution.py:306
  17.3 0.0 copy-start.1
  17.3 0.7 copy-done.1
  18.0 0.0 copy-start.4
  18.0 1.1 %copy-done.4 = bf16[512,768]{1,0:T(8,128)(2,1)S(1)} copy-done((bf16[512,768]{1,0:T(8,128)(2,1)S(1)}, bf16[512,768]{1,0:T(8,128)(2,1)}, u32[]{:S(2)}) %copy-start.4) | copy-done | bytes 786456
  19.1 0.0 copy-start.3
  19.1 1.6 %shard_map.38.small_in = bf16[768,768]{1,0:T(8,128)(2,1)} custom-call(bf16[512,768]{1,0:T(8,128)(2,1)S(1)} %copy-done.4, s32[8,512]{1,0:T(8,128)S(1)} %copy-done.1), custom_call_target="tpu_custom_call" | custom-call | flops 603979776 | bytes 2097152 | tf_op jit(solution)/shard_map/pallas_call | solution.py:315
  20.7 0.0 collective-permute-done.4.refs_6_
  20.7 0.0 collective-permute-done.5.refs_7_
  20.7 0.0 collective-permute-done.refs_1_
  20.7 0.0 collective-permute-done.1.refs_2_
  20.8 0.0 collective-permute-done.2.refs_3_
  20.8 0.0 copy-done
  20.8 0.0 copy-done.3
  20.8 0.1 shard_map.39
  20.9 5.8 %all-to-all-start = ((bf16[16,48,768]{2,1,0:T(8,128)(2,1)}), bf16[16,48,768]{2,1,0:T(8,128)(2,1)S(1)}, u32[]{:S(2)}, u32[]{:S(2)}) async-start(bf16[16,48,768]{2,1,0:T(8,128)(2,1)} %bitcast.7), calls=%async_computation | async-start | bytes 2359296 | tf_op jit(solution)/shard_map/all_to_all | solution.py:333
  26.7 0.7 collective-permute-start.10
  27.4 0.7 collective-permute-start.11
  28.0 0.7 collective-permute-start.9
  28.7 6.5 %collective-permute-start.6 = (f32[8,128]{1,0:T(8,128)S(1)}, f32[8,128]{1,0:T(8,128)S(1)}, u32[]{:S(2)}, u32[]{:S(2)}) collective-permute-start(f32[8,128]{1,0:T(8,128)S(1)} %get-tuple-element.40), channel_id=1, source_target_pairs={{0,1},{1,2},{2,3},{3,0},{4,5},{5,6},{6,7},{7,4},{8,9},{9,10},{10,1... | collective-permute-start | bytes 12296 | tf_op jit(solution)/shard_map/ppermute | solution.py:306
  35.3 0.0 collective-permute-start.7
  35.3 14.5 %collective-permute-done.6.refs_1_ = f32[8,128]{1,0:T(8,128)S(1)} collective-permute-done((f32[8,128]{1,0:T(8,128)S(1)}, f32[8,128]{1,0:T(8,128)S(1)}, u32[]{:S(2)}, u32[]{:S(2)}) %collective-permute-start.6) | collective-permute-done | bytes 4128 | tf_op jit(solution)/shard_map/ppermute | solution.py:306
  49.7 0.0 collective-permute-start.8
  49.7 5.8 %collective-permute-done.7.refs_2_ = f32[8,128]{1,0:T(8,128)S(1)} collective-permute-done((f32[8,128]{1,0:T(8,128)S(1)}, f32[8,128]{1,0:T(8,128)S(1)}, u32[]{:S(2)}, u32[]{:S(2)}) %collective-permute-start.7) | collective-permute-done | bytes 4128 | tf_op jit(solution)/shard_map/ppermute | solution.py:306
  55.5 0.3 collective-permute-done.8.refs_3_
  55.8 0.2 shard_map.40
  56.1 0.0 collective-permute-done.10.refs_2_
  56.1 0.0 collective-permute-done.11.refs_3_
  56.1 0.0 collective-permute-done.9.refs_1_
  56.1 2.1 %shard_map.41.big_ref = f32[16,128]{1,0:T(8,128)S(1)} custom-call(s32[1]{0:T(128)} %bitcast.docs_at, s32[1]{0:T(128)} %bitcast.1.blk_at, bf16[256,768]{1,0:T(8,128)(2,1)S(1)} %get-tuple-element.44.refs_0_, bf16[256,768]{1,0:T(8,128)(2,1)S(1)} %collective-permute-done.9.refs_1_, bf16[256,768]{1,0:T(8,128)(2,1)S(1)} %collective-permute-done.10.refs_2_, ...), custom_call_target="tpu_custom_call" | custom-call | flops 1610612736 | bytes 2097152 | tf_op jit(solution)/shard_map/pallas_call | solution.py:351
  58.2 0.0 all-to-all-done
  58.2 0.0 copy-start.2
  58.2 2.0 %shard_map.42 = f32[16,1,128]{2,1,0:T(1,128)} custom-call(bf16[768,768]{1,0:T(8,128)(2,1)S(1)} %bitcast.6, f32[1,768]{1,0:T(1,128)S(1)} %get-tuple-element.43.row_ref, f32[16,128]{1,0:T(8,128)S(1)} %shard_map.41.big_ref), custom_call_target="tpu_custom_call" | custom-call | flops 905969664 | bytes 2097152 | tf_op jit(solution)/shard_map/pallas_call | solution.py:357
  60.2 7.0 %all-to-all-start.1 = ((f32[16,1,128]{2,1,0:T(1,128)}), f32[16,1,128]{2,1,0:T(1,128)S(1)}, u32[]{:S(2)}, u32[]{:S(2)}) async-start(f32[16,1,128]{2,1,0:T(1,128)} %shard_map.42), calls=%async_computation.1 | async-start | bytes 16384 | tf_op jit(solution)/shard_map/all_to_all | solution.py:364
  67.2 0.0 copy-done.2
  67.2 5.7 %all-to-all-done.1.back_ref = f32[16,1,128]{2,1,0:T(1,128)S(1)} async-done(((f32[16,1,128]{2,1,0:T(1,128)}), f32[16,1,128]{2,1,0:T(1,128)S(1)}, u32[]{:S(2)}, u32[]{:S(2)}) %all-to-all-start.1) | async-done | bytes 8224 | tf_op jit(solution)/shard_map/all_to_all | solution.py:364
  73.0 0.8 %shard_map.44 = f32[1,512]{1,0:T(1,128)} custom-call(f32[16,1,128]{2,1,0:T(1,128)S(1)} %all-to-all-done.1.back_ref, bf16[48,512]{1,0:T(8,128)(2,1)S(1)} %get-tuple-element.49.device_ref, f32[128,512]{1,0:T(8,128)S(1)} %get-tuple-element.50.lane_ref), custom_call_target="tpu_custom_call" | custom-call | flops 2097152 | bytes 262144 | tf_op jit(solution)/shard_map/pallas_call | solution.py:369
  (1 shorter events, 0.0 us)
Async XLA Ops:
  4.1 16.6 %copy-start = (bf16[128,768]{1,0:T(8,128)(2,1)S(1)}, bf16[128,768]{1,0:T(8,128)(2,1)}, u32[]{:S(2)}) copy-start(bf16[128,768]{1,0:T(8,128)(2,1)} %get-tuple-element.30.refs_0_) | copy-start | bytes 589828
  4.1 16.6 %collective-permute-start = (bf16[128,768]{1,0:T(8,128)(2,1)}, bf16[128,768]{1,0:T(8,128)(2,1)S(1)}, u32[]{:S(2)}, u32[]{:S(2)}) collective-permute-start(bf16[128,768]{1,0:T(8,128)(2,1)} %get-tuple-element.31), channel_id=1, source_target_pairs={{2,1},{3,2},{6,5},{7,6},{10,9},{11,10},{14,13},{15,14},{18,17},{19... | collective-permute-start | bytes 589832 | tf_op jit(solution)/shard_map/ppermute | solution.py:312
  5.0 15.8 %collective-permute-start.1 = (bf16[128,768]{1,0:T(8,128)(2,1)}, bf16[128,768]{1,0:T(8,128)(2,1)S(1)}, u32[]{:S(2)}, u32[]{:S(2)}) collective-permute-start(bf16[128,768]{1,0:T(8,128)(2,1)} %get-tuple-element.32), channel_id=1, source_target_pairs={{3,1},{0,2},{7,5},{4,6},{11,9},{8,10},{15,13},{12,14},{19,17},{16,... | collective-permute-start | bytes 589832 | tf_op jit(solution)/shard_map/ppermute | solution.py:312
  11.4 9.3 %collective-permute-start.2 = (bf16[128,768]{1,0:T(8,128)(2,1)}, bf16[128,768]{1,0:T(8,128)(2,1)S(1)}, u32[]{:S(2)}, u32[]{:S(2)}) collective-permute-start(bf16[128,768]{1,0:T(8,128)(2,1)} %get-tuple-element.33), channel_id=1, source_target_pairs={{0,1},{1,2},{4,5},{5,6},{8,9},{9,10},{12,13},{13,14},{16,17},{17,1... | collective-permute-start | bytes 589832 | tf_op jit(solution)/shard_map/ppermute | solution.py:312
  12.7 3.3 %collective-permute-start.3 = (f32[8,128]{1,0:T(8,128)}, f32[8,128]{1,0:T(8,128)S(1)}, u32[]{:S(2)}, u32[]{:S(2)}) collective-permute-start(f32[8,128]{1,0:T(8,128)} %get-tuple-element.35), channel_id=1, source_target_pairs={{0,4},{4,8},{8,12},{12,0},{1,5},{5,9},{9,13},{13,1},{2,6},{6,10},{... | collective-permute-start | bytes 12296 | tf_op jit(solution)/shard_map/ppermute | solution.py:306
  15.1 5.6 %collective-permute-start.4 = (f32[8,128]{1,0:T(8,128)}, f32[8,128]{1,0:T(8,128)S(1)}, u32[]{:S(2)}, u32[]{:S(2)}) collective-permute-start(f32[8,128]{1,0:T(8,128)} %get-tuple-element.36), channel_id=1, source_target_pairs={{0,8},{4,12},{8,0},{12,4},{1,9},{5,13},{9,1},{13,5},{2,10},{6,14},... | collective-permute-start | bytes 12296 | tf_op jit(solution)/shard_map/ppermute | solution.py:306
  16.1 4.6 %collective-permute-start.5 = (f32[8,128]{1,0:T(8,128)}, f32[8,128]{1,0:T(8,128)S(1)}, u32[]{:S(2)}, u32[]{:S(2)}) collective-permute-start(f32[8,128]{1,0:T(8,128)} %get-tuple-element.37), channel_id=1, source_target_pairs={{0,12},{4,0},{8,4},{12,8},{1,13},{5,1},{9,5},{13,9},{2,14},{6,2},{... | collective-permute-start | bytes 12296 | tf_op jit(solution)/shard_map/ppermute | solution.py:306
  17.3 0.7 copy-start.1
  18.0 1.1 %copy-start.4 = (bf16[512,768]{1,0:T(8,128)(2,1)S(1)}, bf16[512,768]{1,0:T(8,128)(2,1)}, u32[]{:S(2)}) copy-start(bf16[512,768]{1,0:T(8,128)(2,1)} %get-tuple-element.28.rows_ref) | copy-start | bytes 2359300
  19.1 1.7 %copy-start.3 = (f32[8,128]{1,0:T(8,128)S(1)}, f32[8,128]{1,0:T(8,128)}, u32[]{:S(2)}) copy-start(f32[8,128]{1,0:T(8,128)} %get-tuple-element.34.refs_4_) | copy-start | bytes 12292
  20.9 37.3 %all-to-all-start = ((bf16[16,48,768]{2,1,0:T(8,128)(2,1)}), bf16[16,48,768]{2,1,0:T(8,128)(2,1)S(1)}, u32[]{:S(2)}, u32[]{:S(2)}) async-start(bf16[16,48,768]{2,1,0:T(8,128)(2,1)} %bitcast.7), calls=%async_computation | async-start | bytes 2359296 | tf_op jit(solution)/shard_map/all_to_all | solution.py:333
  26.7 29.4 %collective-permute-start.10 = (bf16[256,768]{1,0:T(8,128)(2,1)S(1)}, bf16[256,768]{1,0:T(8,128)(2,1)S(1)}, u32[]{:S(2)}, u32[]{:S(2)}) collective-permute-start(bf16[256,768]{1,0:T(8,128)(2,1)S(1)} %get-tuple-element.46), channel_id=1, source_target_pairs={{9,1},{14,6},{1,9},{6,14},{25,17},{30,22},{17,25},{22,30}} | collective-permute-start | bytes 1179656 | tf_op jit(solution)/shard_map/ppermute | solution.py:342
  27.4 28.7 %collective-permute-start.11 = (bf16[256,768]{1,0:T(8,128)(2,1)S(1)}, bf16[256,768]{1,0:T(8,128)(2,1)S(1)}, u32[]{:S(2)}, u32[]{:S(2)}) collective-permute-start(bf16[256,768]{1,0:T(8,128)(2,1)S(1)} %get-tuple-element.47), channel_id=1, source_target_pairs={{13,1},{2,6},{5,9},{10,14},{29,17},{18,22},{21,25},{26,30}} | collective-permute-start | bytes 1179656 | tf_op jit(solution)/shard_map/ppermute | solution.py:342
  28.0 28.0 %collective-permute-start.9 = (bf16[256,768]{1,0:T(8,128)(2,1)S(1)}, bf16[256,768]{1,0:T(8,128)(2,1)S(1)}, u32[]{:S(2)}, u32[]{:S(2)}) collective-permute-start(bf16[256,768]{1,0:T(8,128)(2,1)S(1)} %get-tuple-element.45), channel_id=1, source_target_pairs={{5,1},{10,6},{13,9},{2,14},{21,17},{26,22},{29,25},{18,30}} | collective-permute-start | bytes 1179656 | tf_op jit(solution)/shard_map/ppermute | solution.py:342
  28.7 21.0 %collective-permute-start.6 = (f32[8,128]{1,0:T(8,128)S(1)}, f32[8,128]{1,0:T(8,128)S(1)}, u32[]{:S(2)}, u32[]{:S(2)}) collective-permute-start(f32[8,128]{1,0:T(8,128)S(1)} %get-tuple-element.40), channel_id=1, source_target_pairs={{0,1},{1,2},{2,3},{3,0},{4,5},{5,6},{6,7},{7,4},{8,9},{9,10},{10,1... | collective-permute-start | bytes 12296 | tf_op jit(solution)/shard_map/ppermute | solution.py:306
  35.3 20.2 %collective-permute-start.7 = (f32[8,128]{1,0:T(8,128)S(1)}, f32[8,128]{1,0:T(8,128)S(1)}, u32[]{:S(2)}, u32[]{:S(2)}) collective-permute-start(f32[8,128]{1,0:T(8,128)S(1)} %get-tuple-element.41), channel_id=1, source_target_pairs={{0,2},{1,3},{2,0},{3,1},{4,6},{5,7},{6,4},{7,5},{8,10},{9,11},{10,... | collective-permute-start | bytes 12296 | tf_op jit(solution)/shard_map/ppermute | solution.py:306
  49.7 6.1 %collective-permute-start.8 = (f32[8,128]{1,0:T(8,128)S(1)}, f32[8,128]{1,0:T(8,128)S(1)}, u32[]{:S(2)}, u32[]{:S(2)}) collective-permute-start(f32[8,128]{1,0:T(8,128)S(1)} %get-tuple-element.42), channel_id=1, source_target_pairs={{0,3},{1,0},{2,1},{3,2},{4,7},{5,4},{6,5},{7,6},{8,11},{9,8},{10,9... | collective-permute-start | bytes 12296 | tf_op jit(solution)/shard_map/ppermute | solution.py:306
  58.2 9.0 %copy-start.2 = (s32[8,512]{1,0:T(8,128)S(1)}, s32[8,512]{1,0:T(8,128)}, u32[]{:S(2)}) copy-start(s32[8,512]{1,0:T(8,128)} %get-tuple-element.29.info_ref) | copy-start | bytes 49156
  60.2 12.8 %all-to-all-start.1 = ((f32[16,1,128]{2,1,0:T(1,128)}), f32[16,1,128]{2,1,0:T(1,128)S(1)}, u32[]{:S(2)}, u32[]{:S(2)}) async-start(f32[16,1,128]{2,1,0:T(1,128)} %shard_map.42), calls=%async_computation.1 | async-start | bytes 16384 | tf_op jit(solution)/shard_map/all_to_all | solution.py:364

commit v7 on v3

v7 whole, which is shorter than its diff:
```python
import functools

import jax
import jax.numpy as jnp
from jax import lax
from jax.experimental import pallas as pl
from jax.experimental.pallas import tpu as pltpu
from jax.sharding import PartitionSpec as P

BIG_OWN = 4
LANES = 128


def modulo(x, n):
    return x & (n - 1) if n & (n - 1) == 0 else lax.rem(x, jnp.int32(n))


def quotient(x, n):
    if n & (n - 1) == 0:
        return lax.shift_right_logical(x, jnp.int32(n.bit_length() - 1))
    return lax.div(x, jnp.int32(n))


def iota(shape, axis):
    return lax.broadcasted_iota(jnp.int32, shape, axis)


def dot_nt(a, b):
    return lax.dot_general(a, b, (((1,), (1,)), ((), ())), preferred_element_type=jnp.float32)


def tile_of(rows, most=256):
    tile = most
    while rows % tile:
        tile //= 2
    return tile


def home_of(docs, blocks):
    return max(blocks // 2 - 1, 0) + (docs & min(blocks - 1, 1))


def picked_rows(rows_ref, slot, first, count):
    pick = (iota((count, rows_ref.shape[0]), 0) + first == slot).astype(jnp.float32).astype(jnp.bfloat16)
    return jnp.dot(pick, rows_ref[...], preferred_element_type=jnp.float32).astype(jnp.bfloat16)


def sort_kernel(shards, blocks, cap_big, cap_small, pooled_hbm, weight_hbm, cluster_hbm, small_hbm, rows_hbm, info_hbm,
                pooled_ref, weight_ref, cluster_ref, small_ref, rows_ref, info_ref, sems, small_sems):
    docs = rows_ref.shape[0]
    devices = shards * blocks
    limit = BIG_OWN * shards
    buckets = devices + shards

    fetches = [pltpu.make_async_copy(source, target, sems.at[n]) for n, (source, target) in enumerate(
        ((cluster_hbm, cluster_ref), (weight_hbm, weight_ref), (pooled_hbm, pooled_ref)))]
    for fetch in fetches:
        fetch.start()
    fetches[0].wait()

    cluster = cluster_ref[...]
    is_big = cluster < limit
    owner = modulo(cluster, shards)
    past = jnp.maximum(cluster - limit, 0)
    target = modulo(past, devices)
    bucket = jnp.where(is_big, devices + owner, target)

    padded = -(-buckets // 16) * 16
    hot = (iota((padded, docs), 0) == bucket).astype(jnp.float32)
    earlier = (iota((docs, docs), 0) < iota((docs, docs), 1)).astype(jnp.float32).astype(jnp.bfloat16)
    before = jnp.dot(hot.astype(jnp.bfloat16), earlier, preferred_element_type=jnp.float32)
    rank = jnp.sum(before * hot, axis=0, keepdims=True).astype(jnp.int32)

    info_ref[0:1, :] = jnp.where(is_big, owner * blocks + home_of(owner, blocks), target)
    info_ref[1:2, :] = jnp.where(is_big, cap_small + rank, rank)
    info_ref[2:3, :] = jnp.where(is_big, owner * cap_big + rank, -1)
    info_ref[3:4, :] = jnp.where(is_big, quotient(cluster, shards), quotient(past, devices)) + 1
    info_ref[4:5, :] = bucket
    info_ref[5:8, :] = jnp.zeros((3, docs), jnp.int32)
    sends = [pltpu.make_async_copy(info_ref, info_hbm, sems.at[3])]
    sends[0].start()
    small_slot = jnp.where(is_big, -1, target * cap_small + rank)

    for fetch in fetches[1:]:
        fetch.wait()
    projected = jnp.dot(pooled_ref[...], weight_ref[...], preferred_element_type=jnp.float32)
    squares = jnp.sum(projected * projected, axis=1, keepdims=True)
    rows_ref[...] = (projected / jnp.sqrt(squares + 1e-06)).astype(jnp.bfloat16)
    sends.append(pltpu.make_async_copy(rows_ref, rows_hbm, sems.at[4]))
    sends[-1].start()

    tile = small_ref.shape[0] // small_sems.shape[0]
    for part in range(small_sems.shape[0]):
        small_ref[part * tile:(part + 1) * tile, :] = picked_rows(rows_ref, small_slot, part * tile, tile)
        sends.append(pltpu.make_async_copy(
            small_ref.at[pl.ds(part * tile, tile)], small_hbm.at[pl.ds(part * tile, tile)], small_sems.at[part]))
        sends[-1].start()
    for send in sends:
        send.wait()


def sort_big_kernel(shards, blocks, cap_big, docs_at, rows_ref, info_ref, *out_refs):
    docs = rows_ref.shape[0]
    devices = shards * blocks
    quota, bucket = info_ref[3:4, :].astype(jnp.float32), info_ref[4:5, :]
    lanes = (iota((LANES, docs), 0) == info_ref[1:2, :]).astype(jnp.float32).astype(jnp.bfloat16)
    for shift, ref in enumerate(out_refs):
        to = modulo(docs_at[0] + shift, shards)
        ref[0:cap_big, :] = picked_rows(rows_ref, info_ref[2:3, :], to * cap_big, cap_big)
        table = ref.shape[0] - cap_big
        blk = iota((table, docs), 0)
        mine = (blk < blocks) & ((blk + to * blocks == bucket) | (bucket == devices + to))
        values = jnp.where(mine, quota, 0.0).astype(jnp.bfloat16)
        ref[cap_big:, 0:LANES] = dot_nt(values, lanes).astype(jnp.bfloat16)
        ref[cap_big:, LANES:] = jnp.zeros((table, ref.shape[1] - LANES), jnp.bfloat16)


def group_kernel(shards, blocks, cap_big, blk_at, *refs):
    held, group_ref, ids_refs = refs[:shards], refs[shards], refs[shards + 1:]
    tables = [ref[cap_big:, 0:LANES].astype(jnp.float32) for ref in held]
    total = shards * cap_big
    for shift, ref in enumerate(held):
        group_ref[shift * cap_big:(shift + 1) * cap_big, :] = ref[0:cap_big, :]
    spare = group_ref.shape[0] - total
    own = jnp.zeros((spare, LANES), jnp.float32)
    for shift, table in enumerate(tables):
        own = jnp.where(iota(own.shape, 0) == shift, table[0:1, :], own)
    group_ref[total:, 0:LANES] = own.astype(jnp.bfloat16)
    group_ref[total:, LANES:] = jnp.zeros((spare, group_ref.shape[1] - LANES), jnp.bfloat16)
    turn(tables, blk_at[0], blocks, ids_refs)


def turn(tables, at, count, outs):
    for step, out in enumerate(outs):
        to = modulo(at + step, count)
        out[...] = jnp.zeros(out.shape, jnp.float32)
        for place, table in enumerate(tables):
            out[place:place + 1, :] = jnp.sum(
                jnp.where(iota(table.shape, 0) == to, table, 0.0), axis=0, keepdims=True)


def turn_kernel(count, at_ref, *refs):
    held, outs = refs[:-count], refs[-count:]
    turn([ref[...] for ref in held], at_ref[0], count, outs)


def rows_up(count, to=8):
    return -(-count // to) * to


def small_sources(total, blocks, cap_small):
    at = iota((1, total), 1)
    source = at // cap_small
    return source // blocks, modulo(source, blocks), lax.rem(at, jnp.int32(cap_small))


def big_sources(total, shards, cap_big, cap_small):
    at = iota((1, total), 1)
    return (at // (shards * cap_big), modulo(at // cap_big, shards),
            cap_small + lax.rem(at, jnp.int32(cap_big)))


def ids_from(values, row, lane):
    pick = (iota((LANES, lane.shape[1]), 0) == lane).astype(jnp.float32).astype(jnp.bfloat16)
    found = jnp.dot(values, pick, preferred_element_type=jnp.float32)
    return jnp.sum(jnp.where(iota(found.shape, 0) == row, found, 0.0), axis=0, keepdims=True)


def ids_kernel(shards, blocks, cap_small, docs_at, blk_at, *refs):
    tables, ids_ref = refs[:-1], refs[-1]
    high = tables[0].shape[0]
    values = jnp.concatenate([table[...] for table in tables], axis=0)
    values = jnp.concatenate([values, jnp.zeros_like(values)], axis=0).astype(jnp.bfloat16)
    docs, blk, lane = small_sources(ids_ref.shape[1], blocks, cap_small)
    row = modulo(blk_at[0] + blocks - blk, blocks) * high + modulo(docs_at[0] + shards - docs, shards)
    ids_ref[...] = ids_from(values, row, lane)


def as_column(row):
    return jnp.broadcast_to(row, (8, row.shape[1])).T[:, 0:1]


def block_best(queries, col_ids, first_row, others, row_ids, first_col):
    scores = dot_nt(queries, others)
    allowed = (col_ids == row_ids) & (row_ids > 0.0)
    if first_row is not None:
        allowed &= (iota(scores.shape, 0) + first_row) != (iota(scores.shape, 1) + first_col)
    return jnp.max(jnp.where(allowed, scores, -1.0), axis=0, keepdims=True)


def spread(best, row, lane, rows):
    total = best.shape[1]
    mine = jnp.where(iota((rows, total), 0) == row, best, 0.0)
    place = (iota((LANES, total), 0) == lane).astype(jnp.float32).astype(jnp.bfloat16)
    found = dot_nt(thirds(mine), place)
    return found[:rows] + found[rows:2 * rows] + found[2 * rows:]


def thirds(values):
    high = values.astype(jnp.bfloat16)
    rest = values - high.astype(jnp.float32)
    middle = rest.astype(jnp.bfloat16)
    low = (rest - middle.astype(jnp.float32)).astype(jnp.bfloat16)
    return jnp.concatenate([high, middle, low], axis=0)


def big_kernel(shards, blocks, cap_big, cap_small, docs_at, *refs):
    held, back_ref = refs[:-1], refs[-1]
    size = shards * cap_big
    spare = held[0].shape[0] - size
    high = back_ref.shape[0] // blocks
    step, shift, lane = big_sources(blocks * size, shards, cap_big, cap_small)
    values = jnp.concatenate([ref[size:, 0:LANES] for ref in held], axis=0)
    row_ids = ids_from(values, step * spare + shift, lane)
    col_ids = as_column(row_ids)
    bests = [jnp.full((1, size), -1.0, jnp.float32) for _ in held]
    for row, queries in enumerate(held):
        for col, others in enumerate(held):
            same = 0 if row == col else None
            bests[col] = jnp.maximum(bests[col], block_best(
                queries[0:size, :], col_ids[row * size:(row + 1) * size], same,
                others[0:size, :], row_ids[:, col * size:(col + 1) * size], same))
    docs = modulo(docs_at[0] + shards - shift, shards)
    back_ref[...] = spread(jnp.concatenate(bests, axis=1), step * high + docs, lane, back_ref.shape[0])


def small_kernel(shards, blocks, cap_small, blk_at, rows_ref, row_ref, big_ref, *back_refs):
    total = rows_ref.shape[0]
    high = back_refs[0].shape[0]
    col_ids = as_column(row_ref[...])
    tile = tile_of(total)
    best = jnp.full((1, total), -1.0, jnp.float32)
    for at in range(0, total, tile):
        best = jnp.maximum(best, block_best(
            rows_ref[at:at + tile, :], col_ids[at:at + tile], at, rows_ref[...], row_ref[...], 0))
    docs, blk, lane = small_sources(total, blocks, cap_small)
    row = modulo(blk + blocks - blk_at[0], blocks) * high + docs
    back = big_ref[...] + spread(best, row, lane, big_ref.shape[0])
    for step, ref in enumerate(back_refs):
        ref[...] = back[step * high:(step + 1) * high, :]


def masks_kernel(shards, blocks, docs_at, blk_at, info_ref, row_ref, lane_ref):
    device = info_ref[0:1, :]
    high = row_ref.shape[0] // (3 * shards)
    row = (modulo(docs_at[0] + shards - device // blocks, shards) * high
           + modulo(blk_at[0] + blocks - modulo(device, blocks), blocks))
    mask = (iota((shards * high, row_ref.shape[1]), 0) == row).astype(jnp.float32)
    row_ref[...] = jnp.concatenate([mask] * 3, axis=0).astype(jnp.bfloat16)
    lane_ref[...] = (iota(lane_ref.shape, 0) == info_ref[1:2, :]).astype(jnp.float32)


def finish_kernel(*refs):
    held, (row_ref, lane_ref, out_ref) = refs[:-3], refs[-3:]
    values = thirds(jnp.concatenate([ref[...] for ref in held], axis=0))
    found = lax.dot_general(values, row_ref[...], (((0,), (0,)), ((), ())), preferred_element_type=jnp.float32)
    out_ref[...] = jnp.sum(jnp.where(lane_ref[...] > 0.0, found, 0.0), axis=0, keepdims=True)


def call(kernel, outs, ins, flops, moved, limit=16, scratch=()):
    specs = [pl.BlockSpec(memory_space=space) for _, _, space in outs]
    return pl.pallas_call(
        kernel,
        out_shape=[space(shape, dtype) if space is pltpu.HBM else jax.ShapeDtypeStruct(shape, dtype)
                   for shape, dtype, space in outs],
        in_specs=[pl.BlockSpec(memory_space=space) for space in ins],
        out_specs=specs,
        scratch_shapes=scratch,
        cost_estimate=pl.CostEstimate(flops=flops, bytes_accessed=moved, transcendentals=0),
        compiler_params=pltpu.CompilerParams(vmem_limit_bytes=limit << 20),
    )


def body(pooled, proj_weight, cluster):
    shards = lax.axis_size("docs")
    blocks = lax.axis_size("blk")
    devices = shards * blocks
    docs = pooled.shape[0]
    feature = proj_weight.shape[1]
    big_count = docs // 4
    small_count = docs - big_count
    cap_big = 2 * big_count // shards
    cap_small = 2 * small_count // devices
    small_slots = devices * cap_small
    big_slots = shards * cap_big
    big_total = blocks * big_slots
    sizes = (shards, blocks, cap_big, cap_small)
    f32, bf16, i32 = jnp.float32, jnp.bfloat16, jnp.int32
    vmem, hbm, smem, dma = pltpu.VMEM, pltpu.HBM, pltpu.SMEM, pltpu.SemaphoreType.DMA

    docs_at, blk_at = (lax.axis_index(axis).astype(i32).reshape(1) for axis in ("docs", "blk"))

    def along(x, axis, count, by):
        return lax.ppermute(x, axis, [(i, (i + by) % count) for i in range(count)])

    small_sent, rows, info = call(
        functools.partial(sort_kernel, *sizes),
        [((small_slots, feature), bf16, hbm), ((docs, feature), bf16, hbm), ((8, docs), i32, hbm)],
        [hbm, hbm, hbm],
        2 * docs * feature * (pooled.shape[1] + small_slots), 4 << 20, 60,
        [vmem(pooled.shape, bf16), vmem(proj_weight.shape, bf16), vmem((1, docs), i32),
         vmem((small_slots, feature), bf16), vmem((docs, feature), bf16), vmem((8, docs), i32),
         dma((5,)), dma((3,))],
    )(pooled, proj_weight, cluster.reshape(1, docs))

    got_small = lax.all_to_all(
        small_sent.reshape(devices, cap_small, feature), ("docs", "blk"),
        split_axis=0, concat_axis=0, tiled=True).reshape(small_slots, feature)

    big_sent = call(
        functools.partial(sort_big_kernel, shards, blocks, cap_big),
        [((cap_big + rows_up(blocks, 16), feature), bf16, vmem)] * shards,
        [smem, vmem, vmem],
        2 * docs * feature * big_slots, 2 << 20,
    )(docs_at, rows, info)
    held = [big_sent[0]] + [along(big_sent[by], "docs", shards, by) for by in range(1, shards)]

    group, *tables = call(
        functools.partial(group_kernel, shards, blocks, cap_big),
        [((big_slots + rows_up(shards, 16), feature), bf16, vmem)]
        + [((rows_up(shards), LANES), f32, vmem)] * blocks,
        [smem] + [vmem] * shards,
        big_slots * feature, 1 << 20,
    )(blk_at, *held)

    parts = [group]
    for step in range(1, blocks):
        pairs = [(d * blocks + (home_of(d, blocks) + step) % blocks, d * blocks + home_of(d, blocks))
                 for d in range(shards)]
        parts.append(lax.ppermute(group, ("docs", "blk"), pairs))
    tables = [tables[0]] + [along(tables[by], "blk", blocks, by) for by in range(1, blocks)]

    back_big, = call(
        functools.partial(big_kernel, *sizes),
        [((blocks * rows_up(shards), LANES), f32, vmem)], [smem] + [vmem] * blocks,
        2 * big_total * big_total * feature, 2 << 20,
    )(docs_at, *parts)

    small_ids, = call(
        functools.partial(ids_kernel, shards, blocks, cap_small),
        [((1, small_slots), f32, vmem)], [smem, smem] + [vmem] * blocks,
        2 * rows_up(shards) * blocks * LANES * small_slots, 1 << 16,
    )(docs_at, blk_at, *tables)

    back = call(
        functools.partial(small_kernel, shards, blocks, cap_small),
        [((rows_up(shards), LANES), f32, vmem)] * blocks, [smem, vmem, vmem, vmem],
        2 * small_slots * small_slots * feature, 2 << 20,
    )(blk_at, got_small, small_ids, back_big)
    back = [back[0]] + [along(back[by], "blk", blocks, by) for by in range(1, blocks)]
    back = call(
        functools.partial(turn_kernel, shards),
        [((rows_up(blocks), LANES), f32, vmem)] * shards, [smem] + [vmem] * blocks,
        shards * blocks * LANES, 1 << 16,
    )(docs_at, *back)
    back = [back[0]] + [along(back[by], "docs", shards, by) for by in range(1, shards)]

    masks = call(
        functools.partial(masks_kernel, shards, blocks),
        [((3 * shards * rows_up(blocks), docs), bf16, vmem), ((LANES, docs), f32, vmem)], [smem, smem, vmem],
        docs * LANES, 1 << 18,
    )(docs_at, blk_at, info)
    out, = call(
        finish_kernel, [((1, docs), f32, vmem)], [vmem] * (shards + 2),
        6 * docs * LANES * devices, 1 << 18,
    )(*back, *masks)
    return out.reshape(docs)


def solution(mesh):
    in_specs = (P(("slab", "docs", "blk"), None), P(), P(("slab", "docs", "blk")))
    out_specs = P(("slab", "docs", "blk"))
    return jax.shard_map(body, mesh=mesh, in_specs=in_specs, out_specs=out_specs, check_vma=False)
```

time: 69.4 us -> 68.4 us (0.986)
  Pallas kernels: 14.2 us -> 9.86 us
  starting transfers between devices: 21.2 us -> 23.6 us
  waiting for transfers between devices: 32.8 us -> 34.5 us
    ppermute x6 -> x12, waiting for transfers between devices: 27.1 us -> 34.5 us  [along(): return lax.ppermute(x, axis, [(i, (i + by) % count) for i in range(count)])]
    ppermute x6 -> x12, starting transfers between devices: 5.95 us -> 13.3 us  [along(): return lax.ppermute(x, axis, [(i, (i + by) % count) for i in range(count)])]
    all_to_all x2 -> x1, waiting for transfers between devices: 5.77 us -> 0.01 us  [body(): lax.all_to_all(small_sent.reshape(devices, cap_small, feature), ('docs',...]
    all_to_all x2 -> x1, starting transfers between devices: 12.6 us -> 7.47 us  [body(): lax.all_to_all(small_sent.reshape(devices, cap_small, feature), ('docs',...]
    pallas_call x6 -> x7, Pallas kernels: 9.22 us -> 5.42 us  [the longest x1 2.19 us: body(): call(functools.partial(big_kernel, *sizes), [((blocks * rows_up(shards),...]
  transfers between devices with their start and end apart: 11 -> 16, of which waited for: 6 -> 10; matrix products, arithmetic and copies ran while one was open for 0% -> 0% of each run, Pallas kernels for 7% -> 5%
where the time goes in v7:
time: 68.4 us; the launch traced here: 68.1 us
  waiting for transfers between devices  34.5 us (50%)
  starting transfers between devices  23.6 us (35%)
  Pallas kernels  9.86 us (14%)
    ppermute x12, waiting for transfers between devices, along(): return lax.ppermute(x, axis, [(i, (i + by) % count) for i in range(count)])  34.5 us
    ppermute x12, starting transfers between devices, along(): return lax.ppermute(x, axis, [(i, (i + by) % count) for i in range(count)])  13.3 us
    all_to_all x1, starting transfers between devices, body(): lax.all_to_all(small_sent.reshape(devices, cap_small, feature), ('docs',...  7.47 us
    pallas_call x1, Pallas kernels, body(): call(functools.partial(sort_kernel, *sizes), [((small_slots, feature), bf...  4.39 us
    ppermute x3, starting transfers between devices, body(): parts.append(lax.ppermute(group, ('docs', 'blk'), pairs))  2.83 us
    pallas_call x1, Pallas kernels, body(): call(functools.partial(big_kernel, *sizes), [((blocks * rows_up(shards),...  2.19 us
    pallas_call x1, Pallas kernels, body(): call(functools.partial(small_kernel, shards, blocks, cap_small), [((rows_...  1.39 us
  transfers between devices with their start and end apart: 16, of which 10 were waited for; matrix products, arithmetic and copies ran while one was open for 0% of the time, Pallas kernels for 5%

profile of v7, /device:TPU:1, one launch (start us, length us, event | category | flops | bytes accessed | tf_op | source)
XLA Modules:
  0.0 68.1 jit_solution(3117551187466021532)
XLA Ops:
  0.0 4.4 %shard_map.37 = (bf16[768,768]{1,0:T(8,128)(2,1)}, bf16[512,768]{1,0:T(8,128)(2,1)}, s32[8,512]{1,0:T(8,128)}) custom-call(bf16[512,768]{1,0:T(8,128)(2,1)} %pooled_hbm.1, bf16[768,768]{1,0:T(8,128)(2,1)} %weight_hbm.1, s32[1,512]{1,0:T(1,128)} %bitcast.8), custom_call_target="tpu_custom_call" | custom-call | flops 1207959552 | bytes 4194304 | tf_op jit(solution)/shard_map/pallas_call | solution.py:296
  4.4 0.0 copy-start
  4.4 0.0 copy-start.1
  4.4 7.5 %all-to-all-start = ((bf16[16,48,768]{2,1,0:T(8,128)(2,1)}), bf16[16,48,768]{2,1,0:T(8,128)(2,1)S(1)}, u32[]{:S(2)}, u32[]{:S(2)}) async-start(bf16[16,48,768]{2,1,0:T(8,128)(2,1)} %bitcast.7), calls=%async_computation | async-start | bytes 2359296 | tf_op jit(solution)/shard_map/all_to_all | solution.py:306
  11.9 0.0 copy-done
  11.9 0.0 copy-done.1
  11.9 0.8 %shard_map.38 = (bf16[80,768]{1,0:T(8,128)(2,1)S(1)}, bf16[80,768]{1,0:T(8,128)(2,1)S(1)}, bf16[80,768]{1,0:T(8,128)(2,1)S(1)}, bf16[80,768]{1,0:T(8,128)(2,1)S(1)}) custom-call(s32[1]{0:T(128)} %bitcast.docs_at.at_ref, bf16[512,768]{1,0:T(8,128)(2,1)S(1)} %copy-done, s32[8,512]{1,0:T(8,128)S(1)} %copy-done.1), custom_call_target="tpu_custom_call" | custom-call | flops 201326592 | bytes 2097152 | tf_op jit(solution)/shard_map/pallas_call | solution.py:310
  12.7 1.7 %collective-permute-start = (bf16[80,768]{1,0:T(8,128)(2,1)S(1)}, bf16[80,768]{1,0:T(8,128)(2,1)S(1)}, u32[]{:S(2)}, u32[]{:S(2)}) collective-permute-start(bf16[80,768]{1,0:T(8,128)(2,1)S(1)} %get-tuple-element.31), channel_id=1, source_target_pairs={{0,4},{4,8},{8,12},{12,0},{1,5},{5,9},{9,13},{13,1},{2,6},{6,10},{... | collective-permute-start | bytes 368648 | tf_op jit(solution)/shard_map/ppermute | solution.py:294
  14.4 0.0 collective-permute-start.1
  14.4 0.5 collective-permute-start.2
  14.9 9.7 %collective-permute-done.refs_1_ = bf16[80,768]{1,0:T(8,128)(2,1)S(1)} collective-permute-done((bf16[80,768]{1,0:T(8,128)(2,1)S(1)}, bf16[80,768]{1,0:T(8,128)(2,1)S(1)}, u32[]{:S(2)}, u32[]{:S(2)}) %collective-permute-start) | collective-permute-done | bytes 122912 | tf_op jit(solution)/shard_map/ppermute | solution.py:294
  24.7 6.7 %collective-permute-done.1.refs_2_ = bf16[80,768]{1,0:T(8,128)(2,1)S(1)} collective-permute-done((bf16[80,768]{1,0:T(8,128)(2,1)S(1)}, bf16[80,768]{1,0:T(8,128)(2,1)S(1)}, u32[]{:S(2)}, u32[]{:S(2)}) %collective-permute-start.1) | collective-permute-done | bytes 122912 | tf_op jit(solution)/shard_map/ppermute | solution.py:294
  31.4 0.5 collective-permute-done.2.refs_3_
  31.8 0.1 shard_map.39
  31.9 0.7 %collective-permute-start.6 = (bf16[272,768]{1,0:T(8,128)(2,1)S(1)}, bf16[272,768]{1,0:T(8,128)(2,1)S(1)}, u32[]{:S(2)}, u32[]{:S(2)}) collective-permute-start(bf16[272,768]{1,0:T(8,128)(2,1)S(1)} %get-tuple-element.38.refs_0_), channel_id=1, source_target_pairs={{2,1},{7,6},{10,9},{15,14},{18,17},{23,22},{26,25},{31,30}} | collective-permute-start | bytes 1253384 | tf_op jit(solution)/shard_map/ppermute | solution.py:330
  32.6 1.5 %collective-permute-start.7 = (bf16[272,768]{1,0:T(8,128)(2,1)S(1)}, bf16[272,768]{1,0:T(8,128)(2,1)S(1)}, u32[]{:S(2)}, u32[]{:S(2)}) collective-permute-start(bf16[272,768]{1,0:T(8,128)(2,1)S(1)} %get-tuple-element.38.refs_0_), channel_id=1, source_target_pairs={{3,1},{4,6},{11,9},{12,14},{19,17},{20,22},{27,25},{28,30}} | collective-permute-start | bytes 1253384 | tf_op jit(solution)/shard_map/ppermute | solution.py:330
  34.1 0.7 %collective-permute-start.8 = (bf16[272,768]{1,0:T(8,128)(2,1)S(1)}, bf16[272,768]{1,0:T(8,128)(2,1)S(1)}, u32[]{:S(2)}, u32[]{:S(2)}) collective-permute-start(bf16[272,768]{1,0:T(8,128)(2,1)S(1)} %get-tuple-element.38.refs_0_), channel_id=1, source_target_pairs={{0,1},{5,6},{8,9},{13,14},{16,17},{21,22},{24,25},{29,30}} | collective-permute-start | bytes 1253384 | tf_op jit(solution)/shard_map/ppermute | solution.py:330
  34.7 0.9 %collective-permute-start.3 = (f32[8,128]{1,0:T(8,128)S(1)}, f32[8,128]{1,0:T(8,128)S(1)}, u32[]{:S(2)}, u32[]{:S(2)}) collective-permute-start(f32[8,128]{1,0:T(8,128)S(1)} %get-tuple-element.35), channel_id=1, source_target_pairs={{0,1},{1,2},{2,3},{3,0},{4,5},{5,6},{6,7},{7,4},{8,9},{9,10},{10,1... | collective-permute-start | bytes 12296 | tf_op jit(solution)/shard_map/ppermute | solution.py:294
  35.7 2.6 %collective-permute-start.4 = (f32[8,128]{1,0:T(8,128)S(1)}, f32[8,128]{1,0:T(8,128)S(1)}, u32[]{:S(2)}, u32[]{:S(2)}) collective-permute-start(f32[8,128]{1,0:T(8,128)S(1)} %get-tuple-element.36), channel_id=1, source_target_pairs={{0,2},{1,3},{2,0},{3,1},{4,6},{5,7},{6,4},{7,5},{8,10},{9,11},{10,... | collective-permute-start | bytes 12296 | tf_op jit(solution)/shard_map/ppermute | solution.py:294
  38.3 8.0 %collective-permute-done.3.refs_1_ = f32[8,128]{1,0:T(8,128)S(1)} collective-permute-done((f32[8,128]{1,0:T(8,128)S(1)}, f32[8,128]{1,0:T(8,128)S(1)}, u32[]{:S(2)}, u32[]{:S(2)}) %collective-permute-start.3) | collective-permute-done | bytes 4128 | tf_op jit(solution)/shard_map/ppermute | solution.py:294
  46.3 0.0 collective-permute-start.5
  46.3 0.0 collective-permute-done.4.refs_2_
  46.3 3.1 %collective-permute-done.5.refs_3_ = f32[8,128]{1,0:T(8,128)S(1)} collective-permute-done((f32[8,128]{1,0:T(8,128)S(1)}, f32[8,128]{1,0:T(8,128)S(1)}, u32[]{:S(2)}, u32[]{:S(2)}) %collective-permute-start.5) | collective-permute-done | bytes 4128 | tf_op jit(solution)/shard_map/ppermute | solution.py:294
  49.4 0.2 shard_map.40.row_ref
  49.6 0.0 collective-permute-done.6.refs_1_
  49.6 0.0 collective-permute-done.7.refs_2_
  49.6 0.0 collective-permute-done.8.refs_3_
  49.6 2.2 %shard_map.41.big_ref = f32[32,128]{1,0:T(8,128)S(1)} custom-call(s32[1]{0:T(128)} %bitcast.docs_at.at_ref, bf16[272,768]{1,0:T(8,128)(2,1)S(1)} %get-tuple-element.38.refs_0_, bf16[272,768]{1,0:T(8,128)(2,1)S(1)} %collective-permute-done.6.refs_1_, bf16[272,768]{1,0:T(8,128)(2,1)S(1)} %collective-permute-done.7.refs_2_, ...), custom_call_target="tpu_custom_call" | custom-call | flops 1610612736 | bytes 2097152 | tf_op jit(solution)/shard_map/pallas_call | solution.py:333
  51.8 0.0 all-to-all-done
  51.8 1.4 %shard_map.42 = (f32[8,128]{1,0:T(8,128)S(1)}, f32[8,128]{1,0:T(8,128)S(1)}, f32[8,128]{1,0:T(8,128)S(1)}, f32[8,128]{1,0:T(8,128)S(1)}) custom-call(s32[1]{0:T(128)} %bitcast.1.blk_at, bf16[768,768]{1,0:T(8,128)(2,1)S(1)} %bitcast.6, f32[1,768]{1,0:T(1,128)S(1)} %shard_map.40.row_ref, f32[32,128]{1,0:T(8,128)S(1)} %shard_map.41.big_ref), custom_call_target="tpu_custom_call" | custom-call | flops 905969664 | bytes 2097152 | tf_op jit(solution)/shard_map/pallas_call | solution.py:345
  53.2 3.1 %collective-permute-start.10 = (f32[8,128]{1,0:T(8,128)S(1)}, f32[8,128]{1,0:T(8,128)S(1)}, u32[]{:S(2)}, u32[]{:S(2)}) collective-permute-start(f32[8,128]{1,0:T(8,128)S(1)} %get-tuple-element.41), channel_id=1, source_target_pairs={{0,2},{1,3},{2,0},{3,1},{4,6},{5,7},{6,4},{7,5},{8,10},{9,11},{10,... | collective-permute-start | bytes 12296 | tf_op jit(solution)/shard_map/ppermute | solution.py:294
  56.3 0.9 %collective-permute-start.11 = (f32[8,128]{1,0:T(8,128)S(1)}, f32[8,128]{1,0:T(8,128)S(1)}, u32[]{:S(2)}, u32[]{:S(2)}) collective-permute-start(f32[8,128]{1,0:T(8,128)S(1)} %get-tuple-element.42), channel_id=1, source_target_pairs={{0,3},{1,0},{2,1},{3,2},{4,7},{5,4},{6,5},{7,6},{8,11},{9,8},{10,9... | collective-permute-start | bytes 12296 | tf_op jit(solution)/shard_map/ppermute | solution.py:294
  57.2 0.6 collective-permute-start.9
  57.8 0.0 collective-permute-done.10.refs_2_
  57.8 1.0 %collective-permute-done.11.refs_3_ = f32[8,128]{1,0:T(8,128)S(1)} collective-permute-done((f32[8,128]{1,0:T(8,128)S(1)}, f32[8,128]{1,0:T(8,128)S(1)}, u32[]{:S(2)}, u32[]{:S(2)}) %collective-permute-start.11) | collective-permute-done | bytes 4128 | tf_op jit(solution)/shard_map/ppermute | solution.py:294
  58.8 2.7 %collective-permute-done.9.refs_1_ = f32[8,128]{1,0:T(8,128)S(1)} collective-permute-done((f32[8,128]{1,0:T(8,128)S(1)}, f32[8,128]{1,0:T(8,128)S(1)}, u32[]{:S(2)}, u32[]{:S(2)}) %collective-permute-start.9) | collective-permute-done | bytes 4128 | tf_op jit(solution)/shard_map/ppermute | solution.py:294
  61.5 2.4 %collective-permute-start.12 = (f32[8,128]{1,0:T(8,128)S(1)}, f32[8,128]{1,0:T(8,128)S(1)}, u32[]{:S(2)}, u32[]{:S(2)}) collective-permute-start(f32[8,128]{1,0:T(8,128)S(1)} %get-tuple-element.44), channel_id=1, source_target_pairs={{0,4},{4,8},{8,12},{12,0},{1,5},{5,9},{9,13},{13,1},{2,6},{6,10},{... | collective-permute-start | bytes 12296 | tf_op jit(solution)/shard_map/ppermute | solution.py:294
  64.0 0.3 collective-permute-start.13
  64.3 0.2 collective-permute-start.14
  64.5 0.2 collective-permute-done.12.refs_1_
  64.7 1.7 %collective-permute-done.13.refs_2_ = f32[8,128]{1,0:T(8,128)S(1)} collective-permute-done((f32[8,128]{1,0:T(8,128)S(1)}, f32[8,128]{1,0:T(8,128)S(1)}, u32[]{:S(2)}, u32[]{:S(2)}) %collective-permute-start.13) | collective-permute-done | bytes 4128 | tf_op jit(solution)/shard_map/ppermute | solution.py:294
  66.4 0.8 %collective-permute-done.14.refs_3_ = f32[8,128]{1,0:T(8,128)S(1)} collective-permute-done((f32[8,128]{1,0:T(8,128)S(1)}, f32[8,128]{1,0:T(8,128)S(1)}, u32[]{:S(2)}, u32[]{:S(2)}) %collective-permute-start.14) | collective-permute-done | bytes 4128 | tf_op jit(solution)/shard_map/ppermute | solution.py:294
  67.3 0.8 %shard_map.45 = f32[1,512]{1,0:T(1,128)} custom-call(f32[8,128]{1,0:T(8,128)S(1)} %get-tuple-element.43.refs_0_, f32[8,128]{1,0:T(8,128)S(1)} %collective-permute-done.12.refs_1_, f32[8,128]{1,0:T(8,128)S(1)} %collective-permute-done.13.refs_2_, f32[8,128]{1,0:T(8,128)S(1)} %collective-permute-done.14.refs_3_, ...), custom_call_target="tpu_custom_call" | custom-call | flops 6291456 | bytes 262144 | tf_op jit(solution)/shard_map/pallas_call | solution.py:363
  (2 shorter events, 0.1 us)
Async XLA Ops:
  4.4 7.5 %copy-start = (bf16[512,768]{1,0:T(8,128)(2,1)S(1)}, bf16[512,768]{1,0:T(8,128)(2,1)}, u32[]{:S(2)}) copy-start(bf16[512,768]{1,0:T(8,128)(2,1)} %get-tuple-element.28.rows_ref) | copy-start | bytes 2359300
  4.4 7.5 %copy-start.1 = (s32[8,512]{1,0:T(8,128)S(1)}, s32[8,512]{1,0:T(8,128)}, u32[]{:S(2)}) copy-start(s32[8,512]{1,0:T(8,128)} %get-tuple-element.29.info_ref) | copy-start | bytes 49156
  4.4 47.4 %all-to-all-start = ((bf16[16,48,768]{2,1,0:T(8,128)(2,1)}), bf16[16,48,768]{2,1,0:T(8,128)(2,1)S(1)}, u32[]{:S(2)}, u32[]{:S(2)}) async-start(bf16[16,48,768]{2,1,0:T(8,128)(2,1)} %bitcast.7), calls=%async_computation | async-start | bytes 2359296 | tf_op jit(solution)/shard_map/all_to_all | solution.py:306
  12.7 12.0 %collective-permute-start = (bf16[80,768]{1,0:T(8,128)(2,1)S(1)}, bf16[80,768]{1,0:T(8,128)(2,1)S(1)}, u32[]{:S(2)}, u32[]{:S(2)}) collective-permute-start(bf16[80,768]{1,0:T(8,128)(2,1)S(1)} %get-tuple-element.31), channel_id=1, source_target_pairs={{0,4},{4,8},{8,12},{12,0},{1,5},{5,9},{9,13},{13,1},{2,6},{6,10},{... | collective-permute-start | bytes 368648 | tf_op jit(solution)/shard_map/ppermute | solution.py:294
  14.4 17.0 %collective-permute-start.1 = (bf16[80,768]{1,0:T(8,128)(2,1)S(1)}, bf16[80,768]{1,0:T(8,128)(2,1)S(1)}, u32[]{:S(2)}, u32[]{:S(2)}) collective-permute-start(bf16[80,768]{1,0:T(8,128)(2,1)S(1)} %get-tuple-element.32), channel_id=1, source_target_pairs={{0,8},{4,12},{8,0},{12,4},{1,9},{5,13},{9,1},{13,5},{2,10},{6,14},... | collective-permute-start | bytes 368648 | tf_op jit(solution)/shard_map/ppermute | solution.py:294
  14.4 17.4 %collective-permute-start.2 = (bf16[80,768]{1,0:T(8,128)(2,1)S(1)}, bf16[80,768]{1,0:T(8,128)(2,1)S(1)}, u32[]{:S(2)}, u32[]{:S(2)}) collective-permute-start(bf16[80,768]{1,0:T(8,128)(2,1)S(1)} %get-tuple-element.33), channel_id=1, source_target_pairs={{0,12},{4,0},{8,4},{12,8},{1,13},{5,1},{9,5},{13,9},{2,14},{6,2},{... | collective-permute-start | bytes 368648 | tf_op jit(solution)/shard_map/ppermute | solution.py:294
  31.9 17.7 %collective-permute-start.6 = (bf16[272,768]{1,0:T(8,128)(2,1)S(1)}, bf16[272,768]{1,0:T(8,128)(2,1)S(1)}, u32[]{:S(2)}, u32[]{:S(2)}) collective-permute-start(bf16[272,768]{1,0:T(8,128)(2,1)S(1)} %get-tuple-element.38.refs_0_), channel_id=1, source_target_pairs={{2,1},{7,6},{10,9},{15,14},{18,17},{23,22},{26,25},{31,30}} | collective-permute-start | bytes 1253384 | tf_op jit(solution)/shard_map/ppermute | solution.py:330
  32.6 17.0 %collective-permute-start.7 = (bf16[272,768]{1,0:T(8,128)(2,1)S(1)}, bf16[272,768]{1,0:T(8,128)(2,1)S(1)}, u32[]{:S(2)}, u32[]{:S(2)}) collective-permute-start(bf16[272,768]{1,0:T(8,128)(2,1)S(1)} %get-tuple-element.38.refs_0_), channel_id=1, source_target_pairs={{3,1},{4,6},{11,9},{12,14},{19,17},{20,22},{27,25},{28,30}} | collective-permute-start | bytes 1253384 | tf_op jit(solution)/shard_map/ppermute | solution.py:330
  34.1 15.6 %collective-permute-start.8 = (bf16[272,768]{1,0:T(8,128)(2,1)S(1)}, bf16[272,768]{1,0:T(8,128)(2,1)S(1)}, u32[]{:S(2)}, u32[]{:S(2)}) collective-permute-start(bf16[272,768]{1,0:T(8,128)(2,1)S(1)} %get-tuple-element.38.refs_0_), channel_id=1, source_target_pairs={{0,1},{5,6},{8,9},{13,14},{16,17},{21,22},{24,25},{29,30}} | collective-permute-start | bytes 1253384 | tf_op jit(solution)/shard_map/ppermute | solution.py:330
  34.7 11.6 %collective-permute-start.3 = (f32[8,128]{1,0:T(8,128)S(1)}, f32[8,128]{1,0:T(8,128)S(1)}, u32[]{:S(2)}, u32[]{:S(2)}) collective-permute-start(f32[8,128]{1,0:T(8,128)S(1)} %get-tuple-element.35), channel_id=1, source_target_pairs={{0,1},{1,2},{2,3},{3,0},{4,5},{5,6},{6,7},{7,4},{8,9},{9,10},{10,1... | collective-permute-start | bytes 12296 | tf_op jit(solution)/shard_map/ppermute | solution.py:294
  35.7 10.6 %collective-permute-start.4 = (f32[8,128]{1,0:T(8,128)S(1)}, f32[8,128]{1,0:T(8,128)S(1)}, u32[]{:S(2)}, u32[]{:S(2)}) collective-permute-start(f32[8,128]{1,0:T(8,128)S(1)} %get-tuple-element.36), channel_id=1, source_target_pairs={{0,2},{1,3},{2,0},{3,1},{4,6},{5,7},{6,4},{7,5},{8,10},{9,11},{10,... | collective-permute-start | bytes 12296 | tf_op jit(solution)/shard_map/ppermute | solution.py:294
  46.3 3.1 %collective-permute-start.5 = (f32[8,128]{1,0:T(8,128)S(1)}, f32[8,128]{1,0:T(8,128)S(1)}, u32[]{:S(2)}, u32[]{:S(2)}) collective-permute-start(f32[8,128]{1,0:T(8,128)S(1)} %get-tuple-element.37), channel_id=1, source_target_pairs={{0,3},{1,0},{2,1},{3,2},{4,7},{5,4},{6,5},{7,6},{8,11},{9,8},{10,9... | collective-permute-start | bytes 12296 | tf_op jit(solution)/shard_map/ppermute | solution.py:294
  53.2 4.6 %collective-permute-start.10 = (f32[8,128]{1,0:T(8,128)S(1)}, f32[8,128]{1,0:T(8,128)S(1)}, u32[]{:S(2)}, u32[]{:S(2)}) collective-permute-start(f32[8,128]{1,0:T(8,128)S(1)} %get-tuple-element.41), channel_id=1, source_target_pairs={{0,2},{1,3},{2,0},{3,1},{4,6},{5,7},{6,4},{7,5},{8,10},{9,11},{10,... | collective-permute-start | bytes 12296 | tf_op jit(solution)/shard_map/ppermute | solution.py:294
  56.3 2.5 %collective-permute-start.11 = (f32[8,128]{1,0:T(8,128)S(1)}, f32[8,128]{1,0:T(8,128)S(1)}, u32[]{:S(2)}, u32[]{:S(2)}) collective-permute-start(f32[8,128]{1,0:T(8,128)S(1)} %get-tuple-element.42), channel_id=1, source_target_pairs={{0,3},{1,0},{2,1},{3,2},{4,7},{5,4},{6,5},{7,6},{8,11},{9,8},{10,9... | collective-permute-start | bytes 12296 | tf_op jit(solution)/shard_map/ppermute | solution.py:294
  57.2 4.3 %collective-permute-start.9 = (f32[8,128]{1,0:T(8,128)S(1)}, f32[8,128]{1,0:T(8,128)S(1)}, u32[]{:S(2)}, u32[]{:S(2)}) collective-permute-start(f32[8,128]{1,0:T(8,128)S(1)} %get-tuple-element.40), channel_id=1, source_target_pairs={{0,1},{1,2},{2,3},{3,0},{4,5},{5,6},{6,7},{7,4},{8,9},{9,10},{10,1... | collective-permute-start | bytes 12296 | tf_op jit(solution)/shard_map/ppermute | solution.py:294
  61.5 3.2 %collective-permute-start.12 = (f32[8,128]{1,0:T(8,128)S(1)}, f32[8,128]{1,0:T(8,128)S(1)}, u32[]{:S(2)}, u32[]{:S(2)}) collective-permute-start(f32[8,128]{1,0:T(8,128)S(1)} %get-tuple-element.44), channel_id=1, source_target_pairs={{0,4},{4,8},{8,12},{12,0},{1,5},{5,9},{9,13},{13,1},{2,6},{6,10},{... | collective-permute-start | bytes 12296 | tf_op jit(solution)/shard_map/ppermute | solution.py:294
  64.0 2.5 %collective-permute-start.13 = (f32[8,128]{1,0:T(8,128)S(1)}, f32[8,128]{1,0:T(8,128)S(1)}, u32[]{:S(2)}, u32[]{:S(2)}) collective-permute-start(f32[8,128]{1,0:T(8,128)S(1)} %get-tuple-element.45), channel_id=1, source_target_pairs={{0,8},{4,12},{8,0},{12,4},{1,9},{5,13},{9,1},{13,5},{2,10},{6,14},... | collective-permute-start | bytes 12296 | tf_op jit(solution)/shard_map/ppermute | solution.py:294
  64.3 3.0 %collective-permute-start.14 = (f32[8,128]{1,0:T(8,128)S(1)}, f32[8,128]{1,0:T(8,128)S(1)}, u32[]{:S(2)}, u32[]{:S(2)}) collective-permute-start(f32[8,128]{1,0:T(8,128)S(1)} %get-tuple-element.46), channel_id=1, source_target_pairs={{0,12},{4,0},{8,4},{12,8},{1,13},{5,1},{9,5},{13,9},{2,14},{6,2},{... | collective-permute-start | bytes 12296 | tf_op jit(solution)/shard_map/ppermute | solution.py:294

commit v8 on v7

--- a/solution.py
+++ b/solution.py
@@ -99,35 +99,39 @@
         send.wait()
 
 
-def sort_big_kernel(shards, blocks, cap_big, docs_at, rows_ref, info_ref, *out_refs):
+def sort_big_kernel(shards, blocks, cap_big, docs_at, blk_at, rows_ref, info_ref, *refs):
+    big_refs, ids_refs = refs[:shards], refs[shards:]
     docs = rows_ref.shape[0]
     devices = shards * blocks
     quota, bucket = info_ref[3:4, :].astype(jnp.float32), info_ref[4:5, :]
     lanes = (iota((LANES, docs), 0) == info_ref[1:2, :]).astype(jnp.float32).astype(jnp.bfloat16)
-    for shift, ref in enumerate(out_refs):
+
+    def table(mine):
+        return dot_nt(jnp.where(mine, quota, 0.0).astype(jnp.bfloat16), lanes)
+
+    for step, ref in enumerate(ids_refs):
+        target = iota((2 * ref.shape[0], docs), 0) * blocks + modulo(blk_at[0] + step, blocks)
+        ref[...] = table((target == bucket) & (target < devices))[0:ref.shape[0], :]
+    for shift, ref in enumerate(big_refs):
         to = modulo(docs_at[0] + shift, shards)
         ref[0:cap_big, :] = picked_rows(rows_ref, info_ref[2:3, :], to * cap_big, cap_big)
-        table = ref.shape[0] - cap_big
-        blk = iota((table, docs), 0)
-        mine = (blk < blocks) & ((blk + to * blocks == bucket) | (bucket == devices + to))
-        values = jnp.where(mine, quota, 0.0).astype(jnp.bfloat16)
-        ref[cap_big:, 0:LANES] = dot_nt(values, lanes).astype(jnp.bfloat16)
-        ref[cap_big:, LANES:] = jnp.zeros((table, ref.shape[1] - LANES), jnp.bfloat16)
-
-
-def group_kernel(shards, blocks, cap_big, blk_at, *refs):
-    held, group_ref, ids_refs = refs[:shards], refs[shards], refs[shards + 1:]
-    tables = [ref[cap_big:, 0:LANES].astype(jnp.float32) for ref in held]
-    total = shards * cap_big
+        spare = ref.shape[0] - cap_big
+        ref[cap_big:, 0:LANES] = table(
+            (iota((spare, docs), 0) == 0) & (bucket == devices + to)).astype(jnp.bfloat16)
+        ref[cap_big:, LANES:] = jnp.zeros((spare, ref.shape[1] - LANES), jnp.bfloat16)
+
+
+def group_kernel(cap_big, *refs):
+    held, group_ref = refs[:-1], refs[-1]
+    total = len(held) * cap_big
+    spare = group_ref.shape[0] - total
+    own = jnp.zeros((spare, LANES), jnp.float32)
     for shift, ref in enumerate(held):
         group_ref[shift * cap_big:(shift + 1) * cap_big, :] = ref[0:cap_big, :]
-    spare = group_ref.shape[0] - total
-    own = jnp.zeros((spare, LANES), jnp.float32)
-    for shift, table in enumerate(tables):
+        table = ref[cap_big:, 0:LANES].astype(jnp.float32)
         own = jnp.where(iota(own.shape, 0) == shift, table[0:1, :], own)
     group_ref[total:, 0:LANES] = own.astype(jnp.bfloat16)
     group_ref[total:, LANES:] = jnp.zeros((spare, group_ref.shape[1] - LANES), jnp.bfloat16)
-    turn(tables, blk_at[0], blocks, ids_refs)
 
 
 def turn(tables, at, count, outs):
@@ -172,7 +176,7 @@
     values = jnp.concatenate([table[...] for table in tables], axis=0)
     values = jnp.concatenate([values, jnp.zeros_like(values)], axis=0).astype(jnp.bfloat16)
     docs, blk, lane = small_sources(ids_ref.shape[1], blocks, cap_small)
-    row = modulo(blk_at[0] + blocks - blk, blocks) * high + modulo(docs_at[0] + shards - docs, shards)
+    row = modulo(docs_at[0] + shards - docs, shards) * high + modulo(blk_at[0] + blocks - blk, blocks)
     ids_ref[...] = ids_from(values, row, lane)
 
 
@@ -204,11 +208,11 @@
     return jnp.concatenate([high, middle, low], axis=0)
 
 
-def big_kernel(shards, blocks, cap_big, cap_small, docs_at, *refs):
-    held, back_ref = refs[:-1], refs[-1]
+def big_kernel(shards, blocks, cap_big, cap_small, docs_at, small_ref, *refs):
+    held, back_refs = refs[:blocks], refs[blocks:]
     size = shards * cap_big
     spare = held[0].shape[0] - size
-    high = back_ref.shape[0] // blocks
+    high = back_refs[0].shape[0]
     step, shift, lane = big_sources(blocks * size, shards, cap_big, cap_small)
     values = jnp.concatenate([ref[size:, 0:LANES] for ref in held], axis=0)
     row_ids = ids_from(values, step * spare + shift, lane)
@@ -221,12 +225,14 @@
                 queries[0:size, :], col_ids[row * size:(row + 1) * size], same,
                 others[0:size, :], row_ids[:, col * size:(col + 1) * size], same))
     docs = modulo(docs_at[0] + shards - shift, shards)
-    back_ref[...] = spread(jnp.concatenate(bests, axis=1), step * high + docs, lane, back_ref.shape[0])
-
-
-def small_kernel(shards, blocks, cap_small, blk_at, rows_ref, row_ref, big_ref, *back_refs):
+    back = small_ref[...] + spread(jnp.concatenate(bests, axis=1), step * high + docs, lane, small_ref.shape[0])
+    for step, ref in enumerate(back_refs):
+        ref[...] = back[step * high:(step + 1) * high, :]
+
+
+def small_kernel(shards, blocks, cap_small, blk_at, rows_ref, row_ref, back_ref):
     total = rows_ref.shape[0]
-    high = back_refs[0].shape[0]
+    high = back_ref.shape[0] // blocks
     col_ids = as_column(row_ref[...])
     tile = tile_of(total)
     best = jnp.full((1, total), -1.0, jnp.float32)
@@ -235,9 +241,7 @@
             rows_ref[at:at + tile, :], col_ids[at:at + tile], at, rows_ref[...], row_ref[...], 0))
     docs, blk, lane = small_sources(total, blocks, cap_small)
     row = modulo(blk + blocks - blk_at[0], blocks) * high + docs
-    back = big_ref[...] + spread(best, row, lane, big_ref.shape[0])
-    for step, ref in enumerate(back_refs):
-        ref[...] = back[step * high:(step + 1) * high, :]
+    back_ref[...] = spread(best, row, lane, back_ref.shape[0])
 
 
 def masks_kernel(shards, blocks, docs_at, blk_at, info_ref, row_ref, lane_ref):
@@ -309,51 +313,52 @@
 
     big_sent = call(
         functools.partial(sort_big_kernel, shards, blocks, cap_big),
-        [((cap_big + rows_up(blocks, 16), feature), bf16, vmem)] * shards,
-        [smem, vmem, vmem],
+        [((cap_big + 16, feature), bf16, vmem)] * shards + [((rows_up(shards), LANES), f32, vmem)] * blocks,
+        [smem, smem, vmem, vmem],
         2 * docs * feature * big_slots, 2 << 20,
-    )(docs_at, rows, info)
+    )(docs_at, blk_at, rows, info)
+    big_sent, tables = big_sent[:shards], big_sent[shards:]
+    tables = [tables[0]] + [along(tables[by], "blk", blocks, by) for by in range(1, blocks)]
     held = [big_sent[0]] + [along(big_sent[by], "docs", shards, by) for by in range(1, shards)]
 
-    group, *tables = call(
-        functools.partial(group_kernel, shards, blocks, cap_big),
-        [((big_slots + rows_up(shards, 16), feature), bf16, vmem)]
-        + [((rows_up(shards), LANES), f32, vmem)] * blocks,
-        [smem] + [vmem] * shards,
+    group, = call(
+        functools.partial(group_kernel, cap_big),
+        [((big_slots + rows_up(shards, 16), feature), bf16, vmem)], [vmem] * shards,
         big_slots * feature, 1 << 20,
-    )(blk_at, *held)
-
+    )(*held)
     parts = [group]
     for step in range(1, blocks):
         pairs = [(d * blocks + (home_of(d, blocks) + step) % blocks, d * blocks + home_of(d, blocks))
                  for d in range(shards)]
         parts.append(lax.ppermute(group, ("docs", "blk"), pairs))
-    tables = [tables[0]] + [along(tables[by], "blk", blocks, by) for by in range(1, blocks)]
-
-    back_big, = call(
-        functools.partial(big_kernel, *sizes),
-        [((blocks * rows_up(shards), LANES), f32, vmem)], [smem] + [vmem] * blocks,
-        2 * big_total * big_total * feature, 2 << 20,
-    )(docs_at, *parts)
-
+
+    def turned(tables):
+        tables = call(
+            functools.partial(turn_kernel, shards),
+            [((rows_up(blocks), LANES), f32, vmem)] * shards, [smem] + [vmem] * blocks,
+            shards * blocks * LANES, 1 << 16,
+        )(docs_at, *tables)
+        return [tables[0]] + [along(tables[by], "docs", shards, by) for by in range(1, shards)]
+
+    tables = turned(tables)
     small_ids, = call(
         functools.partial(ids_kernel, shards, blocks, cap_small),
-        [((1, small_slots), f32, vmem)], [smem, smem] + [vmem] * blocks,
-        2 * rows_up(shards) * blocks * LANES * small_slots, 1 << 16,
+        [((1, small_slots), f32, vmem)], [smem, smem] + [vmem] * shards,
+        2 * rows_up(blocks) * shards * LANES * small_slots, 1 << 16,
     )(docs_at, blk_at, *tables)
 
+    back_small, = call(
+        functools.partial(small_kernel, shards, blocks, cap_small),
+        [((blocks * rows_up(shards), LANES), f32, vmem)], [smem, vmem, vmem],
+        2 * small_slots * small_slots * feature, 2 << 20,
+    )(blk_at, got_small, small_ids)
     back = call(
-        functools.partial(small_kernel, shards, blocks, cap_small),
-        [((rows_up(shards), LANES), f32, vmem)] * blocks, [smem, vmem, vmem, vmem],
-        2 * small_slots * small_slots * feature, 2 << 20,
-    )(blk_at, got_small, small_ids, back_big)
+        functools.partial(big_kernel, *sizes),
+        [((rows_up(shards), LANES), f32, vmem)] * blocks, [smem, vmem] + [vmem] * blocks,
+        2 * big_total * big_total * feature, 2 << 20,
+    )(docs_at, back_small, *parts)
     back = [back[0]] + [along(back[by], "blk", blocks, by) for by in range(1, blocks)]
-    back = call(
-        functools.partial(turn_kernel, shards),
-        [((rows_up(blocks), LANES), f32, vmem)] * shards, [smem] + [vmem] * blocks,
-        shards * blocks * LANES, 1 << 16,
-    )(docs_at, *back)
-    back = [back[0]] + [along(back[by], "docs", shards, by) for by in range(1, shards)]
+    back = turned(back)
 
     masks = call(
         functools.partial(masks_kernel, shards, blocks),

time: 68.4 us -> 71 us (1.038)
  starting transfers between devices: 23.6 us -> 25.7 us
    ppermute x12 -> x15, starting transfers between devices: 13.3 us -> 15.4 us  [along(): return lax.ppermute(x, axis, [(i, (i + by) % count) for i in range(count)])]
    ppermute x12 -> x15, waiting for transfers between devices: 34.5 us -> 34.8 us  [along(): return lax.ppermute(x, axis, [(i, (i + by) % count) for i in range(count)])]
    pallas_call x4 -> x5, Pallas kernels: 3.65 us -> 3.69 us  [the longest x1 2.25 us: body(): call(functools.partial(big_kernel, *sizes), [((rows_up(shards), LANES), f...]
  transfers between devices with their start and end apart: 16 -> 19, of which waited for: 10 -> 13; matrix products, arithmetic and copies ran while one was open for 0% -> 0% of each run, Pallas kernels for 5% -> 4%
where the time goes in v8:
time: 71 us; the launch traced here: 70.7 us
  waiting for transfers between devices  34.8 us (49%)
  starting transfers between devices  25.7 us (36%)
  Pallas kernels  10 us (14%)
    ppermute x15, waiting for transfers between devices, along(): return lax.ppermute(x, axis, [(i, (i + by) % count) for i in range(count)])  34.8 us
    ppermute x15, starting transfers between devices, along(): return lax.ppermute(x, axis, [(i, (i + by) % count) for i in range(count)])  15.4 us
    all_to_all x1, starting transfers between devices, body(): lax.all_to_all(small_sent.reshape(devices, cap_small, feature), ('docs',...  7.47 us
    pallas_call x1, Pallas kernels, body(): call(functools.partial(sort_kernel, *sizes), [((small_slots, feature), bf...  4.39 us
    ppermute x3, starting transfers between devices, body(): parts.append(lax.ppermute(group, ('docs', 'blk'), pairs))  2.83 us
    pallas_call x1, Pallas kernels, body(): call(functools.partial(big_kernel, *sizes), [((rows_up(shards), LANES), f...  2.25 us
  transfers between devices with their start and end apart: 19, of which 13 were waited for; matrix products, arithmetic and copies ran while one was open for 0% of the time, Pallas kernels for 4%

profile of v8, /device:TPU:1, one launch (start us, length us, event | category | flops | bytes accessed | tf_op | source)
XLA Modules:
  0.0 70.7 jit_solution(10527435366178456592)
XLA Ops:
  0.0 4.4 %shard_map.37 = (bf16[768,768]{1,0:T(8,128)(2,1)}, bf16[512,768]{1,0:T(8,128)(2,1)}, s32[8,512]{1,0:T(8,128)}) custom-call(bf16[512,768]{1,0:T(8,128)(2,1)} %pooled_hbm.1, bf16[768,768]{1,0:T(8,128)(2,1)} %weight_hbm.1, s32[1,512]{1,0:T(1,128)} %bitcast.8), custom_call_target="tpu_custom_call" | custom-call | flops 1207959552 | bytes 4194304 | tf_op jit(solution)/shard_map/pallas_call | solution.py:300
  4.4 0.0 copy-start
  4.4 0.0 copy-start.1
  4.4 7.5 %all-to-all-start = ((bf16[16,48,768]{2,1,0:T(8,128)(2,1)}), bf16[16,48,768]{2,1,0:T(8,128)(2,1)S(1)}, u32[]{:S(2)}, u32[]{:S(2)}) async-start(bf16[16,48,768]{2,1,0:T(8,128)(2,1)} %bitcast.7), calls=%async_computation | async-start | bytes 2359296 | tf_op jit(solution)/shard_map/all_to_all | solution.py:310
  11.9 0.0 copy-done
  11.9 0.0 copy-done.1
  11.9 0.9 %shard_map.38 = (bf16[80,768]{1,0:T(8,128)(2,1)S(1)}, bf16[80,768]{1,0:T(8,128)(2,1)S(1)}, bf16[80,768]{1,0:T(8,128)(2,1)S(1)}, bf16[80,768]{1,0:T(8,128)(2,1)S(...) custom-call(s32[1]{0:T(128)} %bitcast.docs_at.at_ref, ...), custom_call_target="tpu_custom_call" | custom-call | flops 201326592 | bytes 2097152 | tf_op jit(solution)/shard_map/pallas_call | solution.py:314
  12.8 1.7 %collective-permute-start.6 = (bf16[80,768]{1,0:T(8,128)(2,1)S(1)}, bf16[80,768]{1,0:T(8,128)(2,1)S(1)}, u32[]{:S(2)}, u32[]{:S(2)}) collective-permute-start(bf16[80,768]{1,0:T(8,128)(2,1)S(1)} %get-tuple-element.42), channel_id=1, source_target_pairs={{0,4},{4,8},{8,12},{12,0},{1,5},{5,9},{9,13},{13,1},{2,6},{6,10},{... | collective-permute-start | bytes 368648 | tf_op jit(solution)/shard_map/ppermute | solution.py:298
  14.5 0.0 collective-permute-start.7
  14.5 0.5 collective-permute-start.8
  15.1 9.6 %collective-permute-done.6.refs_1_ = bf16[80,768]{1,0:T(8,128)(2,1)S(1)} collective-permute-done((bf16[80,768]{1,0:T(8,128)(2,1)S(1)}, bf16[80,768]{1,0:T(8,128)(2,1)S(1)}, u32[]{:S(2)}, u32[]{:S(2)}) %collective-permute-start.6) | collective-permute-done | bytes 122912 | tf_op jit(solution)/shard_map/ppermute | solution.py:298
  24.7 6.7 %collective-permute-done.7.refs_2_ = bf16[80,768]{1,0:T(8,128)(2,1)S(1)} collective-permute-done((bf16[80,768]{1,0:T(8,128)(2,1)S(1)}, bf16[80,768]{1,0:T(8,128)(2,1)S(1)}, u32[]{:S(2)}, u32[]{:S(2)}) %collective-permute-start.7) | collective-permute-done | bytes 122912 | tf_op jit(solution)/shard_map/ppermute | solution.py:298
  31.4 0.5 collective-permute-done.8.refs_3_
  31.9 0.7 collective-permute-start.11
  32.6 1.5 %collective-permute-start.10 = (bf16[272,768]{1,0:T(8,128)(2,1)S(1)}, bf16[272,768]{1,0:T(8,128)(2,1)S(1)}, u32[]{:S(2)}, u32[]{:S(2)}) collective-permute-start(bf16[272,768]{1,0:T(8,128)(2,1)S(1)} %shard_map.42.refs_0_), channel_id=1, source_target_pairs={{3,1},{4,6},{11,9},{12,14},{19,17},{20,22},{27,25},{28,30}} | collective-permute-start | bytes 1253384 | tf_op jit(solution)/shard_map/ppermute | solution.py:333
  34.0 0.7 collective-permute-start.9
  34.7 0.1 collective-permute-start
  34.8 3.5 %collective-permute-start.1 = (f32[8,128]{1,0:T(8,128)S(1)}, f32[8,128]{1,0:T(8,128)S(1)}, u32[]{:S(2)}, u32[]{:S(2)}) collective-permute-start(f32[8,128]{1,0:T(8,128)S(1)} %get-tuple-element.35), channel_id=1, source_target_pairs={{0,2},{1,3},{2,0},{3,1},{4,6},{5,7},{6,4},{7,5},{8,10},{9,11},{10,... | collective-permute-start | bytes 12296 | tf_op jit(solution)/shard_map/ppermute | solution.py:298
  38.3 8.1 %collective-permute-done.refs_1_ = f32[8,128]{1,0:T(8,128)S(1)} collective-permute-done((f32[8,128]{1,0:T(8,128)S(1)}, f32[8,128]{1,0:T(8,128)S(1)}, u32[]{:S(2)}, u32[]{:S(2)}) %collective-permute-start) | collective-permute-done | bytes 4128 | tf_op jit(solution)/shard_map/ppermute | solution.py:298
  46.4 0.0 collective-permute-start.2
  46.4 0.0 collective-permute-done.1.refs_2_
  46.4 3.0 %collective-permute-done.2.refs_3_ = f32[8,128]{1,0:T(8,128)S(1)} collective-permute-done((f32[8,128]{1,0:T(8,128)S(1)}, f32[8,128]{1,0:T(8,128)S(1)}, u32[]{:S(2)}, u32[]{:S(2)}) %collective-permute-start.2) | collective-permute-done | bytes 4128 | tf_op jit(solution)/shard_map/ppermute | solution.py:298
  49.4 2.3 %collective-permute-start.3 = (f32[8,128]{1,0:T(8,128)S(1)}, f32[8,128]{1,0:T(8,128)S(1)}, u32[]{:S(2)}, u32[]{:S(2)}) collective-permute-start(f32[8,128]{1,0:T(8,128)S(1)} %get-tuple-element.38), channel_id=1, source_target_pairs={{0,4},{4,8},{8,12},{12,0},{1,5},{5,9},{9,13},{13,1},{2,6},{6,10},{... | collective-permute-start | bytes 12296 | tf_op jit(solution)/shard_map/ppermute | solution.py:298
  51.7 0.3 collective-permute-start.4
  52.0 0.5 collective-permute-done.3.refs_1_
  52.5 1.2 %collective-permute-start.5 = (f32[8,128]{1,0:T(8,128)S(1)}, f32[8,128]{1,0:T(8,128)S(1)}, u32[]{:S(2)}, u32[]{:S(2)}) collective-permute-start(f32[8,128]{1,0:T(8,128)S(1)} %get-tuple-element.40), channel_id=1, source_target_pairs={{0,12},{4,0},{8,4},{12,8},{1,13},{5,1},{9,5},{13,9},{2,14},{6,2},{... | collective-permute-start | bytes 12296 | tf_op jit(solution)/shard_map/ppermute | solution.py:298
  53.7 0.5 collective-permute-done.4.refs_2_
  54.2 1.9 %collective-permute-done.5.refs_3_ = f32[8,128]{1,0:T(8,128)S(1)} collective-permute-done((f32[8,128]{1,0:T(8,128)S(1)}, f32[8,128]{1,0:T(8,128)S(1)}, u32[]{:S(2)}, u32[]{:S(2)}) %collective-permute-start.5) | collective-permute-done | bytes 4128 | tf_op jit(solution)/shard_map/ppermute | solution.py:298
  56.0 0.2 shard_map.40.row_ref
  56.2 0.0 all-to-all-done
  56.2 1.4 %shard_map.41.small_ref = f32[32,128]{1,0:T(8,128)S(1)} custom-call(s32[1]{0:T(128)} %bitcast.1.blk_at, bf16[768,768]{1,0:T(8,128)(2,1)S(1)} %bitcast.6, f32[1,768]{1,0:T(1,128)S(1)} %shard_map.40.row_ref), custom_call_target="tpu_custom_call" | custom-call | flops 905969664 | bytes 2097152 | tf_op jit(solution)/shard_map/pallas_call | solution.py:350
  57.6 0.0 collective-permute-done.11.refs_3_
  57.6 0.0 collective-permute-done.10.refs_2_
  57.6 0.0 collective-permute-done.9.refs_1_
  57.6 2.2 %shard_map.43 = (f32[8,128]{1,0:T(8,128)S(1)}, f32[8,128]{1,0:T(8,128)S(1)}, f32[8,128]{1,0:T(8,128)S(1)}, f32[8,128]{1,0:T(8,128)S(1)}) custom-call(s32[1]{0:T(128)} %bitcast.docs_at.at_ref, f32[32,128]{1,0:T(8,128)S(1)} %shard_map.41.small_ref, bf16[272,768]{1,0:T(8,128)(2,1)S(1)} %shard_map.42.refs_0_, ...), custom_call_target="tpu_custom_call" | custom-call | flops 1610612736 | bytes 2097152 | tf_op jit(solution)/shard_map/pallas_call | solution.py:355
  59.9 0.4 collective-permute-start.12
  60.3 0.8 %collective-permute-start.13 = (f32[8,128]{1,0:T(8,128)S(1)}, f32[8,128]{1,0:T(8,128)S(1)}, u32[]{:S(2)}, u32[]{:S(2)}) collective-permute-start(f32[8,128]{1,0:T(8,128)S(1)} %get-tuple-element.47), channel_id=1, source_target_pairs={{0,2},{1,3},{2,0},{3,1},{4,6},{5,7},{6,4},{7,5},{8,10},{9,11},{10,... | collective-permute-start | bytes 12296 | tf_op jit(solution)/shard_map/ppermute | solution.py:298
  61.1 2.3 %collective-permute-start.14 = (f32[8,128]{1,0:T(8,128)S(1)}, f32[8,128]{1,0:T(8,128)S(1)}, u32[]{:S(2)}, u32[]{:S(2)}) collective-permute-start(f32[8,128]{1,0:T(8,128)S(1)} %get-tuple-element.48), channel_id=1, source_target_pairs={{0,3},{1,0},{2,1},{3,2},{4,7},{5,4},{6,5},{7,6},{8,11},{9,8},{10,9... | collective-permute-start | bytes 12296 | tf_op jit(solution)/shard_map/ppermute | solution.py:298
  63.4 0.8 %collective-permute-done.12.refs_1_ = f32[8,128]{1,0:T(8,128)S(1)} collective-permute-done((f32[8,128]{1,0:T(8,128)S(1)}, f32[8,128]{1,0:T(8,128)S(1)}, u32[]{:S(2)}, u32[]{:S(2)}) %collective-permute-start.12) | collective-permute-done | bytes 4128 | tf_op jit(solution)/shard_map/ppermute | solution.py:298
  64.2 0.0 collective-permute-done.13.refs_2_
  64.2 0.3 collective-permute-done.14.refs_3_
  64.6 1.9 %collective-permute-start.15 = (f32[8,128]{1,0:T(8,128)S(1)}, f32[8,128]{1,0:T(8,128)S(1)}, u32[]{:S(2)}, u32[]{:S(2)}) collective-permute-start(f32[8,128]{1,0:T(8,128)S(1)} %get-tuple-element.50), channel_id=1, source_target_pairs={{0,4},{4,8},{8,12},{12,0},{1,5},{5,9},{9,13},{13,1},{2,6},{6,10},{... | collective-permute-start | bytes 12296 | tf_op jit(solution)/shard_map/ppermute | solution.py:298
  66.5 0.4 collective-permute-start.16
  66.9 0.1 collective-permute-start.17
  67.0 0.2 collective-permute-done.15.refs_1_
  67.2 1.7 %collective-permute-done.16.refs_2_ = f32[8,128]{1,0:T(8,128)S(1)} collective-permute-done((f32[8,128]{1,0:T(8,128)S(1)}, f32[8,128]{1,0:T(8,128)S(1)}, u32[]{:S(2)}, u32[]{:S(2)}) %collective-permute-start.16) | collective-permute-done | bytes 4128 | tf_op jit(solution)/shard_map/ppermute | solution.py:298
  68.9 0.9 %collective-permute-done.17.refs_3_ = f32[8,128]{1,0:T(8,128)S(1)} collective-permute-done((f32[8,128]{1,0:T(8,128)S(1)}, f32[8,128]{1,0:T(8,128)S(1)}, u32[]{:S(2)}, u32[]{:S(2)}) %collective-permute-start.17) | collective-permute-done | bytes 4128 | tf_op jit(solution)/shard_map/ppermute | solution.py:298
  69.9 0.8 %shard_map.46 = f32[1,512]{1,0:T(1,128)} custom-call(f32[8,128]{1,0:T(8,128)S(1)} %get-tuple-element.49.refs_0_, f32[8,128]{1,0:T(8,128)S(1)} %collective-permute-done.15.refs_1_, f32[8,128]{1,0:T(8,128)S(1)} %collective-permute-done.16.refs_2_, f32[8,128]{1,0:T(8,128)S(1)} %collective-permute-done.17.refs_3_, ...), custom_call_target="tpu_custom_call" | custom-call | flops 6291456 | bytes 262144 | tf_op jit(solution)/shard_map/pallas_call | solution.py:368
  (4 shorter events, 0.1 us)
Async XLA Ops:
  4.4 7.5 %copy-start = (bf16[512,768]{1,0:T(8,128)(2,1)S(1)}, bf16[512,768]{1,0:T(8,128)(2,1)}, u32[]{:S(2)}) copy-start(bf16[512,768]{1,0:T(8,128)(2,1)} %get-tuple-element.31.rows_ref) | copy-start | bytes 2359300
  4.4 7.5 %copy-start.1 = (s32[8,512]{1,0:T(8,128)S(1)}, s32[8,512]{1,0:T(8,128)}, u32[]{:S(2)}) copy-start(s32[8,512]{1,0:T(8,128)} %get-tuple-element.32.info_ref) | copy-start | bytes 49156
  4.4 51.8 %all-to-all-start = ((bf16[16,48,768]{2,1,0:T(8,128)(2,1)}), bf16[16,48,768]{2,1,0:T(8,128)(2,1)S(1)}, u32[]{:S(2)}, u32[]{:S(2)}) async-start(bf16[16,48,768]{2,1,0:T(8,128)(2,1)} %bitcast.7), calls=%async_computation | async-start | bytes 2359296 | tf_op jit(solution)/shard_map/all_to_all | solution.py:310
  12.8 11.8 %collective-permute-start.6 = (bf16[80,768]{1,0:T(8,128)(2,1)S(1)}, bf16[80,768]{1,0:T(8,128)(2,1)S(1)}, u32[]{:S(2)}, u32[]{:S(2)}) collective-permute-start(bf16[80,768]{1,0:T(8,128)(2,1)S(1)} %get-tuple-element.42), channel_id=1, source_target_pairs={{0,4},{4,8},{8,12},{12,0},{1,5},{5,9},{9,13},{13,1},{2,6},{6,10},{... | collective-permute-start | bytes 368648 | tf_op jit(solution)/shard_map/ppermute | solution.py:298
  14.5 16.8 %collective-permute-start.7 = (bf16[80,768]{1,0:T(8,128)(2,1)S(1)}, bf16[80,768]{1,0:T(8,128)(2,1)S(1)}, u32[]{:S(2)}, u32[]{:S(2)}) collective-permute-start(bf16[80,768]{1,0:T(8,128)(2,1)S(1)} %get-tuple-element.43), channel_id=1, source_target_pairs={{0,8},{4,12},{8,0},{12,4},{1,9},{5,13},{9,1},{13,5},{2,10},{6,14},... | collective-permute-start | bytes 368648 | tf_op jit(solution)/shard_map/ppermute | solution.py:298
  14.5 17.3 %collective-permute-start.8 = (bf16[80,768]{1,0:T(8,128)(2,1)S(1)}, bf16[80,768]{1,0:T(8,128)(2,1)S(1)}, u32[]{:S(2)}, u32[]{:S(2)}) collective-permute-start(bf16[80,768]{1,0:T(8,128)(2,1)S(1)} %get-tuple-element.44), channel_id=1, source_target_pairs={{0,12},{4,0},{8,4},{12,8},{1,13},{5,1},{9,5},{13,9},{2,14},{6,2},{... | collective-permute-start | bytes 368648 | tf_op jit(solution)/shard_map/ppermute | solution.py:298
  31.9 25.7 %collective-permute-start.11 = (bf16[272,768]{1,0:T(8,128)(2,1)S(1)}, bf16[272,768]{1,0:T(8,128)(2,1)S(1)}, u32[]{:S(2)}, u32[]{:S(2)}) collective-permute-start(bf16[272,768]{1,0:T(8,128)(2,1)S(1)} %shard_map.42.refs_0_), channel_id=1, source_target_pairs={{0,1},{5,6},{8,9},{13,14},{16,17},{21,22},{24,25},{29,30}} | collective-permute-start | bytes 1253384 | tf_op jit(solution)/shard_map/ppermute | solution.py:333
  32.6 25.0 %collective-permute-start.10 = (bf16[272,768]{1,0:T(8,128)(2,1)S(1)}, bf16[272,768]{1,0:T(8,128)(2,1)S(1)}, u32[]{:S(2)}, u32[]{:S(2)}) collective-permute-start(bf16[272,768]{1,0:T(8,128)(2,1)S(1)} %shard_map.42.refs_0_), channel_id=1, source_target_pairs={{3,1},{4,6},{11,9},{12,14},{19,17},{20,22},{27,25},{28,30}} | collective-permute-start | bytes 1253384 | tf_op jit(solution)/shard_map/ppermute | solution.py:333
  34.0 23.6 %collective-permute-start.9 = (bf16[272,768]{1,0:T(8,128)(2,1)S(1)}, bf16[272,768]{1,0:T(8,128)(2,1)S(1)}, u32[]{:S(2)}, u32[]{:S(2)}) collective-permute-start(bf16[272,768]{1,0:T(8,128)(2,1)S(1)} %shard_map.42.refs_0_), channel_id=1, source_target_pairs={{2,1},{7,6},{10,9},{15,14},{18,17},{23,22},{26,25},{31,30}} | collective-permute-start | bytes 1253384 | tf_op jit(solution)/shard_map/ppermute | solution.py:333
  34.7 11.7 %collective-permute-start = (f32[8,128]{1,0:T(8,128)S(1)}, f32[8,128]{1,0:T(8,128)S(1)}, u32[]{:S(2)}, u32[]{:S(2)}) collective-permute-start(f32[8,128]{1,0:T(8,128)S(1)} %get-tuple-element.34), channel_id=1, source_target_pairs={{0,1},{1,2},{2,3},{3,0},{4,5},{5,6},{6,7},{7,4},{8,9},{9,10},{10,1... | collective-permute-start | bytes 12296 | tf_op jit(solution)/shard_map/ppermute | solution.py:298
  34.8 11.6 %collective-permute-start.1 = (f32[8,128]{1,0:T(8,128)S(1)}, f32[8,128]{1,0:T(8,128)S(1)}, u32[]{:S(2)}, u32[]{:S(2)}) collective-permute-start(f32[8,128]{1,0:T(8,128)S(1)} %get-tuple-element.35), channel_id=1, source_target_pairs={{0,2},{1,3},{2,0},{3,1},{4,6},{5,7},{6,4},{7,5},{8,10},{9,11},{10,... | collective-permute-start | bytes 12296 | tf_op jit(solution)/shard_map/ppermute | solution.py:298
  46.4 3.0 %collective-permute-start.2 = (f32[8,128]{1,0:T(8,128)S(1)}, f32[8,128]{1,0:T(8,128)S(1)}, u32[]{:S(2)}, u32[]{:S(2)}) collective-permute-start(f32[8,128]{1,0:T(8,128)S(1)} %get-tuple-element.36), channel_id=1, source_target_pairs={{0,3},{1,0},{2,1},{3,2},{4,7},{5,4},{6,5},{7,6},{8,11},{9,8},{10,9... | collective-permute-start | bytes 12296 | tf_op jit(solution)/shard_map/ppermute | solution.py:298
  49.4 3.0 %collective-permute-start.3 = (f32[8,128]{1,0:T(8,128)S(1)}, f32[8,128]{1,0:T(8,128)S(1)}, u32[]{:S(2)}, u32[]{:S(2)}) collective-permute-start(f32[8,128]{1,0:T(8,128)S(1)} %get-tuple-element.38), channel_id=1, source_target_pairs={{0,4},{4,8},{8,12},{12,0},{1,5},{5,9},{9,13},{13,1},{2,6},{6,10},{... | collective-permute-start | bytes 12296 | tf_op jit(solution)/shard_map/ppermute | solution.py:298
  51.7 2.5 %collective-permute-start.4 = (f32[8,128]{1,0:T(8,128)S(1)}, f32[8,128]{1,0:T(8,128)S(1)}, u32[]{:S(2)}, u32[]{:S(2)}) collective-permute-start(f32[8,128]{1,0:T(8,128)S(1)} %get-tuple-element.39), channel_id=1, source_target_pairs={{0,8},{4,12},{8,0},{12,4},{1,9},{5,13},{9,1},{13,5},{2,10},{6,14},... | collective-permute-start | bytes 12296 | tf_op jit(solution)/shard_map/ppermute | solution.py:298
  52.5 3.6 %collective-permute-start.5 = (f32[8,128]{1,0:T(8,128)S(1)}, f32[8,128]{1,0:T(8,128)S(1)}, u32[]{:S(2)}, u32[]{:S(2)}) collective-permute-start(f32[8,128]{1,0:T(8,128)S(1)} %get-tuple-element.40), channel_id=1, source_target_pairs={{0,12},{4,0},{8,4},{12,8},{1,13},{5,1},{9,5},{13,9},{2,14},{6,2},{... | collective-permute-start | bytes 12296 | tf_op jit(solution)/shard_map/ppermute | solution.py:298
  59.9 4.3 %collective-permute-start.12 = (f32[8,128]{1,0:T(8,128)S(1)}, f32[8,128]{1,0:T(8,128)S(1)}, u32[]{:S(2)}, u32[]{:S(2)}) collective-permute-start(f32[8,128]{1,0:T(8,128)S(1)} %get-tuple-element.46), channel_id=1, source_target_pairs={{0,1},{1,2},{2,3},{3,0},{4,5},{5,6},{6,7},{7,4},{8,9},{9,10},{10,1... | collective-permute-start | bytes 12296 | tf_op jit(solution)/shard_map/ppermute | solution.py:298
  60.3 3.9 %collective-permute-start.13 = (f32[8,128]{1,0:T(8,128)S(1)}, f32[8,128]{1,0:T(8,128)S(1)}, u32[]{:S(2)}, u32[]{:S(2)}) collective-permute-start(f32[8,128]{1,0:T(8,128)S(1)} %get-tuple-element.47), channel_id=1, source_target_pairs={{0,2},{1,3},{2,0},{3,1},{4,6},{5,7},{6,4},{7,5},{8,10},{9,11},{10,... | collective-permute-start | bytes 12296 | tf_op jit(solution)/shard_map/ppermute | solution.py:298
  61.1 3.5 %collective-permute-start.14 = (f32[8,128]{1,0:T(8,128)S(1)}, f32[8,128]{1,0:T(8,128)S(1)}, u32[]{:S(2)}, u32[]{:S(2)}) collective-permute-start(f32[8,128]{1,0:T(8,128)S(1)} %get-tuple-element.48), channel_id=1, source_target_pairs={{0,3},{1,0},{2,1},{3,2},{4,7},{5,4},{6,5},{7,6},{8,11},{9,8},{10,9... | collective-permute-start | bytes 12296 | tf_op jit(solution)/shard_map/ppermute | solution.py:298
  64.6 2.7 %collective-permute-start.15 = (f32[8,128]{1,0:T(8,128)S(1)}, f32[8,128]{1,0:T(8,128)S(1)}, u32[]{:S(2)}, u32[]{:S(2)}) collective-permute-start(f32[8,128]{1,0:T(8,128)S(1)} %get-tuple-element.50), channel_id=1, source_target_pairs={{0,4},{4,8},{8,12},{12,0},{1,5},{5,9},{9,13},{13,1},{2,6},{6,10},{... | collective-permute-start | bytes 12296 | tf_op jit(solution)/shard_map/ppermute | solution.py:298
  66.5 2.5 %collective-permute-start.16 = (f32[8,128]{1,0:T(8,128)S(1)}, f32[8,128]{1,0:T(8,128)S(1)}, u32[]{:S(2)}, u32[]{:S(2)}) collective-permute-start(f32[8,128]{1,0:T(8,128)S(1)} %get-tuple-element.51), channel_id=1, source_target_pairs={{0,8},{4,12},{8,0},{12,4},{1,9},{5,13},{9,1},{13,5},{2,10},{6,14},... | collective-permute-start | bytes 12296 | tf_op jit(solution)/shard_map/ppermute | solution.py:298
  66.9 3.0 %collective-permute-start.17 = (f32[8,128]{1,0:T(8,128)S(1)}, f32[8,128]{1,0:T(8,128)S(1)}, u32[]{:S(2)}, u32[]{:S(2)}) collective-permute-start(f32[8,128]{1,0:T(8,128)S(1)} %get-tuple-element.52), channel_id=1, source_target_pairs={{0,12},{4,0},{8,4},{12,8},{1,13},{5,1},{9,5},{13,9},{2,14},{6,2},{... | collective-permute-start | bytes 12296 | tf_op jit(solution)/shard_map/ppermute | solution.py:298

commit v9 on v8

--- a/solution.py
+++ b/solution.py
@@ -121,9 +121,10 @@
         ref[cap_big:, LANES:] = jnp.zeros((spare, ref.shape[1] - LANES), jnp.bfloat16)
 
 
-def group_kernel(cap_big, *refs):
-    held, group_ref = refs[:-1], refs[-1]
-    total = len(held) * cap_big
+def group_kernel(shards, blocks, cap_big, docs_at, *refs):
+    held, tables = refs[:shards], refs[shards:shards + blocks]
+    group_ref, ids_refs = refs[shards + blocks], refs[shards + blocks + 1:]
+    total = shards * cap_big
     spare = group_ref.shape[0] - total
     own = jnp.zeros((spare, LANES), jnp.float32)
     for shift, ref in enumerate(held):
@@ -132,6 +133,7 @@
         own = jnp.where(iota(own.shape, 0) == shift, table[0:1, :], own)
     group_ref[total:, 0:LANES] = own.astype(jnp.bfloat16)
     group_ref[total:, LANES:] = jnp.zeros((spare, group_ref.shape[1] - LANES), jnp.bfloat16)
+    turn([table[...] for table in tables], docs_at[0], shards, ids_refs)
 
 
 def turn(tables, at, count, outs):
@@ -321,26 +323,19 @@
     tables = [tables[0]] + [along(tables[by], "blk", blocks, by) for by in range(1, blocks)]
     held = [big_sent[0]] + [along(big_sent[by], "docs", shards, by) for by in range(1, shards)]
 
-    group, = call(
-        functools.partial(group_kernel, cap_big),
-        [((big_slots + rows_up(shards, 16), feature), bf16, vmem)], [vmem] * shards,
+    group, *tables = call(
+        functools.partial(group_kernel, shards, blocks, cap_big),
+        [((big_slots + rows_up(shards, 16), feature), bf16, vmem)] + [((rows_up(blocks), LANES), f32, vmem)] * shards,
+        [smem] + [vmem] * (shards + blocks),
         big_slots * feature, 1 << 20,
-    )(*held)
+    )(docs_at, *held, *tables)
+    tables = [tables[0]] + [along(tables[by], "docs", shards, by) for by in range(1, shards)]
     parts = [group]
     for step in range(1, blocks):
         pairs = [(d * blocks + (home_of(d, blocks) + step) % blocks, d * blocks + home_of(d, blocks))
                  for d in range(shards)]
         parts.append(lax.ppermute(group, ("docs", "blk"), pairs))
 
-    def turned(tables):
-        tables = call(
-            functools.partial(turn_kernel, shards),
-            [((rows_up(blocks), LANES), f32, vmem)] * shards, [smem] + [vmem] * blocks,
-            shards * blocks * LANES, 1 << 16,
-        )(docs_at, *tables)
-        return [tables[0]] + [along(tables[by], "docs", shards, by) for by in range(1, shards)]
-
-    tables = turned(tables)
     small_ids, = call(
         functools.partial(ids_kernel, shards, blocks, cap_small),
         [((1, small_slots), f32, vmem)], [smem, smem] + [vmem] * shards,
@@ -358,7 +353,12 @@
         2 * big_total * big_total * feature, 2 << 20,
     )(docs_at, back_small, *parts)
     back = [back[0]] + [along(back[by], "blk", blocks, by) for by in range(1, blocks)]
-    back = turned(back)
+    back = call(
+        functools.partial(turn_kernel, shards),
+        [((rows_up(blocks), LANES), f32, vmem)] * shards, [smem] + [vmem] * blocks,
+        shards * blocks * LANES, 1 << 16,
+    )(docs_at, *back)
+    back = [back[0]] + [along(back[by], "docs", shards, by) for by in range(1, shards)]
 
     masks = call(
         functools.partial(masks_kernel, shards, blocks),

time: 71 us -> 73.4 us (1.034)
  starting transfers between devices: 25.7 us -> 32.6 us
  waiting for transfers between devices: 34.8 us -> 30.3 us
    ppermute x15, waiting for transfers between devices: 34.8 us -> 29.4 us  [along(): return lax.ppermute(x, axis, [(i, (i + by) % count) for i in range(count)])]
    ppermute x15, starting transfers between devices: 15.4 us -> 18.9 us  [along(): return lax.ppermute(x, axis, [(i, (i + by) % count) for i in range(count)])]
    ppermute x3, starting transfers between devices: 2.83 us -> 6.28 us  [body(): parts.append(lax.ppermute(group, ('docs', 'blk'), pairs))]
    ppermute x3, waiting for transfers between devices: 0.02 us -> 0.99 us  [body(): parts.append(lax.ppermute(group, ('docs', 'blk'), pairs))]
  transfers between devices with their start and end apart: 19 -> 19, of which waited for: 13 -> 11; matrix products, arithmetic and copies ran while one was open for 0% -> 0% of each run, Pallas kernels for 4% -> 4%
where the time goes in v9:
time: 73.4 us; the launch traced here: 73.2 us
  starting transfers between devices  32.6 us (44%)
  waiting for transfers between devices  30.3 us (41%)
  Pallas kernels  10 us (14%)
    ppermute x15, waiting for transfers between devices, along(): return lax.ppermute(x, axis, [(i, (i + by) % count) for i in range(count)])  29.4 us
    ppermute x15, starting transfers between devices, along(): return lax.ppermute(x, axis, [(i, (i + by) % count) for i in range(count)])  18.9 us
    all_to_all x1, starting transfers between devices, body(): lax.all_to_all(small_sent.reshape(devices, cap_small, feature), ('docs',...  7.47 us
    ppermute x3, starting transfers between devices, body(): parts.append(lax.ppermute(group, ('docs', 'blk'), pairs))  6.28 us
    pallas_call x1, Pallas kernels, body(): call(functools.partial(sort_kernel, *sizes), [((small_slots, feature), bf...  4.39 us
    pallas_call x1, Pallas kernels, body(): call(functools.partial(big_kernel, *sizes), [((rows_up(shards), LANES), f...  2.24 us
  transfers between devices with their start and end apart: 19, of which 11 were waited for; matrix products, arithmetic and copies ran while one was open for 0% of the time, Pallas kernels for 4%

profile of v9, /device:TPU:1, one launch (start us, length us, event | category | flops | bytes accessed | tf_op | source)
XLA Modules:
  0.0 73.2 jit_solution(15237919725938816095)
XLA Ops:
  0.0 4.4 %shard_map.37 = (bf16[768,768]{1,0:T(8,128)(2,1)}, bf16[512,768]{1,0:T(8,128)(2,1)}, s32[8,512]{1,0:T(8,128)}) custom-call(bf16[512,768]{1,0:T(8,128)(2,1)} %pooled_hbm.1, bf16[768,768]{1,0:T(8,128)(2,1)} %weight_hbm.1, s32[1,512]{1,0:T(1,128)} %bitcast.8), custom_call_target="tpu_custom_call" | custom-call | flops 1207959552 | bytes 4194304 | tf_op jit(solution)/shard_map/pallas_call | solution.py:302
  4.4 0.0 copy-start
  4.4 0.0 copy-start.1
  4.4 7.5 %all-to-all-start = ((bf16[16,48,768]{2,1,0:T(8,128)(2,1)}), bf16[16,48,768]{2,1,0:T(8,128)(2,1)S(1)}, u32[]{:S(2)}, u32[]{:S(2)}) async-start(bf16[16,48,768]{2,1,0:T(8,128)(2,1)} %bitcast.7), calls=%async_computation | async-start | bytes 2359296 | tf_op jit(solution)/shard_map/all_to_all | solution.py:312
  11.9 0.0 copy-done
  11.9 0.0 copy-done.1
  11.9 0.9 %shard_map.38 = (bf16[80,768]{1,0:T(8,128)(2,1)S(1)}, bf16[80,768]{1,0:T(8,128)(2,1)S(1)}, bf16[80,768]{1,0:T(8,128)(2,1)S(1)}, bf16[80,768]{1,0:T(8,128)(2,1)S(...) custom-call(s32[1]{0:T(128)} %bitcast.docs_at.at_ref, ...), custom_call_target="tpu_custom_call" | custom-call | flops 201326592 | bytes 2097152 | tf_op jit(solution)/shard_map/pallas_call | solution.py:316
  12.8 1.7 %collective-permute-start = (bf16[80,768]{1,0:T(8,128)(2,1)S(1)}, bf16[80,768]{1,0:T(8,128)(2,1)S(1)}, u32[]{:S(2)}, u32[]{:S(2)}) collective-permute-start(bf16[80,768]{1,0:T(8,128)(2,1)S(1)} %get-tuple-element.35), channel_id=1, source_target_pairs={{0,4},{4,8},{8,12},{12,0},{1,5},{5,9},{9,13},{13,1},{2,6},{6,10},{... | collective-permute-start | bytes 368648 | tf_op jit(solution)/shard_map/ppermute | solution.py:300
  14.5 0.0 collective-permute-start.1
  14.5 0.5 collective-permute-start.2
  15.1 1.2 %collective-permute-start.3 = (f32[8,128]{1,0:T(8,128)S(1)}, f32[8,128]{1,0:T(8,128)S(1)}, u32[]{:S(2)}, u32[]{:S(2)}) collective-permute-start(f32[8,128]{1,0:T(8,128)S(1)} %get-tuple-element.39), channel_id=1, source_target_pairs={{0,1},{1,2},{2,3},{3,0},{4,5},{5,6},{6,7},{7,4},{8,9},{9,10},{10,1... | collective-permute-start | bytes 12296 | tf_op jit(solution)/shard_map/ppermute | solution.py:300
  16.3 2.1 %collective-permute-start.4 = (f32[8,128]{1,0:T(8,128)S(1)}, f32[8,128]{1,0:T(8,128)S(1)}, u32[]{:S(2)}, u32[]{:S(2)}) collective-permute-start(f32[8,128]{1,0:T(8,128)S(1)} %get-tuple-element.40), channel_id=1, source_target_pairs={{0,2},{1,3},{2,0},{3,1},{4,6},{5,7},{6,4},{7,5},{8,10},{9,11},{10,... | collective-permute-start | bytes 12296 | tf_op jit(solution)/shard_map/ppermute | solution.py:300
  18.4 16.6 %collective-permute-done.3.refs_5_ = f32[8,128]{1,0:T(8,128)S(1)} collective-permute-done((f32[8,128]{1,0:T(8,128)S(1)}, f32[8,128]{1,0:T(8,128)S(1)}, u32[]{:S(2)}, u32[]{:S(2)}) %collective-permute-start.3) | collective-permute-done | bytes 4128 | tf_op jit(solution)/shard_map/ppermute | solution.py:300
  34.9 0.0 collective-permute-start.5
  34.9 5.8 %collective-permute-done.4.refs_6_ = f32[8,128]{1,0:T(8,128)S(1)} collective-permute-done((f32[8,128]{1,0:T(8,128)S(1)}, f32[8,128]{1,0:T(8,128)S(1)}, u32[]{:S(2)}, u32[]{:S(2)}) %collective-permute-start.4) | collective-permute-done | bytes 4128 | tf_op jit(solution)/shard_map/ppermute | solution.py:300
  40.7 0.3 collective-permute-done.5.refs_7_
  41.1 0.0 collective-permute-done.refs_1_
  41.1 0.0 collective-permute-done.1.refs_2_
  41.1 0.0 collective-permute-done.2.refs_3_
  41.1 0.1 shard_map.39
  41.1 0.7 collective-permute-start.11
  41.8 4.9 %collective-permute-start.10 = (bf16[272,768]{1,0:T(8,128)(2,1)S(1)}, bf16[272,768]{1,0:T(8,128)(2,1)S(1)}, u32[]{:S(2)}, u32[]{:S(2)}) collective-permute-start(bf16[272,768]{1,0:T(8,128)(2,1)S(1)} %get-tuple-element.46.refs_0_), channel_id=1, source_target_pairs={{3,1},{4,6},{11,9},{12,14},{19,17},{20,22},{27,25},{28,30}} | collective-permute-start | bytes 1253384 | tf_op jit(solution)/shard_map/ppermute | solution.py:337
  46.8 0.7 collective-permute-start.9
  47.5 1.5 %collective-permute-start.6 = (f32[8,128]{1,0:T(8,128)S(1)}, f32[8,128]{1,0:T(8,128)S(1)}, u32[]{:S(2)}, u32[]{:S(2)}) collective-permute-start(f32[8,128]{1,0:T(8,128)S(1)} %get-tuple-element.43), channel_id=1, source_target_pairs={{0,4},{4,8},{8,12},{12,0},{1,5},{5,9},{9,13},{13,1},{2,6},{6,10},{... | collective-permute-start | bytes 12296 | tf_op jit(solution)/shard_map/ppermute | solution.py:300
  48.9 0.1 collective-permute-start.7
  49.0 0.7 collective-permute-done.6.refs_1_
  49.7 1.0 %collective-permute-start.8 = (f32[8,128]{1,0:T(8,128)S(1)}, f32[8,128]{1,0:T(8,128)S(1)}, u32[]{:S(2)}, u32[]{:S(2)}) collective-permute-start(f32[8,128]{1,0:T(8,128)S(1)} %get-tuple-element.45), channel_id=1, source_target_pairs={{0,12},{4,0},{8,4},{12,8},{1,13},{5,1},{9,5},{13,9},{2,14},{6,2},{... | collective-permute-start | bytes 12296 | tf_op jit(solution)/shard_map/ppermute | solution.py:300
  50.7 0.7 collective-permute-done.7.refs_2_
  51.4 1.9 %collective-permute-done.8.refs_3_ = f32[8,128]{1,0:T(8,128)S(1)} collective-permute-done((f32[8,128]{1,0:T(8,128)S(1)}, f32[8,128]{1,0:T(8,128)S(1)}, u32[]{:S(2)}, u32[]{:S(2)}) %collective-permute-start.8) | collective-permute-done | bytes 4128 | tf_op jit(solution)/shard_map/ppermute | solution.py:300
  53.3 0.2 shard_map.40.row_ref
  53.4 0.0 all-to-all-done
  53.5 1.4 %shard_map.41.small_ref = f32[32,128]{1,0:T(8,128)S(1)} custom-call(s32[1]{0:T(128)} %bitcast.1.blk_at, bf16[768,768]{1,0:T(8,128)(2,1)S(1)} %bitcast.6, f32[1,768]{1,0:T(1,128)S(1)} %shard_map.40.row_ref), custom_call_target="tpu_custom_call" | custom-call | flops 905969664 | bytes 2097152 | tf_op jit(solution)/shard_map/pallas_call | solution.py:345
  54.8 0.0 collective-permute-done.11.refs_3_
  54.8 1.0 %collective-permute-done.10.refs_2_ = bf16[272,768]{1,0:T(8,128)(2,1)S(1)} collective-permute-done((bf16[272,768]{1,0:T(8,128)(2,1)S(1)}, bf16[272,768]{1,0:T(8,128)(2,1)S(1)}, u32[]{:S(2)}, u32[]{:S(2)}) %collective-permute-start.10) | collective-permute-done | bytes 417824 | tf_op jit(solution)/shard_map/ppermute | solution.py:337
  55.8 0.0 collective-permute-done.9.refs_1_
  55.8 2.2 %shard_map.42 = (f32[8,128]{1,0:T(8,128)S(1)}, f32[8,128]{1,0:T(8,128)S(1)}, f32[8,128]{1,0:T(8,128)S(1)}, f32[8,128]{1,0:T(8,128)S(1)}) custom-call(s32[1]{0:T(128)} %bitcast.docs_at.at_ref, f32[32,128]{1,0:T(8,128)S(1)} %shard_map.41.small_ref, bf16[272,768]{1,0:T(8,128)(2,1)S(1)} %get-tuple-element.46.refs_0_, ...), custom_call_target="tpu_custom_call" | custom-call | flops 1610612736 | bytes 2097152 | tf_op jit(solution)/shard_map/pallas_call | solution.py:350
  58.1 0.1 collective-permute-start.12
  58.1 3.2 %collective-permute-start.13 = (f32[8,128]{1,0:T(8,128)S(1)}, f32[8,128]{1,0:T(8,128)S(1)}, u32[]{:S(2)}, u32[]{:S(2)}) collective-permute-start(f32[8,128]{1,0:T(8,128)S(1)} %get-tuple-element.49), channel_id=1, source_target_pairs={{0,2},{1,3},{2,0},{3,1},{4,6},{5,7},{6,4},{7,5},{8,10},{9,11},{10,... | collective-permute-start | bytes 12296 | tf_op jit(solution)/shard_map/ppermute | solution.py:300
  61.3 2.3 %collective-permute-start.14 = (f32[8,128]{1,0:T(8,128)S(1)}, f32[8,128]{1,0:T(8,128)S(1)}, u32[]{:S(2)}, u32[]{:S(2)}) collective-permute-start(f32[8,128]{1,0:T(8,128)S(1)} %get-tuple-element.50), channel_id=1, source_target_pairs={{0,3},{1,0},{2,1},{3,2},{4,7},{5,4},{6,5},{7,6},{8,11},{9,8},{10,9... | collective-permute-start | bytes 12296 | tf_op jit(solution)/shard_map/ppermute | solution.py:300
  63.6 0.0 collective-permute-done.12.refs_1_
  63.6 0.0 collective-permute-done.13.refs_2_
  63.6 0.7 %collective-permute-done.14.refs_3_ = f32[8,128]{1,0:T(8,128)S(1)} collective-permute-done((f32[8,128]{1,0:T(8,128)S(1)}, f32[8,128]{1,0:T(8,128)S(1)}, u32[]{:S(2)}, u32[]{:S(2)}) %collective-permute-start.14) | collective-permute-done | bytes 4128 | tf_op jit(solution)/shard_map/ppermute | solution.py:300
  64.4 4.9 %collective-permute-start.15 = (f32[8,128]{1,0:T(8,128)S(1)}, f32[8,128]{1,0:T(8,128)S(1)}, u32[]{:S(2)}, u32[]{:S(2)}) collective-permute-start(f32[8,128]{1,0:T(8,128)S(1)} %get-tuple-element.52), channel_id=1, source_target_pairs={{0,4},{4,8},{8,12},{12,0},{1,5},{5,9},{9,13},{13,1},{2,6},{6,10},{... | collective-permute-start | bytes 12296 | tf_op jit(solution)/shard_map/ppermute | solution.py:300
  69.2 0.1 collective-permute-start.16
  69.3 0.4 collective-permute-start.17
  69.7 0.2 collective-permute-done.15.refs_1_
  70.0 1.7 %collective-permute-done.16.refs_2_ = f32[8,128]{1,0:T(8,128)S(1)} collective-permute-done((f32[8,128]{1,0:T(8,128)S(1)}, f32[8,128]{1,0:T(8,128)S(1)}, u32[]{:S(2)}, u32[]{:S(2)}) %collective-permute-start.16) | collective-permute-done | bytes 4128 | tf_op jit(solution)/shard_map/ppermute | solution.py:300
  71.7 0.7 collective-permute-done.17.refs_3_
  72.4 0.8 %shard_map.45 = f32[1,512]{1,0:T(1,128)} custom-call(f32[8,128]{1,0:T(8,128)S(1)} %get-tuple-element.51.refs_0_, f32[8,128]{1,0:T(8,128)S(1)} %collective-permute-done.15.refs_1_, f32[8,128]{1,0:T(8,128)S(1)} %collective-permute-done.16.refs_2_, f32[8,128]{1,0:T(8,128)S(1)} %collective-permute-done.17.refs_3_, ...), custom_call_target="tpu_custom_call" | custom-call | flops 6291456 | bytes 262144 | tf_op jit(solution)/shard_map/pallas_call | solution.py:368
  (2 shorter events, 0.1 us)
Async XLA Ops:
  4.4 7.5 %copy-start = (bf16[512,768]{1,0:T(8,128)(2,1)S(1)}, bf16[512,768]{1,0:T(8,128)(2,1)}, u32[]{:S(2)}) copy-start(bf16[512,768]{1,0:T(8,128)(2,1)} %get-tuple-element.32.rows_ref) | copy-start | bytes 2359300
  4.4 7.5 %copy-start.1 = (s32[8,512]{1,0:T(8,128)S(1)}, s32[8,512]{1,0:T(8,128)}, u32[]{:S(2)}) copy-start(s32[8,512]{1,0:T(8,128)} %get-tuple-element.33.info_ref) | copy-start | bytes 49156
  4.4 49.0 %all-to-all-start = ((bf16[16,48,768]{2,1,0:T(8,128)(2,1)}), bf16[16,48,768]{2,1,0:T(8,128)(2,1)S(1)}, u32[]{:S(2)}, u32[]{:S(2)}) async-start(bf16[16,48,768]{2,1,0:T(8,128)(2,1)} %bitcast.7), calls=%async_computation | async-start | bytes 2359296 | tf_op jit(solution)/shard_map/all_to_all | solution.py:312
  12.8 28.2 %collective-permute-start = (bf16[80,768]{1,0:T(8,128)(2,1)S(1)}, bf16[80,768]{1,0:T(8,128)(2,1)S(1)}, u32[]{:S(2)}, u32[]{:S(2)}) collective-permute-start(bf16[80,768]{1,0:T(8,128)(2,1)S(1)} %get-tuple-element.35), channel_id=1, source_target_pairs={{0,4},{4,8},{8,12},{12,0},{1,5},{5,9},{9,13},{13,1},{2,6},{6,10},{... | collective-permute-start | bytes 368648 | tf_op jit(solution)/shard_map/ppermute | solution.py:300
  14.5 26.5 %collective-permute-start.1 = (bf16[80,768]{1,0:T(8,128)(2,1)S(1)}, bf16[80,768]{1,0:T(8,128)(2,1)S(1)}, u32[]{:S(2)}, u32[]{:S(2)}) collective-permute-start(bf16[80,768]{1,0:T(8,128)(2,1)S(1)} %get-tuple-element.36), channel_id=1, source_target_pairs={{0,8},{4,12},{8,0},{12,4},{1,9},{5,13},{9,1},{13,5},{2,10},{6,14},... | collective-permute-start | bytes 368648 | tf_op jit(solution)/shard_map/ppermute | solution.py:300
  14.5 26.5 %collective-permute-start.2 = (bf16[80,768]{1,0:T(8,128)(2,1)S(1)}, bf16[80,768]{1,0:T(8,128)(2,1)S(1)}, u32[]{:S(2)}, u32[]{:S(2)}) collective-permute-start(bf16[80,768]{1,0:T(8,128)(2,1)S(1)} %get-tuple-element.37), channel_id=1, source_target_pairs={{0,12},{4,0},{8,4},{12,8},{1,13},{5,1},{9,5},{13,9},{2,14},{6,2},{... | collective-permute-start | bytes 368648 | tf_op jit(solution)/shard_map/ppermute | solution.py:300
  15.1 19.9 %collective-permute-start.3 = (f32[8,128]{1,0:T(8,128)S(1)}, f32[8,128]{1,0:T(8,128)S(1)}, u32[]{:S(2)}, u32[]{:S(2)}) collective-permute-start(f32[8,128]{1,0:T(8,128)S(1)} %get-tuple-element.39), channel_id=1, source_target_pairs={{0,1},{1,2},{2,3},{3,0},{4,5},{5,6},{6,7},{7,4},{8,9},{9,10},{10,1... | collective-permute-start | bytes 12296 | tf_op jit(solution)/shard_map/ppermute | solution.py:300
  16.3 24.5 %collective-permute-start.4 = (f32[8,128]{1,0:T(8,128)S(1)}, f32[8,128]{1,0:T(8,128)S(1)}, u32[]{:S(2)}, u32[]{:S(2)}) collective-permute-start(f32[8,128]{1,0:T(8,128)S(1)} %get-tuple-element.40), channel_id=1, source_target_pairs={{0,2},{1,3},{2,0},{3,1},{4,6},{5,7},{6,4},{7,5},{8,10},{9,11},{10,... | collective-permute-start | bytes 12296 | tf_op jit(solution)/shard_map/ppermute | solution.py:300
  34.9 6.1 %collective-permute-start.5 = (f32[8,128]{1,0:T(8,128)S(1)}, f32[8,128]{1,0:T(8,128)S(1)}, u32[]{:S(2)}, u32[]{:S(2)}) collective-permute-start(f32[8,128]{1,0:T(8,128)S(1)} %get-tuple-element.41), channel_id=1, source_target_pairs={{0,3},{1,0},{2,1},{3,2},{4,7},{5,4},{6,5},{7,6},{8,11},{9,8},{10,9... | collective-permute-start | bytes 12296 | tf_op jit(solution)/shard_map/ppermute | solution.py:300
  41.1 13.7 %collective-permute-start.11 = (bf16[272,768]{1,0:T(8,128)(2,1)S(1)}, bf16[272,768]{1,0:T(8,128)(2,1)S(1)}, u32[]{:S(2)}, u32[]{:S(2)}) collective-permute-start(bf16[272,768]{1,0:T(8,128)(2,1)S(1)} %get-tuple-element.46.refs_0_), channel_id=1, source_target_pairs={{0,1},{5,6},{8,9},{13,14},{16,17},{21,22},{24,25},{29,30}} | collective-permute-start | bytes 1253384 | tf_op jit(solution)/shard_map/ppermute | solution.py:337
  41.8 14.0 %collective-permute-start.10 = (bf16[272,768]{1,0:T(8,128)(2,1)S(1)}, bf16[272,768]{1,0:T(8,128)(2,1)S(1)}, u32[]{:S(2)}, u32[]{:S(2)}) collective-permute-start(bf16[272,768]{1,0:T(8,128)(2,1)S(1)} %get-tuple-element.46.refs_0_), channel_id=1, source_target_pairs={{3,1},{4,6},{11,9},{12,14},{19,17},{20,22},{27,25},{28,30}} | collective-permute-start | bytes 1253384 | tf_op jit(solution)/shard_map/ppermute | solution.py:337
  46.8 9.1 %collective-permute-start.9 = (bf16[272,768]{1,0:T(8,128)(2,1)S(1)}, bf16[272,768]{1,0:T(8,128)(2,1)S(1)}, u32[]{:S(2)}, u32[]{:S(2)}) collective-permute-start(bf16[272,768]{1,0:T(8,128)(2,1)S(1)} %get-tuple-element.46.refs_0_), channel_id=1, source_target_pairs={{2,1},{7,6},{10,9},{15,14},{18,17},{23,22},{26,25},{31,30}} | collective-permute-start | bytes 1253384 | tf_op jit(solution)/shard_map/ppermute | solution.py:337
  47.5 2.2 %collective-permute-start.6 = (f32[8,128]{1,0:T(8,128)S(1)}, f32[8,128]{1,0:T(8,128)S(1)}, u32[]{:S(2)}, u32[]{:S(2)}) collective-permute-start(f32[8,128]{1,0:T(8,128)S(1)} %get-tuple-element.43), channel_id=1, source_target_pairs={{0,4},{4,8},{8,12},{12,0},{1,5},{5,9},{9,13},{13,1},{2,6},{6,10},{... | collective-permute-start | bytes 12296 | tf_op jit(solution)/shard_map/ppermute | solution.py:300
  48.9 2.5 %collective-permute-start.7 = (f32[8,128]{1,0:T(8,128)S(1)}, f32[8,128]{1,0:T(8,128)S(1)}, u32[]{:S(2)}, u32[]{:S(2)}) collective-permute-start(f32[8,128]{1,0:T(8,128)S(1)} %get-tuple-element.44), channel_id=1, source_target_pairs={{0,8},{4,12},{8,0},{12,4},{1,9},{5,13},{9,1},{13,5},{2,10},{6,14},... | collective-permute-start | bytes 12296 | tf_op jit(solution)/shard_map/ppermute | solution.py:300
  49.7 3.6 %collective-permute-start.8 = (f32[8,128]{1,0:T(8,128)S(1)}, f32[8,128]{1,0:T(8,128)S(1)}, u32[]{:S(2)}, u32[]{:S(2)}) collective-permute-start(f32[8,128]{1,0:T(8,128)S(1)} %get-tuple-element.45), channel_id=1, source_target_pairs={{0,12},{4,0},{8,4},{12,8},{1,13},{5,1},{9,5},{13,9},{2,14},{6,2},{... | collective-permute-start | bytes 12296 | tf_op jit(solution)/shard_map/ppermute | solution.py:300
  58.1 5.5 %collective-permute-start.12 = (f32[8,128]{1,0:T(8,128)S(1)}, f32[8,128]{1,0:T(8,128)S(1)}, u32[]{:S(2)}, u32[]{:S(2)}) collective-permute-start(f32[8,128]{1,0:T(8,128)S(1)} %get-tuple-element.48), channel_id=1, source_target_pairs={{0,1},{1,2},{2,3},{3,0},{4,5},{5,6},{6,7},{7,4},{8,9},{9,10},{10,1... | collective-permute-start | bytes 12296 | tf_op jit(solution)/shard_map/ppermute | solution.py:300
  58.1 5.5 %collective-permute-start.13 = (f32[8,128]{1,0:T(8,128)S(1)}, f32[8,128]{1,0:T(8,128)S(1)}, u32[]{:S(2)}, u32[]{:S(2)}) collective-permute-start(f32[8,128]{1,0:T(8,128)S(1)} %get-tuple-element.49), channel_id=1, source_target_pairs={{0,2},{1,3},{2,0},{3,1},{4,6},{5,7},{6,4},{7,5},{8,10},{9,11},{10,... | collective-permute-start | bytes 12296 | tf_op jit(solution)/shard_map/ppermute | solution.py:300
  61.3 3.0 %collective-permute-start.14 = (f32[8,128]{1,0:T(8,128)S(1)}, f32[8,128]{1,0:T(8,128)S(1)}, u32[]{:S(2)}, u32[]{:S(2)}) collective-permute-start(f32[8,128]{1,0:T(8,128)S(1)} %get-tuple-element.50), channel_id=1, source_target_pairs={{0,3},{1,0},{2,1},{3,2},{4,7},{5,4},{6,5},{7,6},{8,11},{9,8},{10,9... | collective-permute-start | bytes 12296 | tf_op jit(solution)/shard_map/ppermute | solution.py:300
  64.4 5.6 %collective-permute-start.15 = (f32[8,128]{1,0:T(8,128)S(1)}, f32[8,128]{1,0:T(8,128)S(1)}, u32[]{:S(2)}, u32[]{:S(2)}) collective-permute-start(f32[8,128]{1,0:T(8,128)S(1)} %get-tuple-element.52), channel_id=1, source_target_pairs={{0,4},{4,8},{8,12},{12,0},{1,5},{5,9},{9,13},{13,1},{2,6},{6,10},{... | collective-permute-start | bytes 12296 | tf_op jit(solution)/shard_map/ppermute | solution.py:300
  69.2 2.5 %collective-permute-start.16 = (f32[8,128]{1,0:T(8,128)S(1)}, f32[8,128]{1,0:T(8,128)S(1)}, u32[]{:S(2)}, u32[]{:S(2)}) collective-permute-start(f32[8,128]{1,0:T(8,128)S(1)} %get-tuple-element.53), channel_id=1, source_target_pairs={{0,8},{4,12},{8,0},{12,4},{1,9},{5,13},{9,1},{13,5},{2,10},{6,14},... | collective-permute-start | bytes 12296 | tf_op jit(solution)/shard_map/ppermute | solution.py:300
  69.3 3.0 %collective-permute-start.17 = (f32[8,128]{1,0:T(8,128)S(1)}, f32[8,128]{1,0:T(8,128)S(1)}, u32[]{:S(2)}, u32[]{:S(2)}) collective-permute-start(f32[8,128]{1,0:T(8,128)S(1)} %get-tuple-element.54), channel_id=1, source_target_pairs={{0,12},{4,0},{8,4},{12,8},{1,13},{5,1},{9,5},{13,9},{2,14},{6,2},{... | collective-permute-start | bytes 12296 | tf_op jit(solution)/shard_map/ppermute | solution.py:300

commit v10 on v8

--- a/solution.py
+++ b/solution.py
@@ -47,7 +47,7 @@
 
 def sort_kernel(shards, blocks, cap_big, cap_small, pooled_hbm, weight_hbm, cluster_hbm, small_hbm, rows_hbm, info_hbm,
                 pooled_ref, weight_ref, cluster_ref, small_ref, rows_ref, info_ref, sems, small_sems):
-    docs = rows_ref.shape[0]
+    docs, feature = rows_ref.shape
     devices = shards * blocks
     limit = BIG_OWN * shards
     buckets = devices + shards
@@ -80,6 +80,7 @@
     sends = [pltpu.make_async_copy(info_ref, info_hbm, sems.at[3])]
     sends[0].start()
     small_slot = jnp.where(is_big, -1, target * cap_small + rank)
+    ids = ids_table(iota((devices, docs), 0) == bucket, info_ref)
 
     for fetch in fetches[1:]:
         fetch.wait()
@@ -89,35 +90,39 @@
     sends.append(pltpu.make_async_copy(rows_ref, rows_hbm, sems.at[4]))
     sends[-1].start()
 
-    tile = small_ref.shape[0] // small_sems.shape[0]
+    slabs = feature // LANES
+    group = devices // small_sems.shape[0]
     for part in range(small_sems.shape[0]):
-        small_ref[part * tile:(part + 1) * tile, :] = picked_rows(rows_ref, small_slot, part * tile, tile)
+        first = part * group
+        picked = picked_rows(rows_ref, small_slot, first * cap_small, group * cap_small)
+        for device in range(group):
+            for slab in range(slabs):
+                small_ref[first + device, slab * cap_small:(slab + 1) * cap_small, :] = picked[
+                    device * cap_small:(device + 1) * cap_small, slab * LANES:(slab + 1) * LANES]
+            small_ref[first + device, slabs * cap_small:, :] = jnp.broadcast_to(
+                ids[first + device:first + device + 1, :], (16, LANES)).astype(jnp.bfloat16)
         sends.append(pltpu.make_async_copy(
-            small_ref.at[pl.ds(part * tile, tile)], small_hbm.at[pl.ds(part * tile, tile)], small_sems.at[part]))
+            small_ref.at[pl.ds(first, group)], small_hbm.at[pl.ds(first, group)], small_sems.at[part]))
         sends[-1].start()
     for send in sends:
         send.wait()
 
 
-def sort_big_kernel(shards, blocks, cap_big, docs_at, blk_at, rows_ref, info_ref, *refs):
-    big_refs, ids_refs = refs[:shards], refs[shards:]
-    docs = rows_ref.shape[0]
+def ids_table(mine, info_ref):
+    docs = info_ref.shape[1]
+    quota = info_ref[3:4, :].astype(jnp.float32)
+    lanes = (iota((LANES, docs), 0) == info_ref[1:2, :]).astype(jnp.float32).astype(jnp.bfloat16)
+    return dot_nt(jnp.where(mine, quota, 0.0).astype(jnp.bfloat16), lanes)
+
+
+def sort_big_kernel(shards, blocks, cap_big, docs_at, rows_ref, info_ref, *big_refs):
     devices = shards * blocks
-    quota, bucket = info_ref[3:4, :].astype(jnp.float32), info_ref[4:5, :]
-    lanes = (iota((LANES, docs), 0) == info_ref[1:2, :]).astype(jnp.float32).astype(jnp.bfloat16)
-
-    def table(mine):
-        return dot_nt(jnp.where(mine, quota, 0.0).astype(jnp.bfloat16), lanes)
-
-    for step, ref in enumerate(ids_refs):
-        target = iota((2 * ref.shape[0], docs), 0) * blocks + modulo(blk_at[0] + step, blocks)
-        ref[...] = table((target == bucket) & (target < devices))[0:ref.shape[0], :]
     for shift, ref in enumerate(big_refs):
         to = modulo(docs_at[0] + shift, shards)
         ref[0:cap_big, :] = picked_rows(rows_ref, info_ref[2:3, :], to * cap_big, cap_big)
         spare = ref.shape[0] - cap_big
-        ref[cap_big:, 0:LANES] = table(
-            (iota((spare, docs), 0) == 0) & (bucket == devices + to)).astype(jnp.bfloat16)
+        mine = (iota((spare, info_ref.shape[1]), 0) == 0) & (info_ref[4:5, :] == devices + to)
+        ref[cap_big:, 0:LANES] = ids_table(mine, info_ref).astype(jnp.bfloat16)
         ref[cap_big:, LANES:] = jnp.zeros((spare, ref.shape[1] - LANES), jnp.bfloat16)
 
 
@@ -168,16 +173,6 @@
     pick = (iota((LANES, lane.shape[1]), 0) == lane).astype(jnp.float32).astype(jnp.bfloat16)
     found = jnp.dot(values, pick, preferred_element_type=jnp.float32)
     return jnp.sum(jnp.where(iota(found.shape, 0) == row, found, 0.0), axis=0, keepdims=True)
-
-
-def ids_kernel(shards, blocks, cap_small, docs_at, blk_at, *refs):
-    tables, ids_ref = refs[:-1], refs[-1]
-    high = tables[0].shape[0]
-    values = jnp.concatenate([table[...] for table in tables], axis=0)
-    values = jnp.concatenate([values, jnp.zeros_like(values)], axis=0).astype(jnp.bfloat16)
-    docs, blk, lane = small_sources(ids_ref.shape[1], blocks, cap_small)
-    row = modulo(docs_at[0] + shards - docs, shards) * high + modulo(blk_at[0] + blocks - blk, blocks)
-    ids_ref[...] = ids_from(values, row, lane)
 
 
 def as_column(row):
@@ -230,16 +225,24 @@
         ref[...] = back[step * high:(step + 1) * high, :]
 
 
-def small_kernel(shards, blocks, cap_small, blk_at, rows_ref, row_ref, back_ref):
-    total = rows_ref.shape[0]
+def small_kernel(shards, blocks, cap_small, blk_at, got_ref, back_ref, rows_ref):
+    total, feature = rows_ref.shape
     high = back_ref.shape[0] // blocks
-    col_ids = as_column(row_ref[...])
+    slabs = feature // LANES
+    values = []
+    for device in range(got_ref.shape[0]):
+        for slab in range(slabs):
+            rows_ref[device * cap_small:(device + 1) * cap_small, slab * LANES:(slab + 1) * LANES] = got_ref[
+                device, slab * cap_small:(slab + 1) * cap_small, :]
+        values.append(got_ref[device, slabs * cap_small:, :].astype(jnp.float32)[0:1, :])
+    docs, blk, lane = small_sources(total, blocks, cap_small)
+    row_ids = ids_from(jnp.concatenate(values, axis=0).astype(jnp.bfloat16), docs * blocks + blk, lane)
+    col_ids = as_column(row_ids)
     tile = tile_of(total)
     best = jnp.full((1, total), -1.0, jnp.float32)
     for at in range(0, total, tile):
         best = jnp.maximum(best, block_best(
-            rows_ref[at:at + tile, :], col_ids[at:at + tile], at, rows_ref[...], row_ref[...], 0))
-    docs, blk, lane = small_sources(total, blocks, cap_small)
+            rows_ref[at:at + tile, :], col_ids[at:at + tile], at, rows_ref[...], row_ids, 0))
     row = modulo(blk + blocks - blk_at[0], blocks) * high + docs
     back_ref[...] = spread(best, row, lane, back_ref.shape[0])
 
@@ -284,7 +287,7 @@
     big_count = docs // 4
     small_count = docs - big_count
     cap_big = 2 * big_count // shards
-    cap_small = 2 * small_count // devices
+    cap_small = rows_up(2 * small_count // devices, 16)
     small_slots = devices * cap_small
     big_slots = shards * cap_big
     big_total = blocks * big_slots
@@ -297,30 +300,26 @@
     def along(x, axis, count, by):
         return lax.ppermute(x, axis, [(i, (i + by) % count) for i in range(count)])
 
+    small_rows = feature // LANES * cap_small + 16
     small_sent, rows, info = call(
         functools.partial(sort_kernel, *sizes),
-        [((small_slots, feature), bf16, hbm), ((docs, feature), bf16, hbm), ((8, docs), i32, hbm)],
+        [((devices, small_rows, LANES), bf16, hbm), ((docs, feature), bf16, hbm), ((8, docs), i32, hbm)],
         [hbm, hbm, hbm],
         2 * docs * feature * (pooled.shape[1] + small_slots), 4 << 20, 60,
         [vmem(pooled.shape, bf16), vmem(proj_weight.shape, bf16), vmem((1, docs), i32),
-         vmem((small_slots, feature), bf16), vmem((docs, feature), bf16), vmem((8, docs), i32),
-         dma((5,)), dma((3,))],
+         vmem((devices, small_rows, LANES), bf16), vmem((docs, feature), bf16), vmem((8, docs), i32),
+         dma((5,)), dma((4,))],
     )(pooled, proj_weight, cluster.reshape(1, docs))
 
-    got_small = lax.all_to_all(
-        small_sent.reshape(devices, cap_small, feature), ("docs", "blk"),
-        split_axis=0, concat_axis=0, tiled=True).reshape(small_slots, feature)
+    got_small = lax.all_to_all(small_sent, ("docs", "blk"), split_axis=0, concat_axis=0, tiled=True)
 
     big_sent = call(
         functools.partial(sort_big_kernel, shards, blocks, cap_big),
-        [((cap_big + 16, feature), bf16, vmem)] * shards + [((rows_up(shards), LANES), f32, vmem)] * blocks,
-        [smem, smem, vmem, vmem],
+        [((cap_big + 16, feature), bf16, vmem)] * shards,
+        [smem, vmem, vmem],
         2 * docs * feature * big_slots, 2 << 20,
-    )(docs_at, blk_at, rows, info)
-    big_sent, tables = big_sent[:shards], big_sent[shards:]
-    tables = [tables[0]] + [along(tables[by], "blk", blocks, by) for by in range(1, blocks)]
+    )(docs_at, rows, info)
     held = [big_sent[0]] + [along(big_sent[by], "docs", shards, by) for by in range(1, shards)]
-
     group, = call(
         functools.partial(group_kernel, cap_big),
         [((big_slots + rows_up(shards, 16), feature), bf16, vmem)], [vmem] * shards,
@@ -332,33 +331,24 @@
                  for d in range(shards)]
         parts.append(lax.ppermute(group, ("docs", "blk"), pairs))
 
-    def turned(tables):
-        tables = call(
-            functools.partial(turn_kernel, shards),
-            [((rows_up(blocks), LANES), f32, vmem)] * shards, [smem] + [vmem] * blocks,
-            shards * blocks * LANES, 1 << 16,
-        )(docs_at, *tables)
-        return [tables[0]] + [along(tables[by], "docs", shards, by) for by in range(1, shards)]
-
-    tables = turned(tables)
-    small_ids, = call(
-        functools.partial(ids_kernel, shards, blocks, cap_small),
-        [((1, small_slots), f32, vmem)], [smem, smem] + [vmem] * shards,
-        2 * rows_up(blocks) * shards * LANES * small_slots, 1 << 16,
-    )(docs_at, blk_at, *tables)
-
     back_small, = call(
         functools.partial(small_kernel, shards, blocks, cap_small),
-        [((blocks * rows_up(shards), LANES), f32, vmem)], [smem, vmem, vmem],
-        2 * small_slots * small_slots * feature, 2 << 20,
-    )(blk_at, got_small, small_ids)
+        [((blocks * rows_up(shards), LANES), f32, vmem)], [smem, vmem],
+        2 * small_slots * small_slots * feature, 2 << 20, 16,
+        [vmem((small_slots, feature), bf16)],
+    )(blk_at, got_small)
     back = call(
         functools.partial(big_kernel, *sizes),
         [((rows_up(shards), LANES), f32, vmem)] * blocks, [smem, vmem] + [vmem] * blocks,
         2 * big_total * big_total * feature, 2 << 20,
     )(docs_at, back_small, *parts)
     back = [back[0]] + [along(back[by], "blk", blocks, by) for by in range(1, blocks)]
-    back = turned(back)
+    back = call(
+        functools.partial(turn_kernel, shards),
+        [((rows_up(blocks), LANES), f32, vmem)] * shards, [smem] + [vmem] * blocks,
+        shards * blocks * LANES, 1 << 16,
+    )(docs_at, *back)
+    back = [back[0]] + [along(back[by], "docs", shards, by) for by in range(1, shards)]
 
     masks = call(
         functools.partial(masks_kernel, shards, blocks),

time: 71 us -> 64.6 us (0.910)
  starting transfers between devices: 25.7 us -> 21.7 us
  waiting for transfers between devices: 34.8 us -> 32.7 us
    ppermute x15 -> x9, waiting for transfers between devices: 34.8 us -> 21.1 us  [along(): return lax.ppermute(x, axis, [(i, (i + by) % count) for i in range(count)])]
    all_to_all x1, waiting for transfers between devices: 0.01 us -> 11.6 us  [body(): lax.all_to_all(small_sent, ('docs', 'blk'), split_axis=0, concat_axis=0,...]
    ppermute x15 -> x9, starting transfers between devices: 15.4 us -> 11.6 us  [along(): return lax.ppermute(x, axis, [(i, (i + by) % count) for i in range(count)])]
    pallas_call x4 -> x2, Pallas kernels: 4.62 us -> 4.39 us  [the longest x1 4.37 us: body(): call(functools.partial(sort_kernel, *sizes), [((devices, small_rows, LANE...]
  transfers between devices with their start and end apart: 19 -> 13, of which waited for: 13 -> 8; matrix products, arithmetic and copies ran while one was open for 0% -> 0% of each run, Pallas kernels for 4% -> 4%
where the time goes in v10:
time: 64.6 us; the launch traced here: 64.3 us
  waiting for transfers between devices  32.7 us (51%)
  starting transfers between devices  21.7 us (34%)
  Pallas kernels  9.76 us (15%)
    ppermute x9, waiting for transfers between devices, along(): return lax.ppermute(x, axis, [(i, (i + by) % count) for i in range(count)])  21.1 us
    all_to_all x1, waiting for transfers between devices, body(): lax.all_to_all(small_sent, ('docs', 'blk'), split_axis=0, concat_axis=0,...  11.6 us
    ppermute x9, starting transfers between devices, along(): return lax.ppermute(x, axis, [(i, (i + by) % count) for i in range(count)])  11.6 us
    all_to_all x1, starting transfers between devices, body(): lax.all_to_all(small_sent, ('docs', 'blk'), split_axis=0, concat_axis=0,...  7.47 us
    pallas_call x1, Pallas kernels, body(): call(functools.partial(sort_kernel, *sizes), [((devices, small_rows, LANE...  4.37 us
    ppermute x3, starting transfers between devices, body(): parts.append(lax.ppermute(group, ('docs', 'blk'), pairs))  2.69 us
    pallas_call x1, Pallas kernels, body(): call(functools.partial(big_kernel, *sizes), [((rows_up(shards), LANES), f...  2.24 us
    pallas_call x1, Pallas kernels, body(): call(functools.partial(small_kernel, shards, blocks, cap_small), [((block...  1.47 us
  transfers between devices with their start and end apart: 13, of which 8 were waited for; matrix products, arithmetic and copies ran while one was open for 0% of the time, Pallas kernels for 4%

profile of v10, /device:TPU:1, one launch (start us, length us, event | category | flops | bytes accessed | tf_op | source)
XLA Modules:
  0.0 64.3 jit_solution(17714684317006232157)
XLA Ops:
  0.0 4.4 %shard_map.37 = (bf16[16,304,128]{2,1,0:T(8,128)(2,1)}, bf16[512,768]{1,0:T(8,128)(2,1)}, s32[8,512]{1,0:T(8,128)}) custom-call(bf16[512,768]{1,0:T(8,128)(2,1)} %pooled_hbm.1, bf16[768,768]{1,0:T(8,128)(2,1)} %weight_hbm.1, s32[1,512]{1,0:T(1,128)} %bitcast.4), custom_call_target="tpu_custom_call" | custom-call | flops 1207959552 | bytes 4194304 | tf_op jit(solution)/shard_map/pallas_call | solution.py:304
  4.4 0.0 copy-start
  4.4 0.0 copy-start.1
  4.4 7.5 %all-to-all-start = ((bf16[16,304,128]{2,1,0:T(8,128)(2,1)}), bf16[16,304,128]{2,1,0:T(8,128)(2,1)S(1)}, u32[]{:S(2)}, u32[]{:S(2)}) async-start(bf16[16,304,128]{2,1,0:T(8,128)(2,1)} %get-tuple-element.22), calls=%async_computation | async-start | bytes 2490368 | tf_op jit(solution)/shard_map/all_to_all | solution.py:314
  11.9 0.0 copy-done
  11.9 0.0 copy-done.1
  11.9 0.8 %shard_map.39 = (bf16[80,768]{1,0:T(8,128)(2,1)S(1)}, bf16[80,768]{1,0:T(8,128)(2,1)S(1)}, bf16[80,768]{1,0:T(8,128)(2,1)S(1)}, bf16[80,768]{1,0:T(8,128)(2,1)S(1)}) custom-call(s32[1]{0:T(128)} %bitcast.docs_at.at_ref, bf16[512,768]{1,0:T(8,128)(2,1)S(1)} %copy-done, s32[8,512]{1,0:T(8,128)S(1)} %copy-done.1), custom_call_target="tpu_custom_call" | custom-call | flops 201326592 | bytes 2097152 | tf_op jit(solution)/shard_map/pallas_call | solution.py:316
  12.7 1.7 %collective-permute-start = (bf16[80,768]{1,0:T(8,128)(2,1)S(1)}, bf16[80,768]{1,0:T(8,128)(2,1)S(1)}, u32[]{:S(2)}, u32[]{:S(2)}) collective-permute-start(bf16[80,768]{1,0:T(8,128)(2,1)S(1)} %get-tuple-element.26), channel_id=1, source_target_pairs={{0,4},{4,8},{8,12},{12,0},{1,5},{5,9},{9,13},{13,1},{2,6},{6,10},{... | collective-permute-start | bytes 368648 | tf_op jit(solution)/shard_map/ppermute | solution.py:301
  14.4 0.0 collective-permute-start.1
  14.4 0.5 collective-permute-start.2
  14.9 10.9 %collective-permute-done.refs_1_ = bf16[80,768]{1,0:T(8,128)(2,1)S(1)} collective-permute-done((bf16[80,768]{1,0:T(8,128)(2,1)S(1)}, bf16[80,768]{1,0:T(8,128)(2,1)S(1)}, u32[]{:S(2)}, u32[]{:S(2)}) %collective-permute-start) | collective-permute-done | bytes 122912 | tf_op jit(solution)/shard_map/ppermute | solution.py:301
  25.8 5.9 %collective-permute-done.1.refs_2_ = bf16[80,768]{1,0:T(8,128)(2,1)S(1)} collective-permute-done((bf16[80,768]{1,0:T(8,128)(2,1)S(1)}, bf16[80,768]{1,0:T(8,128)(2,1)S(1)}, u32[]{:S(2)}, u32[]{:S(2)}) %collective-permute-start.1) | collective-permute-done | bytes 122912 | tf_op jit(solution)/shard_map/ppermute | solution.py:301
  31.7 0.8 %collective-permute-done.2.refs_3_ = bf16[80,768]{1,0:T(8,128)(2,1)S(1)} collective-permute-done((bf16[80,768]{1,0:T(8,128)(2,1)S(1)}, bf16[80,768]{1,0:T(8,128)(2,1)S(1)}, u32[]{:S(2)}, u32[]{:S(2)}) %collective-permute-start.2) | collective-permute-done | bytes 122912 | tf_op jit(solution)/shard_map/ppermute | solution.py:301
  32.5 0.7 %collective-permute-start.5 = (bf16[272,768]{1,0:T(8,128)(2,1)S(1)}, bf16[272,768]{1,0:T(8,128)(2,1)S(1)}, u32[]{:S(2)}, u32[]{:S(2)}) collective-permute-start(bf16[272,768]{1,0:T(8,128)(2,1)S(1)} %shard_map.40.refs_0_), channel_id=1, source_target_pairs={{0,1},{5,6},{8,9},{13,14},{16,17},{21,22},{24,25},{29,30}} | collective-permute-start | bytes 1253384 | tf_op jit(solution)/shard_map/ppermute | solution.py:332
  33.2 1.3 %collective-permute-start.4 = (bf16[272,768]{1,0:T(8,128)(2,1)S(1)}, bf16[272,768]{1,0:T(8,128)(2,1)S(1)}, u32[]{:S(2)}, u32[]{:S(2)}) collective-permute-start(bf16[272,768]{1,0:T(8,128)(2,1)S(1)} %shard_map.40.refs_0_), channel_id=1, source_target_pairs={{3,1},{4,6},{11,9},{12,14},{19,17},{20,22},{27,25},{28,30}} | collective-permute-start | bytes 1253384 | tf_op jit(solution)/shard_map/ppermute | solution.py:332
  34.5 0.7 %collective-permute-start.3 = (bf16[272,768]{1,0:T(8,128)(2,1)S(1)}, bf16[272,768]{1,0:T(8,128)(2,1)S(1)}, u32[]{:S(2)}, u32[]{:S(2)}) collective-permute-start(bf16[272,768]{1,0:T(8,128)(2,1)S(1)} %shard_map.40.refs_0_), channel_id=1, source_target_pairs={{2,1},{7,6},{10,9},{15,14},{18,17},{23,22},{26,25},{31,30}} | collective-permute-start | bytes 1253384 | tf_op jit(solution)/shard_map/ppermute | solution.py:332
  35.2 11.6 %all-to-all-done.got_ref = bf16[16,304,128]{2,1,0:T(8,128)(2,1)S(1)} async-done(((bf16[16,304,128]{2,1,0:T(8,128)(2,1)}), bf16[16,304,128]{2,1,0:T(8,128)(2,1)S(1)}, u32[]{:S(2)}, u32[]{:S(2)}) %all-to-all-start) | async-done | bytes 1245216 | tf_op jit(solution)/shard_map/all_to_all | solution.py:314
  46.8 1.5 %shard_map.38.small_ref = f32[32,128]{1,0:T(8,128)S(1)} custom-call(s32[1]{0:T(128)} %bitcast.1.blk_at, bf16[16,304,128]{2,1,0:T(8,128)(2,1)S(1)} %all-to-all-done.got_ref), custom_call_target="tpu_custom_call" | custom-call | flops 905969664 | bytes 2097152 | tf_op jit(solution)/shard_map/pallas_call | solution.py:334
  48.3 0.0 collective-permute-done.5.refs_3_
  48.3 0.0 collective-permute-done.4.refs_2_
  48.3 0.0 collective-permute-done.3.refs_1_
  48.3 2.2 %shard_map.41 = (f32[8,128]{1,0:T(8,128)S(1)}, f32[8,128]{1,0:T(8,128)S(1)}, f32[8,128]{1,0:T(8,128)S(1)}, f32[8,128]{1,0:T(8,128)S(1)}) custom-call(s32[1]{0:T(128)} %bitcast.docs_at.at_ref, f32[32,128]{1,0:T(8,128)S(1)} %shard_map.38.small_ref, bf16[272,768]{1,0:T(8,128)(2,1)S(1)} %shard_map.40.refs_0_, ...), custom_call_target="tpu_custom_call" | custom-call | flops 1610612736 | bytes 2097152 | tf_op jit(solution)/shard_map/pallas_call | solution.py:340
  50.6 1.3 %collective-permute-start.6 = (f32[8,128]{1,0:T(8,128)S(1)}, f32[8,128]{1,0:T(8,128)S(1)}, u32[]{:S(2)}, u32[]{:S(2)}) collective-permute-start(f32[8,128]{1,0:T(8,128)S(1)} %get-tuple-element.30), channel_id=1, source_target_pairs={{0,1},{1,2},{2,3},{3,0},{4,5},{5,6},{6,7},{7,4},{8,9},{9,10},{10,1... | collective-permute-start | bytes 12296 | tf_op jit(solution)/shard_map/ppermute | solution.py:301
  51.8 1.7 %collective-permute-start.7 = (f32[8,128]{1,0:T(8,128)S(1)}, f32[8,128]{1,0:T(8,128)S(1)}, u32[]{:S(2)}, u32[]{:S(2)}) collective-permute-start(f32[8,128]{1,0:T(8,128)S(1)} %get-tuple-element.31), channel_id=1, source_target_pairs={{0,2},{1,3},{2,0},{3,1},{4,6},{5,7},{6,4},{7,5},{8,10},{9,11},{10,... | collective-permute-start | bytes 12296 | tf_op jit(solution)/shard_map/ppermute | solution.py:301
  53.5 2.3 %collective-permute-start.8 = (f32[8,128]{1,0:T(8,128)S(1)}, f32[8,128]{1,0:T(8,128)S(1)}, u32[]{:S(2)}, u32[]{:S(2)}) collective-permute-start(f32[8,128]{1,0:T(8,128)S(1)} %get-tuple-element.32), channel_id=1, source_target_pairs={{0,3},{1,0},{2,1},{3,2},{4,7},{5,4},{6,5},{7,6},{8,11},{9,8},{10,9... | collective-permute-start | bytes 12296 | tf_op jit(solution)/shard_map/ppermute | solution.py:301
  55.8 0.0 collective-permute-done.6.refs_1_
  55.8 0.0 collective-permute-done.7.refs_2_
  55.8 0.7 %collective-permute-done.8.refs_3_ = f32[8,128]{1,0:T(8,128)S(1)} collective-permute-done((f32[8,128]{1,0:T(8,128)S(1)}, f32[8,128]{1,0:T(8,128)S(1)}, u32[]{:S(2)}, u32[]{:S(2)}) %collective-permute-start.8) | collective-permute-done | bytes 4128 | tf_op jit(solution)/shard_map/ppermute | solution.py:301
  56.6 3.6 %collective-permute-start.9 = (f32[8,128]{1,0:T(8,128)S(1)}, f32[8,128]{1,0:T(8,128)S(1)}, u32[]{:S(2)}, u32[]{:S(2)}) collective-permute-start(f32[8,128]{1,0:T(8,128)S(1)} %get-tuple-element.34), channel_id=1, source_target_pairs={{0,4},{4,8},{8,12},{12,0},{1,5},{5,9},{9,13},{13,1},{2,6},{6,10},{... | collective-permute-start | bytes 12296 | tf_op jit(solution)/shard_map/ppermute | solution.py:301
  60.2 0.3 collective-permute-start.10
  60.5 0.2 collective-permute-start.11
  60.7 0.2 collective-permute-done.9.refs_1_
  60.9 1.7 %collective-permute-done.10.refs_2_ = f32[8,128]{1,0:T(8,128)S(1)} collective-permute-done((f32[8,128]{1,0:T(8,128)S(1)}, f32[8,128]{1,0:T(8,128)S(1)}, u32[]{:S(2)}, u32[]{:S(2)}) %collective-permute-start.10) | collective-permute-done | bytes 4128 | tf_op jit(solution)/shard_map/ppermute | solution.py:301
  62.6 0.9 %collective-permute-done.11.refs_3_ = f32[8,128]{1,0:T(8,128)S(1)} collective-permute-done((f32[8,128]{1,0:T(8,128)S(1)}, f32[8,128]{1,0:T(8,128)S(1)}, u32[]{:S(2)}, u32[]{:S(2)}) %collective-permute-start.11) | collective-permute-done | bytes 4128 | tf_op jit(solution)/shard_map/ppermute | solution.py:301
  63.5 0.8 %shard_map.44 = f32[1,512]{1,0:T(1,128)} custom-call(f32[8,128]{1,0:T(8,128)S(1)} %get-tuple-element.33.refs_0_, f32[8,128]{1,0:T(8,128)S(1)} %collective-permute-done.9.refs_1_, f32[8,128]{1,0:T(8,128)S(1)} %collective-permute-done.10.refs_2_, f32[8,128]{1,0:T(8,128)S(1)} %collective-permute-done.11.refs_3_, bf16[96,512]{1,0:T(8,128)(2,1)S(1)} %get-tuple-element.37.refs_4_, ...), custom_call_target="tpu_custom_call" | custom-call | flops 6291456 | bytes 262144 | tf_op jit(solution)/shard_map/pallas_call | solution.py:358
  (3 shorter events, 0.1 us)
Async XLA Ops:
  4.4 7.5 %copy-start = (bf16[512,768]{1,0:T(8,128)(2,1)S(1)}, bf16[512,768]{1,0:T(8,128)(2,1)}, u32[]{:S(2)}) copy-start(bf16[512,768]{1,0:T(8,128)(2,1)} %get-tuple-element.23.rows_ref) | copy-start | bytes 2359300
  4.4 7.5 %copy-start.1 = (s32[8,512]{1,0:T(8,128)S(1)}, s32[8,512]{1,0:T(8,128)}, u32[]{:S(2)}) copy-start(s32[8,512]{1,0:T(8,128)} %get-tuple-element.24.info_ref) | copy-start | bytes 49156
  4.4 42.4 %all-to-all-start = ((bf16[16,304,128]{2,1,0:T(8,128)(2,1)}), bf16[16,304,128]{2,1,0:T(8,128)(2,1)S(1)}, u32[]{:S(2)}, u32[]{:S(2)}) async-start(bf16[16,304,128]{2,1,0:T(8,128)(2,1)} %get-tuple-element.22), calls=%async_computation | async-start | bytes 2490368 | tf_op jit(solution)/shard_map/all_to_all | solution.py:314
  12.7 13.2 %collective-permute-start = (bf16[80,768]{1,0:T(8,128)(2,1)S(1)}, bf16[80,768]{1,0:T(8,128)(2,1)S(1)}, u32[]{:S(2)}, u32[]{:S(2)}) collective-permute-start(bf16[80,768]{1,0:T(8,128)(2,1)S(1)} %get-tuple-element.26), channel_id=1, source_target_pairs={{0,4},{4,8},{8,12},{12,0},{1,5},{5,9},{9,13},{13,1},{2,6},{6,10},{... | collective-permute-start | bytes 368648 | tf_op jit(solution)/shard_map/ppermute | solution.py:301
  14.4 17.3 %collective-permute-start.1 = (bf16[80,768]{1,0:T(8,128)(2,1)S(1)}, bf16[80,768]{1,0:T(8,128)(2,1)S(1)}, u32[]{:S(2)}, u32[]{:S(2)}) collective-permute-start(bf16[80,768]{1,0:T(8,128)(2,1)S(1)} %get-tuple-element.27), channel_id=1, source_target_pairs={{0,8},{4,12},{8,0},{12,4},{1,9},{5,13},{9,1},{13,5},{2,10},{6,14},... | collective-permute-start | bytes 368648 | tf_op jit(solution)/shard_map/ppermute | solution.py:301
  14.4 18.1 %collective-permute-start.2 = (bf16[80,768]{1,0:T(8,128)(2,1)S(1)}, bf16[80,768]{1,0:T(8,128)(2,1)S(1)}, u32[]{:S(2)}, u32[]{:S(2)}) collective-permute-start(bf16[80,768]{1,0:T(8,128)(2,1)S(1)} %get-tuple-element.28), channel_id=1, source_target_pairs={{0,12},{4,0},{8,4},{12,8},{1,13},{5,1},{9,5},{13,9},{2,14},{6,2},{... | collective-permute-start | bytes 368648 | tf_op jit(solution)/shard_map/ppermute | solution.py:301
  32.5 15.8 %collective-permute-start.5 = (bf16[272,768]{1,0:T(8,128)(2,1)S(1)}, bf16[272,768]{1,0:T(8,128)(2,1)S(1)}, u32[]{:S(2)}, u32[]{:S(2)}) collective-permute-start(bf16[272,768]{1,0:T(8,128)(2,1)S(1)} %shard_map.40.refs_0_), channel_id=1, source_target_pairs={{0,1},{5,6},{8,9},{13,14},{16,17},{21,22},{24,25},{29,30}} | collective-permute-start | bytes 1253384 | tf_op jit(solution)/shard_map/ppermute | solution.py:332
  33.2 15.1 %collective-permute-start.4 = (bf16[272,768]{1,0:T(8,128)(2,1)S(1)}, bf16[272,768]{1,0:T(8,128)(2,1)S(1)}, u32[]{:S(2)}, u32[]{:S(2)}) collective-permute-start(bf16[272,768]{1,0:T(8,128)(2,1)S(1)} %shard_map.40.refs_0_), channel_id=1, source_target_pairs={{3,1},{4,6},{11,9},{12,14},{19,17},{20,22},{27,25},{28,30}} | collective-permute-start | bytes 1253384 | tf_op jit(solution)/shard_map/ppermute | solution.py:332
  34.5 13.8 %collective-permute-start.3 = (bf16[272,768]{1,0:T(8,128)(2,1)S(1)}, bf16[272,768]{1,0:T(8,128)(2,1)S(1)}, u32[]{:S(2)}, u32[]{:S(2)}) collective-permute-start(bf16[272,768]{1,0:T(8,128)(2,1)S(1)} %shard_map.40.refs_0_), channel_id=1, source_target_pairs={{2,1},{7,6},{10,9},{15,14},{18,17},{23,22},{26,25},{31,30}} | collective-permute-start | bytes 1253384 | tf_op jit(solution)/shard_map/ppermute | solution.py:332
  50.6 5.2 %collective-permute-start.6 = (f32[8,128]{1,0:T(8,128)S(1)}, f32[8,128]{1,0:T(8,128)S(1)}, u32[]{:S(2)}, u32[]{:S(2)}) collective-permute-start(f32[8,128]{1,0:T(8,128)S(1)} %get-tuple-element.30), channel_id=1, source_target_pairs={{0,1},{1,2},{2,3},{3,0},{4,5},{5,6},{6,7},{7,4},{8,9},{9,10},{10,1... | collective-permute-start | bytes 12296 | tf_op jit(solution)/shard_map/ppermute | solution.py:301
  51.8 4.0 %collective-permute-start.7 = (f32[8,128]{1,0:T(8,128)S(1)}, f32[8,128]{1,0:T(8,128)S(1)}, u32[]{:S(2)}, u32[]{:S(2)}) collective-permute-start(f32[8,128]{1,0:T(8,128)S(1)} %get-tuple-element.31), channel_id=1, source_target_pairs={{0,2},{1,3},{2,0},{3,1},{4,6},{5,7},{6,4},{7,5},{8,10},{9,11},{10,... | collective-permute-start | bytes 12296 | tf_op jit(solution)/shard_map/ppermute | solution.py:301
  53.5 3.0 %collective-permute-start.8 = (f32[8,128]{1,0:T(8,128)S(1)}, f32[8,128]{1,0:T(8,128)S(1)}, u32[]{:S(2)}, u32[]{:S(2)}) collective-permute-start(f32[8,128]{1,0:T(8,128)S(1)} %get-tuple-element.32), channel_id=1, source_target_pairs={{0,3},{1,0},{2,1},{3,2},{4,7},{5,4},{6,5},{7,6},{8,11},{9,8},{10,9... | collective-permute-start | bytes 12296 | tf_op jit(solution)/shard_map/ppermute | solution.py:301
  56.6 4.4 %collective-permute-start.9 = (f32[8,128]{1,0:T(8,128)S(1)}, f32[8,128]{1,0:T(8,128)S(1)}, u32[]{:S(2)}, u32[]{:S(2)}) collective-permute-start(f32[8,128]{1,0:T(8,128)S(1)} %get-tuple-element.34), channel_id=1, source_target_pairs={{0,4},{4,8},{8,12},{12,0},{1,5},{5,9},{9,13},{13,1},{2,6},{6,10},{... | collective-permute-start | bytes 12296 | tf_op jit(solution)/shard_map/ppermute | solution.py:301
  60.2 2.5 %collective-permute-start.10 = (f32[8,128]{1,0:T(8,128)S(1)}, f32[8,128]{1,0:T(8,128)S(1)}, u32[]{:S(2)}, u32[]{:S(2)}) collective-permute-start(f32[8,128]{1,0:T(8,128)S(1)} %get-tuple-element.35), channel_id=1, source_target_pairs={{0,8},{4,12},{8,0},{12,4},{1,9},{5,13},{9,1},{13,5},{2,10},{6,14},... | collective-permute-start | bytes 12296 | tf_op jit(solution)/shard_map/ppermute | solution.py:301
  60.5 3.0 %collective-permute-start.11 = (f32[8,128]{1,0:T(8,128)S(1)}, f32[8,128]{1,0:T(8,128)S(1)}, u32[]{:S(2)}, u32[]{:S(2)}) collective-permute-start(f32[8,128]{1,0:T(8,128)S(1)} %get-tuple-element.36), channel_id=1, source_target_pairs={{0,12},{4,0},{8,4},{12,8},{1,13},{5,1},{9,5},{13,9},{2,14},{6,2},{... | collective-permute-start | bytes 12296 | tf_op jit(solution)/shard_map/ppermute | solution.py:301

commit v11 on v10

--- a/solution.py
+++ b/solution.py
@@ -45,8 +45,14 @@
     return jnp.dot(pick, rows_ref[...], preferred_element_type=jnp.float32).astype(jnp.bfloat16)
 
 
-def sort_kernel(shards, blocks, cap_big, cap_small, pooled_hbm, weight_hbm, cluster_hbm, small_hbm, rows_hbm, info_hbm,
-                pooled_ref, weight_ref, cluster_ref, small_ref, rows_ref, info_ref, sems, small_sems):
+def kinds_of(shards, blocks):
+    return 2 if blocks > 1 and shards > 1 else 1
+
+
+def sort_kernel(shards, blocks, cap_big, cap_small, blk_at, pooled_hbm, weight_hbm, cluster_hbm, small_hbm, info_hbm,
+                *refs):
+    big_hbm = refs[:blocks]
+    pooled_ref, weight_ref, cluster_ref, small_ref, big_ref, rows_ref, info_ref, sems, small_sems, big_sems = refs[blocks:]
     docs, feature = rows_ref.shape
     devices = shards * blocks
     limit = BIG_OWN * shards
@@ -73,22 +79,32 @@
 
     info_ref[0:1, :] = jnp.where(is_big, owner * blocks + home_of(owner, blocks), target)
     info_ref[1:2, :] = jnp.where(is_big, cap_small + rank, rank)
-    info_ref[2:3, :] = jnp.where(is_big, owner * cap_big + rank, -1)
-    info_ref[3:4, :] = jnp.where(is_big, quotient(cluster, shards), quotient(past, devices)) + 1
-    info_ref[4:5, :] = bucket
-    info_ref[5:8, :] = jnp.zeros((3, docs), jnp.int32)
+    info_ref[2:3, :] = jnp.where(is_big, quotient(cluster, shards), quotient(past, devices)) + 1
+    info_ref[3:8, :] = jnp.zeros((5, docs), jnp.int32)
     sends = [pltpu.make_async_copy(info_ref, info_hbm, sems.at[3])]
     sends[0].start()
     small_slot = jnp.where(is_big, -1, target * cap_small + rank)
     ids = ids_table(iota((devices, docs), 0) == bucket, info_ref)
+    kinds = kinds_of(shards, blocks)
+    half = shards // kinds * cap_big
+    big_slot = jnp.where(is_big, modulo(owner, kinds) * half + quotient(owner, kinds) * cap_big + rank, -1)
+    for kind in range(kinds):
+        index = iota((big_ref.shape[1] - half, docs), 0)
+        mine = (index < shards // kinds) & (index * kinds + (devices + kind) == bucket)
+        big_ref[kind, half:, 0:LANES] = ids_table(mine, info_ref).astype(jnp.bfloat16)
+        big_ref[kind, half:, LANES:] = jnp.zeros((index.shape[0], feature - LANES), jnp.bfloat16)
 
     for fetch in fetches[1:]:
         fetch.wait()
     projected = jnp.dot(pooled_ref[...], weight_ref[...], preferred_element_type=jnp.float32)
     squares = jnp.sum(projected * projected, axis=1, keepdims=True)
     rows_ref[...] = (projected / jnp.sqrt(squares + 1e-06)).astype(jnp.bfloat16)
-    sends.append(pltpu.make_async_copy(rows_ref, rows_hbm, sems.at[4]))
-    sends[-1].start()
+    for kind in range(kinds):
+        big_ref[kind, 0:half, :] = picked_rows(rows_ref, big_slot, kind * half, half)
+    for step, out in enumerate(big_hbm):
+        kind = kind_of(blk_at[0] + blocks - step, blocks, kinds)
+        sends.append(pltpu.make_async_copy(big_ref.at[kind], out, big_sems.at[step]))
+        sends[-1].start()
 
     slabs = feature // LANES
     group = devices // small_sems.shape[0]
@@ -110,33 +126,32 @@
 
 def ids_table(mine, info_ref):
     docs = info_ref.shape[1]
-    quota = info_ref[3:4, :].astype(jnp.float32)
+    quota = info_ref[2:3, :].astype(jnp.float32)
     lanes = (iota((LANES, docs), 0) == info_ref[1:2, :]).astype(jnp.float32).astype(jnp.bfloat16)
     return dot_nt(jnp.where(mine, quota, 0.0).astype(jnp.bfloat16), lanes)
 
 
-def sort_big_kernel(shards, blocks, cap_big, docs_at, rows_ref, info_ref, *big_refs):
-    devices = shards * blocks
-    for shift, ref in enumerate(big_refs):
-        to = modulo(docs_at[0] + shift, shards)
-        ref[0:cap_big, :] = picked_rows(rows_ref, info_ref[2:3, :], to * cap_big, cap_big)
-        spare = ref.shape[0] - cap_big
-        mine = (iota((spare, info_ref.shape[1]), 0) == 0) & (info_ref[4:5, :] == devices + to)
-        ref[cap_big:, 0:LANES] = ids_table(mine, info_ref).astype(jnp.bfloat16)
-        ref[cap_big:, LANES:] = jnp.zeros((spare, ref.shape[1] - LANES), jnp.bfloat16)
-
-
-def group_kernel(cap_big, *refs):
-    held, group_ref = refs[:-1], refs[-1]
-    total = len(held) * cap_big
-    spare = group_ref.shape[0] - total
-    own = jnp.zeros((spare, LANES), jnp.float32)
-    for shift, ref in enumerate(held):
-        group_ref[shift * cap_big:(shift + 1) * cap_big, :] = ref[0:cap_big, :]
-        table = ref[cap_big:, 0:LANES].astype(jnp.float32)
-        own = jnp.where(iota(own.shape, 0) == shift, table[0:1, :], own)
-    group_ref[total:, 0:LANES] = own.astype(jnp.bfloat16)
-    group_ref[total:, LANES:] = jnp.zeros((spare, group_ref.shape[1] - LANES), jnp.bfloat16)
+def kind_of(blk, blocks, kinds):
+    return jnp.where(modulo(blk, blocks) == home_of(1, blocks), kinds - 1, 0)
+
+
+def group_kernel(shards, blocks, cap_big, docs_at, small_in, *refs):
+    held, outs = refs[:blocks], refs[blocks + 1:]
+    kinds = kinds_of(shards, blocks)
+    half = shards // kinds * cap_big
+    total = blocks * cap_big
+    tables = [block[half:, 0:LANES].astype(jnp.float32) for block in held]
+    for shift, out in enumerate(outs):
+        place = quotient(modulo(docs_at[0] + shards - shift, shards), kinds)
+        at = pl.multiple_of(place * cap_big, cap_big)
+        spare = out.shape[0] - total
+        own = jnp.zeros((spare, LANES), jnp.float32)
+        for step, block in enumerate(held):
+            out[step * cap_big:(step + 1) * cap_big, :] = block[pl.ds(at, cap_big), :]
+            ids = jnp.sum(jnp.where(iota(tables[step].shape, 0) == place, tables[step], 0.0), axis=0, keepdims=True)
+            own = jnp.where(iota(own.shape, 0) == step, ids, own)
+        out[total:, 0:LANES] = own.astype(jnp.bfloat16)
+        out[total:, LANES:] = jnp.zeros((spare, out.shape[1] - LANES), jnp.bfloat16)
 
 
 def turn(tables, at, count, outs):
@@ -163,9 +178,9 @@
     return source // blocks, modulo(source, blocks), lax.rem(at, jnp.int32(cap_small))
 
 
-def big_sources(total, shards, cap_big, cap_small):
+def big_sources(total, blocks, cap_big, cap_small):
     at = iota((1, total), 1)
-    return (at // (shards * cap_big), modulo(at // cap_big, shards),
+    return (at // (blocks * cap_big), modulo(at // cap_big, blocks),
             cap_small + lax.rem(at, jnp.int32(cap_big)))
 
 
@@ -203,14 +218,14 @@
     return jnp.concatenate([high, middle, low], axis=0)
 
 
-def big_kernel(shards, blocks, cap_big, cap_small, docs_at, small_ref, *refs):
-    held, back_refs = refs[:blocks], refs[blocks:]
-    size = shards * cap_big
+def big_kernel(shards, blocks, cap_big, cap_small, docs_at, *refs):
+    held, back_ref = refs[:-1], refs[-1]
+    size = blocks * cap_big
     spare = held[0].shape[0] - size
-    high = back_refs[0].shape[0]
-    step, shift, lane = big_sources(blocks * size, shards, cap_big, cap_small)
+    high = back_ref.shape[0] // blocks
+    shift, step, lane = big_sources(shards * size, blocks, cap_big, cap_small)
     values = jnp.concatenate([ref[size:, 0:LANES] for ref in held], axis=0)
-    row_ids = ids_from(values, step * spare + shift, lane)
+    row_ids = ids_from(values, shift * spare + step, lane)
     col_ids = as_column(row_ids)
     bests = [jnp.full((1, size), -1.0, jnp.float32) for _ in held]
     for row, queries in enumerate(held):
@@ -219,15 +234,14 @@
             bests[col] = jnp.maximum(bests[col], block_best(
                 queries[0:size, :], col_ids[row * size:(row + 1) * size], same,
                 others[0:size, :], row_ids[:, col * size:(col + 1) * size], same))
-    docs = modulo(docs_at[0] + shards - shift, shards)
-    back = small_ref[...] + spread(jnp.concatenate(bests, axis=1), step * high + docs, lane, small_ref.shape[0])
-    for step, ref in enumerate(back_refs):
-        ref[...] = back[step * high:(step + 1) * high, :]
-
-
-def small_kernel(shards, blocks, cap_small, blk_at, got_ref, back_ref, rows_ref):
+    row = step * high + modulo(docs_at[0] + shift, shards)
+    back_ref[...] = spread(jnp.concatenate(bests, axis=1), row, lane, back_ref.shape[0])
+
+
+def small_kernel(shards, blocks, cap_small, blk_at, got_ref, big_ref, *refs):
+    back_refs, rows_ref = refs[:-1], refs[-1]
     total, feature = rows_ref.shape
-    high = back_ref.shape[0] // blocks
+    high = back_refs[0].shape[0]
     slabs = feature // LANES
     values = []
     for device in range(got_ref.shape[0]):
@@ -244,7 +258,9 @@
         best = jnp.maximum(best, block_best(
             rows_ref[at:at + tile, :], col_ids[at:at + tile], at, rows_ref[...], row_ids, 0))
     row = modulo(blk + blocks - blk_at[0], blocks) * high + docs
-    back_ref[...] = spread(best, row, lane, back_ref.shape[0])
+    back = big_ref[...] + spread(best, row, lane, big_ref.shape[0])
+    for step, ref in enumerate(back_refs):
+        ref[...] = back[step * high:(step + 1) * high, :]
 
 
 def masks_kernel(shards, blocks, docs_at, blk_at, info_ref, row_ref, lane_ref):
@@ -264,7 +280,7 @@
     out_ref[...] = jnp.sum(jnp.where(lane_ref[...] > 0.0, found, 0.0), axis=0, keepdims=True)
 
 
-def call(kernel, outs, ins, flops, moved, limit=16, scratch=()):
+def call(kernel, outs, ins, flops, moved, limit=16, scratch=(), aliases=None):
     specs = [pl.BlockSpec(memory_space=space) for _, _, space in outs]
     return pl.pallas_call(
         kernel,
@@ -273,6 +289,7 @@
         in_specs=[pl.BlockSpec(memory_space=space) for space in ins],
         out_specs=specs,
         scratch_shapes=scratch,
+        input_output_aliases=aliases or {},
         cost_estimate=pl.CostEstimate(flops=flops, bytes_accessed=moved, transcendentals=0),
         compiler_params=pltpu.CompilerParams(vmem_limit_bytes=limit << 20),
     )
@@ -301,47 +318,52 @@
         return lax.ppermute(x, axis, [(i, (i + by) % count) for i in range(count)])
 
     small_rows = feature // LANES * cap_small + 16
-    small_sent, rows, info = call(
+    small_rows = feature // LANES * cap_small + 16
+    kinds = kinds_of(shards, blocks)
+    big_rows = big_slots // kinds + rows_up(shards // kinds, 16)
+    small_sent, info, *big_sent = call(
         functools.partial(sort_kernel, *sizes),
-        [((devices, small_rows, LANES), bf16, hbm), ((docs, feature), bf16, hbm), ((8, docs), i32, hbm)],
-        [hbm, hbm, hbm],
+        [((devices, small_rows, LANES), bf16, hbm), ((8, docs), i32, hbm)] + [((big_rows, feature), bf16, hbm)] * blocks,
+        [smem, hbm, hbm, hbm],
         2 * docs * feature * (pooled.shape[1] + small_slots), 4 << 20, 60,
         [vmem(pooled.shape, bf16), vmem(proj_weight.shape, bf16), vmem((1, docs), i32),
-         vmem((devices, small_rows, LANES), bf16), vmem((docs, feature), bf16), vmem((8, docs), i32),
-         dma((5,)), dma((4,))],
-    )(pooled, proj_weight, cluster.reshape(1, docs))
+         vmem((devices, small_rows, LANES), bf16), vmem((kinds, big_rows, feature), bf16),
+         vmem((docs, feature), bf16), vmem((8, docs), i32), dma((4,)), dma((4,)), dma((blocks,))],
+    )(blk_at, pooled, proj_weight, cluster.reshape(1, docs))
+
+    homes = [home_of(d, blocks) for d in range(kinds)]
+    big_held = [big_sent[0]]
+    for step in range(1, blocks):
+        pairs = [(d * blocks + (home + step) % blocks, d * blocks + home) for d in range(shards) for home in homes]
+        big_held.append(lax.ppermute(big_sent[step], ("docs", "blk"), pairs))
+
+    small_sent, *grouped = call(
+        functools.partial(group_kernel, shards, blocks, cap_big),
+        [((devices, small_rows, LANES), bf16, hbm)]
+        + [((blocks * cap_big + rows_up(blocks, 16), feature), bf16, vmem)] * shards,
+        [smem, hbm] + [vmem] * blocks,
+        shards * blocks * cap_big * feature, 4 << 20, aliases={1: 0},
+    )(docs_at, small_sent, *big_held)
 
     got_small = lax.all_to_all(small_sent, ("docs", "blk"), split_axis=0, concat_axis=0, tiled=True)
 
-    big_sent = call(
-        functools.partial(sort_big_kernel, shards, blocks, cap_big),
-        [((cap_big + 16, feature), bf16, vmem)] * shards,
-        [smem, vmem, vmem],
-        2 * docs * feature * big_slots, 2 << 20,
-    )(docs_at, rows, info)
-    held = [big_sent[0]] + [along(big_sent[by], "docs", shards, by) for by in range(1, shards)]
-    group, = call(
-        functools.partial(group_kernel, cap_big),
-        [((big_slots + rows_up(shards, 16), feature), bf16, vmem)], [vmem] * shards,
-        big_slots * feature, 1 << 20,
-    )(*held)
-    parts = [group]
-    for step in range(1, blocks):
-        pairs = [(d * blocks + (home_of(d, blocks) + step) % blocks, d * blocks + home_of(d, blocks))
+    parts = [grouped[0]]
+    for shift in range(1, shards):
+        pairs = [((d + shift) % shards * blocks + home_of(d, blocks), d * blocks + home_of(d, blocks))
                  for d in range(shards)]
-        parts.append(lax.ppermute(group, ("docs", "blk"), pairs))
-
-    back_small, = call(
+        parts.append(lax.ppermute(grouped[shift], ("docs", "blk"), pairs))
+
+    back_big, = call(
+        functools.partial(big_kernel, *sizes),
+        [((blocks * rows_up(shards), LANES), f32, vmem)], [smem] + [vmem] * shards,
+        2 * big_total * big_total * feature, 2 << 20,
+    )(docs_at, *parts)
+    back = call(
         functools.partial(small_kernel, shards, blocks, cap_small),
-        [((blocks * rows_up(shards), LANES), f32, vmem)], [smem, vmem],
+        [((rows_up(shards), LANES), f32, vmem)] * blocks, [smem, vmem, vmem],
         2 * small_slots * small_slots * feature, 2 << 20, 16,
         [vmem((small_slots, feature), bf16)],
-    )(blk_at, got_small)
-    back = call(
-        functools.partial(big_kernel, *sizes),
-        [((rows_up(shards), LANES), f32, vmem)] * blocks, [smem, vmem] + [vmem] * blocks,
-        2 * big_total * big_total * feature, 2 << 20,
-    )(docs_at, back_small, *parts)
+    )(blk_at, got_small, back_big)
     back = [back[0]] + [along(back[by], "blk", blocks, by) for by in range(1, blocks)]
     back = call(
         functools.partial(turn_kernel, shards),

time: 64.6 us -> 73 us (1.13)
  waiting for transfers between devices: 32.7 us -> 36.8 us
  starting transfers between devices: 21.7 us -> 24.8 us
  local copies, waits for them, and re-layouts: 0.01 us -> 0.94 us
    ppermute x9 -> x6, waiting for transfers between devices: 21.1 us -> 3.1 us  [along(): return lax.ppermute(x, axis, [(i, (i + by) % count) for i in range(count)])]
    all_to_all x1, waiting for transfers between devices: 11.6 us -> 26.2 us  [body(): lax.all_to_all(small_sent, ('docs', 'blk'), split_axis=0, concat_axis=0,...]
    ppermute x3 -> x6, starting transfers between devices: 2.69 us -> 10.5 us  [the longest x3 8.44 us: body(): big_held.append(lax.ppermute(big_sent[step], ('docs', 'blk'), pairs))]
    ppermute x3 -> x6, waiting for transfers between devices: 0.02 us -> 7.53 us  [the longest x3 7.52 us: body(): big_held.append(lax.ppermute(big_sent[step], ('docs', 'blk'), pairs))]
    ppermute x9 -> x6, starting transfers between devices: 11.6 us -> 6.97 us  [along(): return lax.ppermute(x, axis, [(i, (i + by) % count) for i in range(count)])]
    unnamed x4, local copies, waits for them, and re-layouts: 0.01 us -> 0.94 us
    pallas_call x4 -> x3, Pallas kernels: 4.54 us -> 3.79 us  [the longest x1 2.17 us: body(): call(functools.partial(big_kernel, *sizes), [((blocks * rows_up(shards),...]
  transfers between devices with their start and end apart: 13 -> 13, of which waited for: 8 -> 6; matrix products, arithmetic and copies ran while one was open for 0% -> 0% of each run, Pallas kernels for 4% -> 3%
where the time goes in v11:
time: 73 us; the launch traced here: 72.2 us
  waiting for transfers between devices  36.8 us (50%)
  starting transfers between devices  24.8 us (34%)
  Pallas kernels  9.5 us (13%)
  local copies, waits for them, and re-layouts  0.94 us (1%)
    all_to_all x1, waiting for transfers between devices, body(): lax.all_to_all(small_sent, ('docs', 'blk'), split_axis=0, concat_axis=0,...  26.2 us
    ppermute x3, starting transfers between devices, body(): big_held.append(lax.ppermute(big_sent[step], ('docs', 'blk'), pairs))  8.44 us
    ppermute x3, waiting for transfers between devices, body(): big_held.append(lax.ppermute(big_sent[step], ('docs', 'blk'), pairs))  7.52 us
    all_to_all x1, starting transfers between devices, body(): lax.all_to_all(small_sent, ('docs', 'blk'), split_axis=0, concat_axis=0,...  7.32 us
    ppermute x6, starting transfers between devices, along(): return lax.ppermute(x, axis, [(i, (i + by) % count) for i in range(count)])  6.97 us
    pallas_call x1, Pallas kernels, body(): call(functools.partial(sort_kernel, *sizes), [((devices, small_rows, LANE...  4.86 us
    ppermute x6, waiting for transfers between devices, along(): return lax.ppermute(x, axis, [(i, (i + by) % count) for i in range(count)])  3.1 us
    pallas_call x1, Pallas kernels, body(): call(functools.partial(big_kernel, *sizes), [((blocks * rows_up(shards),...  2.17 us
  transfers between devices with their start and end apart: 13, of which 6 were waited for; matrix products, arithmetic and copies ran while one was open for 0% of the time, Pallas kernels for 3%

profile of v11, /device:TPU:1, one launch (start us, length us, event | category | flops | bytes accessed | tf_op | source)
XLA Modules:
  0.0 72.2 jit_solution(4273355931199260927)
XLA Ops:
  0.0 4.9 %shard_map.37 = (bf16[16,304,128]{2,1,0:T(8,128)(2,1)}, s32[8,512]{1,0:T(8,128)}, bf16[144,768]{1,0:T(8,128)(2,1)}, bf16[144,768]{1,0:T(8,128)(2,1)}, bf16[144,7...) custom-call(s32[1]{0:T(128)} %bitcast.1.blk_at, bf16[512,768]{1,0:T(8,128)(2,1)} %pooled_hbm.1, bf16[768,768]{1,0:T(8,128)(2,1)} %weight_hbm.1, ...), custom_call_target="tpu_custom_call" | custom-call | flops 1207959552 | bytes 4194304 | tf_op jit(solution)/shard_map/pallas_call | solution.py:324
  4.9 0.7 collective-permute-start
  5.6 6.5 %collective-permute-start.1 = (bf16[144,768]{1,0:T(8,128)(2,1)}, bf16[144,768]{1,0:T(8,128)(2,1)S(1)}, u32[]{:S(2)}, u32[]{:S(2)}) collective-permute-start(bf16[144,768]{1,0:T(8,128)(2,1)} %get-tuple-element.29), channel_id=1, source_target_pairs={{3,1},{0,2},{7,5},{4,6},{11,9},{8,10},{15,13},{12,14},{19,17},{16,... | collective-permute-start | bytes 663560 | tf_op jit(solution)/shard_map/ppermute | solution.py:338
  12.0 1.3 %collective-permute-start.2 = (bf16[144,768]{1,0:T(8,128)(2,1)}, bf16[144,768]{1,0:T(8,128)(2,1)S(1)}, u32[]{:S(2)}, u32[]{:S(2)}) collective-permute-start(bf16[144,768]{1,0:T(8,128)(2,1)} %get-tuple-element.30), channel_id=1, source_target_pairs={{0,1},{1,2},{4,5},{5,6},{8,9},{9,10},{12,13},{13,14},{16,17},{17,1... | collective-permute-start | bytes 663560 | tf_op jit(solution)/shard_map/ppermute | solution.py:338
  13.3 0.0 collective-permute-done.refs_1_
  13.3 2.8 %collective-permute-done.1.refs_2_ = bf16[144,768]{1,0:T(8,128)(2,1)S(1)} collective-permute-done((bf16[144,768]{1,0:T(8,128)(2,1)}, bf16[144,768]{1,0:T(8,128)(2,1)S(1)}, u32[]{:S(2)}, u32[]{:S(2)}) %collective-permute-start.1) | collective-permute-done | bytes 221216 | tf_op jit(solution)/shard_map/ppermute | solution.py:338
  16.1 4.7 %collective-permute-done.2.refs_3_ = bf16[144,768]{1,0:T(8,128)(2,1)S(1)} collective-permute-done((bf16[144,768]{1,0:T(8,128)(2,1)}, bf16[144,768]{1,0:T(8,128)(2,1)S(1)}, u32[]{:S(2)}, u32[]{:S(2)}) %collective-permute-start.2) | collective-permute-done | bytes 221216 | tf_op jit(solution)/shard_map/ppermute | solution.py:338
  20.9 0.0 copy-start
  20.9 0.9 %copy-done = bf16[144,768]{1,0:T(8,128)(2,1)S(1)} copy-done((bf16[144,768]{1,0:T(8,128)(2,1)S(1)}, bf16[144,768]{1,0:T(8,128)(2,1)}, u32[]{:S(2)}) %copy-start) | copy-done | bytes 221208
  21.8 0.1 shard_map.38
  21.9 7.3 %all-to-all-start = ((bf16[16,304,128]{2,1,0:T(8,128)(2,1)}), bf16[16,304,128]{2,1,0:T(8,128)(2,1)S(1)}, u32[]{:S(2)}, u32[]{:S(2)}) async-start(bf16[16,304,128]{2,1,0:T(8,128)(2,1)} %get-tuple-element.31), calls=%async_computation | async-start | bytes 2490368 | tf_op jit(solution)/shard_map/all_to_all | solution.py:348
  29.2 0.7 collective-permute-start.3
  29.9 0.7 collective-permute-start.4
  30.6 0.7 collective-permute-start.5
  31.3 0.0 collective-permute-done.3.refs_1_
  31.3 0.0 collective-permute-done.4.refs_2_
  31.3 0.0 collective-permute-done.5.refs_3_
  31.3 2.2 %shard_map.39.big_ref = f32[32,128]{1,0:T(8,128)S(1)} custom-call(s32[1]{0:T(128)} %bitcast.docs_at.at_ref, bf16[272,768]{1,0:T(8,128)(2,1)S(1)} %get-tuple-element.32.refs_0_, bf16[272,768]{1,0:T(8,128)(2,1)S(1)} %collective-permute-done.3.refs_1_, bf16[272,768]{1,0:T(8,128)(2,1)S(1)} %collective-permute-done.4.refs_2_, ...), custom_call_target="tpu_custom_call" | custom-call | flops 1610612736 | bytes 2097152 | tf_op jit(solution)/shard_map/pallas_call | solution.py:356
  33.5 0.0 copy-start.1
  33.5 26.2 %all-to-all-done.got_ref = bf16[16,304,128]{2,1,0:T(8,128)(2,1)S(1)} async-done(((bf16[16,304,128]{2,1,0:T(8,128)(2,1)}), bf16[16,304,128]{2,1,0:T(8,128)(2,1)S(1)}, u32[]{:S(2)}, u32[]{:S(2)}) %all-to-all-start) | async-done | bytes 1245216 | tf_op jit(solution)/shard_map/all_to_all | solution.py:348
  59.7 1.5 %shard_map.40 = (f32[8,128]{1,0:T(8,128)S(1)}, f32[8,128]{1,0:T(8,128)S(1)}, f32[8,128]{1,0:T(8,128)S(1)}, f32[8,128]{1,0:T(8,128)S(1)}) custom-call(s32[1]{0:T(128)} %bitcast.1.blk_at, bf16[16,304,128]{2,1,0:T(8,128)(2,1)S(1)} %all-to-all-done.got_ref, f32[32,128]{1,0:T(8,128)S(1)} %shard_map.39.big_ref), custom_call_target="tpu_custom_call" | custom-call | flops 905969664 | bytes 2097152 | tf_op jit(solution)/shard_map/pallas_call | solution.py:361
  61.2 0.1 collective-permute-start.6
  61.3 1.2 %collective-permute-start.7 = (f32[8,128]{1,0:T(8,128)S(1)}, f32[8,128]{1,0:T(8,128)S(1)}, u32[]{:S(2)}, u32[]{:S(2)}) collective-permute-start(f32[8,128]{1,0:T(8,128)S(1)} %get-tuple-element.38), channel_id=1, source_target_pairs={{0,2},{1,3},{2,0},{3,1},{4,6},{5,7},{6,4},{7,5},{8,10},{9,11},{10,... | collective-permute-start | bytes 12296 | tf_op jit(solution)/shard_map/ppermute | solution.py:318
  62.5 2.1 %collective-permute-start.8 = (f32[8,128]{1,0:T(8,128)S(1)}, f32[8,128]{1,0:T(8,128)S(1)}, u32[]{:S(2)}, u32[]{:S(2)}) collective-permute-start(f32[8,128]{1,0:T(8,128)S(1)} %get-tuple-element.39), channel_id=1, source_target_pairs={{0,3},{1,0},{2,1},{3,2},{4,7},{5,4},{6,5},{7,6},{8,11},{9,8},{10,9... | collective-permute-start | bytes 12296 | tf_op jit(solution)/shard_map/ppermute | solution.py:318
  64.5 1.0 %collective-permute-done.6.refs_1_ = f32[8,128]{1,0:T(8,128)S(1)} collective-permute-done((f32[8,128]{1,0:T(8,128)S(1)}, f32[8,128]{1,0:T(8,128)S(1)}, u32[]{:S(2)}, u32[]{:S(2)}) %collective-permute-start.6) | collective-permute-done | bytes 4128 | tf_op jit(solution)/shard_map/ppermute | solution.py:318
  65.5 0.0 collective-permute-done.7.refs_2_
  65.5 0.6 collective-permute-done.8.refs_3_
  66.1 1.0 %collective-permute-start.10 = (f32[8,128]{1,0:T(8,128)S(1)}, f32[8,128]{1,0:T(8,128)S(1)}, u32[]{:S(2)}, u32[]{:S(2)}) collective-permute-start(f32[8,128]{1,0:T(8,128)S(1)} %get-tuple-element.42), channel_id=1, source_target_pairs={{0,8},{4,12},{8,0},{12,4},{1,9},{5,13},{9,1},{13,5},{2,10},{6,14},... | collective-permute-start | bytes 12296 | tf_op jit(solution)/shard_map/ppermute | solution.py:318
  67.1 1.8 %collective-permute-start.11 = (f32[8,128]{1,0:T(8,128)S(1)}, f32[8,128]{1,0:T(8,128)S(1)}, u32[]{:S(2)}, u32[]{:S(2)}) collective-permute-start(f32[8,128]{1,0:T(8,128)S(1)} %get-tuple-element.43), channel_id=1, source_target_pairs={{0,12},{4,0},{8,4},{12,8},{1,13},{5,1},{9,5},{13,9},{2,14},{6,2},{... | collective-permute-start | bytes 12296 | tf_op jit(solution)/shard_map/ppermute | solution.py:318
  68.9 0.9 %collective-permute-start.9 = (f32[8,128]{1,0:T(8,128)S(1)}, f32[8,128]{1,0:T(8,128)S(1)}, u32[]{:S(2)}, u32[]{:S(2)}) collective-permute-start(f32[8,128]{1,0:T(8,128)S(1)} %get-tuple-element.41), channel_id=1, source_target_pairs={{0,4},{4,8},{8,12},{12,0},{1,5},{5,9},{9,13},{13,1},{2,6},{6,10},{... | collective-permute-start | bytes 12296 | tf_op jit(solution)/shard_map/ppermute | solution.py:318
  69.8 0.0 copy-done.1
  69.8 0.0 collective-permute-done.10.refs_2_
  69.8 1.5 %collective-permute-done.11.refs_3_ = f32[8,128]{1,0:T(8,128)S(1)} collective-permute-done((f32[8,128]{1,0:T(8,128)S(1)}, f32[8,128]{1,0:T(8,128)S(1)}, u32[]{:S(2)}, u32[]{:S(2)}) %collective-permute-start.11) | collective-permute-done | bytes 4128 | tf_op jit(solution)/shard_map/ppermute | solution.py:318
  71.4 0.0 collective-permute-done.9.refs_1_
  71.4 0.8 %shard_map.43 = f32[1,512]{1,0:T(1,128)} custom-call(f32[8,128]{1,0:T(8,128)S(1)} %get-tuple-element.40.refs_0_, f32[8,128]{1,0:T(8,128)S(1)} %collective-permute-done.9.refs_1_, f32[8,128]{1,0:T(8,128)S(1)} %collective-permute-done.10.refs_2_, f32[8,128]{1,0:T(8,128)S(1)} %collective-permute-done.11.refs_3_, bf16[96,512]{1,0:T(8,128)(2,1)S(1)} %get-tuple-element.45.refs_4_, ...), custom_call_target="tpu_custom_call" | custom-call | flops 6291456 | bytes 262144 | tf_op jit(solution)/shard_map/pallas_call | solution.py:380
  (2 shorter events, 0.1 us)
Async XLA Ops:
  4.9 8.5 %collective-permute-start = (bf16[144,768]{1,0:T(8,128)(2,1)}, bf16[144,768]{1,0:T(8,128)(2,1)S(1)}, u32[]{:S(2)}, u32[]{:S(2)}) collective-permute-start(bf16[144,768]{1,0:T(8,128)(2,1)} %get-tuple-element.28), channel_id=1, source_target_pairs={{2,1},{3,2},{6,5},{7,6},{10,9},{11,10},{14,13},{15,14},{18,17},{19... | collective-permute-start | bytes 663560 | tf_op jit(solution)/shard_map/ppermute | solution.py:338
  5.6 10.6 %collective-permute-start.1 = (bf16[144,768]{1,0:T(8,128)(2,1)}, bf16[144,768]{1,0:T(8,128)(2,1)S(1)}, u32[]{:S(2)}, u32[]{:S(2)}) collective-permute-start(bf16[144,768]{1,0:T(8,128)(2,1)} %get-tuple-element.29), channel_id=1, source_target_pairs={{3,1},{0,2},{7,5},{4,6},{11,9},{8,10},{15,13},{12,14},{19,17},{16,... | collective-permute-start | bytes 663560 | tf_op jit(solution)/shard_map/ppermute | solution.py:338
  12.0 8.8 %collective-permute-start.2 = (bf16[144,768]{1,0:T(8,128)(2,1)}, bf16[144,768]{1,0:T(8,128)(2,1)S(1)}, u32[]{:S(2)}, u32[]{:S(2)}) collective-permute-start(bf16[144,768]{1,0:T(8,128)(2,1)} %get-tuple-element.30), channel_id=1, source_target_pairs={{0,1},{1,2},{4,5},{5,6},{8,9},{9,10},{12,13},{13,14},{16,17},{17,1... | collective-permute-start | bytes 663560 | tf_op jit(solution)/shard_map/ppermute | solution.py:338
  20.9 0.9 %copy-start = (bf16[144,768]{1,0:T(8,128)(2,1)S(1)}, bf16[144,768]{1,0:T(8,128)(2,1)}, u32[]{:S(2)}) copy-start(bf16[144,768]{1,0:T(8,128)(2,1)} %get-tuple-element.27.refs_0_) | copy-start | bytes 663556
  21.9 37.8 %all-to-all-start = ((bf16[16,304,128]{2,1,0:T(8,128)(2,1)}), bf16[16,304,128]{2,1,0:T(8,128)(2,1)S(1)}, u32[]{:S(2)}, u32[]{:S(2)}) async-start(bf16[16,304,128]{2,1,0:T(8,128)(2,1)} %get-tuple-element.31), calls=%async_computation | async-start | bytes 2490368 | tf_op jit(solution)/shard_map/all_to_all | solution.py:348
  29.2 2.1 %collective-permute-start.3 = (bf16[272,768]{1,0:T(8,128)(2,1)S(1)}, bf16[272,768]{1,0:T(8,128)(2,1)S(1)}, u32[]{:S(2)}, u32[]{:S(2)}) collective-permute-start(bf16[272,768]{1,0:T(8,128)(2,1)S(1)} %get-tuple-element.33), channel_id=1, source_target_pairs={{5,1},{10,6},{13,9},{2,14},{21,17},{26,22},{29,25},{18,30}} | collective-permute-start | bytes 1253384 | tf_op jit(solution)/shard_map/ppermute | solution.py:354
  29.9 1.4 %collective-permute-start.4 = (bf16[272,768]{1,0:T(8,128)(2,1)S(1)}, bf16[272,768]{1,0:T(8,128)(2,1)S(1)}, u32[]{:S(2)}, u32[]{:S(2)}) collective-permute-start(bf16[272,768]{1,0:T(8,128)(2,1)S(1)} %get-tuple-element.34), channel_id=1, source_target_pairs={{9,1},{14,6},{1,9},{6,14},{25,17},{30,22},{17,25},{22,30}} | collective-permute-start | bytes 1253384 | tf_op jit(solution)/shard_map/ppermute | solution.py:354
  30.6 0.7 collective-permute-start.5
  33.5 36.3 %copy-start.1 = (s32[8,512]{1,0:T(8,128)S(1)}, s32[8,512]{1,0:T(8,128)}, u32[]{:S(2)}) copy-start(s32[8,512]{1,0:T(8,128)} %get-tuple-element.44.info_ref) | copy-start | bytes 49156
  61.2 4.3 %collective-permute-start.6 = (f32[8,128]{1,0:T(8,128)S(1)}, f32[8,128]{1,0:T(8,128)S(1)}, u32[]{:S(2)}, u32[]{:S(2)}) collective-permute-start(f32[8,128]{1,0:T(8,128)S(1)} %get-tuple-element.37), channel_id=1, source_target_pairs={{0,1},{1,2},{2,3},{3,0},{4,5},{5,6},{6,7},{7,4},{8,9},{9,10},{10,1... | collective-permute-start | bytes 12296 | tf_op jit(solution)/shard_map/ppermute | solution.py:318
  61.3 4.2 %collective-permute-start.7 = (f32[8,128]{1,0:T(8,128)S(1)}, f32[8,128]{1,0:T(8,128)S(1)}, u32[]{:S(2)}, u32[]{:S(2)}) collective-permute-start(f32[8,128]{1,0:T(8,128)S(1)} %get-tuple-element.38), channel_id=1, source_target_pairs={{0,2},{1,3},{2,0},{3,1},{4,6},{5,7},{6,4},{7,5},{8,10},{9,11},{10,... | collective-permute-start | bytes 12296 | tf_op jit(solution)/shard_map/ppermute | solution.py:318
  62.5 3.6 %collective-permute-start.8 = (f32[8,128]{1,0:T(8,128)S(1)}, f32[8,128]{1,0:T(8,128)S(1)}, u32[]{:S(2)}, u32[]{:S(2)}) collective-permute-start(f32[8,128]{1,0:T(8,128)S(1)} %get-tuple-element.39), channel_id=1, source_target_pairs={{0,3},{1,0},{2,1},{3,2},{4,7},{5,4},{6,5},{7,6},{8,11},{9,8},{10,9... | collective-permute-start | bytes 12296 | tf_op jit(solution)/shard_map/ppermute | solution.py:318
  66.1 3.7 %collective-permute-start.10 = (f32[8,128]{1,0:T(8,128)S(1)}, f32[8,128]{1,0:T(8,128)S(1)}, u32[]{:S(2)}, u32[]{:S(2)}) collective-permute-start(f32[8,128]{1,0:T(8,128)S(1)} %get-tuple-element.42), channel_id=1, source_target_pairs={{0,8},{4,12},{8,0},{12,4},{1,9},{5,13},{9,1},{13,5},{2,10},{6,14},... | collective-permute-start | bytes 12296 | tf_op jit(solution)/shard_map/ppermute | solution.py:318
  67.1 4.3 %collective-permute-start.11 = (f32[8,128]{1,0:T(8,128)S(1)}, f32[8,128]{1,0:T(8,128)S(1)}, u32[]{:S(2)}, u32[]{:S(2)}) collective-permute-start(f32[8,128]{1,0:T(8,128)S(1)} %get-tuple-element.43), channel_id=1, source_target_pairs={{0,12},{4,0},{8,4},{12,8},{1,13},{5,1},{9,5},{13,9},{2,14},{6,2},{... | collective-permute-start | bytes 12296 | tf_op jit(solution)/shard_map/ppermute | solution.py:318
  68.9 2.5 %collective-permute-start.9 = (f32[8,128]{1,0:T(8,128)S(1)}, f32[8,128]{1,0:T(8,128)S(1)}, u32[]{:S(2)}, u32[]{:S(2)}) collective-permute-start(f32[8,128]{1,0:T(8,128)S(1)} %get-tuple-element.41), channel_id=1, source_target_pairs={{0,4},{4,8},{8,12},{12,0},{1,5},{5,9},{9,13},{13,1},{2,6},{6,10},{... | collective-permute-start | bytes 12296 | tf_op jit(solution)/shard_map/ppermute | solution.py:318

commit v12 on v10

--- a/solution.py
+++ b/solution.py
@@ -86,7 +86,7 @@
         fetch.wait()
     projected = jnp.dot(pooled_ref[...], weight_ref[...], preferred_element_type=jnp.float32)
     squares = jnp.sum(projected * projected, axis=1, keepdims=True)
-    rows_ref[...] = (projected / jnp.sqrt(squares + 1e-06)).astype(jnp.bfloat16)
+    rows_ref[...] = (projected * lax.rsqrt(squares + 1e-06)).astype(jnp.bfloat16)
     sends.append(pltpu.make_async_copy(rows_ref, rows_hbm, sems.at[4]))
     sends[-1].start()
 
@@ -163,10 +163,31 @@
     return source // blocks, modulo(source, blocks), lax.rem(at, jnp.int32(cap_small))
 
 
+def big_steps(blocks):
+    return [0] + list(range(2, blocks)) + ([1] if blocks > 1 else [])
+
+
 def big_sources(total, shards, cap_big, cap_small):
     at = iota((1, total), 1)
     return (at // (shards * cap_big), modulo(at // cap_big, shards),
             cap_small + lax.rem(at, jnp.int32(cap_big)))
+
+
+def big_ids(held, sources):
+    part, shift, lane = sources
+    spare = held[0].shape[0] - part.shape[1] // len(held)
+    values = jnp.concatenate([ref[ref.shape[0] - spare:, 0:LANES] for ref in held], axis=0)
+    return ids_from(values, part * spare + shift, lane)
+
+
+def big_pairs(held, row_ids, col_ids, bests, pairs):
+    size = row_ids.shape[1] // len(held)
+    for row, col in pairs:
+        same = 0 if row == col else None
+        bests[col] = jnp.maximum(bests[col], block_best(
+            held[row][0:size, :], col_ids[row * size:(row + 1) * size], same,
+            held[col][0:size, :], row_ids[:, col * size:(col + 1) * size], same))
+    return bests
 
 
 def ids_from(values, row, lane):
@@ -203,26 +224,32 @@
     return jnp.concatenate([high, middle, low], axis=0)
 
 
-def big_kernel(shards, blocks, cap_big, cap_small, docs_at, small_ref, *refs):
+def big_kernel(shards, cap_big, cap_small, *refs):
+    held, best_ref = refs[:-1], refs[-1]
+    size = shards * cap_big
+    row_ids = big_ids(held, big_sources(len(held) * size, shards, cap_big, cap_small))
+    col_ids = as_column(row_ids)
+    pairs = [(row, col) for row in range(len(held)) for col in range(len(held))]
+    bests = big_pairs(held, row_ids, col_ids, [jnp.full((1, size), -1.0, jnp.float32)] * len(held), pairs)
+    best_ref[...] = jnp.concatenate(bests, axis=1)
+
+
+def big_last_kernel(shards, blocks, cap_big, cap_small, docs_at, small_ref, best_ref, *refs):
     held, back_refs = refs[:blocks], refs[blocks:]
     size = shards * cap_big
-    spare = held[0].shape[0] - size
     high = back_refs[0].shape[0]
-    step, shift, lane = big_sources(blocks * size, shards, cap_big, cap_small)
-    values = jnp.concatenate([ref[size:, 0:LANES] for ref in held], axis=0)
-    row_ids = ids_from(values, step * spare + shift, lane)
+    part, shift, lane = big_sources(blocks * size, shards, cap_big, cap_small)
+    row_ids = big_ids(held, (part, shift, lane))
     col_ids = as_column(row_ids)
-    bests = [jnp.full((1, size), -1.0, jnp.float32) for _ in held]
-    for row, queries in enumerate(held):
-        for col, others in enumerate(held):
-            same = 0 if row == col else None
-            bests[col] = jnp.maximum(bests[col], block_best(
-                queries[0:size, :], col_ids[row * size:(row + 1) * size], same,
-                others[0:size, :], row_ids[:, col * size:(col + 1) * size], same))
+    last = blocks - 1
+    pairs = [(row, last) for row in range(blocks)] + [(last, col) for col in range(last)]
+    bests = [best_ref[:, col * size:(col + 1) * size] for col in range(last)]
+    bests = big_pairs(held, row_ids, col_ids, bests + [jnp.full((1, size), -1.0, jnp.float32)], pairs)
     docs = modulo(docs_at[0] + shards - shift, shards)
+    step = jnp.where(part == 0, 0, jnp.where(part == last, 1, part + 1))
     back = small_ref[...] + spread(jnp.concatenate(bests, axis=1), step * high + docs, lane, small_ref.shape[0])
-    for step, ref in enumerate(back_refs):
-        ref[...] = back[step * high:(step + 1) * high, :]
+    for at, ref in enumerate(back_refs):
+        ref[...] = back[at * high:(at + 1) * high, :]
 
 
 def small_kernel(shards, blocks, cap_small, blk_at, got_ref, back_ref, rows_ref):
@@ -326,7 +353,7 @@
         big_slots * feature, 1 << 20,
     )(*held)
     parts = [group]
-    for step in range(1, blocks):
+    for step in big_steps(blocks)[1:]:
         pairs = [(d * blocks + (home_of(d, blocks) + step) % blocks, d * blocks + home_of(d, blocks))
                  for d in range(shards)]
         parts.append(lax.ppermute(group, ("docs", "blk"), pairs))
@@ -337,11 +364,16 @@
         2 * small_slots * small_slots * feature, 2 << 20, 16,
         [vmem((small_slots, feature), bf16)],
     )(blk_at, got_small)
+    early, = call(
+        functools.partial(big_kernel, shards, cap_big, cap_small),
+        [((1, big_total - big_slots), f32, vmem)], [vmem] * (blocks - 1),
+        2 * (big_total - big_slots) ** 2 * feature, 2 << 20,
+    )(*parts[:-1])
     back = call(
-        functools.partial(big_kernel, *sizes),
-        [((rows_up(shards), LANES), f32, vmem)] * blocks, [smem, vmem] + [vmem] * blocks,
-        2 * big_total * big_total * feature, 2 << 20,
-    )(docs_at, back_small, *parts)
+        functools.partial(big_last_kernel, *sizes),
+        [((rows_up(shards), LANES), f32, vmem)] * blocks, [smem] + [vmem] * (blocks + 2),
+        2 * (2 * big_total - big_slots) * big_slots * feature, 2 << 20,
+    )(docs_at, back_small, early, *parts)
     back = [back[0]] + [along(back[by], "blk", blocks, by) for by in range(1, blocks)]
     back = call(
         functools.partial(turn_kernel, shards),

time: 64.6 us -> 64 us (level)
  waiting for transfers between devices: 32.7 us -> 30.9 us
  starting transfers between devices: 21.7 us -> 22.6 us
    all_to_all x1, waiting for transfers between devices: 11.6 us -> 3.6 us  [body(): lax.all_to_all(small_sent, ('docs', 'blk'), split_axis=0, concat_axis=0,...]
    ppermute x3, waiting for transfers between devices: 0.02 us -> 6.71 us  [body(): parts.append(lax.ppermute(group, ('docs', 'blk'), pairs))]
    ppermute x9, starting transfers between devices: 11.6 us -> 12.5 us  [along(): return lax.ppermute(x, axis, [(i, (i + by) % count) for i in range(count)])]
    pallas_call x1 -> x2, Pallas kernels: 2.24 us -> 2.61 us  [the longest x1 1.35 us: body(): call(functools.partial(big_last_kernel, *sizes), [((rows_up(shards), LANE...]
  transfers between devices with their start and end apart: 13 -> 13, of which waited for: 8 -> 8; matrix products, arithmetic and copies ran while one was open for 0% -> 0% of each run, Pallas kernels for 4% -> 6%
where the time goes in v12:
time: 64 us; the launch traced here: 63.7 us
  waiting for transfers between devices  30.9 us (48%)
  starting transfers between devices  22.6 us (35%)
  Pallas kernels  10.1 us (16%)
    ppermute x9, waiting for transfers between devices, along(): return lax.ppermute(x, axis, [(i, (i + by) % count) for i in range(count)])  20.6 us
    ppermute x9, starting transfers between devices, along(): return lax.ppermute(x, axis, [(i, (i + by) % count) for i in range(count)])  12.5 us
    all_to_all x1, starting transfers between devices, body(): lax.all_to_all(small_sent, ('docs', 'blk'), split_axis=0, concat_axis=0,...  7.47 us
    ppermute x3, waiting for transfers between devices, body(): parts.append(lax.ppermute(group, ('docs', 'blk'), pairs))  6.71 us
    pallas_call x1, Pallas kernels, body(): call(functools.partial(sort_kernel, *sizes), [((devices, small_rows, LANE...  4.33 us
    all_to_all x1, waiting for transfers between devices, body(): lax.all_to_all(small_sent, ('docs', 'blk'), split_axis=0, concat_axis=0,...  3.6 us
    ppermute x3, starting transfers between devices, body(): parts.append(lax.ppermute(group, ('docs', 'blk'), pairs))  2.69 us
    pallas_call x1, Pallas kernels, body(): call(functools.partial(small_kernel, shards, blocks, cap_small), [((block...  1.47 us
  transfers between devices with their start and end apart: 13, of which 8 were waited for; matrix products, arithmetic and copies ran while one was open for 0% of the time, Pallas kernels for 6%

profile of v12, /device:TPU:1, one launch (start us, length us, event | category | flops | bytes accessed | tf_op | source)
XLA Modules:
  0.0 63.7 jit_solution(12772162951255548129)
XLA Ops:
  0.0 4.3 %shard_map.37 = (bf16[16,304,128]{2,1,0:T(8,128)(2,1)}, bf16[512,768]{1,0:T(8,128)(2,1)}, s32[8,512]{1,0:T(8,128)}) custom-call(bf16[512,768]{1,0:T(8,128)(2,1)} %pooled_hbm.1, bf16[768,768]{1,0:T(8,128)(2,1)} %weight_hbm.1, s32[1,512]{1,0:T(1,128)} %bitcast.4), custom_call_target="tpu_custom_call" | custom-call | flops 1207959552 | bytes 4194304 | tf_op jit(solution)/shard_map/pallas_call | solution.py:331
  4.3 0.0 copy-start
  4.3 0.0 copy-start.1
  4.4 7.5 %all-to-all-start = ((bf16[16,304,128]{2,1,0:T(8,128)(2,1)}), bf16[16,304,128]{2,1,0:T(8,128)(2,1)S(1)}, u32[]{:S(2)}, u32[]{:S(2)}) async-start(bf16[16,304,128]{2,1,0:T(8,128)(2,1)} %get-tuple-element.22), calls=%async_computation | async-start | bytes 2490368 | tf_op jit(solution)/shard_map/all_to_all | solution.py:341
  11.8 0.0 copy-done
  11.8 0.0 copy-done.1
  11.8 0.8 %shard_map.39 = (bf16[80,768]{1,0:T(8,128)(2,1)S(1)}, bf16[80,768]{1,0:T(8,128)(2,1)S(1)}, bf16[80,768]{1,0:T(8,128)(2,1)S(1)}, bf16[80,768]{1,0:T(8,128)(2,1)S(1)}) custom-call(s32[1]{0:T(128)} %bitcast.docs_at.at_ref, bf16[512,768]{1,0:T(8,128)(2,1)S(1)} %copy-done, s32[8,512]{1,0:T(8,128)S(1)} %copy-done.1), custom_call_target="tpu_custom_call" | custom-call | flops 201326592 | bytes 2097152 | tf_op jit(solution)/shard_map/pallas_call | solution.py:343
  12.6 1.7 %collective-permute-start = (bf16[80,768]{1,0:T(8,128)(2,1)S(1)}, bf16[80,768]{1,0:T(8,128)(2,1)S(1)}, u32[]{:S(2)}, u32[]{:S(2)}) collective-permute-start(bf16[80,768]{1,0:T(8,128)(2,1)S(1)} %get-tuple-element.26), channel_id=1, source_target_pairs={{0,4},{4,8},{8,12},{12,0},{1,5},{5,9},{9,13},{13,1},{2,6},{6,10},{... | collective-permute-start | bytes 368648 | tf_op jit(solution)/shard_map/ppermute | solution.py:328
  14.3 0.0 collective-permute-start.1
  14.3 0.5 collective-permute-start.2
  14.9 10.9 %collective-permute-done.refs_1_ = bf16[80,768]{1,0:T(8,128)(2,1)S(1)} collective-permute-done((bf16[80,768]{1,0:T(8,128)(2,1)S(1)}, bf16[80,768]{1,0:T(8,128)(2,1)S(1)}, u32[]{:S(2)}, u32[]{:S(2)}) %collective-permute-start) | collective-permute-done | bytes 122912 | tf_op jit(solution)/shard_map/ppermute | solution.py:328
  25.8 5.9 %collective-permute-done.1.refs_2_ = bf16[80,768]{1,0:T(8,128)(2,1)S(1)} collective-permute-done((bf16[80,768]{1,0:T(8,128)(2,1)S(1)}, bf16[80,768]{1,0:T(8,128)(2,1)S(1)}, u32[]{:S(2)}, u32[]{:S(2)}) %collective-permute-start.1) | collective-permute-done | bytes 122912 | tf_op jit(solution)/shard_map/ppermute | solution.py:328
  31.7 0.8 %collective-permute-done.2.refs_3_ = bf16[80,768]{1,0:T(8,128)(2,1)S(1)} collective-permute-done((bf16[80,768]{1,0:T(8,128)(2,1)S(1)}, bf16[80,768]{1,0:T(8,128)(2,1)S(1)}, u32[]{:S(2)}, u32[]{:S(2)}) %collective-permute-start.2) | collective-permute-done | bytes 122912 | tf_op jit(solution)/shard_map/ppermute | solution.py:328
  32.5 0.7 %collective-permute-start.4 = (bf16[272,768]{1,0:T(8,128)(2,1)S(1)}, bf16[272,768]{1,0:T(8,128)(2,1)S(1)}, u32[]{:S(2)}, u32[]{:S(2)}) collective-permute-start(bf16[272,768]{1,0:T(8,128)(2,1)S(1)} %shard_map.40.refs_0_), channel_id=1, source_target_pairs={{0,1},{5,6},{8,9},{13,14},{16,17},{21,22},{24,25},{29,30}} | collective-permute-start | bytes 1253384 | tf_op jit(solution)/shard_map/ppermute | solution.py:359
  33.2 1.3 %collective-permute-start.3 = (bf16[272,768]{1,0:T(8,128)(2,1)S(1)}, bf16[272,768]{1,0:T(8,128)(2,1)S(1)}, u32[]{:S(2)}, u32[]{:S(2)}) collective-permute-start(bf16[272,768]{1,0:T(8,128)(2,1)S(1)} %shard_map.40.refs_0_), channel_id=1, source_target_pairs={{3,1},{4,6},{11,9},{12,14},{19,17},{20,22},{27,25},{28,30}} | collective-permute-start | bytes 1253384 | tf_op jit(solution)/shard_map/ppermute | solution.py:359
  34.5 0.7 %collective-permute-start.5 = (bf16[272,768]{1,0:T(8,128)(2,1)S(1)}, bf16[272,768]{1,0:T(8,128)(2,1)S(1)}, u32[]{:S(2)}, u32[]{:S(2)}) collective-permute-start(bf16[272,768]{1,0:T(8,128)(2,1)S(1)} %shard_map.40.refs_0_), channel_id=1, source_target_pairs={{2,1},{7,6},{10,9},{15,14},{18,17},{23,22},{26,25},{31,30}} | collective-permute-start | bytes 1253384 | tf_op jit(solution)/shard_map/ppermute | solution.py:359
  35.2 0.0 collective-permute-done.4.refs_2_
  35.2 6.7 %collective-permute-done.3.refs_1_ = bf16[272,768]{1,0:T(8,128)(2,1)S(1)} collective-permute-done((bf16[272,768]{1,0:T(8,128)(2,1)S(1)}, bf16[272,768]{1,0:T(8,128)(2,1)S(1)}, u32[]{:S(2)}, u32[]{:S(2)}) %collective-permute-start.3) | collective-permute-done | bytes 417824 | tf_op jit(solution)/shard_map/ppermute | solution.py:359
  41.9 1.3 %shard_map.41.best_ref = f32[1,768]{1,0:T(1,128)S(1)} custom-call(bf16[272,768]{1,0:T(8,128)(2,1)S(1)} %shard_map.40.refs_0_, bf16[272,768]{1,0:T(8,128)(2,1)S(1)} %collective-permute-done.3.refs_1_, bf16[272,768]{1,0:T(8,128)(2,1)S(1)} %collective-permute-done.4.refs_2_), custom_call_target="tpu_custom_call" | custom-call | flops 905969664 | bytes 2097152 | tf_op jit(solution)/shard_map/pallas_call | solution.py:367
  43.2 3.6 %all-to-all-done.got_ref = bf16[16,304,128]{2,1,0:T(8,128)(2,1)S(1)} async-done(((bf16[16,304,128]{2,1,0:T(8,128)(2,1)}), bf16[16,304,128]{2,1,0:T(8,128)(2,1)S(1)}, u32[]{:S(2)}, u32[]{:S(2)}) %all-to-all-start) | async-done | bytes 1245216 | tf_op jit(solution)/shard_map/all_to_all | solution.py:341
  46.8 1.5 %shard_map.38.small_ref = f32[32,128]{1,0:T(8,128)S(1)} custom-call(s32[1]{0:T(128)} %bitcast.1.blk_at, bf16[16,304,128]{2,1,0:T(8,128)(2,1)S(1)} %all-to-all-done.got_ref), custom_call_target="tpu_custom_call" | custom-call | flops 905969664 | bytes 2097152 | tf_op jit(solution)/shard_map/pallas_call | solution.py:361
  48.2 0.0 collective-permute-done.5.refs_3_
  48.2 1.4 %shard_map.42 = (f32[8,128]{1,0:T(8,128)S(1)}, f32[8,128]{1,0:T(8,128)S(1)}, f32[8,128]{1,0:T(8,128)S(1)}, f32[8,128]{1,0:T(8,128)S(1)}) custom-call(s32[1]{0:T(128)} %bitcast.docs_at.at_ref, f32[32,128]{1,0:T(8,128)S(1)} %shard_map.38.small_ref, f32[1,768]{1,0:T(1,128)S(1)} %shard_map.41.best_ref, bf16[272,768]{1,0:T(8,128)(2,1)S(1)} %shard_map.40.refs_0_, ...), custom_call_target="tpu_custom_call" | custom-call | flops 704643072 | bytes 2097152 | tf_op jit(solution)/shard_map/pallas_call | solution.py:372
  49.6 4.0 %collective-permute-start.6 = (f32[8,128]{1,0:T(8,128)S(1)}, f32[8,128]{1,0:T(8,128)S(1)}, u32[]{:S(2)}, u32[]{:S(2)}) collective-permute-start(f32[8,128]{1,0:T(8,128)S(1)} %get-tuple-element.30), channel_id=1, source_target_pairs={{0,1},{1,2},{2,3},{3,0},{4,5},{5,6},{6,7},{7,4},{8,9},{9,10},{10,1... | collective-permute-start | bytes 12296 | tf_op jit(solution)/shard_map/ppermute | solution.py:328
  53.6 1.7 %collective-permute-start.7 = (f32[8,128]{1,0:T(8,128)S(1)}, f32[8,128]{1,0:T(8,128)S(1)}, u32[]{:S(2)}, u32[]{:S(2)}) collective-permute-start(f32[8,128]{1,0:T(8,128)S(1)} %get-tuple-element.31), channel_id=1, source_target_pairs={{0,2},{1,3},{2,0},{3,1},{4,6},{5,7},{6,4},{7,5},{8,10},{9,11},{10,... | collective-permute-start | bytes 12296 | tf_op jit(solution)/shard_map/ppermute | solution.py:328
  55.3 2.3 %collective-permute-start.8 = (f32[8,128]{1,0:T(8,128)S(1)}, f32[8,128]{1,0:T(8,128)S(1)}, u32[]{:S(2)}, u32[]{:S(2)}) collective-permute-start(f32[8,128]{1,0:T(8,128)S(1)} %get-tuple-element.32), channel_id=1, source_target_pairs={{0,3},{1,0},{2,1},{3,2},{4,7},{5,4},{6,5},{7,6},{8,11},{9,8},{10,9... | collective-permute-start | bytes 12296 | tf_op jit(solution)/shard_map/ppermute | solution.py:328
  57.6 0.0 collective-permute-done.6.refs_1_
  57.6 0.0 collective-permute-done.7.refs_2_
  57.6 0.7 %collective-permute-done.8.refs_3_ = f32[8,128]{1,0:T(8,128)S(1)} collective-permute-done((f32[8,128]{1,0:T(8,128)S(1)}, f32[8,128]{1,0:T(8,128)S(1)}, u32[]{:S(2)}, u32[]{:S(2)}) %collective-permute-start.8) | collective-permute-done | bytes 4128 | tf_op jit(solution)/shard_map/ppermute | solution.py:328
  58.4 0.9 %collective-permute-start.9 = (f32[8,128]{1,0:T(8,128)S(1)}, f32[8,128]{1,0:T(8,128)S(1)}, u32[]{:S(2)}, u32[]{:S(2)}) collective-permute-start(f32[8,128]{1,0:T(8,128)S(1)} %get-tuple-element.34), channel_id=1, source_target_pairs={{0,4},{4,8},{8,12},{12,0},{1,5},{5,9},{9,13},{13,1},{2,6},{6,10},{... | collective-permute-start | bytes 12296 | tf_op jit(solution)/shard_map/ppermute | solution.py:328
  59.2 0.7 %collective-permute-start.10 = (f32[8,128]{1,0:T(8,128)S(1)}, f32[8,128]{1,0:T(8,128)S(1)}, u32[]{:S(2)}, u32[]{:S(2)}) collective-permute-start(f32[8,128]{1,0:T(8,128)S(1)} %get-tuple-element.35), channel_id=1, source_target_pairs={{0,8},{4,12},{8,0},{12,4},{1,9},{5,13},{9,1},{13,5},{2,10},{6,14},... | collective-permute-start | bytes 12296 | tf_op jit(solution)/shard_map/ppermute | solution.py:328
  59.9 0.7 %collective-permute-start.11 = (f32[8,128]{1,0:T(8,128)S(1)}, f32[8,128]{1,0:T(8,128)S(1)}, u32[]{:S(2)}, u32[]{:S(2)}) collective-permute-start(f32[8,128]{1,0:T(8,128)S(1)} %get-tuple-element.36), channel_id=1, source_target_pairs={{0,12},{4,0},{8,4},{12,8},{1,13},{5,1},{9,5},{13,9},{2,14},{6,2},{... | collective-permute-start | bytes 12296 | tf_op jit(solution)/shard_map/ppermute | solution.py:328
  60.7 0.0 collective-permute-done.9.refs_1_
  60.7 1.0 %collective-permute-done.10.refs_2_ = f32[8,128]{1,0:T(8,128)S(1)} collective-permute-done((f32[8,128]{1,0:T(8,128)S(1)}, f32[8,128]{1,0:T(8,128)S(1)}, u32[]{:S(2)}, u32[]{:S(2)}) %collective-permute-start.10) | collective-permute-done | bytes 4128 | tf_op jit(solution)/shard_map/ppermute | solution.py:328
  61.7 1.2 %collective-permute-done.11.refs_3_ = f32[8,128]{1,0:T(8,128)S(1)} collective-permute-done((f32[8,128]{1,0:T(8,128)S(1)}, f32[8,128]{1,0:T(8,128)S(1)}, u32[]{:S(2)}, u32[]{:S(2)}) %collective-permute-start.11) | collective-permute-done | bytes 4128 | tf_op jit(solution)/shard_map/ppermute | solution.py:328
  62.9 0.8 %shard_map.45 = f32[1,512]{1,0:T(1,128)} custom-call(f32[8,128]{1,0:T(8,128)S(1)} %get-tuple-element.33.refs_0_, f32[8,128]{1,0:T(8,128)S(1)} %collective-permute-done.9.refs_1_, f32[8,128]{1,0:T(8,128)S(1)} %collective-permute-done.10.refs_2_, f32[8,128]{1,0:T(8,128)S(1)} %collective-permute-done.11.refs_3_, bf16[96,512]{1,0:T(8,128)(2,1)S(1)} %get-tuple-element.37.refs_4_, ...), custom_call_target="tpu_custom_call" | custom-call | flops 6291456 | bytes 262144 | tf_op jit(solution)/shard_map/pallas_call | solution.py:390
  (3 shorter events, 0.1 us)
Async XLA Ops:
  4.3 7.5 %copy-start = (bf16[512,768]{1,0:T(8,128)(2,1)S(1)}, bf16[512,768]{1,0:T(8,128)(2,1)}, u32[]{:S(2)}) copy-start(bf16[512,768]{1,0:T(8,128)(2,1)} %get-tuple-element.23.rows_ref) | copy-start | bytes 2359300
  4.3 7.5 %copy-start.1 = (s32[8,512]{1,0:T(8,128)S(1)}, s32[8,512]{1,0:T(8,128)}, u32[]{:S(2)}) copy-start(s32[8,512]{1,0:T(8,128)} %get-tuple-element.24.info_ref) | copy-start | bytes 49156
  4.4 42.4 %all-to-all-start = ((bf16[16,304,128]{2,1,0:T(8,128)(2,1)}), bf16[16,304,128]{2,1,0:T(8,128)(2,1)S(1)}, u32[]{:S(2)}, u32[]{:S(2)}) async-start(bf16[16,304,128]{2,1,0:T(8,128)(2,1)} %get-tuple-element.22), calls=%async_computation | async-start | bytes 2490368 | tf_op jit(solution)/shard_map/all_to_all | solution.py:341
  12.6 13.2 %collective-permute-start = (bf16[80,768]{1,0:T(8,128)(2,1)S(1)}, bf16[80,768]{1,0:T(8,128)(2,1)S(1)}, u32[]{:S(2)}, u32[]{:S(2)}) collective-permute-start(bf16[80,768]{1,0:T(8,128)(2,1)S(1)} %get-tuple-element.26), channel_id=1, source_target_pairs={{0,4},{4,8},{8,12},{12,0},{1,5},{5,9},{9,13},{13,1},{2,6},{6,10},{... | collective-permute-start | bytes 368648 | tf_op jit(solution)/shard_map/ppermute | solution.py:328
  14.3 17.3 %collective-permute-start.1 = (bf16[80,768]{1,0:T(8,128)(2,1)S(1)}, bf16[80,768]{1,0:T(8,128)(2,1)S(1)}, u32[]{:S(2)}, u32[]{:S(2)}) collective-permute-start(bf16[80,768]{1,0:T(8,128)(2,1)S(1)} %get-tuple-element.27), channel_id=1, source_target_pairs={{0,8},{4,12},{8,0},{12,4},{1,9},{5,13},{9,1},{13,5},{2,10},{6,14},... | collective-permute-start | bytes 368648 | tf_op jit(solution)/shard_map/ppermute | solution.py:328
  14.3 18.1 %collective-permute-start.2 = (bf16[80,768]{1,0:T(8,128)(2,1)S(1)}, bf16[80,768]{1,0:T(8,128)(2,1)S(1)}, u32[]{:S(2)}, u32[]{:S(2)}) collective-permute-start(bf16[80,768]{1,0:T(8,128)(2,1)S(1)} %get-tuple-element.28), channel_id=1, source_target_pairs={{0,12},{4,0},{8,4},{12,8},{1,13},{5,1},{9,5},{13,9},{2,14},{6,2},{... | collective-permute-start | bytes 368648 | tf_op jit(solution)/shard_map/ppermute | solution.py:328
  32.5 2.7 %collective-permute-start.4 = (bf16[272,768]{1,0:T(8,128)(2,1)S(1)}, bf16[272,768]{1,0:T(8,128)(2,1)S(1)}, u32[]{:S(2)}, u32[]{:S(2)}) collective-permute-start(bf16[272,768]{1,0:T(8,128)(2,1)S(1)} %shard_map.40.refs_0_), channel_id=1, source_target_pairs={{0,1},{5,6},{8,9},{13,14},{16,17},{21,22},{24,25},{29,30}} | collective-permute-start | bytes 1253384 | tf_op jit(solution)/shard_map/ppermute | solution.py:359
  33.2 8.7 %collective-permute-start.3 = (bf16[272,768]{1,0:T(8,128)(2,1)S(1)}, bf16[272,768]{1,0:T(8,128)(2,1)S(1)}, u32[]{:S(2)}, u32[]{:S(2)}) collective-permute-start(bf16[272,768]{1,0:T(8,128)(2,1)S(1)} %shard_map.40.refs_0_), channel_id=1, source_target_pairs={{3,1},{4,6},{11,9},{12,14},{19,17},{20,22},{27,25},{28,30}} | collective-permute-start | bytes 1253384 | tf_op jit(solution)/shard_map/ppermute | solution.py:359
  34.5 13.7 %collective-permute-start.5 = (bf16[272,768]{1,0:T(8,128)(2,1)S(1)}, bf16[272,768]{1,0:T(8,128)(2,1)S(1)}, u32[]{:S(2)}, u32[]{:S(2)}) collective-permute-start(bf16[272,768]{1,0:T(8,128)(2,1)S(1)} %shard_map.40.refs_0_), channel_id=1, source_target_pairs={{2,1},{7,6},{10,9},{15,14},{18,17},{23,22},{26,25},{31,30}} | collective-permute-start | bytes 1253384 | tf_op jit(solution)/shard_map/ppermute | solution.py:359
  49.6 8.0 %collective-permute-start.6 = (f32[8,128]{1,0:T(8,128)S(1)}, f32[8,128]{1,0:T(8,128)S(1)}, u32[]{:S(2)}, u32[]{:S(2)}) collective-permute-start(f32[8,128]{1,0:T(8,128)S(1)} %get-tuple-element.30), channel_id=1, source_target_pairs={{0,1},{1,2},{2,3},{3,0},{4,5},{5,6},{6,7},{7,4},{8,9},{9,10},{10,1... | collective-permute-start | bytes 12296 | tf_op jit(solution)/shard_map/ppermute | solution.py:328
  53.6 4.0 %collective-permute-start.7 = (f32[8,128]{1,0:T(8,128)S(1)}, f32[8,128]{1,0:T(8,128)S(1)}, u32[]{:S(2)}, u32[]{:S(2)}) collective-permute-start(f32[8,128]{1,0:T(8,128)S(1)} %get-tuple-element.31), channel_id=1, source_target_pairs={{0,2},{1,3},{2,0},{3,1},{4,6},{5,7},{6,4},{7,5},{8,10},{9,11},{10,... | collective-permute-start | bytes 12296 | tf_op jit(solution)/shard_map/ppermute | solution.py:328
  55.3 3.0 %collective-permute-start.8 = (f32[8,128]{1,0:T(8,128)S(1)}, f32[8,128]{1,0:T(8,128)S(1)}, u32[]{:S(2)}, u32[]{:S(2)}) collective-permute-start(f32[8,128]{1,0:T(8,128)S(1)} %get-tuple-element.32), channel_id=1, source_target_pairs={{0,3},{1,0},{2,1},{3,2},{4,7},{5,4},{6,5},{7,6},{8,11},{9,8},{10,9... | collective-permute-start | bytes 12296 | tf_op jit(solution)/shard_map/ppermute | solution.py:328
  58.4 2.3 %collective-permute-start.9 = (f32[8,128]{1,0:T(8,128)S(1)}, f32[8,128]{1,0:T(8,128)S(1)}, u32[]{:S(2)}, u32[]{:S(2)}) collective-permute-start(f32[8,128]{1,0:T(8,128)S(1)} %get-tuple-element.34), channel_id=1, source_target_pairs={{0,4},{4,8},{8,12},{12,0},{1,5},{5,9},{9,13},{13,1},{2,6},{6,10},{... | collective-permute-start | bytes 12296 | tf_op jit(solution)/shard_map/ppermute | solution.py:328
  59.2 2.5 %collective-permute-start.10 = (f32[8,128]{1,0:T(8,128)S(1)}, f32[8,128]{1,0:T(8,128)S(1)}, u32[]{:S(2)}, u32[]{:S(2)}) collective-permute-start(f32[8,128]{1,0:T(8,128)S(1)} %get-tuple-element.35), channel_id=1, source_target_pairs={{0,8},{4,12},{8,0},{12,4},{1,9},{5,13},{9,1},{13,5},{2,10},{6,14},... | collective-permute-start | bytes 12296 | tf_op jit(solution)/shard_map/ppermute | solution.py:328
  59.9 3.0 %collective-permute-start.11 = (f32[8,128]{1,0:T(8,128)S(1)}, f32[8,128]{1,0:T(8,128)S(1)}, u32[]{:S(2)}, u32[]{:S(2)}) collective-permute-start(f32[8,128]{1,0:T(8,128)S(1)} %get-tuple-element.36), channel_id=1, source_target_pairs={{0,12},{4,0},{8,4},{12,8},{1,13},{5,1},{9,5},{13,9},{2,14},{6,2},{... | collective-permute-start | bytes 12296 | tf_op jit(solution)/shard_map/ppermute | solution.py:328

commit v13 on v12

--- a/solution.py
+++ b/solution.py
@@ -45,8 +45,11 @@
     return jnp.dot(pick, rows_ref[...], preferred_element_type=jnp.float32).astype(jnp.bfloat16)
 
 
-def sort_kernel(shards, blocks, cap_big, cap_small, pooled_hbm, weight_hbm, cluster_hbm, small_hbm, rows_hbm, info_hbm,
-                pooled_ref, weight_ref, cluster_ref, small_ref, rows_ref, info_ref, sems, small_sems):
+def sort_kernel(shards, blocks, cap_big, cap_small, docs_at, pooled_hbm, weight_hbm, cluster_hbm, small_hbm, info_hbm,
+                *refs):
+    big_hbm = refs[:shards]
+    (pooled_ref, weight_ref, cluster_ref, small_ref, big_ref, rows_ref, info_ref, sems, small_sems,
+     big_sems) = refs[shards:]
     docs, feature = rows_ref.shape
     devices = shards * blocks
     limit = BIG_OWN * shards
@@ -73,22 +76,29 @@
 
     info_ref[0:1, :] = jnp.where(is_big, owner * blocks + home_of(owner, blocks), target)
     info_ref[1:2, :] = jnp.where(is_big, cap_small + rank, rank)
-    info_ref[2:3, :] = jnp.where(is_big, owner * cap_big + rank, -1)
-    info_ref[3:4, :] = jnp.where(is_big, quotient(cluster, shards), quotient(past, devices)) + 1
-    info_ref[4:5, :] = bucket
-    info_ref[5:8, :] = jnp.zeros((3, docs), jnp.int32)
+    info_ref[2:3, :] = jnp.where(is_big, quotient(cluster, shards), quotient(past, devices)) + 1
+    info_ref[3:8, :] = jnp.zeros((5, docs), jnp.int32)
     sends = [pltpu.make_async_copy(info_ref, info_hbm, sems.at[3])]
     sends[0].start()
     small_slot = jnp.where(is_big, -1, target * cap_small + rank)
     ids = ids_table(iota((devices, docs), 0) == bucket, info_ref)
+    shift = modulo(owner + shards - docs_at[0], shards)
+    big_slot = jnp.where(is_big, shift * cap_big + rank, -1)
+    for by in range(shards):
+        mine = (iota((16, docs), 0) == 0) & is_big & (shift == by)
+        big_ref[by, cap_big:, 0:LANES] = ids_table(mine, info_ref).astype(jnp.bfloat16)
+        big_ref[by, cap_big:, LANES:] = jnp.zeros((16, feature - LANES), jnp.bfloat16)
 
     for fetch in fetches[1:]:
         fetch.wait()
     projected = jnp.dot(pooled_ref[...], weight_ref[...], preferred_element_type=jnp.float32)
     squares = jnp.sum(projected * projected, axis=1, keepdims=True)
     rows_ref[...] = (projected * lax.rsqrt(squares + 1e-06)).astype(jnp.bfloat16)
-    sends.append(pltpu.make_async_copy(rows_ref, rows_hbm, sems.at[4]))
-    sends[-1].start()
+    picked = picked_rows(rows_ref, big_slot, 0, shards * cap_big)
+    for by, out in enumerate(big_hbm):
+        big_ref[by, 0:cap_big, :] = picked[by * cap_big:(by + 1) * cap_big, :]
+        sends.append(pltpu.make_async_copy(big_ref.at[by], out, big_sems.at[by]))
+        sends[-1].start()
 
     slabs = feature // LANES
     group = devices // small_sems.shape[0]
@@ -100,7 +110,7 @@
                 small_ref[first + device, slab * cap_small:(slab + 1) * cap_small, :] = picked[
                     device * cap_small:(device + 1) * cap_small, slab * LANES:(slab + 1) * LANES]
             small_ref[first + device, slabs * cap_small:, :] = jnp.broadcast_to(
-                ids[first + device:first + device + 1, :], (16, LANES)).astype(jnp.bfloat16)
+                ids[first + device:first + device + 1, :], (8, LANES)).astype(jnp.bfloat16)
         sends.append(pltpu.make_async_copy(
             small_ref.at[pl.ds(first, group)], small_hbm.at[pl.ds(first, group)], small_sems.at[part]))
         sends[-1].start()
@@ -110,20 +120,9 @@
 
 def ids_table(mine, info_ref):
     docs = info_ref.shape[1]
-    quota = info_ref[3:4, :].astype(jnp.float32)
+    quota = info_ref[2:3, :].astype(jnp.float32)
     lanes = (iota((LANES, docs), 0) == info_ref[1:2, :]).astype(jnp.float32).astype(jnp.bfloat16)
     return dot_nt(jnp.where(mine, quota, 0.0).astype(jnp.bfloat16), lanes)
-
-
-def sort_big_kernel(shards, blocks, cap_big, docs_at, rows_ref, info_ref, *big_refs):
-    devices = shards * blocks
-    for shift, ref in enumerate(big_refs):
-        to = modulo(docs_at[0] + shift, shards)
-        ref[0:cap_big, :] = picked_rows(rows_ref, info_ref[2:3, :], to * cap_big, cap_big)
-        spare = ref.shape[0] - cap_big
-        mine = (iota((spare, info_ref.shape[1]), 0) == 0) & (info_ref[4:5, :] == devices + to)
-        ref[cap_big:, 0:LANES] = ids_table(mine, info_ref).astype(jnp.bfloat16)
-        ref[cap_big:, LANES:] = jnp.zeros((spare, ref.shape[1] - LANES), jnp.bfloat16)
 
 
 def group_kernel(cap_big, *refs):
@@ -327,30 +326,24 @@
     def along(x, axis, count, by):
         return lax.ppermute(x, axis, [(i, (i + by) % count) for i in range(count)])
 
-    small_rows = feature // LANES * cap_small + 16
-    small_sent, rows, info = call(
+    small_rows = feature // LANES * cap_small + 8
+    small_sent, info, *big_sent = call(
         functools.partial(sort_kernel, *sizes),
-        [((devices, small_rows, LANES), bf16, hbm), ((docs, feature), bf16, hbm), ((8, docs), i32, hbm)],
-        [hbm, hbm, hbm],
+        [((devices, small_rows, LANES), bf16, hbm), ((8, docs), i32, hbm)] + [((cap_big + 16, feature), bf16, hbm)] * shards,
+        [smem, hbm, hbm, hbm],
         2 * docs * feature * (pooled.shape[1] + small_slots), 4 << 20, 60,
         [vmem(pooled.shape, bf16), vmem(proj_weight.shape, bf16), vmem((1, docs), i32),
-         vmem((devices, small_rows, LANES), bf16), vmem((docs, feature), bf16), vmem((8, docs), i32),
-         dma((5,)), dma((4,))],
-    )(pooled, proj_weight, cluster.reshape(1, docs))
+         vmem((devices, small_rows, LANES), bf16), vmem((shards, cap_big + 16, feature), bf16),
+         vmem((docs, feature), bf16), vmem((8, docs), i32), dma((4,)), dma((4,)), dma((shards,))],
+    )(docs_at, pooled, proj_weight, cluster.reshape(1, docs))
 
     got_small = lax.all_to_all(small_sent, ("docs", "blk"), split_axis=0, concat_axis=0, tiled=True)
 
-    big_sent = call(
-        functools.partial(sort_big_kernel, shards, blocks, cap_big),
-        [((cap_big + 16, feature), bf16, vmem)] * shards,
-        [smem, vmem, vmem],
-        2 * docs * feature * big_slots, 2 << 20,
-    )(docs_at, rows, info)
     held = [big_sent[0]] + [along(big_sent[by], "docs", shards, by) for by in range(1, shards)]
     group, = call(
         functools.partial(group_kernel, cap_big),
         [((big_slots + rows_up(shards, 16), feature), bf16, vmem)], [vmem] * shards,
-        big_slots * feature, 1 << 20,
+        big_slots * feature, 64 << 20,
     )(*held)
     parts = [group]
     for step in big_steps(blocks)[1:]:

time: 64 us -> 63.5 us (level)
    pallas_call x1 -> x0, Pallas kernels: 0.79 us -> none  [body(): call(functools.partial(sort_big_kernel, shards, blocks, cap_big), [((cap_...]
  transfers between devices with their start and end apart: 13 -> 13, of which waited for: 8 -> 8; matrix products, arithmetic and copies ran while one was open for 0% -> 0% of each run, Pallas kernels for 6% -> 4%
where the time goes in v13:
time: 63.5 us; the launch traced here: 63.3 us
  waiting for transfers between devices  30.9 us (49%)
  starting transfers between devices  22.7 us (36%)
  Pallas kernels  9.49 us (15%)
    ppermute x9, waiting for transfers between devices, along(): return lax.ppermute(x, axis, [(i, (i + by) % count) for i in range(count)])  21.1 us
    ppermute x9, starting transfers between devices, along(): return lax.ppermute(x, axis, [(i, (i + by) % count) for i in range(count)])  12.5 us
    all_to_all x1, starting transfers between devices, body(): lax.all_to_all(small_sent, ('docs', 'blk'), split_axis=0, concat_axis=0,...  7.47 us
    ppermute x3, waiting for transfers between devices, body(): parts.append(lax.ppermute(group, ('docs', 'blk'), pairs))  6.47 us
    pallas_call x1, Pallas kernels, body(): call(functools.partial(sort_kernel, *sizes), [((devices, small_rows, LANE...  4.54 us
    all_to_all x1, waiting for transfers between devices, body(): lax.all_to_all(small_sent, ('docs', 'blk'), split_axis=0, concat_axis=0,...  3.41 us
    ppermute x3, starting transfers between devices, body(): parts.append(lax.ppermute(group, ('docs', 'blk'), pairs))  2.74 us
    pallas_call x1, Pallas kernels, body(): call(functools.partial(small_kernel, shards, blocks, cap_small), [((block...  1.47 us
  transfers between devices with their start and end apart: 13, of which 8 were waited for; matrix products, arithmetic and copies ran while one was open for 0% of the time, Pallas kernels for 4%

profile of v13, /device:TPU:1, one launch (start us, length us, event | category | flops | bytes accessed | tf_op | source)
XLA Modules:
  0.0 63.3 jit_solution(6875516768886977709)
XLA Ops:
  0.0 4.5 %shard_map.37 = (bf16[16,296,128]{2,1,0:T(8,128)(2,1)}, s32[8,512]{1,0:T(8,128)}, bf16[80,768]{1,0:T(8,128)(2,1)}, bf16[80,768]{1,0:T(8,128)(2,1)}, bf16[80,768]{1,0:T(8,128)(2,1)}, /*index=5*/bf16[80,768]{1,0:T(8,128)(2,1)}) custom-call(s32[1]{0:T(128)} %bitcast.docs_at.at_ref, bf16[512,768]{1,0:T(8,128)(2,1)} %pooled_hbm.1, bf16[768,768]{1,0:T(8,128)(2,1)} %weight_hbm.1, ...), custom_call_target="tpu_custom_call" | custom-call | flops 1207959552 | bytes 4194304 | tf_op jit(solution)/shard_map/pallas_call | solution.py:330
  4.5 0.0 copy-start.4
  4.6 0.0 copy-start.3
  4.6 0.0 copy-start.2
  4.6 0.0 copy-start
  4.6 7.5 %all-to-all-start = ((bf16[16,296,128]{2,1,0:T(8,128)(2,1)}), bf16[16,296,128]{2,1,0:T(8,128)(2,1)S(1)}, u32[]{:S(2)}, u32[]{:S(2)}) async-start(bf16[16,296,128]{2,1,0:T(8,128)(2,1)} %get-tuple-element.21), calls=%async_computation | async-start | bytes 2424832 | tf_op jit(solution)/shard_map/all_to_all | solution.py:340
  12.1 0.0 copy-done.4
  12.1 1.7 %collective-permute-start = (bf16[80,768]{1,0:T(8,128)(2,1)S(1)}, bf16[80,768]{1,0:T(8,128)(2,1)S(1)}, u32[]{:S(2)}, u32[]{:S(2)}) collective-permute-start(bf16[80,768]{1,0:T(8,128)(2,1)S(1)} %copy-done.4), channel_id=1, source_target_pairs={{0,4},{4,8},{8,12},{12,0},{1,5},{5,9},{9,13},{13,1},{2,6},{6,10},{... | collective-permute-start | bytes 368648 | tf_op jit(solution)/shard_map/ppermute | solution.py:327
  13.7 0.0 copy-done.3
  13.7 0.0 collective-permute-start.1
  13.7 0.0 copy-done.2
  13.8 0.5 collective-permute-start.2
  14.3 11.3 %collective-permute-done.refs_1_ = bf16[80,768]{1,0:T(8,128)(2,1)S(1)} collective-permute-done((bf16[80,768]{1,0:T(8,128)(2,1)S(1)}, bf16[80,768]{1,0:T(8,128)(2,1)S(1)}, u32[]{:S(2)}, u32[]{:S(2)}) %collective-permute-start) | collective-permute-done | bytes 122912 | tf_op jit(solution)/shard_map/ppermute | solution.py:327
  25.5 6.3 %collective-permute-done.1.refs_2_ = bf16[80,768]{1,0:T(8,128)(2,1)S(1)} collective-permute-done((bf16[80,768]{1,0:T(8,128)(2,1)S(1)}, bf16[80,768]{1,0:T(8,128)(2,1)S(1)}, u32[]{:S(2)}, u32[]{:S(2)}) %collective-permute-start.1) | collective-permute-done | bytes 122912 | tf_op jit(solution)/shard_map/ppermute | solution.py:327
  31.9 0.5 collective-permute-done.2.refs_3_
  32.3 0.0 copy-done
  32.4 0.7 %collective-permute-start.4 = (bf16[272,768]{1,0:T(8,128)(2,1)S(1)}, bf16[272,768]{1,0:T(8,128)(2,1)S(1)}, u32[]{:S(2)}, u32[]{:S(2)}) collective-permute-start(bf16[272,768]{1,0:T(8,128)(2,1)S(1)} %shard_map.39.refs_0_), channel_id=1, source_target_pairs={{0,1},{5,6},{8,9},{13,14},{16,17},{21,22},{24,25},{29,30}} | collective-permute-start | bytes 1253384 | tf_op jit(solution)/shard_map/ppermute | solution.py:352
  33.1 1.4 %collective-permute-start.3 = (bf16[272,768]{1,0:T(8,128)(2,1)S(1)}, bf16[272,768]{1,0:T(8,128)(2,1)S(1)}, u32[]{:S(2)}, u32[]{:S(2)}) collective-permute-start(bf16[272,768]{1,0:T(8,128)(2,1)S(1)} %shard_map.39.refs_0_), channel_id=1, source_target_pairs={{3,1},{4,6},{11,9},{12,14},{19,17},{20,22},{27,25},{28,30}} | collective-permute-start | bytes 1253384 | tf_op jit(solution)/shard_map/ppermute | solution.py:352
  34.4 0.7 %collective-permute-start.5 = (bf16[272,768]{1,0:T(8,128)(2,1)S(1)}, bf16[272,768]{1,0:T(8,128)(2,1)S(1)}, u32[]{:S(2)}, u32[]{:S(2)}) collective-permute-start(bf16[272,768]{1,0:T(8,128)(2,1)S(1)} %shard_map.39.refs_0_), channel_id=1, source_target_pairs={{2,1},{7,6},{10,9},{15,14},{18,17},{23,22},{26,25},{31,30}} | collective-permute-start | bytes 1253384 | tf_op jit(solution)/shard_map/ppermute | solution.py:352
  35.1 0.0 collective-permute-done.4.refs_2_
  35.1 6.5 %collective-permute-done.3.refs_1_ = bf16[272,768]{1,0:T(8,128)(2,1)S(1)} collective-permute-done((bf16[272,768]{1,0:T(8,128)(2,1)S(1)}, bf16[272,768]{1,0:T(8,128)(2,1)S(1)}, u32[]{:S(2)}, u32[]{:S(2)}) %collective-permute-start.3) | collective-permute-done | bytes 417824 | tf_op jit(solution)/shard_map/ppermute | solution.py:352
  41.6 1.3 %shard_map.40.best_ref = f32[1,768]{1,0:T(1,128)S(1)} custom-call(bf16[272,768]{1,0:T(8,128)(2,1)S(1)} %shard_map.39.refs_0_, bf16[272,768]{1,0:T(8,128)(2,1)S(1)} %collective-permute-done.3.refs_1_, bf16[272,768]{1,0:T(8,128)(2,1)S(1)} %collective-permute-done.4.refs_2_), custom_call_target="tpu_custom_call" | custom-call | flops 905969664 | bytes 2097152 | tf_op jit(solution)/shard_map/pallas_call | solution.py:360
  42.9 3.4 %all-to-all-done.got_ref = bf16[16,296,128]{2,1,0:T(8,128)(2,1)S(1)} async-done(((bf16[16,296,128]{2,1,0:T(8,128)(2,1)}), bf16[16,296,128]{2,1,0:T(8,128)(2,1)S(1)}, u32[]{:S(2)}, u32[]{:S(2)}) %all-to-all-start) | async-done | bytes 1212448 | tf_op jit(solution)/shard_map/all_to_all | solution.py:340
  46.3 1.5 %shard_map.38.small_ref = f32[32,128]{1,0:T(8,128)S(1)} custom-call(s32[1]{0:T(128)} %bitcast.1.blk_at, bf16[16,296,128]{2,1,0:T(8,128)(2,1)S(1)} %all-to-all-done.got_ref), custom_call_target="tpu_custom_call" | custom-call | flops 905969664 | bytes 2097152 | tf_op jit(solution)/shard_map/pallas_call | solution.py:354
  47.8 0.0 copy-start.1
  47.8 0.0 collective-permute-done.5.refs_3_
  47.8 1.3 %shard_map.41 = (f32[8,128]{1,0:T(8,128)S(1)}, f32[8,128]{1,0:T(8,128)S(1)}, f32[8,128]{1,0:T(8,128)S(1)}, f32[8,128]{1,0:T(8,128)S(1)}) custom-call(s32[1]{0:T(128)} %bitcast.docs_at.at_ref, f32[32,128]{1,0:T(8,128)S(1)} %shard_map.38.small_ref, f32[1,768]{1,0:T(1,128)S(1)} %shard_map.40.best_ref, bf16[272,768]{1,0:T(8,128)(2,1)S(1)} %shard_map.39.refs_0_, ...), custom_call_target="tpu_custom_call" | custom-call | flops 704643072 | bytes 2097152 | tf_op jit(solution)/shard_map/pallas_call | solution.py:365
  49.1 4.0 %collective-permute-start.6 = (f32[8,128]{1,0:T(8,128)S(1)}, f32[8,128]{1,0:T(8,128)S(1)}, u32[]{:S(2)}, u32[]{:S(2)}) collective-permute-start(f32[8,128]{1,0:T(8,128)S(1)} %get-tuple-element.27), channel_id=1, source_target_pairs={{0,1},{1,2},{2,3},{3,0},{4,5},{5,6},{6,7},{7,4},{8,9},{9,10},{10,1... | collective-permute-start | bytes 12296 | tf_op jit(solution)/shard_map/ppermute | solution.py:327
  53.1 1.7 %collective-permute-start.7 = (f32[8,128]{1,0:T(8,128)S(1)}, f32[8,128]{1,0:T(8,128)S(1)}, u32[]{:S(2)}, u32[]{:S(2)}) collective-permute-start(f32[8,128]{1,0:T(8,128)S(1)} %get-tuple-element.28), channel_id=1, source_target_pairs={{0,2},{1,3},{2,0},{3,1},{4,6},{5,7},{6,4},{7,5},{8,10},{9,11},{10,... | collective-permute-start | bytes 12296 | tf_op jit(solution)/shard_map/ppermute | solution.py:327
  54.8 2.3 %collective-permute-start.8 = (f32[8,128]{1,0:T(8,128)S(1)}, f32[8,128]{1,0:T(8,128)S(1)}, u32[]{:S(2)}, u32[]{:S(2)}) collective-permute-start(f32[8,128]{1,0:T(8,128)S(1)} %get-tuple-element.29), channel_id=1, source_target_pairs={{0,3},{1,0},{2,1},{3,2},{4,7},{5,4},{6,5},{7,6},{8,11},{9,8},{10,9... | collective-permute-start | bytes 12296 | tf_op jit(solution)/shard_map/ppermute | solution.py:327
  57.1 0.0 collective-permute-done.6.refs_1_
  57.1 0.0 collective-permute-done.7.refs_2_
  57.1 0.7 %collective-permute-done.8.refs_3_ = f32[8,128]{1,0:T(8,128)S(1)} collective-permute-done((f32[8,128]{1,0:T(8,128)S(1)}, f32[8,128]{1,0:T(8,128)S(1)}, u32[]{:S(2)}, u32[]{:S(2)}) %collective-permute-start.8) | collective-permute-done | bytes 4128 | tf_op jit(solution)/shard_map/ppermute | solution.py:327
  57.9 0.9 %collective-permute-start.9 = (f32[8,128]{1,0:T(8,128)S(1)}, f32[8,128]{1,0:T(8,128)S(1)}, u32[]{:S(2)}, u32[]{:S(2)}) collective-permute-start(f32[8,128]{1,0:T(8,128)S(1)} %get-tuple-element.31), channel_id=1, source_target_pairs={{0,4},{4,8},{8,12},{12,0},{1,5},{5,9},{9,13},{13,1},{2,6},{6,10},{... | collective-permute-start | bytes 12296 | tf_op jit(solution)/shard_map/ppermute | solution.py:327
  58.8 0.7 %collective-permute-start.10 = (f32[8,128]{1,0:T(8,128)S(1)}, f32[8,128]{1,0:T(8,128)S(1)}, u32[]{:S(2)}, u32[]{:S(2)}) collective-permute-start(f32[8,128]{1,0:T(8,128)S(1)} %get-tuple-element.32), channel_id=1, source_target_pairs={{0,8},{4,12},{8,0},{12,4},{1,9},{5,13},{9,1},{13,5},{2,10},{6,14},... | collective-permute-start | bytes 12296 | tf_op jit(solution)/shard_map/ppermute | solution.py:327
  59.4 0.7 %collective-permute-start.11 = (f32[8,128]{1,0:T(8,128)S(1)}, f32[8,128]{1,0:T(8,128)S(1)}, u32[]{:S(2)}, u32[]{:S(2)}) collective-permute-start(f32[8,128]{1,0:T(8,128)S(1)} %get-tuple-element.33), channel_id=1, source_target_pairs={{0,12},{4,0},{8,4},{12,8},{1,13},{5,1},{9,5},{13,9},{2,14},{6,2},{... | collective-permute-start | bytes 12296 | tf_op jit(solution)/shard_map/ppermute | solution.py:327
  60.1 0.0 copy-done.1
  60.2 0.0 collective-permute-done.9.refs_1_
  60.2 1.0 %collective-permute-done.10.refs_2_ = f32[8,128]{1,0:T(8,128)S(1)} collective-permute-done((f32[8,128]{1,0:T(8,128)S(1)}, f32[8,128]{1,0:T(8,128)S(1)}, u32[]{:S(2)}, u32[]{:S(2)}) %collective-permute-start.10) | collective-permute-done | bytes 4128 | tf_op jit(solution)/shard_map/ppermute | solution.py:327
  61.2 1.2 %collective-permute-done.11.refs_3_ = f32[8,128]{1,0:T(8,128)S(1)} collective-permute-done((f32[8,128]{1,0:T(8,128)S(1)}, f32[8,128]{1,0:T(8,128)S(1)}, u32[]{:S(2)}, u32[]{:S(2)}) %collective-permute-start.11) | collective-permute-done | bytes 4128 | tf_op jit(solution)/shard_map/ppermute | solution.py:327
  62.5 0.8 %shard_map.44 = f32[1,512]{1,0:T(1,128)} custom-call(f32[8,128]{1,0:T(8,128)S(1)} %get-tuple-element.30.refs_0_, f32[8,128]{1,0:T(8,128)S(1)} %collective-permute-done.9.refs_1_, f32[8,128]{1,0:T(8,128)S(1)} %collective-permute-done.10.refs_2_, f32[8,128]{1,0:T(8,128)S(1)} %collective-permute-done.11.refs_3_, bf16[96,512]{1,0:T(8,128)(2,1)S(1)} %get-tuple-element.35.refs_4_, ...), custom_call_target="tpu_custom_call" | custom-call | flops 6291456 | bytes 262144 | tf_op jit(solution)/shard_map/pallas_call | solution.py:383
  (3 shorter events, 0.1 us)
Async XLA Ops:
  4.5 7.5 %copy-start.4 = (bf16[80,768]{1,0:T(8,128)(2,1)S(1)}, bf16[80,768]{1,0:T(8,128)(2,1)}, u32[]{:S(2)}) copy-start(bf16[80,768]{1,0:T(8,128)(2,1)} %get-tuple-element.23) | copy-start | bytes 368644
  4.6 9.2 %copy-start.3 = (bf16[80,768]{1,0:T(8,128)(2,1)S(1)}, bf16[80,768]{1,0:T(8,128)(2,1)}, u32[]{:S(2)}) copy-start(bf16[80,768]{1,0:T(8,128)(2,1)} %get-tuple-element.24) | copy-start | bytes 368644
  4.6 9.2 %copy-start.2 = (bf16[80,768]{1,0:T(8,128)(2,1)S(1)}, bf16[80,768]{1,0:T(8,128)(2,1)}, u32[]{:S(2)}) copy-start(bf16[80,768]{1,0:T(8,128)(2,1)} %get-tuple-element.25) | copy-start | bytes 368644
  4.6 27.8 %copy-start = (bf16[80,768]{1,0:T(8,128)(2,1)S(1)}, bf16[80,768]{1,0:T(8,128)(2,1)}, u32[]{:S(2)}) copy-start(bf16[80,768]{1,0:T(8,128)(2,1)} %get-tuple-element.22.refs_0_) | copy-start | bytes 368644
  4.6 41.7 %all-to-all-start = ((bf16[16,296,128]{2,1,0:T(8,128)(2,1)}), bf16[16,296,128]{2,1,0:T(8,128)(2,1)S(1)}, u32[]{:S(2)}, u32[]{:S(2)}) async-start(bf16[16,296,128]{2,1,0:T(8,128)(2,1)} %get-tuple-element.21), calls=%async_computation | async-start | bytes 2424832 | tf_op jit(solution)/shard_map/all_to_all | solution.py:340
  12.1 13.5 %collective-permute-start = (bf16[80,768]{1,0:T(8,128)(2,1)S(1)}, bf16[80,768]{1,0:T(8,128)(2,1)S(1)}, u32[]{:S(2)}, u32[]{:S(2)}) collective-permute-start(bf16[80,768]{1,0:T(8,128)(2,1)S(1)} %copy-done.4), channel_id=1, source_target_pairs={{0,4},{4,8},{8,12},{12,0},{1,5},{5,9},{9,13},{13,1},{2,6},{6,10},{... | collective-permute-start | bytes 368648 | tf_op jit(solution)/shard_map/ppermute | solution.py:327
  13.7 18.1 %collective-permute-start.1 = (bf16[80,768]{1,0:T(8,128)(2,1)S(1)}, bf16[80,768]{1,0:T(8,128)(2,1)S(1)}, u32[]{:S(2)}, u32[]{:S(2)}) collective-permute-start(bf16[80,768]{1,0:T(8,128)(2,1)S(1)} %copy-done.3), channel_id=1, source_target_pairs={{0,8},{4,12},{8,0},{12,4},{1,9},{5,13},{9,1},{13,5},{2,10},{6,14},... | collective-permute-start | bytes 368648 | tf_op jit(solution)/shard_map/ppermute | solution.py:327
  13.8 18.6 %collective-permute-start.2 = (bf16[80,768]{1,0:T(8,128)(2,1)S(1)}, bf16[80,768]{1,0:T(8,128)(2,1)S(1)}, u32[]{:S(2)}, u32[]{:S(2)}) collective-permute-start(bf16[80,768]{1,0:T(8,128)(2,1)S(1)} %copy-done.2), channel_id=1, source_target_pairs={{0,12},{4,0},{8,4},{12,8},{1,13},{5,1},{9,5},{13,9},{2,14},{6,2},{... | collective-permute-start | bytes 368648 | tf_op jit(solution)/shard_map/ppermute | solution.py:327
  32.4 2.8 %collective-permute-start.4 = (bf16[272,768]{1,0:T(8,128)(2,1)S(1)}, bf16[272,768]{1,0:T(8,128)(2,1)S(1)}, u32[]{:S(2)}, u32[]{:S(2)}) collective-permute-start(bf16[272,768]{1,0:T(8,128)(2,1)S(1)} %shard_map.39.refs_0_), channel_id=1, source_target_pairs={{0,1},{5,6},{8,9},{13,14},{16,17},{21,22},{24,25},{29,30}} | collective-permute-start | bytes 1253384 | tf_op jit(solution)/shard_map/ppermute | solution.py:352
  33.1 8.5 %collective-permute-start.3 = (bf16[272,768]{1,0:T(8,128)(2,1)S(1)}, bf16[272,768]{1,0:T(8,128)(2,1)S(1)}, u32[]{:S(2)}, u32[]{:S(2)}) collective-permute-start(bf16[272,768]{1,0:T(8,128)(2,1)S(1)} %shard_map.39.refs_0_), channel_id=1, source_target_pairs={{3,1},{4,6},{11,9},{12,14},{19,17},{20,22},{27,25},{28,30}} | collective-permute-start | bytes 1253384 | tf_op jit(solution)/shard_map/ppermute | solution.py:352
  34.4 13.3 %collective-permute-start.5 = (bf16[272,768]{1,0:T(8,128)(2,1)S(1)}, bf16[272,768]{1,0:T(8,128)(2,1)S(1)}, u32[]{:S(2)}, u32[]{:S(2)}) collective-permute-start(bf16[272,768]{1,0:T(8,128)(2,1)S(1)} %shard_map.39.refs_0_), channel_id=1, source_target_pairs={{2,1},{7,6},{10,9},{15,14},{18,17},{23,22},{26,25},{31,30}} | collective-permute-start | bytes 1253384 | tf_op jit(solution)/shard_map/ppermute | solution.py:352
  47.8 12.4 %copy-start.1 = (s32[8,512]{1,0:T(8,128)S(1)}, s32[8,512]{1,0:T(8,128)}, u32[]{:S(2)}) copy-start(s32[8,512]{1,0:T(8,128)} %get-tuple-element.34.info_ref) | copy-start | bytes 49156
  49.1 8.0 %collective-permute-start.6 = (f32[8,128]{1,0:T(8,128)S(1)}, f32[8,128]{1,0:T(8,128)S(1)}, u32[]{:S(2)}, u32[]{:S(2)}) collective-permute-start(f32[8,128]{1,0:T(8,128)S(1)} %get-tuple-element.27), channel_id=1, source_target_pairs={{0,1},{1,2},{2,3},{3,0},{4,5},{5,6},{6,7},{7,4},{8,9},{9,10},{10,1... | collective-permute-start | bytes 12296 | tf_op jit(solution)/shard_map/ppermute | solution.py:327
  53.1 4.0 %collective-permute-start.7 = (f32[8,128]{1,0:T(8,128)S(1)}, f32[8,128]{1,0:T(8,128)S(1)}, u32[]{:S(2)}, u32[]{:S(2)}) collective-permute-start(f32[8,128]{1,0:T(8,128)S(1)} %get-tuple-element.28), channel_id=1, source_target_pairs={{0,2},{1,3},{2,0},{3,1},{4,6},{5,7},{6,4},{7,5},{8,10},{9,11},{10,... | collective-permute-start | bytes 12296 | tf_op jit(solution)/shard_map/ppermute | solution.py:327
  54.8 3.0 %collective-permute-start.8 = (f32[8,128]{1,0:T(8,128)S(1)}, f32[8,128]{1,0:T(8,128)S(1)}, u32[]{:S(2)}, u32[]{:S(2)}) collective-permute-start(f32[8,128]{1,0:T(8,128)S(1)} %get-tuple-element.29), channel_id=1, source_target_pairs={{0,3},{1,0},{2,1},{3,2},{4,7},{5,4},{6,5},{7,6},{8,11},{9,8},{10,9... | collective-permute-start | bytes 12296 | tf_op jit(solution)/shard_map/ppermute | solution.py:327
  57.9 2.3 %collective-permute-start.9 = (f32[8,128]{1,0:T(8,128)S(1)}, f32[8,128]{1,0:T(8,128)S(1)}, u32[]{:S(2)}, u32[]{:S(2)}) collective-permute-start(f32[8,128]{1,0:T(8,128)S(1)} %get-tuple-element.31), channel_id=1, source_target_pairs={{0,4},{4,8},{8,12},{12,0},{1,5},{5,9},{9,13},{13,1},{2,6},{6,10},{... | collective-permute-start | bytes 12296 | tf_op jit(solution)/shard_map/ppermute | solution.py:327
  58.8 2.5 %collective-permute-start.10 = (f32[8,128]{1,0:T(8,128)S(1)}, f32[8,128]{1,0:T(8,128)S(1)}, u32[]{:S(2)}, u32[]{:S(2)}) collective-permute-start(f32[8,128]{1,0:T(8,128)S(1)} %get-tuple-element.32), channel_id=1, source_target_pairs={{0,8},{4,12},{8,0},{12,4},{1,9},{5,13},{9,1},{13,5},{2,10},{6,14},... | collective-permute-start | bytes 12296 | tf_op jit(solution)/shard_map/ppermute | solution.py:327
  59.4 3.0 %collective-permute-start.11 = (f32[8,128]{1,0:T(8,128)S(1)}, f32[8,128]{1,0:T(8,128)S(1)}, u32[]{:S(2)}, u32[]{:S(2)}) collective-permute-start(f32[8,128]{1,0:T(8,128)S(1)} %get-tuple-element.33), channel_id=1, source_target_pairs={{0,12},{4,0},{8,4},{12,8},{1,13},{5,1},{9,5},{13,9},{2,14},{6,2},{... | collective-permute-start | bytes 12296 | tf_op jit(solution)/shard_map/ppermute | solution.py:327

commit v14 on v13

--- a/solution.py
+++ b/solution.py
@@ -343,7 +343,7 @@
     group, = call(
         functools.partial(group_kernel, cap_big),
         [((big_slots + rows_up(shards, 16), feature), bf16, vmem)], [vmem] * shards,
-        big_slots * feature, 64 << 20,
+        big_slots * feature, 1 << 30,
     )(*held)
     parts = [group]
     for step in big_steps(blocks)[1:]:

time: 63.5 us -> 63.5 us (level)
  no operation moved by 1% of the time
where the time goes in v14:
time: 63.5 us; the launch traced here: 63.3 us
  waiting for transfers between devices  30.9 us (49%)
  starting transfers between devices  22.7 us (36%)
  Pallas kernels  9.49 us (15%)
    ppermute x9, waiting for transfers between devices, along(): return lax.ppermute(x, axis, [(i, (i + by) % count) for i in range(count)])  21.1 us
    ppermute x9, starting transfers between devices, along(): return lax.ppermute(x, axis, [(i, (i + by) % count) for i in range(count)])  12.5 us
    all_to_all x1, starting transfers between devices, body(): lax.all_to_all(small_sent, ('docs', 'blk'), split_axis=0, concat_axis=0,...  7.47 us
    ppermute x3, waiting for transfers between devices, body(): parts.append(lax.ppermute(group, ('docs', 'blk'), pairs))  6.47 us
    pallas_call x1, Pallas kernels, body(): call(functools.partial(sort_kernel, *sizes), [((devices, small_rows, LANE...  4.54 us
    all_to_all x1, waiting for transfers between devices, body(): lax.all_to_all(small_sent, ('docs', 'blk'), split_axis=0, concat_axis=0,...  3.41 us
    ppermute x3, starting transfers between devices, body(): parts.append(lax.ppermute(group, ('docs', 'blk'), pairs))  2.74 us
    pallas_call x1, Pallas kernels, body(): call(functools.partial(small_kernel, shards, blocks, cap_small), [((block...  1.47 us
  transfers between devices with their start and end apart: 13, of which 8 were waited for; matrix products, arithmetic and copies ran while one was open for 0% of the time, Pallas kernels for 4%

profile of v14, /device:TPU:1, one launch (start us, length us, event | category | flops | bytes accessed | tf_op | source)
XLA Modules:
  0.0 63.3 jit_solution(6875516768886977709)
XLA Ops:
  0.0 4.5 %shard_map.37 = (bf16[16,296,128]{2,1,0:T(8,128)(2,1)}, s32[8,512]{1,0:T(8,128)}, bf16[80,768]{1,0:T(8,128)(2,1)}, bf16[80,768]{1,0:T(8,128)(2,1)}, bf16[80,768]{1,0:T(8,128)(2,1)}, /*index=5*/bf16[80,768]{1,0:T(8,128)(2,1)}) custom-call(s32[1]{0:T(128)} %bitcast.docs_at.at_ref, bf16[512,768]{1,0:T(8,128)(2,1)} %pooled_hbm.1, bf16[768,768]{1,0:T(8,128)(2,1)} %weight_hbm.1, ...), custom_call_target="tpu_custom_call" | custom-call | flops 1207959552 | bytes 4194304 | tf_op jit(solution)/shard_map/pallas_call | solution.py:330
  4.5 0.0 copy-start.4
  4.6 0.0 copy-start.3
  4.6 0.0 copy-start.2
  4.6 0.0 copy-start
  4.6 7.5 %all-to-all-start = ((bf16[16,296,128]{2,1,0:T(8,128)(2,1)}), bf16[16,296,128]{2,1,0:T(8,128)(2,1)S(1)}, u32[]{:S(2)}, u32[]{:S(2)}) async-start(bf16[16,296,128]{2,1,0:T(8,128)(2,1)} %get-tuple-element.21), calls=%async_computation | async-start | bytes 2424832 | tf_op jit(solution)/shard_map/all_to_all | solution.py:340
  12.1 0.0 copy-done.4
  12.1 1.7 %collective-permute-start = (bf16[80,768]{1,0:T(8,128)(2,1)S(1)}, bf16[80,768]{1,0:T(8,128)(2,1)S(1)}, u32[]{:S(2)}, u32[]{:S(2)}) collective-permute-start(bf16[80,768]{1,0:T(8,128)(2,1)S(1)} %copy-done.4), channel_id=1, source_target_pairs={{0,4},{4,8},{8,12},{12,0},{1,5},{5,9},{9,13},{13,1},{2,6},{6,10},{... | collective-permute-start | bytes 368648 | tf_op jit(solution)/shard_map/ppermute | solution.py:327
  13.7 0.0 copy-done.3
  13.7 0.0 collective-permute-start.1
  13.7 0.0 copy-done.2
  13.8 0.5 collective-permute-start.2
  14.3 11.3 %collective-permute-done.refs_1_ = bf16[80,768]{1,0:T(8,128)(2,1)S(1)} collective-permute-done((bf16[80,768]{1,0:T(8,128)(2,1)S(1)}, bf16[80,768]{1,0:T(8,128)(2,1)S(1)}, u32[]{:S(2)}, u32[]{:S(2)}) %collective-permute-start) | collective-permute-done | bytes 122912 | tf_op jit(solution)/shard_map/ppermute | solution.py:327
  25.5 6.3 %collective-permute-done.1.refs_2_ = bf16[80,768]{1,0:T(8,128)(2,1)S(1)} collective-permute-done((bf16[80,768]{1,0:T(8,128)(2,1)S(1)}, bf16[80,768]{1,0:T(8,128)(2,1)S(1)}, u32[]{:S(2)}, u32[]{:S(2)}) %collective-permute-start.1) | collective-permute-done | bytes 122912 | tf_op jit(solution)/shard_map/ppermute | solution.py:327
  31.9 0.5 collective-permute-done.2.refs_3_
  32.3 0.0 copy-done
  32.4 0.7 %collective-permute-start.4 = (bf16[272,768]{1,0:T(8,128)(2,1)S(1)}, bf16[272,768]{1,0:T(8,128)(2,1)S(1)}, u32[]{:S(2)}, u32[]{:S(2)}) collective-permute-start(bf16[272,768]{1,0:T(8,128)(2,1)S(1)} %shard_map.39.refs_0_), channel_id=1, source_target_pairs={{0,1},{5,6},{8,9},{13,14},{16,17},{21,22},{24,25},{29,30}} | collective-permute-start | bytes 1253384 | tf_op jit(solution)/shard_map/ppermute | solution.py:352
  33.1 1.4 %collective-permute-start.3 = (bf16[272,768]{1,0:T(8,128)(2,1)S(1)}, bf16[272,768]{1,0:T(8,128)(2,1)S(1)}, u32[]{:S(2)}, u32[]{:S(2)}) collective-permute-start(bf16[272,768]{1,0:T(8,128)(2,1)S(1)} %shard_map.39.refs_0_), channel_id=1, source_target_pairs={{3,1},{4,6},{11,9},{12,14},{19,17},{20,22},{27,25},{28,30}} | collective-permute-start | bytes 1253384 | tf_op jit(solution)/shard_map/ppermute | solution.py:352
  34.4 0.7 %collective-permute-start.5 = (bf16[272,768]{1,0:T(8,128)(2,1)S(1)}, bf16[272,768]{1,0:T(8,128)(2,1)S(1)}, u32[]{:S(2)}, u32[]{:S(2)}) collective-permute-start(bf16[272,768]{1,0:T(8,128)(2,1)S(1)} %shard_map.39.refs_0_), channel_id=1, source_target_pairs={{2,1},{7,6},{10,9},{15,14},{18,17},{23,22},{26,25},{31,30}} | collective-permute-start | bytes 1253384 | tf_op jit(solution)/shard_map/ppermute | solution.py:352
  35.1 0.0 collective-permute-done.4.refs_2_
  35.1 6.5 %collective-permute-done.3.refs_1_ = bf16[272,768]{1,0:T(8,128)(2,1)S(1)} collective-permute-done((bf16[272,768]{1,0:T(8,128)(2,1)S(1)}, bf16[272,768]{1,0:T(8,128)(2,1)S(1)}, u32[]{:S(2)}, u32[]{:S(2)}) %collective-permute-start.3) | collective-permute-done | bytes 417824 | tf_op jit(solution)/shard_map/ppermute | solution.py:352
  41.6 1.3 %shard_map.40.best_ref = f32[1,768]{1,0:T(1,128)S(1)} custom-call(bf16[272,768]{1,0:T(8,128)(2,1)S(1)} %shard_map.39.refs_0_, bf16[272,768]{1,0:T(8,128)(2,1)S(1)} %collective-permute-done.3.refs_1_, bf16[272,768]{1,0:T(8,128)(2,1)S(1)} %collective-permute-done.4.refs_2_), custom_call_target="tpu_custom_call" | custom-call | flops 905969664 | bytes 2097152 | tf_op jit(solution)/shard_map/pallas_call | solution.py:360
  42.9 3.4 %all-to-all-done.got_ref = bf16[16,296,128]{2,1,0:T(8,128)(2,1)S(1)} async-done(((bf16[16,296,128]{2,1,0:T(8,128)(2,1)}), bf16[16,296,128]{2,1,0:T(8,128)(2,1)S(1)}, u32[]{:S(2)}, u32[]{:S(2)}) %all-to-all-start) | async-done | bytes 1212448 | tf_op jit(solution)/shard_map/all_to_all | solution.py:340
  46.3 1.5 %shard_map.38.small_ref = f32[32,128]{1,0:T(8,128)S(1)} custom-call(s32[1]{0:T(128)} %bitcast.1.blk_at, bf16[16,296,128]{2,1,0:T(8,128)(2,1)S(1)} %all-to-all-done.got_ref), custom_call_target="tpu_custom_call" | custom-call | flops 905969664 | bytes 2097152 | tf_op jit(solution)/shard_map/pallas_call | solution.py:354
  47.8 0.0 copy-start.1
  47.8 0.0 collective-permute-done.5.refs_3_
  47.8 1.3 %shard_map.41 = (f32[8,128]{1,0:T(8,128)S(1)}, f32[8,128]{1,0:T(8,128)S(1)}, f32[8,128]{1,0:T(8,128)S(1)}, f32[8,128]{1,0:T(8,128)S(1)}) custom-call(s32[1]{0:T(128)} %bitcast.docs_at.at_ref, f32[32,128]{1,0:T(8,128)S(1)} %shard_map.38.small_ref, f32[1,768]{1,0:T(1,128)S(1)} %shard_map.40.best_ref, bf16[272,768]{1,0:T(8,128)(2,1)S(1)} %shard_map.39.refs_0_, ...), custom_call_target="tpu_custom_call" | custom-call | flops 704643072 | bytes 2097152 | tf_op jit(solution)/shard_map/pallas_call | solution.py:365
  49.1 4.0 %collective-permute-start.6 = (f32[8,128]{1,0:T(8,128)S(1)}, f32[8,128]{1,0:T(8,128)S(1)}, u32[]{:S(2)}, u32[]{:S(2)}) collective-permute-start(f32[8,128]{1,0:T(8,128)S(1)} %get-tuple-element.27), channel_id=1, source_target_pairs={{0,1},{1,2},{2,3},{3,0},{4,5},{5,6},{6,7},{7,4},{8,9},{9,10},{10,1... | collective-permute-start | bytes 12296 | tf_op jit(solution)/shard_map/ppermute | solution.py:327
  53.1 1.7 %collective-permute-start.7 = (f32[8,128]{1,0:T(8,128)S(1)}, f32[8,128]{1,0:T(8,128)S(1)}, u32[]{:S(2)}, u32[]{:S(2)}) collective-permute-start(f32[8,128]{1,0:T(8,128)S(1)} %get-tuple-element.28), channel_id=1, source_target_pairs={{0,2},{1,3},{2,0},{3,1},{4,6},{5,7},{6,4},{7,5},{8,10},{9,11},{10,... | collective-permute-start | bytes 12296 | tf_op jit(solution)/shard_map/ppermute | solution.py:327
  54.8 2.3 %collective-permute-start.8 = (f32[8,128]{1,0:T(8,128)S(1)}, f32[8,128]{1,0:T(8,128)S(1)}, u32[]{:S(2)}, u32[]{:S(2)}) collective-permute-start(f32[8,128]{1,0:T(8,128)S(1)} %get-tuple-element.29), channel_id=1, source_target_pairs={{0,3},{1,0},{2,1},{3,2},{4,7},{5,4},{6,5},{7,6},{8,11},{9,8},{10,9... | collective-permute-start | bytes 12296 | tf_op jit(solution)/shard_map/ppermute | solution.py:327
  57.1 0.0 collective-permute-done.6.refs_1_
  57.1 0.0 collective-permute-done.7.refs_2_
  57.1 0.7 %collective-permute-done.8.refs_3_ = f32[8,128]{1,0:T(8,128)S(1)} collective-permute-done((f32[8,128]{1,0:T(8,128)S(1)}, f32[8,128]{1,0:T(8,128)S(1)}, u32[]{:S(2)}, u32[]{:S(2)}) %collective-permute-start.8) | collective-permute-done | bytes 4128 | tf_op jit(solution)/shard_map/ppermute | solution.py:327
  57.9 0.9 %collective-permute-start.9 = (f32[8,128]{1,0:T(8,128)S(1)}, f32[8,128]{1,0:T(8,128)S(1)}, u32[]{:S(2)}, u32[]{:S(2)}) collective-permute-start(f32[8,128]{1,0:T(8,128)S(1)} %get-tuple-element.31), channel_id=1, source_target_pairs={{0,4},{4,8},{8,12},{12,0},{1,5},{5,9},{9,13},{13,1},{2,6},{6,10},{... | collective-permute-start | bytes 12296 | tf_op jit(solution)/shard_map/ppermute | solution.py:327
  58.8 0.7 %collective-permute-start.10 = (f32[8,128]{1,0:T(8,128)S(1)}, f32[8,128]{1,0:T(8,128)S(1)}, u32[]{:S(2)}, u32[]{:S(2)}) collective-permute-start(f32[8,128]{1,0:T(8,128)S(1)} %get-tuple-element.32), channel_id=1, source_target_pairs={{0,8},{4,12},{8,0},{12,4},{1,9},{5,13},{9,1},{13,5},{2,10},{6,14},... | collective-permute-start | bytes 12296 | tf_op jit(solution)/shard_map/ppermute | solution.py:327
  59.4 0.7 %collective-permute-start.11 = (f32[8,128]{1,0:T(8,128)S(1)}, f32[8,128]{1,0:T(8,128)S(1)}, u32[]{:S(2)}, u32[]{:S(2)}) collective-permute-start(f32[8,128]{1,0:T(8,128)S(1)} %get-tuple-element.33), channel_id=1, source_target_pairs={{0,12},{4,0},{8,4},{12,8},{1,13},{5,1},{9,5},{13,9},{2,14},{6,2},{... | collective-permute-start | bytes 12296 | tf_op jit(solution)/shard_map/ppermute | solution.py:327
  60.1 0.0 copy-done.1
  60.2 0.0 collective-permute-done.9.refs_1_
  60.2 1.0 %collective-permute-done.10.refs_2_ = f32[8,128]{1,0:T(8,128)S(1)} collective-permute-done((f32[8,128]{1,0:T(8,128)S(1)}, f32[8,128]{1,0:T(8,128)S(1)}, u32[]{:S(2)}, u32[]{:S(2)}) %collective-permute-start.10) | collective-permute-done | bytes 4128 | tf_op jit(solution)/shard_map/ppermute | solution.py:327
  61.2 1.2 %collective-permute-done.11.refs_3_ = f32[8,128]{1,0:T(8,128)S(1)} collective-permute-done((f32[8,128]{1,0:T(8,128)S(1)}, f32[8,128]{1,0:T(8,128)S(1)}, u32[]{:S(2)}, u32[]{:S(2)}) %collective-permute-start.11) | collective-permute-done | bytes 4128 | tf_op jit(solution)/shard_map/ppermute | solution.py:327
  62.5 0.8 %shard_map.44 = f32[1,512]{1,0:T(1,128)} custom-call(f32[8,128]{1,0:T(8,128)S(1)} %get-tuple-element.30.refs_0_, f32[8,128]{1,0:T(8,128)S(1)} %collective-permute-done.9.refs_1_, f32[8,128]{1,0:T(8,128)S(1)} %collective-permute-done.10.refs_2_, f32[8,128]{1,0:T(8,128)S(1)} %collective-permute-done.11.refs_3_, bf16[96,512]{1,0:T(8,128)(2,1)S(1)} %get-tuple-element.35.refs_4_, ...), custom_call_target="tpu_custom_call" | custom-call | flops 6291456 | bytes 262144 | tf_op jit(solution)/shard_map/pallas_call | solution.py:383
  (3 shorter events, 0.1 us)
Async XLA Ops:
  4.5 7.5 %copy-start.4 = (bf16[80,768]{1,0:T(8,128)(2,1)S(1)}, bf16[80,768]{1,0:T(8,128)(2,1)}, u32[]{:S(2)}) copy-start(bf16[80,768]{1,0:T(8,128)(2,1)} %get-tuple-element.23) | copy-start | bytes 368644
  4.6 9.2 %copy-start.3 = (bf16[80,768]{1,0:T(8,128)(2,1)S(1)}, bf16[80,768]{1,0:T(8,128)(2,1)}, u32[]{:S(2)}) copy-start(bf16[80,768]{1,0:T(8,128)(2,1)} %get-tuple-element.24) | copy-start | bytes 368644
  4.6 9.2 %copy-start.2 = (bf16[80,768]{1,0:T(8,128)(2,1)S(1)}, bf16[80,768]{1,0:T(8,128)(2,1)}, u32[]{:S(2)}) copy-start(bf16[80,768]{1,0:T(8,128)(2,1)} %get-tuple-element.25) | copy-start | bytes 368644
  4.6 27.8 %copy-start = (bf16[80,768]{1,0:T(8,128)(2,1)S(1)}, bf16[80,768]{1,0:T(8,128)(2,1)}, u32[]{:S(2)}) copy-start(bf16[80,768]{1,0:T(8,128)(2,1)} %get-tuple-element.22.refs_0_) | copy-start | bytes 368644
  4.6 41.7 %all-to-all-start = ((bf16[16,296,128]{2,1,0:T(8,128)(2,1)}), bf16[16,296,128]{2,1,0:T(8,128)(2,1)S(1)}, u32[]{:S(2)}, u32[]{:S(2)}) async-start(bf16[16,296,128]{2,1,0:T(8,128)(2,1)} %get-tuple-element.21), calls=%async_computation | async-start | bytes 2424832 | tf_op jit(solution)/shard_map/all_to_all | solution.py:340
  12.1 13.5 %collective-permute-start = (bf16[80,768]{1,0:T(8,128)(2,1)S(1)}, bf16[80,768]{1,0:T(8,128)(2,1)S(1)}, u32[]{:S(2)}, u32[]{:S(2)}) collective-permute-start(bf16[80,768]{1,0:T(8,128)(2,1)S(1)} %copy-done.4), channel_id=1, source_target_pairs={{0,4},{4,8},{8,12},{12,0},{1,5},{5,9},{9,13},{13,1},{2,6},{6,10},{... | collective-permute-start | bytes 368648 | tf_op jit(solution)/shard_map/ppermute | solution.py:327
  13.7 18.1 %collective-permute-start.1 = (bf16[80,768]{1,0:T(8,128)(2,1)S(1)}, bf16[80,768]{1,0:T(8,128)(2,1)S(1)}, u32[]{:S(2)}, u32[]{:S(2)}) collective-permute-start(bf16[80,768]{1,0:T(8,128)(2,1)S(1)} %copy-done.3), channel_id=1, source_target_pairs={{0,8},{4,12},{8,0},{12,4},{1,9},{5,13},{9,1},{13,5},{2,10},{6,14},... | collective-permute-start | bytes 368648 | tf_op jit(solution)/shard_map/ppermute | solution.py:327
  13.8 18.6 %collective-permute-start.2 = (bf16[80,768]{1,0:T(8,128)(2,1)S(1)}, bf16[80,768]{1,0:T(8,128)(2,1)S(1)}, u32[]{:S(2)}, u32[]{:S(2)}) collective-permute-start(bf16[80,768]{1,0:T(8,128)(2,1)S(1)} %copy-done.2), channel_id=1, source_target_pairs={{0,12},{4,0},{8,4},{12,8},{1,13},{5,1},{9,5},{13,9},{2,14},{6,2},{... | collective-permute-start | bytes 368648 | tf_op jit(solution)/shard_map/ppermute | solution.py:327
  32.4 2.8 %collective-permute-start.4 = (bf16[272,768]{1,0:T(8,128)(2,1)S(1)}, bf16[272,768]{1,0:T(8,128)(2,1)S(1)}, u32[]{:S(2)}, u32[]{:S(2)}) collective-permute-start(bf16[272,768]{1,0:T(8,128)(2,1)S(1)} %shard_map.39.refs_0_), channel_id=1, source_target_pairs={{0,1},{5,6},{8,9},{13,14},{16,17},{21,22},{24,25},{29,30}} | collective-permute-start | bytes 1253384 | tf_op jit(solution)/shard_map/ppermute | solution.py:352
  33.1 8.5 %collective-permute-start.3 = (bf16[272,768]{1,0:T(8,128)(2,1)S(1)}, bf16[272,768]{1,0:T(8,128)(2,1)S(1)}, u32[]{:S(2)}, u32[]{:S(2)}) collective-permute-start(bf16[272,768]{1,0:T(8,128)(2,1)S(1)} %shard_map.39.refs_0_), channel_id=1, source_target_pairs={{3,1},{4,6},{11,9},{12,14},{19,17},{20,22},{27,25},{28,30}} | collective-permute-start | bytes 1253384 | tf_op jit(solution)/shard_map/ppermute | solution.py:352
  34.4 13.3 %collective-permute-start.5 = (bf16[272,768]{1,0:T(8,128)(2,1)S(1)}, bf16[272,768]{1,0:T(8,128)(2,1)S(1)}, u32[]{:S(2)}, u32[]{:S(2)}) collective-permute-start(bf16[272,768]{1,0:T(8,128)(2,1)S(1)} %shard_map.39.refs_0_), channel_id=1, source_target_pairs={{2,1},{7,6},{10,9},{15,14},{18,17},{23,22},{26,25},{31,30}} | collective-permute-start | bytes 1253384 | tf_op jit(solution)/shard_map/ppermute | solution.py:352
  47.8 12.4 %copy-start.1 = (s32[8,512]{1,0:T(8,128)S(1)}, s32[8,512]{1,0:T(8,128)}, u32[]{:S(2)}) copy-start(s32[8,512]{1,0:T(8,128)} %get-tuple-element.34.info_ref) | copy-start | bytes 49156
  49.1 8.0 %collective-permute-start.6 = (f32[8,128]{1,0:T(8,128)S(1)}, f32[8,128]{1,0:T(8,128)S(1)}, u32[]{:S(2)}, u32[]{:S(2)}) collective-permute-start(f32[8,128]{1,0:T(8,128)S(1)} %get-tuple-element.27), channel_id=1, source_target_pairs={{0,1},{1,2},{2,3},{3,0},{4,5},{5,6},{6,7},{7,4},{8,9},{9,10},{10,1... | collective-permute-start | bytes 12296 | tf_op jit(solution)/shard_map/ppermute | solution.py:327
  53.1 4.0 %collective-permute-start.7 = (f32[8,128]{1,0:T(8,128)S(1)}, f32[8,128]{1,0:T(8,128)S(1)}, u32[]{:S(2)}, u32[]{:S(2)}) collective-permute-start(f32[8,128]{1,0:T(8,128)S(1)} %get-tuple-element.28), channel_id=1, source_target_pairs={{0,2},{1,3},{2,0},{3,1},{4,6},{5,7},{6,4},{7,5},{8,10},{9,11},{10,... | collective-permute-start | bytes 12296 | tf_op jit(solution)/shard_map/ppermute | solution.py:327
  54.8 3.0 %collective-permute-start.8 = (f32[8,128]{1,0:T(8,128)S(1)}, f32[8,128]{1,0:T(8,128)S(1)}, u32[]{:S(2)}, u32[]{:S(2)}) collective-permute-start(f32[8,128]{1,0:T(8,128)S(1)} %get-tuple-element.29), channel_id=1, source_target_pairs={{0,3},{1,0},{2,1},{3,2},{4,7},{5,4},{6,5},{7,6},{8,11},{9,8},{10,9... | collective-permute-start | bytes 12296 | tf_op jit(solution)/shard_map/ppermute | solution.py:327
  57.9 2.3 %collective-permute-start.9 = (f32[8,128]{1,0:T(8,128)S(1)}, f32[8,128]{1,0:T(8,128)S(1)}, u32[]{:S(2)}, u32[]{:S(2)}) collective-permute-start(f32[8,128]{1,0:T(8,128)S(1)} %get-tuple-element.31), channel_id=1, source_target_pairs={{0,4},{4,8},{8,12},{12,0},{1,5},{5,9},{9,13},{13,1},{2,6},{6,10},{... | collective-permute-start | bytes 12296 | tf_op jit(solution)/shard_map/ppermute | solution.py:327
  58.8 2.5 %collective-permute-start.10 = (f32[8,128]{1,0:T(8,128)S(1)}, f32[8,128]{1,0:T(8,128)S(1)}, u32[]{:S(2)}, u32[]{:S(2)}) collective-permute-start(f32[8,128]{1,0:T(8,128)S(1)} %get-tuple-element.32), channel_id=1, source_target_pairs={{0,8},{4,12},{8,0},{12,4},{1,9},{5,13},{9,1},{13,5},{2,10},{6,14},... | collective-permute-start | bytes 12296 | tf_op jit(solution)/shard_map/ppermute | solution.py:327
  59.4 3.0 %collective-permute-start.11 = (f32[8,128]{1,0:T(8,128)S(1)}, f32[8,128]{1,0:T(8,128)S(1)}, u32[]{:S(2)}, u32[]{:S(2)}) collective-permute-start(f32[8,128]{1,0:T(8,128)S(1)} %get-tuple-element.33), channel_id=1, source_target_pairs={{0,12},{4,0},{8,4},{12,8},{1,13},{5,1},{9,5},{13,9},{2,14},{6,2},{... | collective-permute-start | bytes 12296 | tf_op jit(solution)/shard_map/ppermute | solution.py:327

commit v15 on v14

--- a/solution.py
+++ b/solution.py
@@ -59,7 +59,9 @@
         ((cluster_hbm, cluster_ref), (weight_hbm, weight_ref), (pooled_hbm, pooled_ref)))]
     for fetch in fetches:
         fetch.start()
-    fetches[0].wait()
+    earlier = (iota((docs, docs), 0) < iota((docs, docs), 1)).astype(jnp.float32).astype(jnp.bfloat16)
+    for fetch in fetches:
+        fetch.wait()
 
     cluster = cluster_ref[...]
     is_big = cluster < limit
@@ -70,7 +72,6 @@
 
     padded = -(-buckets // 16) * 16
     hot = (iota((padded, docs), 0) == bucket).astype(jnp.float32)
-    earlier = (iota((docs, docs), 0) < iota((docs, docs), 1)).astype(jnp.float32).astype(jnp.bfloat16)
     before = jnp.dot(hot.astype(jnp.bfloat16), earlier, preferred_element_type=jnp.float32)
     rank = jnp.sum(before * hot, axis=0, keepdims=True).astype(jnp.int32)
 
@@ -81,26 +82,31 @@
     sends = [pltpu.make_async_copy(info_ref, info_hbm, sems.at[3])]
     sends[0].start()
     small_slot = jnp.where(is_big, -1, target * cap_small + rank)
-    ids = ids_table(iota((devices, docs), 0) == bucket, info_ref)
+    quota = info_ref[2:3, :].astype(jnp.float32)
+    lanes = (iota((LANES, docs), 0) == info_ref[1:2, :]).astype(jnp.float32).astype(jnp.bfloat16)
+
+    def ids_table(mine):
+        return dot_nt(jnp.where(mine, quota, 0.0).astype(jnp.bfloat16), lanes)
+
+    ids = ids_table(iota((devices, docs), 0) == bucket)
+    slabs = feature // LANES
     shift = modulo(owner + shards - docs_at[0], shards)
     big_slot = jnp.where(is_big, shift * cap_big + rank, -1)
     for by in range(shards):
         mine = (iota((16, docs), 0) == 0) & is_big & (shift == by)
-        big_ref[by, cap_big:, 0:LANES] = ids_table(mine, info_ref).astype(jnp.bfloat16)
-        big_ref[by, cap_big:, LANES:] = jnp.zeros((16, feature - LANES), jnp.bfloat16)
-
-    for fetch in fetches[1:]:
-        fetch.wait()
+        big_ref[by, slabs * cap_big:, :] = ids_table(mine).astype(jnp.bfloat16)
+
     projected = jnp.dot(pooled_ref[...], weight_ref[...], preferred_element_type=jnp.float32)
     squares = jnp.sum(projected * projected, axis=1, keepdims=True)
     rows_ref[...] = (projected * lax.rsqrt(squares + 1e-06)).astype(jnp.bfloat16)
     picked = picked_rows(rows_ref, big_slot, 0, shards * cap_big)
     for by, out in enumerate(big_hbm):
-        big_ref[by, 0:cap_big, :] = picked[by * cap_big:(by + 1) * cap_big, :]
+        for slab in range(slabs):
+            big_ref[by, slab * cap_big:(slab + 1) * cap_big, :] = picked[
+                by * cap_big:(by + 1) * cap_big, slab * LANES:(slab + 1) * LANES]
         sends.append(pltpu.make_async_copy(big_ref.at[by], out, big_sems.at[by]))
         sends[-1].start()
 
-    slabs = feature // LANES
     group = devices // small_sems.shape[0]
     for part in range(small_sems.shape[0]):
         first = part * group
@@ -118,24 +124,18 @@
         send.wait()
 
 
-def ids_table(mine, info_ref):
-    docs = info_ref.shape[1]
-    quota = info_ref[2:3, :].astype(jnp.float32)
-    lanes = (iota((LANES, docs), 0) == info_ref[1:2, :]).astype(jnp.float32).astype(jnp.bfloat16)
-    return dot_nt(jnp.where(mine, quota, 0.0).astype(jnp.bfloat16), lanes)
-
-
-def group_kernel(cap_big, *refs):
+def group_kernel(slabs, cap_big, *refs):
     held, group_ref = refs[:-1], refs[-1]
     total = len(held) * cap_big
-    spare = group_ref.shape[0] - total
+    spare = group_ref.shape[0] - slabs * total
     own = jnp.zeros((spare, LANES), jnp.float32)
     for shift, ref in enumerate(held):
-        group_ref[shift * cap_big:(shift + 1) * cap_big, :] = ref[0:cap_big, :]
-        table = ref[cap_big:, 0:LANES].astype(jnp.float32)
+        for slab in range(slabs):
+            at = slab * total + shift * cap_big
+            group_ref[at:at + cap_big, :] = ref[slab * cap_big:(slab + 1) * cap_big, :]
+        table = ref[slabs * cap_big:, :].astype(jnp.float32)
         own = jnp.where(iota(own.shape, 0) == shift, table[0:1, :], own)
-    group_ref[total:, 0:LANES] = own.astype(jnp.bfloat16)
-    group_ref[total:, LANES:] = jnp.zeros((spare, group_ref.shape[1] - LANES), jnp.bfloat16)
+    group_ref[slabs * total:, :] = own.astype(jnp.bfloat16)
 
 
 def turn(tables, at, count, outs):
@@ -172,11 +172,19 @@
             cap_small + lax.rem(at, jnp.int32(cap_big)))
 
 
-def big_ids(held, sources):
+def big_ids(held, rows, sources):
     part, shift, lane = sources
-    spare = held[0].shape[0] - part.shape[1] // len(held)
-    values = jnp.concatenate([ref[ref.shape[0] - spare:, 0:LANES] for ref in held], axis=0)
+    spare = held[0].shape[0] - rows
+    values = jnp.concatenate([ref[rows:, :] for ref in held], axis=0)
     return ids_from(values, part * spare + shift, lane)
+
+
+def assemble(held, rows_ref):
+    size, slabs = rows_ref.shape[0] // len(held), rows_ref.shape[1] // LANES
+    for part, ref in enumerate(held):
+        for slab in range(slabs):
+            rows_ref[part * size:(part + 1) * size, slab * LANES:(slab + 1) * LANES] = ref[
+                slab * size:(slab + 1) * size, :]
 
 
 def big_pairs(held, row_ids, col_ids, bests, pairs):
@@ -184,8 +192,8 @@
     for row, col in pairs:
         same = 0 if row == col else None
         bests[col] = jnp.maximum(bests[col], block_best(
-            held[row][0:size, :], col_ids[row * size:(row + 1) * size], same,
-            held[col][0:size, :], row_ids[:, col * size:(col + 1) * size], same))
+            held[row][...], col_ids[row * size:(row + 1) * size], same,
+            held[col][...], row_ids[:, col * size:(col + 1) * size], same))
     return bests
 
 
@@ -224,26 +232,30 @@
 
 
 def big_kernel(shards, cap_big, cap_small, *refs):
-    held, best_ref = refs[:-1], refs[-1]
-    size = shards * cap_big
-    row_ids = big_ids(held, big_sources(len(held) * size, shards, cap_big, cap_small))
+    held, best_ref, rows_ref = refs[:-2], refs[-2], refs[-1]
+    size, slabs = shards * cap_big, rows_ref.shape[1] // LANES
+    assemble(held, rows_ref)
+    row_ids = big_ids(held, slabs * size, big_sources(len(held) * size, shards, cap_big, cap_small))
     col_ids = as_column(row_ids)
+    rows = [rows_ref.at[pl.ds(part * size, size)] for part in range(len(held))]
     pairs = [(row, col) for row in range(len(held)) for col in range(len(held))]
-    bests = big_pairs(held, row_ids, col_ids, [jnp.full((1, size), -1.0, jnp.float32)] * len(held), pairs)
+    bests = big_pairs(rows, row_ids, col_ids, [jnp.full((1, size), -1.0, jnp.float32)] * len(held), pairs)
     best_ref[...] = jnp.concatenate(bests, axis=1)
 
 
-def big_last_kernel(shards, blocks, cap_big, cap_small, docs_at, small_ref, best_ref, *refs):
-    held, back_refs = refs[:blocks], refs[blocks:]
-    size = shards * cap_big
+def big_last_kernel(shards, blocks, cap_big, cap_small, docs_at, small_ref, best_ref, rows_ref, *refs):
+    held, back_refs, last_ref = refs[:blocks], refs[blocks:-1], refs[-1]
+    size, slabs = shards * cap_big, rows_ref.shape[1] // LANES
     high = back_refs[0].shape[0]
+    last = blocks - 1
+    assemble(held[last:], last_ref)
     part, shift, lane = big_sources(blocks * size, shards, cap_big, cap_small)
-    row_ids = big_ids(held, (part, shift, lane))
+    row_ids = big_ids(held, slabs * size, (part, shift, lane))
     col_ids = as_column(row_ids)
-    last = blocks - 1
+    rows = [rows_ref.at[pl.ds(at * size, size)] for at in range(last)] + [last_ref]
     pairs = [(row, last) for row in range(blocks)] + [(last, col) for col in range(last)]
     bests = [best_ref[:, col * size:(col + 1) * size] for col in range(last)]
-    bests = big_pairs(held, row_ids, col_ids, bests + [jnp.full((1, size), -1.0, jnp.float32)], pairs)
+    bests = big_pairs(rows, row_ids, col_ids, bests + [jnp.full((1, size), -1.0, jnp.float32)], pairs)
     docs = modulo(docs_at[0] + shards - shift, shards)
     step = jnp.where(part == 0, 0, jnp.where(part == last, 1, part + 1))
     back = small_ref[...] + spread(jnp.concatenate(bests, axis=1), step * high + docs, lane, small_ref.shape[0])
@@ -326,14 +338,17 @@
     def along(x, axis, count, by):
         return lax.ppermute(x, axis, [(i, (i + by) % count) for i in range(count)])
 
-    small_rows = feature // LANES * cap_small + 8
+    slabs = feature // LANES
+    small_rows = slabs * cap_small + 8
+    big_rows = slabs * cap_big + 16
+    group_rows = slabs * big_slots + rows_up(shards, 16)
     small_sent, info, *big_sent = call(
         functools.partial(sort_kernel, *sizes),
-        [((devices, small_rows, LANES), bf16, hbm), ((8, docs), i32, hbm)] + [((cap_big + 16, feature), bf16, hbm)] * shards,
+        [((devices, small_rows, LANES), bf16, hbm), ((8, docs), i32, hbm)] + [((big_rows, LANES), bf16, hbm)] * shards,
         [smem, hbm, hbm, hbm],
         2 * docs * feature * (pooled.shape[1] + small_slots), 4 << 20, 60,
         [vmem(pooled.shape, bf16), vmem(proj_weight.shape, bf16), vmem((1, docs), i32),
-         vmem((devices, small_rows, LANES), bf16), vmem((shards, cap_big + 16, feature), bf16),
+         vmem((devices, small_rows, LANES), bf16), vmem((shards, big_rows, LANES), bf16),
          vmem((docs, feature), bf16), vmem((8, docs), i32), dma((4,)), dma((4,)), dma((shards,))],
     )(docs_at, pooled, proj_weight, cluster.reshape(1, docs))
 
@@ -341,9 +356,9 @@
 
     held = [big_sent[0]] + [along(big_sent[by], "docs", shards, by) for by in range(1, shards)]
     group, = call(
-        functools.partial(group_kernel, cap_big),
-        [((big_slots + rows_up(shards, 16), feature), bf16, vmem)], [vmem] * shards,
-        big_slots * feature, 1 << 30,
+        functools.partial(group_kernel, slabs, cap_big),
+        [((group_rows, LANES), bf16, vmem)], [vmem] * shards,
+        big_slots * feature, 1 << 20,
     )(*held)
     parts = [group]
     for step in big_steps(blocks)[1:]:
@@ -357,16 +372,18 @@
         2 * small_slots * small_slots * feature, 2 << 20, 16,
         [vmem((small_slots, feature), bf16)],
     )(blk_at, got_small)
-    early, = call(
+    early, early_rows = call(
         functools.partial(big_kernel, shards, cap_big, cap_small),
-        [((1, big_total - big_slots), f32, vmem)], [vmem] * (blocks - 1),
+        [((1, big_total - big_slots), f32, vmem), ((big_total - big_slots, feature), bf16, vmem)],
+        [vmem] * (blocks - 1),
         2 * (big_total - big_slots) ** 2 * feature, 2 << 20,
     )(*parts[:-1])
     back = call(
         functools.partial(big_last_kernel, *sizes),
-        [((rows_up(shards), LANES), f32, vmem)] * blocks, [smem] + [vmem] * (blocks + 2),
-        2 * (2 * big_total - big_slots) * big_slots * feature, 2 << 20,
-    )(docs_at, back_small, early, *parts)
+        [((rows_up(shards), LANES), f32, vmem)] * blocks, [smem] + [vmem] * (blocks + 3),
+        2 * (2 * big_total - big_slots) * big_slots * feature, 2 << 20, 16,
+        [vmem((big_slots, feature), bf16)],
+    )(docs_at, back_small, early, early_rows, *parts)
     back = [back[0]] + [along(back[by], "blk", blocks, by) for by in range(1, blocks)]
     back = call(
         functools.partial(turn_kernel, shards),

time: 63.5 us -> 66.4 us (1.046)
  waiting for transfers between devices: 30.9 us -> 28.2 us
  starting transfers between devices: 22.7 us -> 25 us
  local copies, waits for them, and re-layouts: 0.02 us -> 1.81 us
  Pallas kernels: 9.49 us -> 10.9 us
    unnamed x10 -> x16, local copies, waits for them, and re-layouts: 0.02 us -> 1.81 us
    ppermute x9, starting transfers between devices: 12.5 us -> 14.1 us  [along(): return lax.ppermute(x, axis, [(i, (i + by) % count) for i in range(count)])]
    all_to_all x1, waiting for transfers between devices: 3.41 us -> 1.88 us  [body(): lax.all_to_all(small_sent, ('docs', 'blk'), split_axis=0, concat_axis=0,...]
    pallas_call x1, Pallas kernels: 1.34 us -> 2.35 us  [body(): call(functools.partial(big_last_kernel, *sizes), [((rows_up(shards), LANE...]
    ppermute x9, waiting for transfers between devices: 21.1 us -> 20.1 us  [along(): return lax.ppermute(x, axis, [(i, (i + by) % count) for i in range(count)])]
    ppermute x3, starting transfers between devices: 2.74 us -> 3.42 us  [body(): parts.append(lax.ppermute(group, ('docs', 'blk'), pairs))]
where the time goes in v15:
time: 66.4 us; the launch traced here: 66 us
  waiting for transfers between devices  28.2 us (42%)
  starting transfers between devices  25 us (38%)
  Pallas kernels  10.9 us (16%)
  local copies, waits for them, and re-layouts  1.81 us (3%)
    ppermute x9, waiting for transfers between devices, along(): return lax.ppermute(x, axis, [(i, (i + by) % count) for i in range(count)])  20.1 us
    ppermute x9, starting transfers between devices, along(): return lax.ppermute(x, axis, [(i, (i + by) % count) for i in range(count)])  14.1 us
    all_to_all x1, starting transfers between devices, body(): lax.all_to_all(small_sent, ('docs', 'blk'), split_axis=0, concat_axis=0,...  7.47 us
    ppermute x3, waiting for transfers between devices, body(): parts.append(lax.ppermute(group, ('docs', 'blk'), pairs))  6.23 us
    pallas_call x1, Pallas kernels, body(): call(functools.partial(sort_kernel, *sizes), [((devices, small_rows, LANE...  4.86 us
    ppermute x3, starting transfers between devices, body(): parts.append(lax.ppermute(group, ('docs', 'blk'), pairs))  3.42 us
    pallas_call x1, Pallas kernels, body(): call(functools.partial(big_last_kernel, *sizes), [((rows_up(shards), LANE...  2.35 us
    all_to_all x1, waiting for transfers between devices, body(): lax.all_to_all(small_sent, ('docs', 'blk'), split_axis=0, concat_axis=0,...  1.88 us
  transfers between devices with their start and end apart: 13, of which 8 were waited for; matrix products, arithmetic and copies ran while one was open for 0% of the time, Pallas kernels for 4%

profile of v15, /device:TPU:1, one launch (start us, length us, event | category | flops | bytes accessed | tf_op | source)
XLA Modules:
  0.0 66.0 jit_solution(12614614773437846035)
XLA Ops:
  0.0 4.9 %shard_map.37 = (bf16[16,296,128]{2,1,0:T(8,128)(2,1)}, s32[8,512]{1,0:T(8,128)}, bf16[400,128]{1,0:T(8,128)(2,1)}, bf16[400,128]{1,0:T(8,128)(2,1)}, bf16[400,1...) custom-call(s32[1]{0:T(128)} %bitcast.docs_at.at_ref, bf16[512,768]{1,0:T(8,128)(2,1)} %pooled_hbm.1, ...), custom_call_target="tpu_custom_call" | custom-call | flops 1207959552 | bytes 4194304 | tf_op jit(solution)/shard_map/pallas_call | solution.py:345
  4.9 0.0 copy-start.7
  4.9 0.0 copy-start.6
  4.9 0.0 copy-start.5
  4.9 0.0 copy-start.3
  4.9 7.5 %all-to-all-start = ((bf16[16,296,128]{2,1,0:T(8,128)(2,1)}), bf16[16,296,128]{2,1,0:T(8,128)(2,1)S(1)}, u32[]{:S(2)}, u32[]{:S(2)}) async-start(bf16[16,296,128]{2,1,0:T(8,128)(2,1)} %get-tuple-element.23), calls=%async_computation | async-start | bytes 2424832 | tf_op jit(solution)/shard_map/all_to_all | solution.py:355
  12.4 0.0 copy-done.7
  12.4 1.7 %collective-permute-start = (bf16[400,128]{1,0:T(8,128)(2,1)S(1)}, bf16[400,128]{1,0:T(8,128)(2,1)S(1)}, u32[]{:S(2)}, u32[]{:S(2)}) collective-permute-start(bf16[400,128]{1,0:T(8,128)(2,1)S(1)} %copy-done.7), channel_id=1, source_target_pairs={{0,4},{4,8},{8,12},{12,0},{1,5},{5,9},{9,13},{13,1},{2,6},{6,10},{... | collective-permute-start | bytes 307208 | tf_op jit(solution)/shard_map/ppermute | solution.py:339
  14.1 0.0 copy-done.6
  14.1 0.0 collective-permute-start.1
  14.1 0.0 copy-done.5
  14.1 0.5 collective-permute-start.2
  14.6 9.1 %collective-permute-done.refs_1_ = bf16[400,128]{1,0:T(8,128)(2,1)S(1)} collective-permute-done((bf16[400,128]{1,0:T(8,128)(2,1)S(1)}, bf16[400,128]{1,0:T(8,128)(2,1)S(1)}, u32[]{:S(2)}, u32[]{:S(2)}) %collective-permute-start) | collective-permute-done | bytes 102432 | tf_op jit(solution)/shard_map/ppermute | solution.py:339
  23.8 7.4 %collective-permute-done.1.refs_2_ = bf16[400,128]{1,0:T(8,128)(2,1)S(1)} collective-permute-done((bf16[400,128]{1,0:T(8,128)(2,1)S(1)}, bf16[400,128]{1,0:T(8,128)(2,1)S(1)}, u32[]{:S(2)}, u32[]{:S(2)}) %collective-permute-start.1) | collective-permute-done | bytes 102432 | tf_op jit(solution)/shard_map/ppermute | solution.py:339
  31.1 0.6 collective-permute-done.2.refs_3_
  31.7 0.0 copy-done.3
  31.7 1.3 %collective-permute-start.3 = (bf16[1552,128]{1,0:T(8,128)(2,1)S(1)}, bf16[1552,128]{1,0:T(8,128)(2,1)S(1)}, u32[]{:S(2)}, u32[]{:S(2)}) collective-permute-start(bf16[1552,128]{1,0:T(8,128)(2,1)S(1)} %shard_map.39.refs_0_), channel_id=1, source_target_pairs={{3,1},{4,6},{11,9},{12,14},{19,17},{20,22},{27,25},{28,30}} | collective-permute-start | bytes 1191944 | tf_op jit(solution)/shard_map/ppermute | solution.py:367
  33.1 0.7 %collective-permute-start.4 = (bf16[1552,128]{1,0:T(8,128)(2,1)S(1)}, bf16[1552,128]{1,0:T(8,128)(2,1)S(1)}, u32[]{:S(2)}, u32[]{:S(2)}) collective-permute-start(bf16[1552,128]{1,0:T(8,128)(2,1)S(1)} %shard_map.39.refs_0_), channel_id=1, source_target_pairs={{0,1},{5,6},{8,9},{13,14},{16,17},{21,22},{24,25},{29,30}} | collective-permute-start | bytes 1191944 | tf_op jit(solution)/shard_map/ppermute | solution.py:367
  33.8 1.4 %collective-permute-start.5 = (bf16[1552,128]{1,0:T(8,128)(2,1)S(1)}, bf16[1552,128]{1,0:T(8,128)(2,1)}, u32[]{:S(2)}, u32[]{:S(2)}) collective-permute-start(bf16[1552,128]{1,0:T(8,128)(2,1)S(1)} %shard_map.39.refs_0_), channel_id=1, source_target_pairs={{2,1},{7,6},{10,9},{15,14},{18,17},{23,22},{26,25},{31,30}} | collective-permute-start | bytes 1191944 | tf_op jit(solution)/shard_map/ppermute | solution.py:367
  35.2 6.2 %collective-permute-done.3.refs_1_ = bf16[1552,128]{1,0:T(8,128)(2,1)S(1)} collective-permute-done((bf16[1552,128]{1,0:T(8,128)(2,1)S(1)}, bf16[1552,128]{1,0:T(8,128)(2,1)S(1)}, u32[]{:S(2)}, u32[]{:S(2)}) %collective-permute-start.3) | collective-permute-done | bytes 397344 | tf_op jit(solution)/shard_map/ppermute | solution.py:367
  41.4 0.0 collective-permute-done.4.refs_2_
  41.4 0.0 copy-start
  41.4 0.8 %copy-done = bf16[1552,128]{1,0:T(8,128)(2,1)} copy-done((bf16[1552,128]{1,0:T(8,128)(2,1)}, bf16[1552,128]{1,0:T(8,128)(2,1)S(1)}, u32[]{:S(2)}) %copy-start) | copy-done | bytes 397336
  42.2 0.0 copy-start.1
  42.2 1.0 %copy-done.1 = bf16[1552,128]{1,0:T(8,128)(2,1)S(1)} copy-done((bf16[1552,128]{1,0:T(8,128)(2,1)S(1)}, bf16[1552,128]{1,0:T(8,128)(2,1)}, u32[]{:S(2)}) %copy-start.1) | copy-done | bytes 397336
  43.2 1.3 %shard_map.40 = (f32[1,768]{1,0:T(1,128)S(1)}, bf16[768,768]{1,0:T(8,128)(2,1)S(1)}) custom-call(bf16[1552,128]{1,0:T(8,128)(2,1)S(1)} %shard_map.39.refs_0_, bf16[1552,128]{1,0:T(8,128)(2,1)S(1)} %collective-permute-done.3.refs_1_, bf16[1552,128]{1,0:T(8,128)(2,1)S(1)} %copy-done.1), custom_call_target="tpu_custom_call" | custom-call | flops 905969664 | bytes 2097152 | tf_op jit(solution)/shard_map/pallas_call | solution.py:375
  44.5 1.9 %all-to-all-done.got_ref = bf16[16,296,128]{2,1,0:T(8,128)(2,1)S(1)} async-done(((bf16[16,296,128]{2,1,0:T(8,128)(2,1)}), bf16[16,296,128]{2,1,0:T(8,128)(2,1)S(1)}, u32[]{:S(2)}, u32[]{:S(2)}) %all-to-all-start) | async-done | bytes 1212448 | tf_op jit(solution)/shard_map/all_to_all | solution.py:355
  46.4 0.0 copy-start.2
  46.4 1.5 %shard_map.38.small_ref = f32[32,128]{1,0:T(8,128)S(1)} custom-call(s32[1]{0:T(128)} %bitcast.1.blk_at, bf16[16,296,128]{2,1,0:T(8,128)(2,1)S(1)} %all-to-all-done.got_ref), custom_call_target="tpu_custom_call" | custom-call | flops 905969664 | bytes 2097152 | tf_op jit(solution)/shard_map/pallas_call | solution.py:369
  47.9 0.0 collective-permute-done.5.refs_3_
  47.9 0.0 copy-done.2
  47.9 0.0 copy-start.4
  47.9 2.3 %shard_map.41 = (f32[8,128]{1,0:T(8,128)S(1)}, f32[8,128]{1,0:T(8,128)S(1)}, f32[8,128]{1,0:T(8,128)S(1)}, f32[8,128]{1,0:T(8,128)S(1)}) custom-call(s32[1]{0:T(128)} %bitcast.docs_at.at_ref, f32[32,128]{1,0:T(8,128)S(1)} %shard_map.38.small_ref, f32[1,768]{1,0:T(1,128)S(1)} %get-tuple-element.28.best_ref, bf16[768,768]{1,0:T(8,128)(2,1)S(1)} %get-tuple-element.29.rows_ref, ...), custom_call_target="tpu_custom_call" | custom-call | flops 704643072 | bytes 2097152 | tf_op jit(solution)/shard_map/pallas_call | solution.py:381
  50.3 5.6 %collective-permute-start.6 = (f32[8,128]{1,0:T(8,128)S(1)}, f32[8,128]{1,0:T(8,128)S(1)}, u32[]{:S(2)}, u32[]{:S(2)}) collective-permute-start(f32[8,128]{1,0:T(8,128)S(1)} %get-tuple-element.31), channel_id=1, source_target_pairs={{0,1},{1,2},{2,3},{3,0},{4,5},{5,6},{6,7},{7,4},{8,9},{9,10},{10,1... | collective-permute-start | bytes 12296 | tf_op jit(solution)/shard_map/ppermute | solution.py:339
  55.9 1.7 %collective-permute-start.7 = (f32[8,128]{1,0:T(8,128)S(1)}, f32[8,128]{1,0:T(8,128)S(1)}, u32[]{:S(2)}, u32[]{:S(2)}) collective-permute-start(f32[8,128]{1,0:T(8,128)S(1)} %get-tuple-element.32), channel_id=1, source_target_pairs={{0,2},{1,3},{2,0},{3,1},{4,6},{5,7},{6,4},{7,5},{8,10},{9,11},{10,... | collective-permute-start | bytes 12296 | tf_op jit(solution)/shard_map/ppermute | solution.py:339
  57.6 2.3 %collective-permute-start.8 = (f32[8,128]{1,0:T(8,128)S(1)}, f32[8,128]{1,0:T(8,128)S(1)}, u32[]{:S(2)}, u32[]{:S(2)}) collective-permute-start(f32[8,128]{1,0:T(8,128)S(1)} %get-tuple-element.33), channel_id=1, source_target_pairs={{0,3},{1,0},{2,1},{3,2},{4,7},{5,4},{6,5},{7,6},{8,11},{9,8},{10,9... | collective-permute-start | bytes 12296 | tf_op jit(solution)/shard_map/ppermute | solution.py:339
  59.9 0.0 collective-permute-done.6.refs_1_
  59.9 0.0 collective-permute-done.7.refs_2_
  59.9 0.7 %collective-permute-done.8.refs_3_ = f32[8,128]{1,0:T(8,128)S(1)} collective-permute-done((f32[8,128]{1,0:T(8,128)S(1)}, f32[8,128]{1,0:T(8,128)S(1)}, u32[]{:S(2)}, u32[]{:S(2)}) %collective-permute-start.8) | collective-permute-done | bytes 4128 | tf_op jit(solution)/shard_map/ppermute | solution.py:339
  60.7 0.1 collective-permute-start.9
  60.7 1.5 %collective-permute-start.10 = (f32[8,128]{1,0:T(8,128)S(1)}, f32[8,128]{1,0:T(8,128)S(1)}, u32[]{:S(2)}, u32[]{:S(2)}) collective-permute-start(f32[8,128]{1,0:T(8,128)S(1)} %get-tuple-element.36), channel_id=1, source_target_pairs={{0,8},{4,12},{8,0},{12,4},{1,9},{5,13},{9,1},{13,5},{2,10},{6,14},... | collective-permute-start | bytes 12296 | tf_op jit(solution)/shard_map/ppermute | solution.py:339
  62.2 0.7 %collective-permute-start.11 = (f32[8,128]{1,0:T(8,128)S(1)}, f32[8,128]{1,0:T(8,128)S(1)}, u32[]{:S(2)}, u32[]{:S(2)}) collective-permute-start(f32[8,128]{1,0:T(8,128)S(1)} %get-tuple-element.37), channel_id=1, source_target_pairs={{0,12},{4,0},{8,4},{12,8},{1,13},{5,1},{9,5},{13,9},{2,14},{6,2},{... | collective-permute-start | bytes 12296 | tf_op jit(solution)/shard_map/ppermute | solution.py:339
  62.9 0.0 copy-done.4
  62.9 0.0 collective-permute-done.9.refs_1_
  63.0 0.5 collective-permute-done.10.refs_2_
  63.4 1.8 %collective-permute-done.11.refs_3_ = f32[8,128]{1,0:T(8,128)S(1)} collective-permute-done((f32[8,128]{1,0:T(8,128)S(1)}, f32[8,128]{1,0:T(8,128)S(1)}, u32[]{:S(2)}, u32[]{:S(2)}) %collective-permute-start.11) | collective-permute-done | bytes 4128 | tf_op jit(solution)/shard_map/ppermute | solution.py:339
  65.2 0.8 %shard_map.44 = f32[1,512]{1,0:T(1,128)} custom-call(f32[8,128]{1,0:T(8,128)S(1)} %get-tuple-element.34.refs_0_, f32[8,128]{1,0:T(8,128)S(1)} %collective-permute-done.9.refs_1_, f32[8,128]{1,0:T(8,128)S(1)} %collective-permute-done.10.refs_2_, f32[8,128]{1,0:T(8,128)S(1)} %collective-permute-done.11.refs_3_, bf16[96,512]{1,0:T(8,128)(2,1)S(1)} %get-tuple-element.39.refs_4_, ...), custom_call_target="tpu_custom_call" | custom-call | flops 6291456 | bytes 262144 | tf_op jit(solution)/shard_map/pallas_call | solution.py:400
  (3 shorter events, 0.1 us)
Async XLA Ops:
  4.9 7.5 %copy-start.7 = (bf16[400,128]{1,0:T(8,128)(2,1)S(1)}, bf16[400,128]{1,0:T(8,128)(2,1)}, u32[]{:S(2)}) copy-start(bf16[400,128]{1,0:T(8,128)(2,1)} %get-tuple-element.25) | copy-start | bytes 307204
  4.9 9.2 %copy-start.6 = (bf16[400,128]{1,0:T(8,128)(2,1)S(1)}, bf16[400,128]{1,0:T(8,128)(2,1)}, u32[]{:S(2)}) copy-start(bf16[400,128]{1,0:T(8,128)(2,1)} %get-tuple-element.26) | copy-start | bytes 307204
  4.9 9.2 %copy-start.5 = (bf16[400,128]{1,0:T(8,128)(2,1)S(1)}, bf16[400,128]{1,0:T(8,128)(2,1)}, u32[]{:S(2)}) copy-start(bf16[400,128]{1,0:T(8,128)(2,1)} %get-tuple-element.27) | copy-start | bytes 307204
  4.9 26.8 %copy-start.3 = (bf16[400,128]{1,0:T(8,128)(2,1)S(1)}, bf16[400,128]{1,0:T(8,128)(2,1)}, u32[]{:S(2)}) copy-start(bf16[400,128]{1,0:T(8,128)(2,1)} %get-tuple-element.24.refs_0_) | copy-start | bytes 307204
  4.9 41.5 %all-to-all-start = ((bf16[16,296,128]{2,1,0:T(8,128)(2,1)}), bf16[16,296,128]{2,1,0:T(8,128)(2,1)S(1)}, u32[]{:S(2)}, u32[]{:S(2)}) async-start(bf16[16,296,128]{2,1,0:T(8,128)(2,1)} %get-tuple-element.23), calls=%async_computation | async-start | bytes 2424832 | tf_op jit(solution)/shard_map/all_to_all | solution.py:355
  12.4 11.4 %collective-permute-start = (bf16[400,128]{1,0:T(8,128)(2,1)S(1)}, bf16[400,128]{1,0:T(8,128)(2,1)S(1)}, u32[]{:S(2)}, u32[]{:S(2)}) collective-permute-start(bf16[400,128]{1,0:T(8,128)(2,1)S(1)} %copy-done.7), channel_id=1, source_target_pairs={{0,4},{4,8},{8,12},{12,0},{1,5},{5,9},{9,13},{13,1},{2,6},{6,10},{... | collective-permute-start | bytes 307208 | tf_op jit(solution)/shard_map/ppermute | solution.py:339
  14.1 17.1 %collective-permute-start.1 = (bf16[400,128]{1,0:T(8,128)(2,1)S(1)}, bf16[400,128]{1,0:T(8,128)(2,1)S(1)}, u32[]{:S(2)}, u32[]{:S(2)}) collective-permute-start(bf16[400,128]{1,0:T(8,128)(2,1)S(1)} %copy-done.6), channel_id=1, source_target_pairs={{0,8},{4,12},{8,0},{12,4},{1,9},{5,13},{9,1},{13,5},{2,10},{6,14},... | collective-permute-start | bytes 307208 | tf_op jit(solution)/shard_map/ppermute | solution.py:339
  14.1 17.6 %collective-permute-start.2 = (bf16[400,128]{1,0:T(8,128)(2,1)S(1)}, bf16[400,128]{1,0:T(8,128)(2,1)S(1)}, u32[]{:S(2)}, u32[]{:S(2)}) collective-permute-start(bf16[400,128]{1,0:T(8,128)(2,1)S(1)} %copy-done.5), channel_id=1, source_target_pairs={{0,12},{4,0},{8,4},{12,8},{1,13},{5,1},{9,5},{13,9},{2,14},{6,2},{... | collective-permute-start | bytes 307208 | tf_op jit(solution)/shard_map/ppermute | solution.py:339
  31.7 9.7 %collective-permute-start.3 = (bf16[1552,128]{1,0:T(8,128)(2,1)S(1)}, bf16[1552,128]{1,0:T(8,128)(2,1)S(1)}, u32[]{:S(2)}, u32[]{:S(2)}) collective-permute-start(bf16[1552,128]{1,0:T(8,128)(2,1)S(1)} %shard_map.39.refs_0_), channel_id=1, source_target_pairs={{3,1},{4,6},{11,9},{12,14},{19,17},{20,22},{27,25},{28,30}} | collective-permute-start | bytes 1191944 | tf_op jit(solution)/shard_map/ppermute | solution.py:367
  33.1 8.3 %collective-permute-start.4 = (bf16[1552,128]{1,0:T(8,128)(2,1)S(1)}, bf16[1552,128]{1,0:T(8,128)(2,1)S(1)}, u32[]{:S(2)}, u32[]{:S(2)}) collective-permute-start(bf16[1552,128]{1,0:T(8,128)(2,1)S(1)} %shard_map.39.refs_0_), channel_id=1, source_target_pairs={{0,1},{5,6},{8,9},{13,14},{16,17},{21,22},{24,25},{29,30}} | collective-permute-start | bytes 1191944 | tf_op jit(solution)/shard_map/ppermute | solution.py:367
  33.8 14.1 %collective-permute-start.5 = (bf16[1552,128]{1,0:T(8,128)(2,1)S(1)}, bf16[1552,128]{1,0:T(8,128)(2,1)}, u32[]{:S(2)}, u32[]{:S(2)}) collective-permute-start(bf16[1552,128]{1,0:T(8,128)(2,1)S(1)} %shard_map.39.refs_0_), channel_id=1, source_target_pairs={{2,1},{7,6},{10,9},{15,14},{18,17},{23,22},{26,25},{31,30}} | collective-permute-start | bytes 1191944 | tf_op jit(solution)/shard_map/ppermute | solution.py:367
  41.4 0.8 %copy-start = (bf16[1552,128]{1,0:T(8,128)(2,1)}, bf16[1552,128]{1,0:T(8,128)(2,1)S(1)}, u32[]{:S(2)}) copy-start(bf16[1552,128]{1,0:T(8,128)(2,1)S(1)} %collective-permute-done.4.refs_2_) | copy-start | bytes 1191940
  42.2 1.0 %copy-start.1 = (bf16[1552,128]{1,0:T(8,128)(2,1)S(1)}, bf16[1552,128]{1,0:T(8,128)(2,1)}, u32[]{:S(2)}) copy-start(bf16[1552,128]{1,0:T(8,128)(2,1)} %copy-done) | copy-start | bytes 1191940
  46.4 1.5 %copy-start.2 = (bf16[1552,128]{1,0:T(8,128)(2,1)S(1)}, bf16[1552,128]{1,0:T(8,128)(2,1)}, u32[]{:S(2)}) copy-start(bf16[1552,128]{1,0:T(8,128)(2,1)} %copy-done) | copy-start | bytes 1191940
  47.9 15.0 %copy-start.4 = (s32[8,512]{1,0:T(8,128)S(1)}, s32[8,512]{1,0:T(8,128)}, u32[]{:S(2)}) copy-start(s32[8,512]{1,0:T(8,128)} %get-tuple-element.38.info_ref) | copy-start | bytes 49156
  50.3 9.6 %collective-permute-start.6 = (f32[8,128]{1,0:T(8,128)S(1)}, f32[8,128]{1,0:T(8,128)S(1)}, u32[]{:S(2)}, u32[]{:S(2)}) collective-permute-start(f32[8,128]{1,0:T(8,128)S(1)} %get-tuple-element.31), channel_id=1, source_target_pairs={{0,1},{1,2},{2,3},{3,0},{4,5},{5,6},{6,7},{7,4},{8,9},{9,10},{10,1... | collective-permute-start | bytes 12296 | tf_op jit(solution)/shard_map/ppermute | solution.py:339
  55.9 4.0 %collective-permute-start.7 = (f32[8,128]{1,0:T(8,128)S(1)}, f32[8,128]{1,0:T(8,128)S(1)}, u32[]{:S(2)}, u32[]{:S(2)}) collective-permute-start(f32[8,128]{1,0:T(8,128)S(1)} %get-tuple-element.32), channel_id=1, source_target_pairs={{0,2},{1,3},{2,0},{3,1},{4,6},{5,7},{6,4},{7,5},{8,10},{9,11},{10,... | collective-permute-start | bytes 12296 | tf_op jit(solution)/shard_map/ppermute | solution.py:339
  57.6 3.0 %collective-permute-start.8 = (f32[8,128]{1,0:T(8,128)S(1)}, f32[8,128]{1,0:T(8,128)S(1)}, u32[]{:S(2)}, u32[]{:S(2)}) collective-permute-start(f32[8,128]{1,0:T(8,128)S(1)} %get-tuple-element.33), channel_id=1, source_target_pairs={{0,3},{1,0},{2,1},{3,2},{4,7},{5,4},{6,5},{7,6},{8,11},{9,8},{10,9... | collective-permute-start | bytes 12296 | tf_op jit(solution)/shard_map/ppermute | solution.py:339
  60.7 2.3 %collective-permute-start.9 = (f32[8,128]{1,0:T(8,128)S(1)}, f32[8,128]{1,0:T(8,128)S(1)}, u32[]{:S(2)}, u32[]{:S(2)}) collective-permute-start(f32[8,128]{1,0:T(8,128)S(1)} %get-tuple-element.35), channel_id=1, source_target_pairs={{0,4},{4,8},{8,12},{12,0},{1,5},{5,9},{9,13},{13,1},{2,6},{6,10},{... | collective-permute-start | bytes 12296 | tf_op jit(solution)/shard_map/ppermute | solution.py:339
  60.7 2.7 %collective-permute-start.10 = (f32[8,128]{1,0:T(8,128)S(1)}, f32[8,128]{1,0:T(8,128)S(1)}, u32[]{:S(2)}, u32[]{:S(2)}) collective-permute-start(f32[8,128]{1,0:T(8,128)S(1)} %get-tuple-element.36), channel_id=1, source_target_pairs={{0,8},{4,12},{8,0},{12,4},{1,9},{5,13},{9,1},{13,5},{2,10},{6,14},... | collective-permute-start | bytes 12296 | tf_op jit(solution)/shard_map/ppermute | solution.py:339
  62.2 3.0 %collective-permute-start.11 = (f32[8,128]{1,0:T(8,128)S(1)}, f32[8,128]{1,0:T(8,128)S(1)}, u32[]{:S(2)}, u32[]{:S(2)}) collective-permute-start(f32[8,128]{1,0:T(8,128)S(1)} %get-tuple-element.37), channel_id=1, source_target_pairs={{0,12},{4,0},{8,4},{12,8},{1,13},{5,1},{9,5},{13,9},{2,14},{6,2},{... | collective-permute-start | bytes 12296 | tf_op jit(solution)/shard_map/ppermute | solution.py:339

commit v16 on v14

--- a/solution.py
+++ b/solution.py
@@ -59,6 +59,7 @@
         ((cluster_hbm, cluster_ref), (weight_hbm, weight_ref), (pooled_hbm, pooled_ref)))]
     for fetch in fetches:
         fetch.start()
+    earlier = (iota((docs, docs), 0) < iota((docs, docs), 1)).astype(jnp.float32).astype(jnp.bfloat16)
     fetches[0].wait()
 
     cluster = cluster_ref[...]
@@ -70,7 +71,6 @@
 
     padded = -(-buckets // 16) * 16
     hot = (iota((padded, docs), 0) == bucket).astype(jnp.float32)
-    earlier = (iota((docs, docs), 0) < iota((docs, docs), 1)).astype(jnp.float32).astype(jnp.bfloat16)
     before = jnp.dot(hot.astype(jnp.bfloat16), earlier, preferred_element_type=jnp.float32)
     rank = jnp.sum(before * hot, axis=0, keepdims=True).astype(jnp.int32)
 
@@ -81,12 +81,18 @@
     sends = [pltpu.make_async_copy(info_ref, info_hbm, sems.at[3])]
     sends[0].start()
     small_slot = jnp.where(is_big, -1, target * cap_small + rank)
-    ids = ids_table(iota((devices, docs), 0) == bucket, info_ref)
+    quota = info_ref[2:3, :].astype(jnp.float32)
+    lanes = (iota((LANES, docs), 0) == info_ref[1:2, :]).astype(jnp.float32).astype(jnp.bfloat16)
+
+    def ids_table(mine):
+        return dot_nt(jnp.where(mine, quota, 0.0).astype(jnp.bfloat16), lanes)
+
+    ids = ids_table(iota((devices, docs), 0) == bucket)
     shift = modulo(owner + shards - docs_at[0], shards)
     big_slot = jnp.where(is_big, shift * cap_big + rank, -1)
     for by in range(shards):
         mine = (iota((16, docs), 0) == 0) & is_big & (shift == by)
-        big_ref[by, cap_big:, 0:LANES] = ids_table(mine, info_ref).astype(jnp.bfloat16)
+        big_ref[by, cap_big:, 0:LANES] = ids_table(mine).astype(jnp.bfloat16)
         big_ref[by, cap_big:, LANES:] = jnp.zeros((16, feature - LANES), jnp.bfloat16)
 
     for fetch in fetches[1:]:
@@ -118,13 +124,6 @@
         send.wait()
 
 
-def ids_table(mine, info_ref):
-    docs = info_ref.shape[1]
-    quota = info_ref[2:3, :].astype(jnp.float32)
-    lanes = (iota((LANES, docs), 0) == info_ref[1:2, :]).astype(jnp.float32).astype(jnp.bfloat16)
-    return dot_nt(jnp.where(mine, quota, 0.0).astype(jnp.bfloat16), lanes)
-
-
 def group_kernel(cap_big, *refs):
     held, group_ref = refs[:-1], refs[-1]
     total = len(held) * cap_big
@@ -138,18 +137,17 @@
     group_ref[total:, LANES:] = jnp.zeros((spare, group_ref.shape[1] - LANES), jnp.bfloat16)
 
 
-def turn(tables, at, count, outs):
-    for step, out in enumerate(outs):
-        to = modulo(at + step, count)
-        out[...] = jnp.zeros(out.shape, jnp.float32)
-        for place, table in enumerate(tables):
-            out[place:place + 1, :] = jnp.sum(
-                jnp.where(iota(table.shape, 0) == to, table, 0.0), axis=0, keepdims=True)
-
-
-def turn_kernel(count, at_ref, *refs):
-    held, outs = refs[:-count], refs[-count:]
-    turn([ref[...] for ref in held], at_ref[0], count, outs)
+def halves_of(order, bit):
+    return [index for index in order if not index >> bit & 1], [index for index in order if index >> bit & 1]
+
+
+def halve_kernel(order, bit, kept_ref, moved_ref, *outs):
+    half = kept_ref.shape[0]
+    for out, rows in zip(outs, halves_of(order, bit)):
+        for at, index in enumerate(rows):
+            row = order.index(index)
+            ref = kept_ref if row < half else moved_ref
+            out[at:at + 1, :] = ref[row % half:row % half + 1, :]
 
 
 def rows_up(count, to=8):
@@ -233,10 +231,9 @@
     best_ref[...] = jnp.concatenate(bests, axis=1)
 
 
-def big_last_kernel(shards, blocks, cap_big, cap_small, docs_at, small_ref, best_ref, *refs):
-    held, back_refs = refs[:blocks], refs[blocks:]
+def big_last_kernel(shards, blocks, cap_big, cap_small, docs_at, blk_at, small_ref, best_ref, *refs):
+    held, (kept_ref, moved_ref) = refs[:blocks], refs[blocks:]
     size = shards * cap_big
-    high = back_refs[0].shape[0]
     part, shift, lane = big_sources(blocks * size, shards, cap_big, cap_small)
     row_ids = big_ids(held, (part, shift, lane))
     col_ids = as_column(row_ids)
@@ -245,15 +242,16 @@
     bests = [best_ref[:, col * size:(col + 1) * size] for col in range(last)]
     bests = big_pairs(held, row_ids, col_ids, bests + [jnp.full((1, size), -1.0, jnp.float32)], pairs)
     docs = modulo(docs_at[0] + shards - shift, shards)
-    step = jnp.where(part == 0, 0, jnp.where(part == last, 1, part + 1))
-    back = small_ref[...] + spread(jnp.concatenate(bests, axis=1), step * high + docs, lane, small_ref.shape[0])
-    for at, ref in enumerate(back_refs):
-        ref[...] = back[at * high:(at + 1) * high, :]
-
-
-def small_kernel(shards, blocks, cap_small, blk_at, got_ref, back_ref, rows_ref):
+    blk = modulo(blk_at[0] + jnp.where(part == 0, 0, jnp.where(part == last, 1, part + 1)), blocks)
+    row = (blk ^ blk_at[0]) * shards + (docs ^ docs_at[0])
+    back = small_ref[...] + spread(jnp.concatenate(bests, axis=1), row, lane, small_ref.shape[0])
+    half = small_ref.shape[0] // 2
+    kept_ref[...] = back[:half, :]
+    moved_ref[...] = back[half:, :]
+
+
+def small_kernel(shards, blocks, cap_small, docs_at, blk_at, got_ref, back_ref, rows_ref):
     total, feature = rows_ref.shape
-    high = back_ref.shape[0] // blocks
     slabs = feature // LANES
     values = []
     for device in range(got_ref.shape[0]):
@@ -269,16 +267,14 @@
     for at in range(0, total, tile):
         best = jnp.maximum(best, block_best(
             rows_ref[at:at + tile, :], col_ids[at:at + tile], at, rows_ref[...], row_ids, 0))
-    row = modulo(blk + blocks - blk_at[0], blocks) * high + docs
+    row = (blk ^ blk_at[0]) * shards + (docs ^ docs_at[0])
     back_ref[...] = spread(best, row, lane, back_ref.shape[0])
 
 
-def masks_kernel(shards, blocks, docs_at, blk_at, info_ref, row_ref, lane_ref):
+def masks_kernel(shards, blocks, order, docs_at, blk_at, info_ref, row_ref, lane_ref):
     device = info_ref[0:1, :]
-    high = row_ref.shape[0] // (3 * shards)
-    row = (modulo(docs_at[0] + shards - device // blocks, shards) * high
-           + modulo(blk_at[0] + blocks - modulo(device, blocks), blocks))
-    mask = (iota((shards * high, row_ref.shape[1]), 0) == row).astype(jnp.float32)
+    row = (modulo(device, blocks) ^ blk_at[0]) * shards + (device // blocks ^ docs_at[0])
+    mask = jnp.concatenate([(row == index).astype(jnp.float32) for index in order], axis=0)
     row_ref[...] = jnp.concatenate([mask] * 3, axis=0).astype(jnp.bfloat16)
     lane_ref[...] = (iota(lane_ref.shape, 0) == info_ref[1:2, :]).astype(jnp.float32)
 
@@ -343,7 +339,7 @@
     group, = call(
         functools.partial(group_kernel, cap_big),
         [((big_slots + rows_up(shards, 16), feature), bf16, vmem)], [vmem] * shards,
-        big_slots * feature, 1 << 30,
+        big_slots * feature, 1 << 20,
     )(*held)
     parts = [group]
     for step in big_steps(blocks)[1:]:
@@ -353,10 +349,10 @@
 
     back_small, = call(
         functools.partial(small_kernel, shards, blocks, cap_small),
-        [((blocks * rows_up(shards), LANES), f32, vmem)], [smem, vmem],
+        [((devices, LANES), f32, vmem)], [smem, smem, vmem],
         2 * small_slots * small_slots * feature, 2 << 20, 16,
         [vmem((small_slots, feature), bf16)],
-    )(blk_at, got_small)
+    )(docs_at, blk_at, got_small)
     early, = call(
         functools.partial(big_kernel, shards, cap_big, cap_small),
         [((1, big_total - big_slots), f32, vmem)], [vmem] * (blocks - 1),
@@ -364,24 +360,28 @@
     )(*parts[:-1])
     back = call(
         functools.partial(big_last_kernel, *sizes),
-        [((rows_up(shards), LANES), f32, vmem)] * blocks, [smem] + [vmem] * (blocks + 2),
+        [((devices // 2, LANES), f32, vmem)] * 2, [smem, smem] + [vmem] * (blocks + 2),
         2 * (2 * big_total - big_slots) * big_slots * feature, 2 << 20,
-    )(docs_at, back_small, early, *parts)
-    back = [back[0]] + [along(back[by], "blk", blocks, by) for by in range(1, blocks)]
-    back = call(
-        functools.partial(turn_kernel, shards),
-        [((rows_up(blocks), LANES), f32, vmem)] * shards, [smem] + [vmem] * blocks,
-        shards * blocks * LANES, 1 << 16,
-    )(docs_at, *back)
-    back = [back[0]] + [along(back[by], "docs", shards, by) for by in range(1, shards)]
+    )(docs_at, blk_at, back_small, early, *parts)
+    order = list(range(devices))
+    for bit in reversed(range(devices.bit_length() - 1)):
+        if bit < devices.bit_length() - 2:
+            back = call(
+                functools.partial(halve_kernel, order, bit),
+                [((devices // 2, LANES), f32, vmem)] * 2, [vmem, vmem], devices * LANES, 1 << 14,
+            )(*back)
+        order = sum(halves_of(order, bit), [])
+        far_docs, far_blk = (1 << bit) % shards, (1 << bit) // shards
+        pairs = [(d * blocks + b, (d ^ far_docs) * blocks + (b ^ far_blk)) for d in range(shards) for b in range(blocks)]
+        back = [back[0], lax.ppermute(back[1], ("docs", "blk"), pairs)]
 
     masks = call(
-        functools.partial(masks_kernel, shards, blocks),
-        [((3 * shards * rows_up(blocks), docs), bf16, vmem), ((LANES, docs), f32, vmem)], [smem, smem, vmem],
+        functools.partial(masks_kernel, shards, blocks, order),
+        [((3 * devices, docs), bf16, vmem), ((LANES, docs), f32, vmem)], [smem, smem, vmem],
         docs * LANES, 1 << 18,
     )(docs_at, blk_at, info)
     out, = call(
-        finish_kernel, [((1, docs), f32, vmem)], [vmem] * (shards + 2),
+        finish_kernel, [((1, docs), f32, vmem)], [vmem] * 4,
         6 * docs * LANES * devices, 1 << 18,
     )(*back, *masks)
     return out.reshape(docs)

time: 63.5 us -> 65 us (1.024)
  waiting for transfers between devices: 30.9 us -> 32.5 us
    ppermute x9 -> x3, starting transfers between devices: 12.5 us -> 2.23 us  [along(): return lax.ppermute(x, axis, [(i, (i + by) % count) for i in range(count)])]
    ppermute x0 -> x4, starting transfers between devices: none -> 9.94 us  [body(): back = [back[0], lax.ppermute(back[1], ('docs', 'blk'), pairs)]]
    ppermute x0 -> x4, waiting for transfers between devices: none -> 4.56 us  [body(): back = [back[0], lax.ppermute(back[1], ('docs', 'blk'), pairs)]]
    ppermute x9 -> x3, waiting for transfers between devices: 21.1 us -> 18 us  [along(): return lax.ppermute(x, axis, [(i, (i + by) % count) for i in range(count)])]
    pallas_call x5 -> x7, Pallas kernels: 3.66 us -> 3.61 us  [the longest x1 1.46 us: body(): call(functools.partial(small_kernel, shards, blocks, cap_small), [((devic...]
  transfers between devices with their start and end apart: 13 -> 11, of which waited for: 8 -> 9; matrix products, arithmetic and copies ran while one was open for 0% -> 0% of each run, Pallas kernels for 4% -> 4%
where the time goes in v16:
time: 65 us; the launch traced here: 64.4 us
  waiting for transfers between devices  32.5 us (50%)
  starting transfers between devices  22.4 us (34%)
  Pallas kernels  9.44 us (15%)
    ppermute x3, waiting for transfers between devices, along(): return lax.ppermute(x, axis, [(i, (i + by) % count) for i in range(count)])  18 us
    ppermute x4, starting transfers between devices, body(): back = [back[0], lax.ppermute(back[1], ('docs', 'blk'), pairs)]  9.94 us
    all_to_all x1, starting transfers between devices, body(): lax.all_to_all(small_sent, ('docs', 'blk'), split_axis=0, concat_axis=0,...  7.47 us
    ppermute x3, waiting for transfers between devices, body(): parts.append(lax.ppermute(group, ('docs', 'blk'), pairs))  6.46 us
    ppermute x4, waiting for transfers between devices, body(): back = [back[0], lax.ppermute(back[1], ('docs', 'blk'), pairs)]  4.56 us
    pallas_call x1, Pallas kernels, body(): call(functools.partial(sort_kernel, *sizes), [((devices, small_rows, LANE...  4.54 us
    all_to_all x1, waiting for transfers between devices, body(): lax.all_to_all(small_sent, ('docs', 'blk'), split_axis=0, concat_axis=0,...  3.41 us
    ppermute x3, starting transfers between devices, body(): parts.append(lax.ppermute(group, ('docs', 'blk'), pairs))  2.74 us
  transfers between devices with their start and end apart: 11, of which 9 were waited for; matrix products, arithmetic and copies ran while one was open for 0% of the time, Pallas kernels for 4%

profile of v16, /device:TPU:1, one launch (start us, length us, event | category | flops | bytes accessed | tf_op | source)
XLA Modules:
  0.0 64.4 jit_solution(5206084432532550617)
XLA Ops:
  0.0 4.5 %shard_map.37 = (bf16[16,296,128]{2,1,0:T(8,128)(2,1)}, s32[8,512]{1,0:T(8,128)}, bf16[80,768]{1,0:T(8,128)(2,1)}, bf16[80,768]{1,0:T(8,128)(2,1)}, bf16[80,768]{1,0:T(8,128)(2,1)}, /*index=5*/bf16[80,768]{1,0:T(8,128)(2,1)}) custom-call(s32[1]{0:T(128)} %bitcast.docs_at, bf16[512,768]{1,0:T(8,128)(2,1)} %pooled_hbm.1, bf16[768,768]{1,0:T(8,128)(2,1)} %weight_hbm.1, ...), custom_call_target="tpu_custom_call" | custom-call | flops 1207959552 | bytes 4194304 | tf_op jit(solution)/shard_map/pallas_call | solution.py:326
  4.5 0.0 copy-start.4
  4.6 0.0 copy-start.3
  4.6 0.0 copy-start.2
  4.6 0.0 copy-start
  4.6 7.5 %all-to-all-start = ((bf16[16,296,128]{2,1,0:T(8,128)(2,1)}), bf16[16,296,128]{2,1,0:T(8,128)(2,1)S(1)}, u32[]{:S(2)}, u32[]{:S(2)}) async-start(bf16[16,296,128]{2,1,0:T(8,128)(2,1)} %get-tuple-element.21), calls=%async_computation | async-start | bytes 2424832 | tf_op jit(solution)/shard_map/all_to_all | solution.py:336
  12.1 0.0 copy-done.4
  12.1 1.7 %collective-permute-start = (bf16[80,768]{1,0:T(8,128)(2,1)S(1)}, bf16[80,768]{1,0:T(8,128)(2,1)S(1)}, u32[]{:S(2)}, u32[]{:S(2)}) collective-permute-start(bf16[80,768]{1,0:T(8,128)(2,1)S(1)} %copy-done.4), channel_id=1, source_target_pairs={{0,4},{4,8},{8,12},{12,0},{1,5},{5,9},{9,13},{13,1},{2,6},{6,10},{... | collective-permute-start | bytes 368648 | tf_op jit(solution)/shard_map/ppermute | solution.py:323
  13.7 0.0 copy-done.3
  13.7 0.0 collective-permute-start.1
  13.7 0.0 copy-done.2
  13.8 0.5 collective-permute-start.2
  14.3 11.3 %collective-permute-done.refs_1_ = bf16[80,768]{1,0:T(8,128)(2,1)S(1)} collective-permute-done((bf16[80,768]{1,0:T(8,128)(2,1)S(1)}, bf16[80,768]{1,0:T(8,128)(2,1)S(1)}, u32[]{:S(2)}, u32[]{:S(2)}) %collective-permute-start) | collective-permute-done | bytes 122912 | tf_op jit(solution)/shard_map/ppermute | solution.py:323
  25.5 6.3 %collective-permute-done.1.refs_2_ = bf16[80,768]{1,0:T(8,128)(2,1)S(1)} collective-permute-done((bf16[80,768]{1,0:T(8,128)(2,1)S(1)}, bf16[80,768]{1,0:T(8,128)(2,1)S(1)}, u32[]{:S(2)}, u32[]{:S(2)}) %collective-permute-start.1) | collective-permute-done | bytes 122912 | tf_op jit(solution)/shard_map/ppermute | solution.py:323
  31.9 0.5 collective-permute-done.2.refs_3_
  32.3 0.0 copy-done
  32.4 0.7 %collective-permute-start.4 = (bf16[272,768]{1,0:T(8,128)(2,1)S(1)}, bf16[272,768]{1,0:T(8,128)(2,1)S(1)}, u32[]{:S(2)}, u32[]{:S(2)}) collective-permute-start(bf16[272,768]{1,0:T(8,128)(2,1)S(1)} %shard_map.39.refs_0_), channel_id=1, source_target_pairs={{0,1},{5,6},{8,9},{13,14},{16,17},{21,22},{24,25},{29,30}} | collective-permute-start | bytes 1253384 | tf_op jit(solution)/shard_map/ppermute | solution.py:348
  33.1 1.4 %collective-permute-start.3 = (bf16[272,768]{1,0:T(8,128)(2,1)S(1)}, bf16[272,768]{1,0:T(8,128)(2,1)S(1)}, u32[]{:S(2)}, u32[]{:S(2)}) collective-permute-start(bf16[272,768]{1,0:T(8,128)(2,1)S(1)} %shard_map.39.refs_0_), channel_id=1, source_target_pairs={{3,1},{4,6},{11,9},{12,14},{19,17},{20,22},{27,25},{28,30}} | collective-permute-start | bytes 1253384 | tf_op jit(solution)/shard_map/ppermute | solution.py:348
  34.4 0.7 %collective-permute-start.5 = (bf16[272,768]{1,0:T(8,128)(2,1)S(1)}, bf16[272,768]{1,0:T(8,128)(2,1)S(1)}, u32[]{:S(2)}, u32[]{:S(2)}) collective-permute-start(bf16[272,768]{1,0:T(8,128)(2,1)S(1)} %shard_map.39.refs_0_), channel_id=1, source_target_pairs={{2,1},{7,6},{10,9},{15,14},{18,17},{23,22},{26,25},{31,30}} | collective-permute-start | bytes 1253384 | tf_op jit(solution)/shard_map/ppermute | solution.py:348
  35.1 0.0 collective-permute-done.4.refs_2_
  35.1 6.5 %collective-permute-done.3.refs_1_ = bf16[272,768]{1,0:T(8,128)(2,1)S(1)} collective-permute-done((bf16[272,768]{1,0:T(8,128)(2,1)S(1)}, bf16[272,768]{1,0:T(8,128)(2,1)S(1)}, u32[]{:S(2)}, u32[]{:S(2)}) %collective-permute-start.3) | collective-permute-done | bytes 417824 | tf_op jit(solution)/shard_map/ppermute | solution.py:348
  41.6 1.3 %shard_map.40.best_ref = f32[1,768]{1,0:T(1,128)S(1)} custom-call(bf16[272,768]{1,0:T(8,128)(2,1)S(1)} %shard_map.39.refs_0_, bf16[272,768]{1,0:T(8,128)(2,1)S(1)} %collective-permute-done.3.refs_1_, bf16[272,768]{1,0:T(8,128)(2,1)S(1)} %collective-permute-done.4.refs_2_), custom_call_target="tpu_custom_call" | custom-call | flops 905969664 | bytes 2097152 | tf_op jit(solution)/shard_map/pallas_call | solution.py:356
  42.9 3.4 %all-to-all-done.got_ref = bf16[16,296,128]{2,1,0:T(8,128)(2,1)S(1)} async-done(((bf16[16,296,128]{2,1,0:T(8,128)(2,1)}), bf16[16,296,128]{2,1,0:T(8,128)(2,1)S(1)}, u32[]{:S(2)}, u32[]{:S(2)}) %all-to-all-start) | async-done | bytes 1212448 | tf_op jit(solution)/shard_map/all_to_all | solution.py:336
  46.3 1.5 %shard_map.38.small_ref = f32[16,128]{1,0:T(8,128)S(1)} custom-call(s32[1]{0:T(128)} %bitcast.docs_at, s32[1]{0:T(128)} %bitcast.1.blk_at, bf16[16,296,128]{2,1,0:T(8,128)(2,1)S(1)} %all-to-all-done.got_ref), custom_call_target="tpu_custom_call" | custom-call | flops 905969664 | bytes 2097152 | tf_op jit(solution)/shard_map/pallas_call | solution.py:350
  47.7 0.0 copy-start.1
  47.7 0.0 collective-permute-done.5.refs_3_
  47.7 1.3 %shard_map.41 = (f32[8,128]{1,0:T(8,128)S(1)}, f32[8,128]{1,0:T(8,128)S(1)}) custom-call(s32[1]{0:T(128)} %bitcast.docs_at, s32[1]{0:T(128)} %bitcast.1.blk_at, f32[16,128]{1,0:T(8,128)S(1)} %shard_map.38.small_ref, f32[1,768]{1,0:T(1,128)S(1)} %shard_map.40.best_ref, bf16[272,768]{1,0:T(8,128)(2,1)S(1)} %shard_map.39.refs_0_, ...), custom_call_target="tpu_custom_call" | custom-call | flops 704643072 | bytes 2097152 | tf_op jit(solution)/shard_map/pallas_call | solution.py:361
  49.0 5.7 %collective-permute-start.6 = (f32[8,128]{1,0:T(8,128)S(1)}, f32[8,128]{1,0:T(8,128)S(1)}, u32[]{:S(2)}, u32[]{:S(2)}) collective-permute-start(f32[8,128]{1,0:T(8,128)S(1)} %get-tuple-element.27), channel_id=1, source_target_pairs={{0,2},{1,3},{2,0},{3,1},{4,6},{5,7},{6,4},{7,5},{8,10},{9,11},{10,... | collective-permute-start | bytes 12296 | tf_op jit(solution)/shard_map/ppermute | solution.py:376
  54.7 1.0 %collective-permute-done.6.moved_ref = f32[8,128]{1,0:T(8,128)S(1)} collective-permute-done((f32[8,128]{1,0:T(8,128)S(1)}, f32[8,128]{1,0:T(8,128)S(1)}, u32[]{:S(2)}, u32[]{:S(2)}) %collective-permute-start.6) | collective-permute-done | bytes 4128 | tf_op jit(solution)/shard_map/ppermute | solution.py:376
  55.7 0.7 %collective-permute-start.7 = (f32[8,128]{1,0:T(8,128)S(1)}, f32[8,128]{1,0:T(8,128)S(1)}, u32[]{:S(2)}, u32[]{:S(2)}) collective-permute-start(f32[8,128]{1,0:T(8,128)S(1)} %get-tuple-element.29), channel_id=1, source_target_pairs={{0,1},{1,0},{2,3},{3,2},{4,5},{5,4},{6,7},{7,6},{8,9},{9,8},{10,11... | collective-permute-start | bytes 12296 | tf_op jit(solution)/shard_map/ppermute | solution.py:376
  56.5 1.7 %collective-permute-done.7.moved_ref = f32[8,128]{1,0:T(8,128)S(1)} collective-permute-done((f32[8,128]{1,0:T(8,128)S(1)}, f32[8,128]{1,0:T(8,128)S(1)}, u32[]{:S(2)}, u32[]{:S(2)}) %collective-permute-start.7) | collective-permute-done | bytes 4128 | tf_op jit(solution)/shard_map/ppermute | solution.py:376
  58.2 1.4 %collective-permute-start.8 = (f32[8,128]{1,0:T(8,128)S(1)}, f32[8,128]{1,0:T(8,128)S(1)}, u32[]{:S(2)}, u32[]{:S(2)}) collective-permute-start(f32[8,128]{1,0:T(8,128)S(1)} %get-tuple-element.31), channel_id=1, source_target_pairs={{0,8},{1,9},{2,10},{3,11},{4,12},{5,13},{6,14},{7,15},{8,0},{9,1},... | collective-permute-start | bytes 12296 | tf_op jit(solution)/shard_map/ppermute | solution.py:376
  59.6 1.1 %collective-permute-done.8.moved_ref = f32[8,128]{1,0:T(8,128)S(1)} collective-permute-done((f32[8,128]{1,0:T(8,128)S(1)}, f32[8,128]{1,0:T(8,128)S(1)}, u32[]{:S(2)}, u32[]{:S(2)}) %collective-permute-start.8) | collective-permute-done | bytes 4128 | tf_op jit(solution)/shard_map/ppermute | solution.py:376
  60.6 2.2 %collective-permute-start.9 = (f32[8,128]{1,0:T(8,128)S(1)}, f32[8,128]{1,0:T(8,128)S(1)}, u32[]{:S(2)}, u32[]{:S(2)}) collective-permute-start(f32[8,128]{1,0:T(8,128)S(1)} %get-tuple-element.33), channel_id=1, source_target_pairs={{0,4},{1,5},{2,6},{3,7},{4,0},{5,1},{6,2},{7,3},{8,12},{9,13},{10,... | collective-permute-start | bytes 12296 | tf_op jit(solution)/shard_map/ppermute | solution.py:376
  62.8 0.0 copy-done.1
  62.8 0.8 %collective-permute-done.9.refs_1_ = f32[8,128]{1,0:T(8,128)S(1)} collective-permute-done((f32[8,128]{1,0:T(8,128)S(1)}, f32[8,128]{1,0:T(8,128)S(1)}, u32[]{:S(2)}, u32[]{:S(2)}) %collective-permute-start.9) | collective-permute-done | bytes 4128 | tf_op jit(solution)/shard_map/ppermute | solution.py:376
  63.6 0.8 %shard_map.46 = f32[1,512]{1,0:T(1,128)} custom-call(f32[8,128]{1,0:T(8,128)S(1)} %get-tuple-element.32.refs_0_, f32[8,128]{1,0:T(8,128)S(1)} %collective-permute-done.9.refs_1_, bf16[48,512]{1,0:T(8,128)(2,1)S(1)} %get-tuple-element.35.refs_2_, f32[128,512]{1,0:T(8,128)S(1)} %get-tuple-element.36.refs_3_), custom_call_target="tpu_custom_call" | custom-call | flops 6291456 | bytes 262144 | tf_op jit(solution)/shard_map/pallas_call | solution.py:383
  (5 shorter events, 0.1 us)
Async XLA Ops:
  4.5 7.5 %copy-start.4 = (bf16[80,768]{1,0:T(8,128)(2,1)S(1)}, bf16[80,768]{1,0:T(8,128)(2,1)}, u32[]{:S(2)}) copy-start(bf16[80,768]{1,0:T(8,128)(2,1)} %get-tuple-element.23) | copy-start | bytes 368644
  4.6 9.2 %copy-start.3 = (bf16[80,768]{1,0:T(8,128)(2,1)S(1)}, bf16[80,768]{1,0:T(8,128)(2,1)}, u32[]{:S(2)}) copy-start(bf16[80,768]{1,0:T(8,128)(2,1)} %get-tuple-element.24) | copy-start | bytes 368644
  4.6 9.2 %copy-start.2 = (bf16[80,768]{1,0:T(8,128)(2,1)S(1)}, bf16[80,768]{1,0:T(8,128)(2,1)}, u32[]{:S(2)}) copy-start(bf16[80,768]{1,0:T(8,128)(2,1)} %get-tuple-element.25) | copy-start | bytes 368644
  4.6 27.8 %copy-start = (bf16[80,768]{1,0:T(8,128)(2,1)S(1)}, bf16[80,768]{1,0:T(8,128)(2,1)}, u32[]{:S(2)}) copy-start(bf16[80,768]{1,0:T(8,128)(2,1)} %get-tuple-element.22.refs_0_) | copy-start | bytes 368644
  4.6 41.7 %all-to-all-start = ((bf16[16,296,128]{2,1,0:T(8,128)(2,1)}), bf16[16,296,128]{2,1,0:T(8,128)(2,1)S(1)}, u32[]{:S(2)}, u32[]{:S(2)}) async-start(bf16[16,296,128]{2,1,0:T(8,128)(2,1)} %get-tuple-element.21), calls=%async_computation | async-start | bytes 2424832 | tf_op jit(solution)/shard_map/all_to_all | solution.py:336
  12.1 13.5 %collective-permute-start = (bf16[80,768]{1,0:T(8,128)(2,1)S(1)}, bf16[80,768]{1,0:T(8,128)(2,1)S(1)}, u32[]{:S(2)}, u32[]{:S(2)}) collective-permute-start(bf16[80,768]{1,0:T(8,128)(2,1)S(1)} %copy-done.4), channel_id=1, source_target_pairs={{0,4},{4,8},{8,12},{12,0},{1,5},{5,9},{9,13},{13,1},{2,6},{6,10},{... | collective-permute-start | bytes 368648 | tf_op jit(solution)/shard_map/ppermute | solution.py:323
  13.7 18.1 %collective-permute-start.1 = (bf16[80,768]{1,0:T(8,128)(2,1)S(1)}, bf16[80,768]{1,0:T(8,128)(2,1)S(1)}, u32[]{:S(2)}, u32[]{:S(2)}) collective-permute-start(bf16[80,768]{1,0:T(8,128)(2,1)S(1)} %copy-done.3), channel_id=1, source_target_pairs={{0,8},{4,12},{8,0},{12,4},{1,9},{5,13},{9,1},{13,5},{2,10},{6,14},... | collective-permute-start | bytes 368648 | tf_op jit(solution)/shard_map/ppermute | solution.py:323
  13.8 18.6 %collective-permute-start.2 = (bf16[80,768]{1,0:T(8,128)(2,1)S(1)}, bf16[80,768]{1,0:T(8,128)(2,1)S(1)}, u32[]{:S(2)}, u32[]{:S(2)}) collective-permute-start(bf16[80,768]{1,0:T(8,128)(2,1)S(1)} %copy-done.2), channel_id=1, source_target_pairs={{0,12},{4,0},{8,4},{12,8},{1,13},{5,1},{9,5},{13,9},{2,14},{6,2},{... | collective-permute-start | bytes 368648 | tf_op jit(solution)/shard_map/ppermute | solution.py:323
  32.4 2.8 %collective-permute-start.4 = (bf16[272,768]{1,0:T(8,128)(2,1)S(1)}, bf16[272,768]{1,0:T(8,128)(2,1)S(1)}, u32[]{:S(2)}, u32[]{:S(2)}) collective-permute-start(bf16[272,768]{1,0:T(8,128)(2,1)S(1)} %shard_map.39.refs_0_), channel_id=1, source_target_pairs={{0,1},{5,6},{8,9},{13,14},{16,17},{21,22},{24,25},{29,30}} | collective-permute-start | bytes 1253384 | tf_op jit(solution)/shard_map/ppermute | solution.py:348
  33.1 8.5 %collective-permute-start.3 = (bf16[272,768]{1,0:T(8,128)(2,1)S(1)}, bf16[272,768]{1,0:T(8,128)(2,1)S(1)}, u32[]{:S(2)}, u32[]{:S(2)}) collective-permute-start(bf16[272,768]{1,0:T(8,128)(2,1)S(1)} %shard_map.39.refs_0_), channel_id=1, source_target_pairs={{3,1},{4,6},{11,9},{12,14},{19,17},{20,22},{27,25},{28,30}} | collective-permute-start | bytes 1253384 | tf_op jit(solution)/shard_map/ppermute | solution.py:348
  34.4 13.3 %collective-permute-start.5 = (bf16[272,768]{1,0:T(8,128)(2,1)S(1)}, bf16[272,768]{1,0:T(8,128)(2,1)S(1)}, u32[]{:S(2)}, u32[]{:S(2)}) collective-permute-start(bf16[272,768]{1,0:T(8,128)(2,1)S(1)} %shard_map.39.refs_0_), channel_id=1, source_target_pairs={{2,1},{7,6},{10,9},{15,14},{18,17},{23,22},{26,25},{31,30}} | collective-permute-start | bytes 1253384 | tf_op jit(solution)/shard_map/ppermute | solution.py:348
  47.7 15.0 %copy-start.1 = (s32[8,512]{1,0:T(8,128)S(1)}, s32[8,512]{1,0:T(8,128)}, u32[]{:S(2)}) copy-start(s32[8,512]{1,0:T(8,128)} %get-tuple-element.34.info_ref) | copy-start | bytes 49156
  49.0 6.7 %collective-permute-start.6 = (f32[8,128]{1,0:T(8,128)S(1)}, f32[8,128]{1,0:T(8,128)S(1)}, u32[]{:S(2)}, u32[]{:S(2)}) collective-permute-start(f32[8,128]{1,0:T(8,128)S(1)} %get-tuple-element.27), channel_id=1, source_target_pairs={{0,2},{1,3},{2,0},{3,1},{4,6},{5,7},{6,4},{7,5},{8,10},{9,11},{10,... | collective-permute-start | bytes 12296 | tf_op jit(solution)/shard_map/ppermute | solution.py:376
  55.7 2.5 %collective-permute-start.7 = (f32[8,128]{1,0:T(8,128)S(1)}, f32[8,128]{1,0:T(8,128)S(1)}, u32[]{:S(2)}, u32[]{:S(2)}) collective-permute-start(f32[8,128]{1,0:T(8,128)S(1)} %get-tuple-element.29), channel_id=1, source_target_pairs={{0,1},{1,0},{2,3},{3,2},{4,5},{5,4},{6,7},{7,6},{8,9},{9,8},{10,11... | collective-permute-start | bytes 12296 | tf_op jit(solution)/shard_map/ppermute | solution.py:376
  58.2 2.5 %collective-permute-start.8 = (f32[8,128]{1,0:T(8,128)S(1)}, f32[8,128]{1,0:T(8,128)S(1)}, u32[]{:S(2)}, u32[]{:S(2)}) collective-permute-start(f32[8,128]{1,0:T(8,128)S(1)} %get-tuple-element.31), channel_id=1, source_target_pairs={{0,8},{1,9},{2,10},{3,11},{4,12},{5,13},{6,14},{7,15},{8,0},{9,1},... | collective-permute-start | bytes 12296 | tf_op jit(solution)/shard_map/ppermute | solution.py:376
  60.6 3.0 %collective-permute-start.9 = (f32[8,128]{1,0:T(8,128)S(1)}, f32[8,128]{1,0:T(8,128)S(1)}, u32[]{:S(2)}, u32[]{:S(2)}) collective-permute-start(f32[8,128]{1,0:T(8,128)S(1)} %get-tuple-element.33), channel_id=1, source_target_pairs={{0,4},{1,5},{2,6},{3,7},{4,0},{5,1},{6,2},{7,3},{8,12},{9,13},{10,... | collective-permute-start | bytes 12296 | tf_op jit(solution)/shard_map/ppermute | solution.py:376

commit v17 on v14

--- a/solution.py
+++ b/solution.py
@@ -334,7 +334,7 @@
         2 * docs * feature * (pooled.shape[1] + small_slots), 4 << 20, 60,
         [vmem(pooled.shape, bf16), vmem(proj_weight.shape, bf16), vmem((1, docs), i32),
          vmem((devices, small_rows, LANES), bf16), vmem((shards, cap_big + 16, feature), bf16),
-         vmem((docs, feature), bf16), vmem((8, docs), i32), dma((4,)), dma((4,)), dma((shards,))],
+         vmem((docs, feature), bf16), vmem((8, docs), i32), dma((4,)), dma((2,)), dma((shards,))],
     )(docs_at, pooled, proj_weight, cluster.reshape(1, docs))
 
     got_small = lax.all_to_all(small_sent, ("docs", "blk"), split_axis=0, concat_axis=0, tiled=True)
@@ -343,7 +343,7 @@
     group, = call(
         functools.partial(group_kernel, cap_big),
         [((big_slots + rows_up(shards, 16), feature), bf16, vmem)], [vmem] * shards,
-        big_slots * feature, 1 << 30,
+        big_slots * feature, 1 << 20,
     )(*held)
     parts = [group]
     for step in big_steps(blocks)[1:]:

time: 63.5 us -> 63.6 us (level)
  no operation moved by 1% of the time
where the time goes in v17:
time: 63.6 us; the launch traced here: 63.3 us
  waiting for transfers between devices  30.9 us (49%)
  starting transfers between devices  22.7 us (36%)
  Pallas kernels  9.56 us (15%)
    ppermute x9, waiting for transfers between devices, along(): return lax.ppermute(x, axis, [(i, (i + by) % count) for i in range(count)])  21.1 us
    ppermute x9, starting transfers between devices, along(): return lax.ppermute(x, axis, [(i, (i + by) % count) for i in range(count)])  12.5 us
    all_to_all x1, starting transfers between devices, body(): lax.all_to_all(small_sent, ('docs', 'blk'), split_axis=0, concat_axis=0,...  7.47 us
    ppermute x3, waiting for transfers between devices, body(): parts.append(lax.ppermute(group, ('docs', 'blk'), pairs))  6.47 us
    pallas_call x1, Pallas kernels, body(): call(functools.partial(sort_kernel, *sizes), [((devices, small_rows, LANE...  4.61 us
    all_to_all x1, waiting for transfers between devices, body(): lax.all_to_all(small_sent, ('docs', 'blk'), split_axis=0, concat_axis=0,...  3.4 us
    ppermute x3, starting transfers between devices, body(): parts.append(lax.ppermute(group, ('docs', 'blk'), pairs))  2.74 us
    pallas_call x1, Pallas kernels, body(): call(functools.partial(small_kernel, shards, blocks, cap_small), [((block...  1.47 us
  transfers between devices with their start and end apart: 13, of which 8 were waited for; matrix products, arithmetic and copies ran while one was open for 0% of the time, Pallas kernels for 4%

profile of v17, /device:TPU:1, one launch (start us, length us, event | category | flops | bytes accessed | tf_op | source)
XLA Modules:
  0.0 63.3 jit_solution(14203980107073067440)
XLA Ops:
  0.0 4.6 %shard_map.37 = (bf16[16,296,128]{2,1,0:T(8,128)(2,1)}, s32[8,512]{1,0:T(8,128)}, bf16[80,768]{1,0:T(8,128)(2,1)}, bf16[80,768]{1,0:T(8,128)(2,1)}, bf16[80,768]{1,0:T(8,128)(2,1)}, /*index=5*/bf16[80,768]{1,0:T(8,128)(2,1)}) custom-call(s32[1]{0:T(128)} %bitcast.docs_at.at_ref, bf16[512,768]{1,0:T(8,128)(2,1)} %pooled_hbm.1, bf16[768,768]{1,0:T(8,128)(2,1)} %weight_hbm.1, ...), custom_call_target="tpu_custom_call" | custom-call | flops 1207959552 | bytes 4194304 | tf_op jit(solution)/shard_map/pallas_call | solution.py:330
  4.6 0.0 copy-start.4
  4.6 0.0 copy-start.3
  4.6 0.0 copy-start.2
  4.6 0.0 copy-start
  4.7 7.5 %all-to-all-start = ((bf16[16,296,128]{2,1,0:T(8,128)(2,1)}), bf16[16,296,128]{2,1,0:T(8,128)(2,1)S(1)}, u32[]{:S(2)}, u32[]{:S(2)}) async-start(bf16[16,296,128]{2,1,0:T(8,128)(2,1)} %get-tuple-element.21), calls=%async_computation | async-start | bytes 2424832 | tf_op jit(solution)/shard_map/all_to_all | solution.py:340
  12.1 0.0 copy-done.4
  12.1 1.7 %collective-permute-start = (bf16[80,768]{1,0:T(8,128)(2,1)S(1)}, bf16[80,768]{1,0:T(8,128)(2,1)S(1)}, u32[]{:S(2)}, u32[]{:S(2)}) collective-permute-start(bf16[80,768]{1,0:T(8,128)(2,1)S(1)} %copy-done.4), channel_id=1, source_target_pairs={{0,4},{4,8},{8,12},{12,0},{1,5},{5,9},{9,13},{13,1},{2,6},{6,10},{... | collective-permute-start | bytes 368648 | tf_op jit(solution)/shard_map/ppermute | solution.py:327
  13.8 0.0 copy-done.3
  13.8 0.0 collective-permute-start.1
  13.8 0.0 copy-done.2
  13.8 0.5 collective-permute-start.2
  14.4 11.3 %collective-permute-done.refs_1_ = bf16[80,768]{1,0:T(8,128)(2,1)S(1)} collective-permute-done((bf16[80,768]{1,0:T(8,128)(2,1)S(1)}, bf16[80,768]{1,0:T(8,128)(2,1)S(1)}, u32[]{:S(2)}, u32[]{:S(2)}) %collective-permute-start) | collective-permute-done | bytes 122912 | tf_op jit(solution)/shard_map/ppermute | solution.py:327
  25.6 6.3 %collective-permute-done.1.refs_2_ = bf16[80,768]{1,0:T(8,128)(2,1)S(1)} collective-permute-done((bf16[80,768]{1,0:T(8,128)(2,1)S(1)}, bf16[80,768]{1,0:T(8,128)(2,1)S(1)}, u32[]{:S(2)}, u32[]{:S(2)}) %collective-permute-start.1) | collective-permute-done | bytes 122912 | tf_op jit(solution)/shard_map/ppermute | solution.py:327
  31.9 0.5 collective-permute-done.2.refs_3_
  32.4 0.0 copy-done
  32.4 0.7 %collective-permute-start.4 = (bf16[272,768]{1,0:T(8,128)(2,1)S(1)}, bf16[272,768]{1,0:T(8,128)(2,1)S(1)}, u32[]{:S(2)}, u32[]{:S(2)}) collective-permute-start(bf16[272,768]{1,0:T(8,128)(2,1)S(1)} %shard_map.39.refs_0_), channel_id=1, source_target_pairs={{0,1},{5,6},{8,9},{13,14},{16,17},{21,22},{24,25},{29,30}} | collective-permute-start | bytes 1253384 | tf_op jit(solution)/shard_map/ppermute | solution.py:352
  33.1 1.4 %collective-permute-start.3 = (bf16[272,768]{1,0:T(8,128)(2,1)S(1)}, bf16[272,768]{1,0:T(8,128)(2,1)S(1)}, u32[]{:S(2)}, u32[]{:S(2)}) collective-permute-start(bf16[272,768]{1,0:T(8,128)(2,1)S(1)} %shard_map.39.refs_0_), channel_id=1, source_target_pairs={{3,1},{4,6},{11,9},{12,14},{19,17},{20,22},{27,25},{28,30}} | collective-permute-start | bytes 1253384 | tf_op jit(solution)/shard_map/ppermute | solution.py:352
  34.5 0.7 %collective-permute-start.5 = (bf16[272,768]{1,0:T(8,128)(2,1)S(1)}, bf16[272,768]{1,0:T(8,128)(2,1)S(1)}, u32[]{:S(2)}, u32[]{:S(2)}) collective-permute-start(bf16[272,768]{1,0:T(8,128)(2,1)S(1)} %shard_map.39.refs_0_), channel_id=1, source_target_pairs={{2,1},{7,6},{10,9},{15,14},{18,17},{23,22},{26,25},{31,30}} | collective-permute-start | bytes 1253384 | tf_op jit(solution)/shard_map/ppermute | solution.py:352
  35.2 0.0 collective-permute-done.4.refs_2_
  35.2 6.5 %collective-permute-done.3.refs_1_ = bf16[272,768]{1,0:T(8,128)(2,1)S(1)} collective-permute-done((bf16[272,768]{1,0:T(8,128)(2,1)S(1)}, bf16[272,768]{1,0:T(8,128)(2,1)S(1)}, u32[]{:S(2)}, u32[]{:S(2)}) %collective-permute-start.3) | collective-permute-done | bytes 417824 | tf_op jit(solution)/shard_map/ppermute | solution.py:352
  41.7 1.3 %shard_map.40.best_ref = f32[1,768]{1,0:T(1,128)S(1)} custom-call(bf16[272,768]{1,0:T(8,128)(2,1)S(1)} %shard_map.39.refs_0_, bf16[272,768]{1,0:T(8,128)(2,1)S(1)} %collective-permute-done.3.refs_1_, bf16[272,768]{1,0:T(8,128)(2,1)S(1)} %collective-permute-done.4.refs_2_), custom_call_target="tpu_custom_call" | custom-call | flops 905969664 | bytes 2097152 | tf_op jit(solution)/shard_map/pallas_call | solution.py:360
  43.0 3.4 %all-to-all-done.got_ref = bf16[16,296,128]{2,1,0:T(8,128)(2,1)S(1)} async-done(((bf16[16,296,128]{2,1,0:T(8,128)(2,1)}), bf16[16,296,128]{2,1,0:T(8,128)(2,1)S(1)}, u32[]{:S(2)}, u32[]{:S(2)}) %all-to-all-start) | async-done | bytes 1212448 | tf_op jit(solution)/shard_map/all_to_all | solution.py:340
  46.4 1.5 %shard_map.38.small_ref = f32[32,128]{1,0:T(8,128)S(1)} custom-call(s32[1]{0:T(128)} %bitcast.1.blk_at, bf16[16,296,128]{2,1,0:T(8,128)(2,1)S(1)} %all-to-all-done.got_ref), custom_call_target="tpu_custom_call" | custom-call | flops 905969664 | bytes 2097152 | tf_op jit(solution)/shard_map/pallas_call | solution.py:354
  47.8 0.0 copy-start.1
  47.8 0.0 collective-permute-done.5.refs_3_
  47.8 1.3 %shard_map.41 = (f32[8,128]{1,0:T(8,128)S(1)}, f32[8,128]{1,0:T(8,128)S(1)}, f32[8,128]{1,0:T(8,128)S(1)}, f32[8,128]{1,0:T(8,128)S(1)}) custom-call(s32[1]{0:T(128)} %bitcast.docs_at.at_ref, f32[32,128]{1,0:T(8,128)S(1)} %shard_map.38.small_ref, f32[1,768]{1,0:T(1,128)S(1)} %shard_map.40.best_ref, bf16[272,768]{1,0:T(8,128)(2,1)S(1)} %shard_map.39.refs_0_, ...), custom_call_target="tpu_custom_call" | custom-call | flops 704643072 | bytes 2097152 | tf_op jit(solution)/shard_map/pallas_call | solution.py:365
  49.2 4.0 %collective-permute-start.6 = (f32[8,128]{1,0:T(8,128)S(1)}, f32[8,128]{1,0:T(8,128)S(1)}, u32[]{:S(2)}, u32[]{:S(2)}) collective-permute-start(f32[8,128]{1,0:T(8,128)S(1)} %get-tuple-element.27), channel_id=1, source_target_pairs={{0,1},{1,2},{2,3},{3,0},{4,5},{5,6},{6,7},{7,4},{8,9},{9,10},{10,1... | collective-permute-start | bytes 12296 | tf_op jit(solution)/shard_map/ppermute | solution.py:327
  53.2 1.7 %collective-permute-start.7 = (f32[8,128]{1,0:T(8,128)S(1)}, f32[8,128]{1,0:T(8,128)S(1)}, u32[]{:S(2)}, u32[]{:S(2)}) collective-permute-start(f32[8,128]{1,0:T(8,128)S(1)} %get-tuple-element.28), channel_id=1, source_target_pairs={{0,2},{1,3},{2,0},{3,1},{4,6},{5,7},{6,4},{7,5},{8,10},{9,11},{10,... | collective-permute-start | bytes 12296 | tf_op jit(solution)/shard_map/ppermute | solution.py:327
  54.9 2.3 %collective-permute-start.8 = (f32[8,128]{1,0:T(8,128)S(1)}, f32[8,128]{1,0:T(8,128)S(1)}, u32[]{:S(2)}, u32[]{:S(2)}) collective-permute-start(f32[8,128]{1,0:T(8,128)S(1)} %get-tuple-element.29), channel_id=1, source_target_pairs={{0,3},{1,0},{2,1},{3,2},{4,7},{5,4},{6,5},{7,6},{8,11},{9,8},{10,9... | collective-permute-start | bytes 12296 | tf_op jit(solution)/shard_map/ppermute | solution.py:327
  57.2 0.0 collective-permute-done.6.refs_1_
  57.2 0.0 collective-permute-done.7.refs_2_
  57.2 0.7 %collective-permute-done.8.refs_3_ = f32[8,128]{1,0:T(8,128)S(1)} collective-permute-done((f32[8,128]{1,0:T(8,128)S(1)}, f32[8,128]{1,0:T(8,128)S(1)}, u32[]{:S(2)}, u32[]{:S(2)}) %collective-permute-start.8) | collective-permute-done | bytes 4128 | tf_op jit(solution)/shard_map/ppermute | solution.py:327
  58.0 0.9 %collective-permute-start.9 = (f32[8,128]{1,0:T(8,128)S(1)}, f32[8,128]{1,0:T(8,128)S(1)}, u32[]{:S(2)}, u32[]{:S(2)}) collective-permute-start(f32[8,128]{1,0:T(8,128)S(1)} %get-tuple-element.31), channel_id=1, source_target_pairs={{0,4},{4,8},{8,12},{12,0},{1,5},{5,9},{9,13},{13,1},{2,6},{6,10},{... | collective-permute-start | bytes 12296 | tf_op jit(solution)/shard_map/ppermute | solution.py:327
  58.8 0.7 %collective-permute-start.10 = (f32[8,128]{1,0:T(8,128)S(1)}, f32[8,128]{1,0:T(8,128)S(1)}, u32[]{:S(2)}, u32[]{:S(2)}) collective-permute-start(f32[8,128]{1,0:T(8,128)S(1)} %get-tuple-element.32), channel_id=1, source_target_pairs={{0,8},{4,12},{8,0},{12,4},{1,9},{5,13},{9,1},{13,5},{2,10},{6,14},... | collective-permute-start | bytes 12296 | tf_op jit(solution)/shard_map/ppermute | solution.py:327
  59.5 0.7 %collective-permute-start.11 = (f32[8,128]{1,0:T(8,128)S(1)}, f32[8,128]{1,0:T(8,128)S(1)}, u32[]{:S(2)}, u32[]{:S(2)}) collective-permute-start(f32[8,128]{1,0:T(8,128)S(1)} %get-tuple-element.33), channel_id=1, source_target_pairs={{0,12},{4,0},{8,4},{12,8},{1,13},{5,1},{9,5},{13,9},{2,14},{6,2},{... | collective-permute-start | bytes 12296 | tf_op jit(solution)/shard_map/ppermute | solution.py:327
  60.2 0.0 copy-done.1
  60.3 0.0 collective-permute-done.9.refs_1_
  60.3 1.0 %collective-permute-done.10.refs_2_ = f32[8,128]{1,0:T(8,128)S(1)} collective-permute-done((f32[8,128]{1,0:T(8,128)S(1)}, f32[8,128]{1,0:T(8,128)S(1)}, u32[]{:S(2)}, u32[]{:S(2)}) %collective-permute-start.10) | collective-permute-done | bytes 4128 | tf_op jit(solution)/shard_map/ppermute | solution.py:327
  61.3 1.2 %collective-permute-done.11.refs_3_ = f32[8,128]{1,0:T(8,128)S(1)} collective-permute-done((f32[8,128]{1,0:T(8,128)S(1)}, f32[8,128]{1,0:T(8,128)S(1)}, u32[]{:S(2)}, u32[]{:S(2)}) %collective-permute-start.11) | collective-permute-done | bytes 4128 | tf_op jit(solution)/shard_map/ppermute | solution.py:327
  62.5 0.8 %shard_map.44 = f32[1,512]{1,0:T(1,128)} custom-call(f32[8,128]{1,0:T(8,128)S(1)} %get-tuple-element.30.refs_0_, f32[8,128]{1,0:T(8,128)S(1)} %collective-permute-done.9.refs_1_, f32[8,128]{1,0:T(8,128)S(1)} %collective-permute-done.10.refs_2_, f32[8,128]{1,0:T(8,128)S(1)} %collective-permute-done.11.refs_3_, bf16[96,512]{1,0:T(8,128)(2,1)S(1)} %get-tuple-element.35.refs_4_, ...), custom_call_target="tpu_custom_call" | custom-call | flops 6291456 | bytes 262144 | tf_op jit(solution)/shard_map/pallas_call | solution.py:383
  (3 shorter events, 0.1 us)
Async XLA Ops:
  4.6 7.5 %copy-start.4 = (bf16[80,768]{1,0:T(8,128)(2,1)S(1)}, bf16[80,768]{1,0:T(8,128)(2,1)}, u32[]{:S(2)}) copy-start(bf16[80,768]{1,0:T(8,128)(2,1)} %get-tuple-element.23) | copy-start | bytes 368644
  4.6 9.2 %copy-start.3 = (bf16[80,768]{1,0:T(8,128)(2,1)S(1)}, bf16[80,768]{1,0:T(8,128)(2,1)}, u32[]{:S(2)}) copy-start(bf16[80,768]{1,0:T(8,128)(2,1)} %get-tuple-element.24) | copy-start | bytes 368644
  4.6 9.2 %copy-start.2 = (bf16[80,768]{1,0:T(8,128)(2,1)S(1)}, bf16[80,768]{1,0:T(8,128)(2,1)}, u32[]{:S(2)}) copy-start(bf16[80,768]{1,0:T(8,128)(2,1)} %get-tuple-element.25) | copy-start | bytes 368644
  4.6 27.8 %copy-start = (bf16[80,768]{1,0:T(8,128)(2,1)S(1)}, bf16[80,768]{1,0:T(8,128)(2,1)}, u32[]{:S(2)}) copy-start(bf16[80,768]{1,0:T(8,128)(2,1)} %get-tuple-element.22.refs_0_) | copy-start | bytes 368644
  4.7 41.7 %all-to-all-start = ((bf16[16,296,128]{2,1,0:T(8,128)(2,1)}), bf16[16,296,128]{2,1,0:T(8,128)(2,1)S(1)}, u32[]{:S(2)}, u32[]{:S(2)}) async-start(bf16[16,296,128]{2,1,0:T(8,128)(2,1)} %get-tuple-element.21), calls=%async_computation | async-start | bytes 2424832 | tf_op jit(solution)/shard_map/all_to_all | solution.py:340
  12.1 13.5 %collective-permute-start = (bf16[80,768]{1,0:T(8,128)(2,1)S(1)}, bf16[80,768]{1,0:T(8,128)(2,1)S(1)}, u32[]{:S(2)}, u32[]{:S(2)}) collective-permute-start(bf16[80,768]{1,0:T(8,128)(2,1)S(1)} %copy-done.4), channel_id=1, source_target_pairs={{0,4},{4,8},{8,12},{12,0},{1,5},{5,9},{9,13},{13,1},{2,6},{6,10},{... | collective-permute-start | bytes 368648 | tf_op jit(solution)/shard_map/ppermute | solution.py:327
  13.8 18.1 %collective-permute-start.1 = (bf16[80,768]{1,0:T(8,128)(2,1)S(1)}, bf16[80,768]{1,0:T(8,128)(2,1)S(1)}, u32[]{:S(2)}, u32[]{:S(2)}) collective-permute-start(bf16[80,768]{1,0:T(8,128)(2,1)S(1)} %copy-done.3), channel_id=1, source_target_pairs={{0,8},{4,12},{8,0},{12,4},{1,9},{5,13},{9,1},{13,5},{2,10},{6,14},... | collective-permute-start | bytes 368648 | tf_op jit(solution)/shard_map/ppermute | solution.py:327
  13.8 18.6 %collective-permute-start.2 = (bf16[80,768]{1,0:T(8,128)(2,1)S(1)}, bf16[80,768]{1,0:T(8,128)(2,1)S(1)}, u32[]{:S(2)}, u32[]{:S(2)}) collective-permute-start(bf16[80,768]{1,0:T(8,128)(2,1)S(1)} %copy-done.2), channel_id=1, source_target_pairs={{0,12},{4,0},{8,4},{12,8},{1,13},{5,1},{9,5},{13,9},{2,14},{6,2},{... | collective-permute-start | bytes 368648 | tf_op jit(solution)/shard_map/ppermute | solution.py:327
  32.4 2.8 %collective-permute-start.4 = (bf16[272,768]{1,0:T(8,128)(2,1)S(1)}, bf16[272,768]{1,0:T(8,128)(2,1)S(1)}, u32[]{:S(2)}, u32[]{:S(2)}) collective-permute-start(bf16[272,768]{1,0:T(8,128)(2,1)S(1)} %shard_map.39.refs_0_), channel_id=1, source_target_pairs={{0,1},{5,6},{8,9},{13,14},{16,17},{21,22},{24,25},{29,30}} | collective-permute-start | bytes 1253384 | tf_op jit(solution)/shard_map/ppermute | solution.py:352
  33.1 8.5 %collective-permute-start.3 = (bf16[272,768]{1,0:T(8,128)(2,1)S(1)}, bf16[272,768]{1,0:T(8,128)(2,1)S(1)}, u32[]{:S(2)}, u32[]{:S(2)}) collective-permute-start(bf16[272,768]{1,0:T(8,128)(2,1)S(1)} %shard_map.39.refs_0_), channel_id=1, source_target_pairs={{3,1},{4,6},{11,9},{12,14},{19,17},{20,22},{27,25},{28,30}} | collective-permute-start | bytes 1253384 | tf_op jit(solution)/shard_map/ppermute | solution.py:352
  34.5 13.3 %collective-permute-start.5 = (bf16[272,768]{1,0:T(8,128)(2,1)S(1)}, bf16[272,768]{1,0:T(8,128)(2,1)S(1)}, u32[]{:S(2)}, u32[]{:S(2)}) collective-permute-start(bf16[272,768]{1,0:T(8,128)(2,1)S(1)} %shard_map.39.refs_0_), channel_id=1, source_target_pairs={{2,1},{7,6},{10,9},{15,14},{18,17},{23,22},{26,25},{31,30}} | collective-permute-start | bytes 1253384 | tf_op jit(solution)/shard_map/ppermute | solution.py:352
  47.8 12.4 %copy-start.1 = (s32[8,512]{1,0:T(8,128)S(1)}, s32[8,512]{1,0:T(8,128)}, u32[]{:S(2)}) copy-start(s32[8,512]{1,0:T(8,128)} %get-tuple-element.34.info_ref) | copy-start | bytes 49156
  49.2 8.0 %collective-permute-start.6 = (f32[8,128]{1,0:T(8,128)S(1)}, f32[8,128]{1,0:T(8,128)S(1)}, u32[]{:S(2)}, u32[]{:S(2)}) collective-permute-start(f32[8,128]{1,0:T(8,128)S(1)} %get-tuple-element.27), channel_id=1, source_target_pairs={{0,1},{1,2},{2,3},{3,0},{4,5},{5,6},{6,7},{7,4},{8,9},{9,10},{10,1... | collective-permute-start | bytes 12296 | tf_op jit(solution)/shard_map/ppermute | solution.py:327
  53.2 4.0 %collective-permute-start.7 = (f32[8,128]{1,0:T(8,128)S(1)}, f32[8,128]{1,0:T(8,128)S(1)}, u32[]{:S(2)}, u32[]{:S(2)}) collective-permute-start(f32[8,128]{1,0:T(8,128)S(1)} %get-tuple-element.28), channel_id=1, source_target_pairs={{0,2},{1,3},{2,0},{3,1},{4,6},{5,7},{6,4},{7,5},{8,10},{9,11},{10,... | collective-permute-start | bytes 12296 | tf_op jit(solution)/shard_map/ppermute | solution.py:327
  54.9 3.0 %collective-permute-start.8 = (f32[8,128]{1,0:T(8,128)S(1)}, f32[8,128]{1,0:T(8,128)S(1)}, u32[]{:S(2)}, u32[]{:S(2)}) collective-permute-start(f32[8,128]{1,0:T(8,128)S(1)} %get-tuple-element.29), channel_id=1, source_target_pairs={{0,3},{1,0},{2,1},{3,2},{4,7},{5,4},{6,5},{7,6},{8,11},{9,8},{10,9... | collective-permute-start | bytes 12296 | tf_op jit(solution)/shard_map/ppermute | solution.py:327
  58.0 2.3 %collective-permute-start.9 = (f32[8,128]{1,0:T(8,128)S(1)}, f32[8,128]{1,0:T(8,128)S(1)}, u32[]{:S(2)}, u32[]{:S(2)}) collective-permute-start(f32[8,128]{1,0:T(8,128)S(1)} %get-tuple-element.31), channel_id=1, source_target_pairs={{0,4},{4,8},{8,12},{12,0},{1,5},{5,9},{9,13},{13,1},{2,6},{6,10},{... | collective-permute-start | bytes 12296 | tf_op jit(solution)/shard_map/ppermute | solution.py:327
  58.8 2.5 %collective-permute-start.10 = (f32[8,128]{1,0:T(8,128)S(1)}, f32[8,128]{1,0:T(8,128)S(1)}, u32[]{:S(2)}, u32[]{:S(2)}) collective-permute-start(f32[8,128]{1,0:T(8,128)S(1)} %get-tuple-element.32), channel_id=1, source_target_pairs={{0,8},{4,12},{8,0},{12,4},{1,9},{5,13},{9,1},{13,5},{2,10},{6,14},... | collective-permute-start | bytes 12296 | tf_op jit(solution)/shard_map/ppermute | solution.py:327
  59.5 3.0 %collective-permute-start.11 = (f32[8,128]{1,0:T(8,128)S(1)}, f32[8,128]{1,0:T(8,128)S(1)}, u32[]{:S(2)}, u32[]{:S(2)}) collective-permute-start(f32[8,128]{1,0:T(8,128)S(1)} %get-tuple-element.33), channel_id=1, source_target_pairs={{0,12},{4,0},{8,4},{12,8},{1,13},{5,1},{9,5},{13,9},{2,14},{6,2},{... | collective-permute-start | bytes 12296 | tf_op jit(solution)/shard_map/ppermute | solution.py:327

commit v18 on v13

--- a/solution.py
+++ b/solution.py
@@ -163,7 +163,7 @@
 
 
 def big_steps(blocks):
-    return [0] + list(range(2, blocks)) + ([1] if blocks > 1 else [])
+    return [step for step in range(blocks) if step != blocks // 2] + ([blocks // 2] if blocks > 1 else [])
 
 
 def big_sources(total, shards, cap_big, cap_small):
@@ -245,7 +245,7 @@
     bests = [best_ref[:, col * size:(col + 1) * size] for col in range(last)]
     bests = big_pairs(held, row_ids, col_ids, bests + [jnp.full((1, size), -1.0, jnp.float32)], pairs)
     docs = modulo(docs_at[0] + shards - shift, shards)
-    step = jnp.where(part == 0, 0, jnp.where(part == last, 1, part + 1))
+    step = jnp.where(part == last, blocks // 2, jnp.where(part < blocks // 2, part, part + 1))
     back = small_ref[...] + spread(jnp.concatenate(bests, axis=1), step * high + docs, lane, small_ref.shape[0])
     for at, ref in enumerate(back_refs):
         ref[...] = back[at * high:(at + 1) * high, :]

time: 63.5 us -> 65.9 us (1.038)
  starting transfers between devices: 22.7 us -> 26.3 us
  waiting for transfers between devices: 30.9 us -> 29.7 us
    ppermute x3, waiting for transfers between devices: 6.47 us -> 0.01 us  [body(): parts.append(lax.ppermute(group, ('docs', 'blk'), pairs))]
    all_to_all x1, waiting for transfers between devices: 3.41 us -> 8.16 us  [body(): lax.all_to_all(small_sent, ('docs', 'blk'), split_axis=0, concat_axis=0,...]
    ppermute x9, starting transfers between devices: 12.5 us -> 15.4 us  [along(): return lax.ppermute(x, axis, [(i, (i + by) % count) for i in range(count)])]
where the time goes in v18:
time: 65.9 us; the launch traced here: 65.7 us
  waiting for transfers between devices  29.7 us (45%)
  starting transfers between devices  26.3 us (40%)
  Pallas kernels  9.5 us (14%)
    ppermute x9, waiting for transfers between devices, along(): return lax.ppermute(x, axis, [(i, (i + by) % count) for i in range(count)])  21.6 us
    ppermute x9, starting transfers between devices, along(): return lax.ppermute(x, axis, [(i, (i + by) % count) for i in range(count)])  15.4 us
    all_to_all x1, waiting for transfers between devices, body(): lax.all_to_all(small_sent, ('docs', 'blk'), split_axis=0, concat_axis=0,...  8.16 us
    all_to_all x1, starting transfers between devices, body(): lax.all_to_all(small_sent, ('docs', 'blk'), split_axis=0, concat_axis=0,...  7.47 us
    pallas_call x1, Pallas kernels, body(): call(functools.partial(sort_kernel, *sizes), [((devices, small_rows, LANE...  4.54 us
    ppermute x3, starting transfers between devices, body(): parts.append(lax.ppermute(group, ('docs', 'blk'), pairs))  3.35 us
    pallas_call x1, Pallas kernels, body(): call(functools.partial(small_kernel, shards, blocks, cap_small), [((block...  1.47 us
    pallas_call x1, Pallas kernels, body(): call(functools.partial(big_last_kernel, *sizes), [((rows_up(shards), LANE...  1.33 us
  transfers between devices with their start and end apart: 13, of which 8 were waited for; matrix products, arithmetic and copies ran while one was open for 0% of the time, Pallas kernels for 4%

profile of v18, /device:TPU:1, one launch (start us, length us, event | category | flops | bytes accessed | tf_op | source)
XLA Modules:
  0.0 65.7 jit_solution(3892566650792297123)
XLA Ops:
  0.0 4.5 %shard_map.37 = (bf16[16,296,128]{2,1,0:T(8,128)(2,1)}, s32[8,512]{1,0:T(8,128)}, bf16[80,768]{1,0:T(8,128)(2,1)}, bf16[80,768]{1,0:T(8,128)(2,1)}, bf16[80,768]{1,0:T(8,128)(2,1)}, /*index=5*/bf16[80,768]{1,0:T(8,128)(2,1)}) custom-call(s32[1]{0:T(128)} %bitcast.docs_at.at_ref, bf16[512,768]{1,0:T(8,128)(2,1)} %pooled_hbm.1, bf16[768,768]{1,0:T(8,128)(2,1)} %weight_hbm.1, ...), custom_call_target="tpu_custom_call" | custom-call | flops 1207959552 | bytes 4194304 | tf_op jit(solution)/shard_map/pallas_call | solution.py:330
  4.5 0.0 copy-start.4
  4.6 0.0 copy-start.3
  4.6 0.0 copy-start.2
  4.6 0.0 copy-start
  4.6 7.5 %all-to-all-start = ((bf16[16,296,128]{2,1,0:T(8,128)(2,1)}), bf16[16,296,128]{2,1,0:T(8,128)(2,1)S(1)}, u32[]{:S(2)}, u32[]{:S(2)}) async-start(bf16[16,296,128]{2,1,0:T(8,128)(2,1)} %get-tuple-element.21), calls=%async_computation | async-start | bytes 2424832 | tf_op jit(solution)/shard_map/all_to_all | solution.py:340
  12.1 0.0 copy-done.4
  12.1 1.7 %collective-permute-start = (bf16[80,768]{1,0:T(8,128)(2,1)S(1)}, bf16[80,768]{1,0:T(8,128)(2,1)S(1)}, u32[]{:S(2)}, u32[]{:S(2)}) collective-permute-start(bf16[80,768]{1,0:T(8,128)(2,1)S(1)} %copy-done.4), channel_id=1, source_target_pairs={{0,4},{4,8},{8,12},{12,0},{1,5},{5,9},{9,13},{13,1},{2,6},{6,10},{... | collective-permute-start | bytes 368648 | tf_op jit(solution)/shard_map/ppermute | solution.py:327
  13.7 0.0 copy-done.3
  13.7 0.0 collective-permute-start.1
  13.7 0.0 copy-done.2
  13.8 0.5 collective-permute-start.2
  14.3 11.3 %collective-permute-done.refs_1_ = bf16[80,768]{1,0:T(8,128)(2,1)S(1)} collective-permute-done((bf16[80,768]{1,0:T(8,128)(2,1)S(1)}, bf16[80,768]{1,0:T(8,128)(2,1)S(1)}, u32[]{:S(2)}, u32[]{:S(2)}) %collective-permute-start) | collective-permute-done | bytes 122912 | tf_op jit(solution)/shard_map/ppermute | solution.py:327
  25.5 6.3 %collective-permute-done.1.refs_2_ = bf16[80,768]{1,0:T(8,128)(2,1)S(1)} collective-permute-done((bf16[80,768]{1,0:T(8,128)(2,1)S(1)}, bf16[80,768]{1,0:T(8,128)(2,1)S(1)}, u32[]{:S(2)}, u32[]{:S(2)}) %collective-permute-start.1) | collective-permute-done | bytes 122912 | tf_op jit(solution)/shard_map/ppermute | solution.py:327
  31.9 0.5 collective-permute-done.2.refs_3_
  32.3 0.0 copy-done
  32.4 0.7 %collective-permute-start.4 = (bf16[272,768]{1,0:T(8,128)(2,1)S(1)}, bf16[272,768]{1,0:T(8,128)(2,1)S(1)}, u32[]{:S(2)}, u32[]{:S(2)}) collective-permute-start(bf16[272,768]{1,0:T(8,128)(2,1)S(1)} %shard_map.39.refs_0_), channel_id=1, source_target_pairs={{0,1},{5,6},{8,9},{13,14},{16,17},{21,22},{24,25},{29,30}} | collective-permute-start | bytes 1253384 | tf_op jit(solution)/shard_map/ppermute | solution.py:352
  33.1 0.7 %collective-permute-start.3 = (bf16[272,768]{1,0:T(8,128)(2,1)S(1)}, bf16[272,768]{1,0:T(8,128)(2,1)S(1)}, u32[]{:S(2)}, u32[]{:S(2)}) collective-permute-start(bf16[272,768]{1,0:T(8,128)(2,1)S(1)} %shard_map.39.refs_0_), channel_id=1, source_target_pairs={{2,1},{7,6},{10,9},{15,14},{18,17},{23,22},{26,25},{31,30}} | collective-permute-start | bytes 1253384 | tf_op jit(solution)/shard_map/ppermute | solution.py:352
  33.8 2.0 %collective-permute-start.5 = (bf16[272,768]{1,0:T(8,128)(2,1)S(1)}, bf16[272,768]{1,0:T(8,128)(2,1)S(1)}, u32[]{:S(2)}, u32[]{:S(2)}) collective-permute-start(bf16[272,768]{1,0:T(8,128)(2,1)S(1)} %shard_map.39.refs_0_), channel_id=1, source_target_pairs={{3,1},{4,6},{11,9},{12,14},{19,17},{20,22},{27,25},{28,30}} | collective-permute-start | bytes 1253384 | tf_op jit(solution)/shard_map/ppermute | solution.py:352
  35.7 0.0 collective-permute-done.4.refs_2_
  35.7 0.0 collective-permute-done.3.refs_1_
  35.8 1.3 %shard_map.40.best_ref = f32[1,768]{1,0:T(1,128)S(1)} custom-call(bf16[272,768]{1,0:T(8,128)(2,1)S(1)} %shard_map.39.refs_0_, bf16[272,768]{1,0:T(8,128)(2,1)S(1)} %collective-permute-done.3.refs_1_, bf16[272,768]{1,0:T(8,128)(2,1)S(1)} %collective-permute-done.4.refs_2_), custom_call_target="tpu_custom_call" | custom-call | flops 905969664 | bytes 2097152 | tf_op jit(solution)/shard_map/pallas_call | solution.py:360
  37.0 8.2 %all-to-all-done.got_ref = bf16[16,296,128]{2,1,0:T(8,128)(2,1)S(1)} async-done(((bf16[16,296,128]{2,1,0:T(8,128)(2,1)}), bf16[16,296,128]{2,1,0:T(8,128)(2,1)S(1)}, u32[]{:S(2)}, u32[]{:S(2)}) %all-to-all-start) | async-done | bytes 1212448 | tf_op jit(solution)/shard_map/all_to_all | solution.py:340
  45.2 1.5 %shard_map.38.small_ref = f32[32,128]{1,0:T(8,128)S(1)} custom-call(s32[1]{0:T(128)} %bitcast.1.blk_at, bf16[16,296,128]{2,1,0:T(8,128)(2,1)S(1)} %all-to-all-done.got_ref), custom_call_target="tpu_custom_call" | custom-call | flops 905969664 | bytes 2097152 | tf_op jit(solution)/shard_map/pallas_call | solution.py:354
  46.7 0.0 copy-start.1
  46.7 0.0 collective-permute-done.5.refs_3_
  46.7 1.3 %shard_map.41 = (f32[8,128]{1,0:T(8,128)S(1)}, f32[8,128]{1,0:T(8,128)S(1)}, f32[8,128]{1,0:T(8,128)S(1)}, f32[8,128]{1,0:T(8,128)S(1)}) custom-call(s32[1]{0:T(128)} %bitcast.docs_at.at_ref, f32[32,128]{1,0:T(8,128)S(1)} %shard_map.38.small_ref, f32[1,768]{1,0:T(1,128)S(1)} %shard_map.40.best_ref, bf16[272,768]{1,0:T(8,128)(2,1)S(1)} %shard_map.39.refs_0_, ...), custom_call_target="tpu_custom_call" | custom-call | flops 704643072 | bytes 2097152 | tf_op jit(solution)/shard_map/pallas_call | solution.py:365
  48.0 5.1 %collective-permute-start.6 = (f32[8,128]{1,0:T(8,128)S(1)}, f32[8,128]{1,0:T(8,128)S(1)}, u32[]{:S(2)}, u32[]{:S(2)}) collective-permute-start(f32[8,128]{1,0:T(8,128)S(1)} %get-tuple-element.27), channel_id=1, source_target_pairs={{0,1},{1,2},{2,3},{3,0},{4,5},{5,6},{6,7},{7,4},{8,9},{9,10},{10,1... | collective-permute-start | bytes 12296 | tf_op jit(solution)/shard_map/ppermute | solution.py:327
  53.1 1.7 %collective-permute-start.7 = (f32[8,128]{1,0:T(8,128)S(1)}, f32[8,128]{1,0:T(8,128)S(1)}, u32[]{:S(2)}, u32[]{:S(2)}) collective-permute-start(f32[8,128]{1,0:T(8,128)S(1)} %get-tuple-element.28), channel_id=1, source_target_pairs={{0,2},{1,3},{2,0},{3,1},{4,6},{5,7},{6,4},{7,5},{8,10},{9,11},{10,... | collective-permute-start | bytes 12296 | tf_op jit(solution)/shard_map/ppermute | solution.py:327
  54.8 2.3 %collective-permute-start.8 = (f32[8,128]{1,0:T(8,128)S(1)}, f32[8,128]{1,0:T(8,128)S(1)}, u32[]{:S(2)}, u32[]{:S(2)}) collective-permute-start(f32[8,128]{1,0:T(8,128)S(1)} %get-tuple-element.29), channel_id=1, source_target_pairs={{0,3},{1,0},{2,1},{3,2},{4,7},{5,4},{6,5},{7,6},{8,11},{9,8},{10,9... | collective-permute-start | bytes 12296 | tf_op jit(solution)/shard_map/ppermute | solution.py:327
  57.1 0.0 collective-permute-done.6.refs_1_
  57.1 0.0 collective-permute-done.7.refs_2_
  57.1 0.7 %collective-permute-done.8.refs_3_ = f32[8,128]{1,0:T(8,128)S(1)} collective-permute-done((f32[8,128]{1,0:T(8,128)S(1)}, f32[8,128]{1,0:T(8,128)S(1)}, u32[]{:S(2)}, u32[]{:S(2)}) %collective-permute-start.8) | collective-permute-done | bytes 4128 | tf_op jit(solution)/shard_map/ppermute | solution.py:327
  57.9 3.6 %collective-permute-start.9 = (f32[8,128]{1,0:T(8,128)S(1)}, f32[8,128]{1,0:T(8,128)S(1)}, u32[]{:S(2)}, u32[]{:S(2)}) collective-permute-start(f32[8,128]{1,0:T(8,128)S(1)} %get-tuple-element.31), channel_id=1, source_target_pairs={{0,4},{4,8},{8,12},{12,0},{1,5},{5,9},{9,13},{13,1},{2,6},{6,10},{... | collective-permute-start | bytes 12296 | tf_op jit(solution)/shard_map/ppermute | solution.py:327
  61.6 0.3 collective-permute-start.10
  61.8 0.2 collective-permute-start.11
  62.0 0.0 copy-done.1
  62.1 0.2 collective-permute-done.9.refs_1_
  62.3 1.7 %collective-permute-done.10.refs_2_ = f32[8,128]{1,0:T(8,128)S(1)} collective-permute-done((f32[8,128]{1,0:T(8,128)S(1)}, f32[8,128]{1,0:T(8,128)S(1)}, u32[]{:S(2)}, u32[]{:S(2)}) %collective-permute-start.10) | collective-permute-done | bytes 4128 | tf_op jit(solution)/shard_map/ppermute | solution.py:327
  64.0 0.8 %collective-permute-done.11.refs_3_ = f32[8,128]{1,0:T(8,128)S(1)} collective-permute-done((f32[8,128]{1,0:T(8,128)S(1)}, f32[8,128]{1,0:T(8,128)S(1)}, u32[]{:S(2)}, u32[]{:S(2)}) %collective-permute-start.11) | collective-permute-done | bytes 4128 | tf_op jit(solution)/shard_map/ppermute | solution.py:327
  64.9 0.8 %shard_map.44 = f32[1,512]{1,0:T(1,128)} custom-call(f32[8,128]{1,0:T(8,128)S(1)} %get-tuple-element.30.refs_0_, f32[8,128]{1,0:T(8,128)S(1)} %collective-permute-done.9.refs_1_, f32[8,128]{1,0:T(8,128)S(1)} %collective-permute-done.10.refs_2_, f32[8,128]{1,0:T(8,128)S(1)} %collective-permute-done.11.refs_3_, bf16[96,512]{1,0:T(8,128)(2,1)S(1)} %get-tuple-element.35.refs_4_, ...), custom_call_target="tpu_custom_call" | custom-call | flops 6291456 | bytes 262144 | tf_op jit(solution)/shard_map/pallas_call | solution.py:383
  (3 shorter events, 0.1 us)
Async XLA Ops:
  4.5 7.5 %copy-start.4 = (bf16[80,768]{1,0:T(8,128)(2,1)S(1)}, bf16[80,768]{1,0:T(8,128)(2,1)}, u32[]{:S(2)}) copy-start(bf16[80,768]{1,0:T(8,128)(2,1)} %get-tuple-element.23) | copy-start | bytes 368644
  4.6 9.2 %copy-start.3 = (bf16[80,768]{1,0:T(8,128)(2,1)S(1)}, bf16[80,768]{1,0:T(8,128)(2,1)}, u32[]{:S(2)}) copy-start(bf16[80,768]{1,0:T(8,128)(2,1)} %get-tuple-element.24) | copy-start | bytes 368644
  4.6 9.2 %copy-start.2 = (bf16[80,768]{1,0:T(8,128)(2,1)S(1)}, bf16[80,768]{1,0:T(8,128)(2,1)}, u32[]{:S(2)}) copy-start(bf16[80,768]{1,0:T(8,128)(2,1)} %get-tuple-element.25) | copy-start | bytes 368644
  4.6 27.8 %copy-start = (bf16[80,768]{1,0:T(8,128)(2,1)S(1)}, bf16[80,768]{1,0:T(8,128)(2,1)}, u32[]{:S(2)}) copy-start(bf16[80,768]{1,0:T(8,128)(2,1)} %get-tuple-element.22.refs_0_) | copy-start | bytes 368644
  4.6 40.6 %all-to-all-start = ((bf16[16,296,128]{2,1,0:T(8,128)(2,1)}), bf16[16,296,128]{2,1,0:T(8,128)(2,1)S(1)}, u32[]{:S(2)}, u32[]{:S(2)}) async-start(bf16[16,296,128]{2,1,0:T(8,128)(2,1)} %get-tuple-element.21), calls=%async_computation | async-start | bytes 2424832 | tf_op jit(solution)/shard_map/all_to_all | solution.py:340
  12.1 13.5 %collective-permute-start = (bf16[80,768]{1,0:T(8,128)(2,1)S(1)}, bf16[80,768]{1,0:T(8,128)(2,1)S(1)}, u32[]{:S(2)}, u32[]{:S(2)}) collective-permute-start(bf16[80,768]{1,0:T(8,128)(2,1)S(1)} %copy-done.4), channel_id=1, source_target_pairs={{0,4},{4,8},{8,12},{12,0},{1,5},{5,9},{9,13},{13,1},{2,6},{6,10},{... | collective-permute-start | bytes 368648 | tf_op jit(solution)/shard_map/ppermute | solution.py:327
  13.7 18.1 %collective-permute-start.1 = (bf16[80,768]{1,0:T(8,128)(2,1)S(1)}, bf16[80,768]{1,0:T(8,128)(2,1)S(1)}, u32[]{:S(2)}, u32[]{:S(2)}) collective-permute-start(bf16[80,768]{1,0:T(8,128)(2,1)S(1)} %copy-done.3), channel_id=1, source_target_pairs={{0,8},{4,12},{8,0},{12,4},{1,9},{5,13},{9,1},{13,5},{2,10},{6,14},... | collective-permute-start | bytes 368648 | tf_op jit(solution)/shard_map/ppermute | solution.py:327
  13.8 18.6 %collective-permute-start.2 = (bf16[80,768]{1,0:T(8,128)(2,1)S(1)}, bf16[80,768]{1,0:T(8,128)(2,1)S(1)}, u32[]{:S(2)}, u32[]{:S(2)}) collective-permute-start(bf16[80,768]{1,0:T(8,128)(2,1)S(1)} %copy-done.2), channel_id=1, source_target_pairs={{0,12},{4,0},{8,4},{12,8},{1,13},{5,1},{9,5},{13,9},{2,14},{6,2},{... | collective-permute-start | bytes 368648 | tf_op jit(solution)/shard_map/ppermute | solution.py:327
  32.4 3.4 %collective-permute-start.4 = (bf16[272,768]{1,0:T(8,128)(2,1)S(1)}, bf16[272,768]{1,0:T(8,128)(2,1)S(1)}, u32[]{:S(2)}, u32[]{:S(2)}) collective-permute-start(bf16[272,768]{1,0:T(8,128)(2,1)S(1)} %shard_map.39.refs_0_), channel_id=1, source_target_pairs={{0,1},{5,6},{8,9},{13,14},{16,17},{21,22},{24,25},{29,30}} | collective-permute-start | bytes 1253384 | tf_op jit(solution)/shard_map/ppermute | solution.py:352
  33.1 2.7 %collective-permute-start.3 = (bf16[272,768]{1,0:T(8,128)(2,1)S(1)}, bf16[272,768]{1,0:T(8,128)(2,1)S(1)}, u32[]{:S(2)}, u32[]{:S(2)}) collective-permute-start(bf16[272,768]{1,0:T(8,128)(2,1)S(1)} %shard_map.39.refs_0_), channel_id=1, source_target_pairs={{2,1},{7,6},{10,9},{15,14},{18,17},{23,22},{26,25},{31,30}} | collective-permute-start | bytes 1253384 | tf_op jit(solution)/shard_map/ppermute | solution.py:352
  33.8 12.9 %collective-permute-start.5 = (bf16[272,768]{1,0:T(8,128)(2,1)S(1)}, bf16[272,768]{1,0:T(8,128)(2,1)S(1)}, u32[]{:S(2)}, u32[]{:S(2)}) collective-permute-start(bf16[272,768]{1,0:T(8,128)(2,1)S(1)} %shard_map.39.refs_0_), channel_id=1, source_target_pairs={{3,1},{4,6},{11,9},{12,14},{19,17},{20,22},{27,25},{28,30}} | collective-permute-start | bytes 1253384 | tf_op jit(solution)/shard_map/ppermute | solution.py:352
  46.7 15.4 %copy-start.1 = (s32[8,512]{1,0:T(8,128)S(1)}, s32[8,512]{1,0:T(8,128)}, u32[]{:S(2)}) copy-start(s32[8,512]{1,0:T(8,128)} %get-tuple-element.34.info_ref) | copy-start | bytes 49156
  48.0 9.1 %collective-permute-start.6 = (f32[8,128]{1,0:T(8,128)S(1)}, f32[8,128]{1,0:T(8,128)S(1)}, u32[]{:S(2)}, u32[]{:S(2)}) collective-permute-start(f32[8,128]{1,0:T(8,128)S(1)} %get-tuple-element.27), channel_id=1, source_target_pairs={{0,1},{1,2},{2,3},{3,0},{4,5},{5,6},{6,7},{7,4},{8,9},{9,10},{10,1... | collective-permute-start | bytes 12296 | tf_op jit(solution)/shard_map/ppermute | solution.py:327
  53.1 4.0 %collective-permute-start.7 = (f32[8,128]{1,0:T(8,128)S(1)}, f32[8,128]{1,0:T(8,128)S(1)}, u32[]{:S(2)}, u32[]{:S(2)}) collective-permute-start(f32[8,128]{1,0:T(8,128)S(1)} %get-tuple-element.28), channel_id=1, source_target_pairs={{0,2},{1,3},{2,0},{3,1},{4,6},{5,7},{6,4},{7,5},{8,10},{9,11},{10,... | collective-permute-start | bytes 12296 | tf_op jit(solution)/shard_map/ppermute | solution.py:327
  54.8 3.0 %collective-permute-start.8 = (f32[8,128]{1,0:T(8,128)S(1)}, f32[8,128]{1,0:T(8,128)S(1)}, u32[]{:S(2)}, u32[]{:S(2)}) collective-permute-start(f32[8,128]{1,0:T(8,128)S(1)} %get-tuple-element.29), channel_id=1, source_target_pairs={{0,3},{1,0},{2,1},{3,2},{4,7},{5,4},{6,5},{7,6},{8,11},{9,8},{10,9... | collective-permute-start | bytes 12296 | tf_op jit(solution)/shard_map/ppermute | solution.py:327
  57.9 4.4 %collective-permute-start.9 = (f32[8,128]{1,0:T(8,128)S(1)}, f32[8,128]{1,0:T(8,128)S(1)}, u32[]{:S(2)}, u32[]{:S(2)}) collective-permute-start(f32[8,128]{1,0:T(8,128)S(1)} %get-tuple-element.31), channel_id=1, source_target_pairs={{0,4},{4,8},{8,12},{12,0},{1,5},{5,9},{9,13},{13,1},{2,6},{6,10},{... | collective-permute-start | bytes 12296 | tf_op jit(solution)/shard_map/ppermute | solution.py:327
  61.6 2.5 %collective-permute-start.10 = (f32[8,128]{1,0:T(8,128)S(1)}, f32[8,128]{1,0:T(8,128)S(1)}, u32[]{:S(2)}, u32[]{:S(2)}) collective-permute-start(f32[8,128]{1,0:T(8,128)S(1)} %get-tuple-element.32), channel_id=1, source_target_pairs={{0,8},{4,12},{8,0},{12,4},{1,9},{5,13},{9,1},{13,5},{2,10},{6,14},... | collective-permute-start | bytes 12296 | tf_op jit(solution)/shard_map/ppermute | solution.py:327
  61.8 3.0 %collective-permute-start.11 = (f32[8,128]{1,0:T(8,128)S(1)}, f32[8,128]{1,0:T(8,128)S(1)}, u32[]{:S(2)}, u32[]{:S(2)}) collective-permute-start(f32[8,128]{1,0:T(8,128)S(1)} %get-tuple-element.33), channel_id=1, source_target_pairs={{0,12},{4,0},{8,4},{12,8},{1,13},{5,1},{9,5},{13,9},{2,14},{6,2},{... | collective-permute-start | bytes 12296 | tf_op jit(solution)/shard_map/ppermute | solution.py:327
